TPU v7x, 512 devices: a whole 4x4x16 slice. The times are simulated.
512 devices in a mesh: fsdp: 32 (over x_hi, z), seq: 16 (over y, x_lo, core).
Axes of the slice: x: 4 (x_hi: 2, x_lo: 2; x = x_hi * 2 + x_lo), y: 4, z: 16, core: 2. Of those that a mesh axis runs over, the one named last changes fastest.
Arguments:
- tokens: bfloat16 [2048, 4096], P('seq', 'fsdp'), may hold values from -6 to 6
- out_grad: bfloat16 [2048, 4096], P('seq', 'fsdp'), may hold values from -0.00390625 to 0.00390625
- loss_mask: int32 [2048], P('seq'), may hold values 0 or 1
- w_in0: bfloat16 [10240, 4096], P('fsdp', 'seq'), may hold values from -0.09375 to 0.09375
- w_in1: bfloat16 [10240, 4096], P('fsdp', 'seq'), may hold values from -0.09375 to 0.09375
- w_out: bfloat16 [10240, 4096], P('fsdp', 'seq'), may hold values from -0.0625 to 0.0625
- tan_in0: bfloat16 [2, 10240, 4096], P(None, 'fsdp', 'seq'), may hold values from -0.09375 to 0.09375
- tan_in1: bfloat16 [2, 10240, 4096], P(None, 'fsdp', 'seq'), may hold values from -0.09375 to 0.09375
- tan_out: bfloat16 [2, 10240, 4096], P(None, 'fsdp', 'seq'), may hold values from -0.0625 to 0.0625
Outputs:
- block_out: bfloat16 [2048, 4096], P('seq', 'fsdp')
- projection: float32 [4, 2], replicated
All inputs are finite; a program needn't handle non-finite values. No bound on the sum of `loss_mask` on one device may be relied on, other than what follows from the above.
Results may differ from a plain program's by a relative error of at most 0.0049.
Values may be sent and summed in bfloat16 or wider, within the bound.
No kernel may reach another device: no remote copies, remote signals or barrier semaphores. Data moves between devices by JAX's collectives and lax.ppermute only.
A program may use at most 128 MiB of HBM per device.

v0:
```python
import math

import jax
import jax.numpy as jnp
from jax import lax
from jax.sharding import PartitionSpec as P

EXAMPLES = 4


def gelu_value_slope(value):
    coeff = math.sqrt(2.0 / math.pi)
    inner = coeff * (value + 0.044715 * value * value * value)
    tangent = jnp.tanh(inner)
    act = 0.5 * value * (1.0 + tangent)
    slope = 0.5 * (1.0 + tangent) + 0.5 * value * (1.0 - tangent * tangent) * coeff * (
        1.0 + 3.0 * 0.044715 * value * value
    )
    return (act, slope)


def shards(tokens, out_grad, loss_mask, w_in0, w_in1, w_out, tan_in0, tan_in1, tan_out):
    complete_input, full_u = (
        lax.all_gather(tokens, "fsdp", axis=1, tiled=True),
        lax.all_gather(out_grad, "fsdp", axis=1, tiled=True),
    )
    rows = complete_input.shape[0]
    num_dirs = tan_in0.shape[0]

    def accumulate_upward(partial_segments):
        leading_operand = jnp.einsum(
            "jn,ztn->zjt", complete_input, partial_segments[0], preferred_element_type=jnp.float32
        )
        trailing_operand = jnp.einsum(
            "jn,ztn->zjt", complete_input, partial_segments[1], preferred_element_type=jnp.float32
        )
        return (leading_operand, trailing_operand)

    gate_list = []
    upper_list = []
    leading_operand, trailing_operand = accumulate_upward(
        (
            lax.all_gather(w_in0[None], "seq", axis=2, tiled=True),
            lax.all_gather(w_in1[None], "seq", axis=2, tiled=True),
        )
    )
    gate_list.append(leading_operand)
    upper_list.append(trailing_operand)
    for direction in range(num_dirs):
        leading_operand, trailing_operand = accumulate_upward(
            (
                lax.all_gather(tan_in0[direction : direction + 1], "seq", axis=2, tiled=True),
                lax.all_gather(tan_in1[direction : direction + 1], "seq", axis=2, tiled=True),
            )
        )
        gate_list.append(leading_operand)
        upper_list.append(trailing_operand)
    gates = jnp.concatenate(gate_list, axis=0)
    uppers = jnp.concatenate(upper_list, axis=0)
    act, slope = gelu_value_slope(gates[0])
    hidden = (act * uppers[0]).astype(jnp.bfloat16)
    hidden_tan = (slope[None] * gates[1:] * uppers[0][None] + act[None] * uppers[1:]).astype(
        jnp.bfloat16
    )
    stack_out = jnp.concatenate([w_out[None], tan_out], axis=0)
    piece = lax.all_gather(stack_out, "seq", axis=2, tiled=True)
    primal = jnp.dot(hidden, piece[0], preferred_element_type=jnp.float32)
    tangent = jnp.einsum("krf,fn->krn", hidden_tan, piece[0], preferred_element_type=jnp.float32)
    tangent = tangent + jnp.einsum(
        "rf,kfn->krn", hidden, piece[1:], preferred_element_type=jnp.float32
    )
    outputs = jnp.concatenate([primal[None], tangent], axis=0)
    out_part = outputs[0]
    row_dots = jnp.sum(outputs[1:] * full_u.astype(jnp.float32)[None], axis=2)
    block_out = lax.psum_scatter(out_part, "fsdp", scatter_dimension=1, tiled=True).astype(
        jnp.bfloat16
    )
    length = rows * lax.axis_size("seq") // EXAMPLES
    positions = lax.axis_index("seq") * rows + jnp.arange(rows, dtype=jnp.int32)
    example_of = positions // length
    select = (example_of[:, None] == jnp.arange(EXAMPLES, dtype=jnp.int32)[None, :]).astype(
        jnp.float32
    )
    select = select * loss_mask.astype(jnp.float32)[:, None]
    local_terms = jnp.dot(select.T, row_dots.T, precision=lax.Precision.HIGHEST)
    projection = lax.psum(local_terms, ("fsdp", "seq"))
    return (block_out, projection)


def solution(mesh):
    placed = (
        P("seq", "fsdp"),
        P("seq", "fsdp"),
        P("seq"),
        P("fsdp", "seq"),
        P("fsdp", "seq"),
        P("fsdp", "seq"),
        P(None, "fsdp", "seq"),
        P(None, "fsdp", "seq"),
        P(None, "fsdp", "seq"),
    )
    return jax.shard_map(
        shards, mesh=mesh, in_specs=placed, out_specs=(P("seq", "fsdp"), P()), check_vma=False
    )
```

profile of v0, /device:TPU:24, one launch (start us, length us, event | category | flops | bytes accessed | tf_op | source)
XLA Modules:
  0.0 1299.4 jit_solution(905960425996708743)
XLA Ops:
  7.2 0.0 copy-start.6
  7.2 0.0 all-gather.12.cloned.1.call-start
  7.2 0.7 all-gather.12.cloned.1.call-update
  7.9 0.0 all-gather.28.cloned.1.call-start
  8.0 0.7 all-gather.28.cloned.1.call-update
  8.7 0.0 all-gather.26.cloned.1.call-start
  8.7 0.7 all-gather.26.cloned.1.call-update
  9.4 0.0 all-gather.14.cloned.1.call-start
  9.4 1.8 pad_maximum_fusion
  11.3 0.0 all-gather.14.cloned.1.call-update
  11.3 0.0 all-gather.24.cloned.1.call-start
  11.4 0.5 all-gather.24.cloned.1.call-update
  11.9 0.0 all-gather.18.cloned.1.call-start
  11.9 1.7 fusion.76
  13.7 0.0 all-gather.18.cloned.1.call-update
  13.7 0.0 all-gather.16.cloned.1.call-start
  13.8 0.7 all-gather.16.cloned.1.call-update
  14.5 0.0 all-gather.22.cloned.1.call-start
  14.5 0.0 copy-done.6
  14.5 0.7 fusion.75
  15.3 0.0 all-gather.22.cloned.1.call-update
  15.3 0.0 all-gather.20.cloned.1.call-start
  15.3 0.7 all-gather.20.cloned.1.call-update
  16.0 0.0 reduce-scatter.2.cloned.1.call-start
  16.1 134.8 %all-gather.12.cloned.1.call-done = bf16[128,4096]{1,0:T(8,128)(2,1)} async-done(((bf16[128,128]{1,0:T(8,128)(2,1)}), bf16[128,4096]{1,0:T(8,128)(2,1)}) %all-gather.12.cloned.1.call-update) | async-done | bytes 1048592 | tf_op jit(solution)/shard_map/all_gather | solution.py:24
  150.8 0.0 copy-start
  150.8 42.4 %all-gather.28.cloned.1.call-done = bf16[320,4096]{1,0:T(8,128)(2,1)} async-done(((bf16[320,256]{1,0:T(8,128)(2,1)}), bf16[320,4096]{1,0:T(8,128)(2,1)}) %all-gather.28.cloned.1.call-update) | async-done | bytes 2621456 | tf_op jit(solution)/shard_map/all_gather | solution.py:44
  193.2 2.8 fusion.78
  196.1 46.4 %all-gather.26.cloned.1.call-done = bf16[320,4096]{1,0:T(8,128)(2,1)} async-done(((bf16[320,256]{1,0:T(8,128)(2,1)}), bf16[320,4096]{1,0:T(8,128)(2,1)}) %all-gather.26.cloned.1.call-update) | async-done | bytes 2621456 | tf_op jit(solution)/shard_map/all_gather | solution.py:43
  242.5 0.0 copy-done
  242.5 2.6 fusion.77
  245.0 0.0 copy-start.7
  245.1 65.1 %all-gather.14.cloned.1.call-done = bf16[3,320,4096]{2,1,0:T(8,128)(2,1)} async-done(((bf16[3,320,256]{2,1,0:T(8,128)(2,1)}), bf16[3,320,4096]{2,1,0:T(8,128)(2,1)}) %all-gather.14.cloned.1.call-update) | async-done | bytes 7864336 | tf_op jit(solution)/shard_map/all_gather | solution.py:66
  310.2 3.8 fusion.12
  314.0 0.0 reduce-scatter.2.cloned.1.call-update
  314.0 0.0 copy-done.7
  314.1 135.2 %all-gather.24.cloned.1.call-done = bf16[128,4096]{1,0:T(8,128)(2,1)} async-done(((bf16[128,128]{1,0:T(8,128)(2,1)}), bf16[128,4096]{1,0:T(8,128)(2,1)}) %all-gather.24.cloned.1.call-update) | async-done | bytes 1048592 | tf_op jit(solution)/shard_map/all_gather | solution.py:25
  449.3 1.4 convert_element_type.27
  450.7 0.8 fusion.37
  451.6 40.0 %all-gather.18.cloned.1.call-done = bf16[1,320,4096]{2,1,0:T(8,128)(2,1)} async-done(((bf16[1,320,256]{2,1,0:T(8,128)(2,1)}), bf16[1,320,4096]{2,1,0:T(8,128)(2,1)}) %all-gather.18.cloned.1.call-update) | async-done | bytes 2621456 | tf_op jit(solution)/shard_map/all_gather | solution.py:52
  491.6 3.2 fusion.20
  494.8 46.0 %all-gather.16.cloned.1.call-done = bf16[1,320,4096]{2,1,0:T(8,128)(2,1)} async-done(((bf16[1,320,256]{2,1,0:T(8,128)(2,1)}), bf16[1,320,4096]{2,1,0:T(8,128)(2,1)}) %all-gather.16.cloned.1.call-update) | async-done | bytes 2621456 | tf_op jit(solution)/shard_map/all_gather | solution.py:52
  540.8 3.3 fusion.17
  544.0 46.0 %all-gather.22.cloned.1.call-done = bf16[1,320,4096]{2,1,0:T(8,128)(2,1)} async-done(((bf16[1,320,256]{2,1,0:T(8,128)(2,1)}), bf16[1,320,4096]{2,1,0:T(8,128)(2,1)}) %all-gather.22.cloned.1.call-update) | async-done | bytes 2621456 | tf_op jit(solution)/shard_map/all_gather | solution.py:53
  590.0 3.3 fusion.26
  593.3 46.0 %all-gather.20.cloned.1.call-done = bf16[1,320,4096]{2,1,0:T(8,128)(2,1)} async-done(((bf16[1,320,256]{2,1,0:T(8,128)(2,1)}), bf16[1,320,4096]{2,1,0:T(8,128)(2,1)}) %all-gather.20.cloned.1.call-update) | async-done | bytes 2621456 | tf_op jit(solution)/shard_map/all_gather | solution.py:53
  639.3 0.0 copy-start.1
  639.3 0.0 copy-start.2
  639.3 0.0 copy-start.3
  639.3 0.0 copy-start.4
  639.3 0.0 copy-start.5
  639.3 2.7 fusion.23
  641.9 0.0 copy-done.1
  641.9 0.0 copy-done.2
  642.0 0.0 copy-done.3
  642.0 0.0 copy-done.4
  642.0 0.0 copy-done.5
  642.0 3.1 fusion.2
  645.1 4.2 fusion.16
  649.3 0.2 fusion.59
  649.5 105.2 %psum.7 = f32[4,2]{0,1:T(2,128)} all-reduce(f32[4,2]{0,1:T(2,128)S(1)} %fusion.59), channel_id=1, replica_groups=mesh['fsdp'=32,'seq'=16] {'fsdp','seq'}, use_global_device_ids=true, to_apply=%region_2.3 | all-reduce | flops 8 | bytes 64 | tf_op jit(solution)/shard_map/psum | solution.py:86
  754.7 536.4 %reduce-scatter.2.cloned.1.call-done = f32[128,128]{1,0:T(8,128)} async-done(((f32[128,4096]{1,0:T(8,128)}), f32[128,128]{1,0:T(8,128)}) %reduce-scatter.2.cloned.1.call-update) | async-done | bytes 65552 | tf_op jit(solution)/shard_map/reduce_scatter | solution.py:75
  1291.1 1.5 convert_element_type.23
  (2 shorter events, 0.0 us)
Async XLA Ops:
  7.2 7.3 copy-start.6
  7.2 143.6 %all-gather.12.cloned.1.call-start = ((), (), s32[]{:S(2)}) async-start(), calls=%async_computation.1 | async-start | bytes 1081344 | tf_op jit(solution)/shard_map/all_gather | solution.py:24
  7.9 185.3 %all-gather.28.cloned.1.call-start = ((), (), s32[]{:S(2)}) async-start(), calls=%async_computation.10 | async-start | bytes 2785280 | tf_op jit(solution)/shard_map/all_gather | solution.py:44
  8.7 233.8 %all-gather.26.cloned.1.call-start = ((), (), s32[]{:S(2)}) async-start(), calls=%async_computation.9 | async-start | bytes 2785280 | tf_op jit(solution)/shard_map/all_gather | solution.py:43
  9.4 300.8 %all-gather.14.cloned.1.call-start = ((), (), s32[]{:S(2)}) async-start(), calls=%async_computation.2 | async-start | bytes 8355840 | tf_op jit(solution)/shard_map/all_gather | solution.py:66
  11.3 438.0 %all-gather.24.cloned.1.call-start = ((), (), s32[]{:S(2)}) async-start(), calls=%async_computation.8 | async-start | bytes 1081344 | tf_op jit(solution)/shard_map/all_gather | solution.py:25
  11.9 479.7 %all-gather.18.cloned.1.call-start = ((), (), s32[]{:S(2)}) async-start(), calls=%async_computation.5 | async-start | bytes 2785280 | tf_op jit(solution)/shard_map/all_gather | solution.py:52
  13.7 527.1 %all-gather.16.cloned.1.call-start = ((), (), s32[]{:S(2)}) async-start(), calls=%async_computation.4 | async-start | bytes 2785280 | tf_op jit(solution)/shard_map/all_gather | solution.py:52
  14.5 575.6 %all-gather.22.cloned.1.call-start = ((), (), s32[]{:S(2)}) async-start(), calls=%async_computation.7 | async-start | bytes 2785280 | tf_op jit(solution)/shard_map/all_gather | solution.py:53
  15.3 624.0 %all-gather.20.cloned.1.call-start = ((), (), s32[]{:S(2)}) async-start(), calls=%async_computation.6 | async-start | bytes 2785280 | tf_op jit(solution)/shard_map/all_gather | solution.py:53
  16.0 1275.1 %reduce-scatter.2.cloned.1.call-start = ((), (), s32[]{:S(2)}) async-start(), calls=%async_computation.3 | async-start | bytes 2162688 | tf_op jit(solution)/shard_map/reduce_scatter | solution.py:75
  150.8 91.6 %copy-start = (bf16[128,4096]{1,0:T(8,128)(2,1)S(1)}, bf16[128,4096]{1,0:T(8,128)(2,1)}, u32[]{:S(2)}) copy-start(bf16[128,4096]{1,0:T(8,128)(2,1)} %all-gather.12.cloned.1.call-done) | copy-start | bytes 3145732
  245.0 69.0 %copy-start.7 = (s32[128]{0:T(128)S(1)}, s32[128]{0:T(128)}, u32[]{:S(2)}) copy-start(s32[128]{0:T(128)} %param.11) | copy-start | bytes 1540
  639.3 2.7 copy-start.1
  639.3 2.7 copy-start.2
  639.3 2.7 copy-start.3
  639.3 2.7 copy-start.4
  639.3 2.7 copy-start.5
Sparse Core Ops, SparseCore 0:
  10.9 139.8 all-gather.11
  152.9 40.2 all-gather.27
  195.3 47.1 all-gather.25
  244.4 65.7 all-gather.13
  312.9 136.3 all-gather.23
  451.2 40.2 all-gather.17
  493.6 47.1 all-gather.15
  542.8 47.1 all-gather.21
  592.1 47.1 all-gather.19
  643.5 647.5 reduce-scatter.1
where the time goes:
time: 1300 us
  waiting for transfers between devices  1140 us (88%)
  blocking collectives  105 us (8%)
  matrix products  29.2 us (2%)
  between operations  14.3 us (1%)
    reduce_scatter x1, waiting for transfers between devices, shards(): lax.psum_scatter(out_part, 'fsdp', scatter_dimension=1, tiled=True)  536 us
    all_gather x1, waiting for transfers between devices, shards(): lax.all_gather(out_grad, 'fsdp', axis=1, tiled=True)  135 us
    all_gather x1, waiting for transfers between devices, shards(): lax.all_gather(tokens, 'fsdp', axis=1, tiled=True)  135 us
    psum x1, blocking collectives, shards(): projection = lax.psum(local_terms, ('fsdp', 'seq'))  105 us
    all_gather x2, waiting for transfers between devices, shards(): lax.all_gather(tan_in1[direction:direction + 1], 'seq', axis=2, tiled=True)  92 us
    all_gather x2, waiting for transfers between devices, shards(): lax.all_gather(tan_in0[direction:direction + 1], 'seq', axis=2, tiled=True)  86 us
    all_gather x1, waiting for transfers between devices, shards(): piece = lax.all_gather(stack_out, 'seq', axis=2, tiled=True)  65.1 us
    all_gather x1, waiting for transfers between devices, shards(): lax.all_gather(w_in0[None], 'seq', axis=2, tiled=True)  46.4 us
  transfers between devices with their start and end apart: 10, of which 10 were waited for; matrix products, arithmetic and copies ran while one was open for 3% of the time, Pallas kernels for 0%

commit v1 on v0

v1 whole, which is shorter than its diff:
```python
import functools
import math

import jax
import jax.numpy as jnp
from jax import lax
from jax.experimental import pallas as pl
from jax.experimental.pallas import tpu as pltpu
from jax.sharding import PartitionSpec as P

EXAMPLES = 4
F32 = jnp.float32
BF16 = jnp.bfloat16
NT = (((1,), (1,)), ((), ()))

X_PAIRS = [[i, i + 16] for i in range(16)]
Z_NEAR = [[h * 16 + q * 4 + r for r in range(4)] for h in range(2) for q in range(4)]
Z_FAR = [[h * 16 + q * 4 + r for q in range(4)] for h in range(2) for r in range(4)]
Z_ALL = [list(range(16)), list(range(16, 32))]


def gelu_value_slope(value):
    coeff = math.sqrt(2.0 / math.pi)
    inner = coeff * (value + 0.044715 * value * value * value)
    tangent = jnp.tanh(inner)
    act = 0.5 * value * (1.0 + tangent)
    slope = 0.5 * (1.0 + tangent) + 0.5 * value * (1.0 - tangent * tangent) * coeff * (
        1.0 + 3.0 * 0.044715 * value * value
    )
    return (act, slope)


def z_shift(array, step):
    perm = [(h * 16 + (z + step) % 16, h * 16 + z) for h in range(2) for z in range(16)]
    return lax.ppermute(array, "fsdp", perm)


def contract_blocks(place, parts, weights, counts):
    x_hi, z_lo = place[0], place[1]
    sums = [None] * len(counts)
    for shift in range(4):
        near = (z_lo + shift) % 4
        lanes = pl.ds(pl.multiple_of((near % 2) * 128, 128), 128)
        for other in range(2):
            row = jnp.bitwise_xor(x_hi, other)
            for at, which in enumerate(counts):
                term = lax.dot_general(
                    parts[which][shift](other),
                    weights[row, 0, near // 2, at, :, lanes],
                    NT,
                    preferred_element_type=F32,
                )
                sums[at] = term if sums[at] is None else sums[at] + term
    return sums


def readers(own, plus, minus, two_x, two_g):
    def full(ref, which):
        return lambda other: ref[0, other, which]

    def single(ref):
        return lambda other: ref[0, other]

    return [
        [full(own, 0), full(plus, 0), single(two_x), full(minus, 0)],
        [full(own, 1), full(plus, 1), single(two_g), full(minus, 1)],
    ]


def primal_kernel(
    place, own, plus, minus, two_x, two_g, weights, hidden, act_out, factor_out, dh_out, sums
):
    step = pl.program_id(0)
    terms = contract_blocks(
        place, readers(own, plus, minus, two_x, two_g), weights, (0, 0, 1)
    )

    @pl.when(step == 0)
    def _():
        for at in range(3):
            sums[at] = terms[at]

    @pl.when(step > 0)
    def _():
        for at in range(3):
            sums[at] += terms[at]

    @pl.when(step == pl.num_programs(0) - 1)
    def _():
        upper = sums[1]
        act, slope = gelu_value_slope(sums[0])
        hidden[...] = (act * upper).astype(BF16)
        act_out[...] = act
        factor_out[...] = slope * upper
        dh_out[...] = sums[2]


def output_kernel(hidden, weights, out):
    for at in range(weights.shape[0]):
        value = jnp.dot(hidden[...], weights[at, 0], preferred_element_type=F32)
        out[2 * at] = value[:, :128]
        out[2 * at + 1] = value[:, 128:]


def tangent_kernel(
    place, own, plus, minus, two_x, two_g, weights, hidden, act, factor, dh, mask, out, sums
):
    step = pl.program_id(0)
    terms = contract_blocks(
        place, readers(own, plus, minus, two_x, two_g), weights, (0, 0, 0, 0, 1, 1)
    )

    @pl.when(step == 0)
    def _():
        for at in range(6):
            sums[at] = terms[at]

    @pl.when(step > 0)
    def _():
        for at in range(6):
            sums[at] += terms[at]

    @pl.when(step == pl.num_programs(0) - 1)
    def _():
        rows = lax.broadcasted_iota(jnp.int32, (8, 128), 0)
        lanes = lax.broadcasted_iota(jnp.int32, (8, 128), 1)
        total = jnp.zeros((8, 128), F32)
        for k in range(2):
            tangent = (factor[...] * sums[k] + act[...] * sums[2 + k]).astype(BF16)
            value = tangent.astype(F32) * dh[...] + hidden[...].astype(F32) * sums[4 + k]
            value = jnp.sum(value, axis=1, keepdims=True) * mask[...]
            value = jnp.sum(value, axis=0, keepdims=True)
            total = jnp.where((rows == place[2]) & (lanes == k), value, total)
        out[...] = total


def activation_specs():
    full = pl.BlockSpec((1, 2, 2, 128, 128), lambda s, p: (s, 0, 0, 0, 0))
    single = pl.BlockSpec((1, 2, 128, 128), lambda s, p: (s, 0, 0, 0))
    return [full, full, full, single, single]


def whole(shape):
    return pl.BlockSpec(shape, lambda s, p: (0,) * len(shape))


def weight_spec(count):
    return pl.BlockSpec((2, 1, 2, count, 320, 256), lambda s, p: (0, s, 0, 0, 0, 0))


def shards(tokens, out_grad, loss_mask, w_in0, w_in1, w_out, tan_in0, tan_in1, tan_out):
    fsdp = lax.axis_index("fsdp")
    seq = lax.axis_index("seq")
    rows = tokens.shape[0]
    length = rows * lax.axis_size("seq") // EXAMPLES
    place = jnp.stack([fsdp // 16, fsdp % 4, seq * rows // length]).astype(jnp.int32)

    stack_w = jnp.stack([w_in0, w_in1, w_out])
    stack_t = jnp.concatenate([tan_in0, tan_in1, tan_out], axis=0)
    stack_t, stack_w = lax.optimization_barrier((stack_t, stack_w))
    full_w = lax.all_gather(stack_w, "seq", axis=0).reshape(2, 4, 2, 3, 320, 256)
    full_t = lax.all_gather(stack_t, "seq", axis=0).reshape(2, 4, 2, 6, 320, 256)

    both = jnp.stack([tokens, out_grad])
    other = lax.ppermute(both, "fsdp", [(i, (i + 16) % 32) for i in range(32)])
    own = lax.all_gather(jnp.stack([both, other]), "fsdp", axis=0, axis_index_groups=Z_FAR)
    plus = z_shift(own, 1)
    minus = z_shift(own, -1)
    two_x = z_shift(own[:, :, 0], 2)
    two_g = z_shift(own[:, :, 1], -2)
    acts = (own, plus, minus, two_x, two_g)

    flat = jax.ShapeDtypeStruct((128, 320), F32)
    hidden, act, factor, dh = pl.pallas_call(
        primal_kernel,
        out_shape=(jax.ShapeDtypeStruct((128, 320), BF16), flat, flat, flat),
        grid_spec=pltpu.PrefetchScalarGridSpec(
            num_scalar_prefetch=1,
            grid=(4,),
            in_specs=activation_specs() + [weight_spec(3)],
            out_specs=(whole((128, 320)),) * 4,
            scratch_shapes=[pltpu.VMEM((3, 128, 320), F32)],
        ),
        compiler_params=pltpu.CompilerParams(vmem_limit_bytes=32 * 2**20),
        cost_estimate=pl.CostEstimate(
            flops=2 * 3 * 128 * 320 * 4096, bytes_accessed=10 * 2**20, transcendentals=40960
        ),
        name="primal",
    )(place, *acts, full_w)

    partial = pl.pallas_call(
        output_kernel,
        out_shape=jax.ShapeDtypeStruct((32, 128, 128), F32),
        grid=(4,),
        in_specs=[
            pl.BlockSpec((128, 320), lambda s: (0, 0)),
            pl.BlockSpec((4, 1, 320, 256), lambda s: (s, 2, 0, 0)),
        ],
        out_specs=pl.BlockSpec((8, 128, 128), lambda s: (s, 0, 0)),
        compiler_params=pltpu.CompilerParams(vmem_limit_bytes=32 * 2**20),
        cost_estimate=pl.CostEstimate(
            flops=2 * 128 * 320 * 4096, bytes_accessed=5 * 2**20, transcendentals=0
        ),
        name="block_sums",
    )(hidden, full_w.reshape(16, 3, 320, 256))

    part = partial.reshape(2, 4, 4, 128, 128)
    part = jnp.sum(lax.all_to_all(part, "fsdp", 0, 0, axis_index_groups=X_PAIRS), axis=0)
    part = jnp.swapaxes(part, 0, 1)
    part = jnp.sum(lax.all_to_all(part, "fsdp", 0, 0, axis_index_groups=Z_NEAR), axis=0)
    part = jnp.sum(lax.all_to_all(part, "fsdp", 0, 0, axis_index_groups=Z_FAR), axis=0)
    block_out = part.astype(BF16)

    terms = pl.pallas_call(
        tangent_kernel,
        out_shape=jax.ShapeDtypeStruct((8, 128), F32),
        grid_spec=pltpu.PrefetchScalarGridSpec(
            num_scalar_prefetch=1,
            grid=(4,),
            in_specs=activation_specs()
            + [weight_spec(6)]
            + [whole((128, 320))] * 4
            + [whole((128, 1))],
            out_specs=whole((8, 128)),
            scratch_shapes=[pltpu.VMEM((6, 128, 320), F32)],
        ),
        compiler_params=pltpu.CompilerParams(vmem_limit_bytes=40 * 2**20),
        cost_estimate=pl.CostEstimate(
            flops=2 * 6 * 128 * 320 * 4096, bytes_accessed=18 * 2**20, transcendentals=0
        ),
        name="tangents",
    )(place, *acts, full_t, hidden, act, factor, dh, loss_mask.astype(F32)[:, None])

    def gather_sum(value, axis, groups, size):
        copies = jnp.broadcast_to(value[None], (size,) + value.shape)
        got = lax.all_to_all(copies, axis, 0, 0, axis_index_groups=groups)
        return jnp.sum(got, axis=0)

    terms = gather_sum(terms, "fsdp", Z_ALL, 16)
    terms = gather_sum(terms, "fsdp", X_PAIRS, 2)
    terms = gather_sum(terms, "seq", None, 16)
    return (block_out, terms[:EXAMPLES, :2])


def solution(mesh):
    placed = (
        P("seq", "fsdp"),
        P("seq", "fsdp"),
        P("seq"),
        P("fsdp", "seq"),
        P("fsdp", "seq"),
        P("fsdp", "seq"),
        P(None, "fsdp", "seq"),
        P(None, "fsdp", "seq"),
        P(None, "fsdp", "seq"),
    )
    return jax.shard_map(
        shards, mesh=mesh, in_specs=placed, out_specs=(P("seq", "fsdp"), P()), check_vma=False
    )
```

time: 1300 us -> 305 us (0.23)
  waiting for transfers between devices: 1140 us -> 170 us
  blocking collectives: 105 us -> 31.7 us
  starting transfers between devices: 0.39 us -> 50.6 us
  matrix products: 29.2 us -> 0 us
  Pallas kernels: 0 us -> 18.3 us
    reduce_scatter x1 -> x0, waiting for transfers between devices: 536 us -> none  [shards(): lax.psum_scatter(out_part, 'fsdp', scatter_dimension=1, tiled=True)]
    all_gather x9 -> x2, waiting for transfers between devices: 602 us -> 97.1 us  [the longest x1 97.1 us: shards(): lax.all_gather(stack_t, 'seq', axis=0).reshape(2, 4, 2, 6, 320, 256)]
    psum x1 -> x0, blocking collectives: 105 us -> none  [shards(): projection = lax.psum(local_terms, ('fsdp', 'seq'))]
    all_to_all x0 -> x6, waiting for transfers between devices: none -> 57.9 us  [the longest x1 24.6 us: shards(): lax.all_to_all(part, 'fsdp', 0, 0, axis_index_groups=Z_NEAR)]
    all_to_all x0 -> x6, starting transfers between devices: none -> 32.1 us  [the longest x3 19.4 us: gather_sum(): got = lax.all_to_all(copies, axis, 0, 0, axis_index_groups=groups)]
    all_gather x0 -> x1, blocking collectives: none -> 31.7 us  [shards(): lax.all_gather(jnp.stack([both, other]), 'fsdp', axis=0, axis_index_group...]
    dot_general x10 -> x0, matrix products: 29.2 us -> none  [the longest x3 9.07 us: accumulate_upward(): jnp.einsum('jn,ztn->zjt', complete_input, partial_segments[0], preferred_...]
    ppermute x0 -> x5, starting transfers between devices: none -> 18.5 us  [the longest x4 13.6 us: z_shift(): return lax.ppermute(array, 'fsdp', perm)]
  transfers between devices with their start and end apart: 10 -> 13, of which waited for: 10 -> 9; matrix products, arithmetic and copies ran while one was open for 3% -> 2% of each run, Pallas kernels for 0% -> 6%
where the time goes in v1:
time: 305 us; the launch traced here: 301 us
  waiting for transfers between devices  170 us (56%)
  starting transfers between devices  50.6 us (17%)
  blocking collectives  31.7 us (10%)
  Pallas kernels  18.3 us (6%)
  between operations  14.3 us (5%)
  other arithmetic  8.35 us (3%)
  local copies, waits for them, and re-layouts  7.88 us (3%)
    all_gather x1, waiting for transfers between devices, shards(): lax.all_gather(stack_t, 'seq', axis=0).reshape(2, 4, 2, 6, 320, 256)  97.1 us
    all_gather x1, blocking collectives, shards(): lax.all_gather(jnp.stack([both, other]), 'fsdp', axis=0, axis_index_group...  31.7 us
    all_to_all x1, waiting for transfers between devices, shards(): lax.all_to_all(part, 'fsdp', 0, 0, axis_index_groups=Z_NEAR)  24.6 us
    all_to_all x3, starting transfers between devices, gather_sum(): got = lax.all_to_all(copies, axis, 0, 0, axis_index_groups=groups)  19.4 us
    all_to_all x3, waiting for transfers between devices, gather_sum(): got = lax.all_to_all(copies, axis, 0, 0, axis_index_groups=groups)  18.3 us
    all_to_all x1, waiting for transfers between devices, shards(): lax.all_to_all(part, 'fsdp', 0, 0, axis_index_groups=Z_FAR)  15 us
    ppermute x4, starting transfers between devices, z_shift(): return lax.ppermute(array, 'fsdp', perm)  13.6 us
    ppermute x4, waiting for transfers between devices, z_shift(): return lax.ppermute(array, 'fsdp', perm)  11.5 us
  transfers between devices with their start and end apart: 13, of which 9 were waited for; matrix products, arithmetic and copies ran while one was open for 2% of the time, Pallas kernels for 6%

profile of v1, /device:TPU:24, one launch (start us, length us, event | category | flops | bytes accessed | tf_op | source)
XLA Modules:
  0.0 301.1 jit_solution(8117805573639820443)
XLA Ops:
  7.2 0.0 all-gather.6.cloned.1.call-start
  7.2 2.2 pad_maximum_fusion
  9.4 2.0 pad_maximum_fusion.1
  11.4 0.0 all-gather.6.cloned.1.call-update
  11.4 0.0 all-gather.8.cloned.1.call-start
  11.5 0.7 all-gather.8.cloned.1.call-update
  12.2 0.8 fusion
  13.0 4.9 %collective-permute-start = (bf16[2,128,128]{2,1,0:T(8,128)(2,1)S(1)}, bf16[2,128,128]{2,1,0:T(8,128)(2,1)S(1)}, u32[]{:S(2)}, u32[]{:S(2)}) collective-permute-start(bf16[2,128,128]{2,1,0:T(8,128)(2,1)S(1)} %get-tuple-element.19), channel_id=1, source_target_pairs={{0,256},{16,272},{32,288},{48,304},{64,320},{80,336},{96,352},{112... | collective-permute-start | bytes 196616 | tf_op jit(solution)/shard_map/ppermute | solution.py:165
  17.9 2.7 collective-permute-done
  20.6 31.7 %all-gather = bf16[8,2,128,128]{3,2,1,0:T(8,128)(2,1)S(1)} all-gather(bf16[2,2,128,128]{3,2,1,0:T(8,128)(2,1)S(1)} %pad_maximum_fusion.2), channel_id=2, replica_groups={{0,64,128,192},{16,80,144,208},{32,96,160,224},{48,112,176,240},{256,32..., dimensions={0}, use_global_device_ids=true | all-gather | bytes 655360 | tf_op jit(solution)/shard_map/all_gather | solution.py:166
  52.4 4.9 %collective-permute-start.1 = (bf16[4,2,2,128,128]{4,3,1,0,2:T(8,128)(2,1)S(1)}, bf16[4,2,2,128,128]{4,3,1,0,2:T(8,128)(2,1)S(1)}, u32[]{:S(2)}, u32[]{:S(2)}) collective-permute-start(bf16[4,2,2,128,128]{4,3,1,0,2:T(8,128)(2,1)S(1)} %bitcast.30), channel_id=1, source_target_pairs={{16,0},{32,16},{48,32},{64,48},{80,64},{96,80},{112,96},{128,112},... | collective-permute-start | bytes 1572872 | tf_op jit(solution)/shard_map/ppermute | solution.py:35
  57.3 1.9 collective-permute-start.2
  59.2 0.9 slice_bitcast_fusion
  60.1 3.4 %collective-permute-start.3 = (bf16[4,2,128,128]{3,2,1,0:T(8,128)(2,1)}, bf16[4,2,128,128]{3,2,1,0:T(8,128)(2,1)S(1)}, u32[]{:S(2)}, u32[]{:S(2)}) collective-permute-start(bf16[4,2,128,128]{3,2,1,0:T(8,128)(2,1)} %get-tuple-element.17), channel_id=1, source_target_pairs={{32,0},{48,16},{64,32},{80,48},{96,64},{112,80},{128,96},{144,112}... | collective-permute-start | bytes 786440 | tf_op jit(solution)/shard_map/ppermute | solution.py:35
  63.5 3.4 %collective-permute-start.4 = (bf16[4,2,128,128]{3,2,1,0:T(8,128)(2,1)}, bf16[4,2,128,128]{3,2,1,0:T(8,128)(2,1)S(1)}, u32[]{:S(2)}, u32[]{:S(2)}) collective-permute-start(bf16[4,2,128,128]{3,2,1,0:T(8,128)(2,1)} %get-tuple-element.16), channel_id=1, source_target_pairs={{224,0},{240,16},{0,32},{16,48},{32,64},{48,80},{64,96},{80,112},{... | collective-permute-start | bytes 786440 | tf_op jit(solution)/shard_map/ppermute | solution.py:35
  66.9 0.1 pad_add_fusion.place
  67.0 6.3 %collective-permute-done.1 = bf16[4,2,2,128,128]{4,3,1,0,2:T(8,128)(2,1)S(1)} collective-permute-done((bf16[4,2,2,128,128]{4,3,1,0,2:T(8,128)(2,1)S(1)}, bf16[4,2,2,128,128]{4,3,1,0,2:T(8,128)(2,1)S(1)}, u32[]{:S(2)}, u32[]{:S(2)}) %collective-permute-start.1) | collective-permute-done | bytes 524320 | tf_op jit(solution)/shard_map/ppermute | solution.py:35
  73.3 5.3 %collective-permute-done.2 = bf16[4,2,2,128,128]{4,3,1,0,2:T(8,128)(2,1)S(1)} collective-permute-done((bf16[4,2,2,128,128]{4,3,1,0,2:T(8,128)(2,1)S(1)}, bf16[4,2,2,128,128]{4,3,1,0,2:T(8,128)(2,1)S(1)}, u32[]{:S(2)}, u32[]{:S(2)}) %collective-permute-start.2) | collective-permute-done | bytes 524320 | tf_op jit(solution)/shard_map/ppermute | solution.py:35
  78.6 0.0 collective-permute-done.3.two_x
  78.6 0.0 collective-permute-done.4.two_g
  78.6 0.0 all-gather.6.cloned.1.call-done
  78.6 0.0 copy-start
  78.6 3.2 %copy-done = bf16[48,320,256]{2,1,0:T(8,128)(2,1)S(1)} copy-done((bf16[48,320,256]{2,1,0:T(8,128)(2,1)S(1)}, bf16[48,320,256]{2,1,0:T(8,128)(2,1)}, u32[]{:S(2)}) %copy-start) | copy-done | bytes 7864344
  81.9 0.0 copy-start.1
  81.9 5.2 %primal.1 = (bf16[128,320]{1,0:T(8,128)(2,1)S(1)}, f32[128,320]{1,0:T(8,128)S(1)}, f32[128,320]{1,0:T(8,128)S(1)}, f32[128,320]{1,0:T(8,128)S(1)}) custom-call(s32[3]{0:T(128)S(1)} %pad_add_fusion.place, bf16[4,2,2,128,128]{4,3,2,1,0:T(8,128)(2,1)S(1)} %bitcast.26, bf16[4,2,2,128,128]{4,3,2,1,0:T(8,128)(2,1)S(1)} %copy.38.plus, ...), custom_call_target="tpu_custom_call" | custom-call | flops 1006632960 | bytes 10485760 | tf_op jit(solution)/shard_map/primal/pallas_call | solution.py:174
  87.0 0.0 copy-start.2
  87.0 0.0 copy-done.1
  87.0 2.7 block_sums.1
  89.8 4.8 %all-to-all-start = ((f32[2,4,4,128,128]{4,3,2,1,0:T(8,128)}), f32[2,4,4,128,128]{4,3,2,1,0:T(8,128)}, u32[]{:S(2)}, u32[]{:S(2)}) async-start(f32[2,4,4,128,128]{4,3,2,1,0:T(8,128)} %bitcast.16), calls=%async_computation | async-start | bytes 4194304 | tf_op jit(solution)/shard_map/all_to_all | solution.py:208
  94.6 0.0 copy-done.2
  94.6 0.1 copy.44.mask
  94.7 97.1 %all-gather.8.cloned.1.call-done = bf16[96,320,256]{2,1,0:T(8,128)(2,1)} async-done(((bf16[6,320,256]{2,1,0:T(8,128)(2,1)}), bf16[96,320,256]{2,1,0:T(8,128)(2,1)}) %all-gather.8.cloned.1.call-update) | async-done | bytes 15728656 | tf_op jit(solution)/shard_map/all_gather | solution.py:162
  191.8 10.4 %tangents.1 = f32[8,128]{1,0:T(8,128)S(1)} custom-call(s32[3]{0:T(128)S(1)} %pad_add_fusion.place, bf16[4,2,2,128,128]{4,3,2,1,0:T(8,128)(2,1)S(1)} %bitcast.27, bf16[4,2,2,128,128]{4,3,2,1,0:T(8,128)(2,1)S(1)} %copy.38.plus, bf16[4,2,2,128,128]{4,3,2,1,0:T(8,128)(2,1)S(1)} %copy.39.minus, bf16[4,2,128,128]{3,2,1,0:T(8,128)(2,1)S(1)} %collective-permute-done.3.two_x, ...), custom_call_target="tpu_custom_call" | custom-call | flops 2013265920 | bytes 18874368 | tf_op jit(solution)/shard_map/tangents/pallas_call | solution.py:214
  202.3 0.0 all-to-all-done
  202.3 0.6 broadcast_in_dim.9
  202.9 9.8 %all-to-all-start.3 = ((f32[16,8,128]{2,1,0:T(8,128)}), f32[16,8,128]{2,1,0:T(8,128)S(1)}, u32[]{:S(2)}, u32[]{:S(2)}) async-start(f32[16,8,128]{2,1,0:T(8,128)} %broadcast_in_dim.9), calls=%async_computation.3 | async-start | bytes 131072 | tf_op jit(solution)/shard_map/all_to_all | solution.py:236
  212.7 1.8 reduce_sum.54
  214.5 1.0 copy.40
  215.6 10.2 %all-to-all-done.3 = f32[16,8,128]{2,1,0:T(8,128)S(1)} async-done(((f32[16,8,128]{2,1,0:T(8,128)}), f32[16,8,128]{2,1,0:T(8,128)S(1)}, u32[]{:S(2)}, u32[]{:S(2)}) %all-to-all-start.3) | async-done | bytes 65568 | tf_op jit(solution)/shard_map/all_to_all | solution.py:236
  225.8 3.5 %all-to-all-start.1 = ((f32[4,4,128,128]{3,2,1,0:T(8,128)}), f32[4,4,128,128]{3,2,1,0:T(8,128)S(1)}, u32[]{:S(2)}, u32[]{:S(2)}) async-start(f32[4,4,128,128]{3,2,1,0:T(8,128)} %copy.40), calls=%async_computation.1 | async-start | bytes 2097152 | tf_op jit(solution)/shard_map/all_to_all | solution.py:210
  229.3 24.6 %all-to-all-done.1 = f32[4,4,128,128]{3,2,1,0:T(8,128)S(1)} async-done(((f32[4,4,128,128]{3,2,1,0:T(8,128)}), f32[4,4,128,128]{3,2,1,0:T(8,128)S(1)}, u32[]{:S(2)}, u32[]{:S(2)}) %all-to-all-start.1) | async-done | bytes 1048608 | tf_op jit(solution)/shard_map/all_to_all | solution.py:210
  253.9 0.6 broadcast_in_dim.10
  254.5 5.1 %all-to-all-start.4 = ((f32[2,8,128]{2,1,0:T(8,128)}), f32[2,8,128]{2,1,0:T(8,128)S(1)}, u32[]{:S(2)}, u32[]{:S(2)}) async-start(f32[2,8,128]{2,1,0:T(8,128)} %broadcast_in_dim.10), calls=%async_computation.4 | async-start | bytes 16384 | tf_op jit(solution)/shard_map/all_to_all | solution.py:236
  259.6 0.8 reduce_sum.55
  260.4 4.5 %all-to-all-done.4 = f32[2,8,128]{2,1,0:T(8,128)S(1)} async-done(((f32[2,8,128]{2,1,0:T(8,128)}), f32[2,8,128]{2,1,0:T(8,128)S(1)}, u32[]{:S(2)}, u32[]{:S(2)}) %all-to-all-start.4) | async-done | bytes 8224 | tf_op jit(solution)/shard_map/all_to_all | solution.py:236
  265.0 4.3 %all-to-all-start.2 = ((f32[4,128,128]{2,1,0:T(8,128)}), f32[4,128,128]{2,1,0:T(8,128)S(1)}, u32[]{:S(2)}, u32[]{:S(2)}) async-start(f32[4,128,128]{2,1,0:T(8,128)} %reduce_sum.55), calls=%async_computation.2 | async-start | bytes 524288 | tf_op jit(solution)/shard_map/all_to_all | solution.py:211
  269.3 15.0 %all-to-all-done.2 = f32[4,128,128]{2,1,0:T(8,128)S(1)} async-done(((f32[4,128,128]{2,1,0:T(8,128)}), f32[4,128,128]{2,1,0:T(8,128)S(1)}, u32[]{:S(2)}, u32[]{:S(2)}) %all-to-all-start.2) | async-done | bytes 262176 | tf_op jit(solution)/shard_map/all_to_all | solution.py:211
  284.3 0.6 broadcast_in_dim.11
  284.9 4.5 %all-to-all-start.5 = ((f32[16,8,128]{2,1,0:T(8,128)}), f32[16,8,128]{2,1,0:T(8,128)S(1)}, u32[]{:S(2)}, u32[]{:S(2)}) async-start(f32[16,8,128]{2,1,0:T(8,128)} %broadcast_in_dim.11), calls=%async_computation.5 | async-start | bytes 131072 | tf_op jit(solution)/shard_map/all_to_all | solution.py:236
  289.4 0.6 reduce_sum.56
  290.1 3.5 %all-to-all-done.5 = f32[16,8,128]{2,1,0:T(8,128)S(1)} async-done(((f32[16,8,128]{2,1,0:T(8,128)}), f32[16,8,128]{2,1,0:T(8,128)S(1)}, u32[]{:S(2)}, u32[]{:S(2)}) %all-to-all-start.5) | async-done | bytes 65568 | tf_op jit(solution)/shard_map/all_to_all | solution.py:236
  293.6 0.7 copy.45
  (9 shorter events, 0.2 us)
Async XLA Ops:
  7.2 71.4 %all-gather.6.cloned.1.call-start = ((), (), s32[]{:S(2)}) async-start(), calls=%async_computation.6 | async-start | bytes 8355840 | tf_op jit(solution)/shard_map/all_gather | solution.py:161
  11.4 180.4 %all-gather.8.cloned.1.call-start = ((), (), s32[]{:S(2)}) async-start(), calls=%async_computation.7 | async-start | bytes 16711680 | tf_op jit(solution)/shard_map/all_gather | solution.py:162
  13.0 7.7 %collective-permute-start = (bf16[2,128,128]{2,1,0:T(8,128)(2,1)S(1)}, bf16[2,128,128]{2,1,0:T(8,128)(2,1)S(1)}, u32[]{:S(2)}, u32[]{:S(2)}) collective-permute-start(bf16[2,128,128]{2,1,0:T(8,128)(2,1)S(1)} %get-tuple-element.19), channel_id=1, source_target_pairs={{0,256},{16,272},{32,288},{48,304},{64,320},{80,336},{96,352},{112... | collective-permute-start | bytes 196616 | tf_op jit(solution)/shard_map/ppermute | solution.py:165
  52.4 20.9 %collective-permute-start.1 = (bf16[4,2,2,128,128]{4,3,1,0,2:T(8,128)(2,1)S(1)}, bf16[4,2,2,128,128]{4,3,1,0,2:T(8,128)(2,1)S(1)}, u32[]{:S(2)}, u32[]{:S(2)}) collective-permute-start(bf16[4,2,2,128,128]{4,3,1,0,2:T(8,128)(2,1)S(1)} %bitcast.30), channel_id=1, source_target_pairs={{16,0},{32,16},{48,32},{64,48},{80,64},{96,80},{112,96},{128,112},... | collective-permute-start | bytes 1572872 | tf_op jit(solution)/shard_map/ppermute | solution.py:35
  57.3 21.2 %collective-permute-start.2 = (bf16[4,2,2,128,128]{4,3,1,0,2:T(8,128)(2,1)S(1)}, bf16[4,2,2,128,128]{4,3,1,0,2:T(8,128)(2,1)S(1)}, u32[]{:S(2)}, u32[]{:S(2)}) collective-permute-start(bf16[4,2,2,128,128]{4,3,1,0,2:T(8,128)(2,1)S(1)} %bitcast.31), channel_id=1, source_target_pairs={{240,0},{0,16},{16,32},{32,48},{48,64},{64,80},{80,96},{96,112},{1... | collective-permute-start | bytes 1572872 | tf_op jit(solution)/shard_map/ppermute | solution.py:35
  60.1 18.5 %collective-permute-start.3 = (bf16[4,2,128,128]{3,2,1,0:T(8,128)(2,1)}, bf16[4,2,128,128]{3,2,1,0:T(8,128)(2,1)S(1)}, u32[]{:S(2)}, u32[]{:S(2)}) collective-permute-start(bf16[4,2,128,128]{3,2,1,0:T(8,128)(2,1)} %get-tuple-element.17), channel_id=1, source_target_pairs={{32,0},{48,16},{64,32},{80,48},{96,64},{112,80},{128,96},{144,112}... | collective-permute-start | bytes 786440 | tf_op jit(solution)/shard_map/ppermute | solution.py:35
  63.5 15.1 %collective-permute-start.4 = (bf16[4,2,128,128]{3,2,1,0:T(8,128)(2,1)}, bf16[4,2,128,128]{3,2,1,0:T(8,128)(2,1)S(1)}, u32[]{:S(2)}, u32[]{:S(2)}) collective-permute-start(bf16[4,2,128,128]{3,2,1,0:T(8,128)(2,1)} %get-tuple-element.16), channel_id=1, source_target_pairs={{224,0},{240,16},{0,32},{16,48},{32,64},{48,80},{64,96},{80,112},{... | collective-permute-start | bytes 786440 | tf_op jit(solution)/shard_map/ppermute | solution.py:35
  78.6 3.2 %copy-start = (bf16[48,320,256]{2,1,0:T(8,128)(2,1)S(1)}, bf16[48,320,256]{2,1,0:T(8,128)(2,1)}, u32[]{:S(2)}) copy-start(bf16[48,320,256]{2,1,0:T(8,128)(2,1)} %all-gather.6.cloned.1.call-done) | copy-start | bytes 23592964
  81.9 5.2 %copy-start.1 = (bf16[48,320,256]{2,1,0:T(8,128)(2,1)S(1)}, bf16[48,320,256]{2,1,0:T(8,128)(2,1)}, u32[]{:S(2)}) copy-start(bf16[48,320,256]{2,1,0:T(8,128)(2,1)} %all-gather.6.cloned.1.call-done) | copy-start | bytes 23592964
  87.0 7.5 %copy-start.2 = (s32[128]{0:T(128)S(1)}, s32[128]{0:T(128)}, u32[]{:S(2)}) copy-start(s32[128]{0:T(128)} %param.11) | copy-start | bytes 1540
  89.8 112.5 %all-to-all-start = ((f32[2,4,4,128,128]{4,3,2,1,0:T(8,128)}), f32[2,4,4,128,128]{4,3,2,1,0:T(8,128)}, u32[]{:S(2)}, u32[]{:S(2)}) async-start(f32[2,4,4,128,128]{4,3,2,1,0:T(8,128)} %bitcast.16), calls=%async_computation | async-start | bytes 4194304 | tf_op jit(solution)/shard_map/all_to_all | solution.py:208
  202.9 22.9 %all-to-all-start.3 = ((f32[16,8,128]{2,1,0:T(8,128)}), f32[16,8,128]{2,1,0:T(8,128)S(1)}, u32[]{:S(2)}, u32[]{:S(2)}) async-start(f32[16,8,128]{2,1,0:T(8,128)} %broadcast_in_dim.9), calls=%async_computation.3 | async-start | bytes 131072 | tf_op jit(solution)/shard_map/all_to_all | solution.py:236
  225.8 28.1 %all-to-all-start.1 = ((f32[4,4,128,128]{3,2,1,0:T(8,128)}), f32[4,4,128,128]{3,2,1,0:T(8,128)S(1)}, u32[]{:S(2)}, u32[]{:S(2)}) async-start(f32[4,4,128,128]{3,2,1,0:T(8,128)} %copy.40), calls=%async_computation.1 | async-start | bytes 2097152 | tf_op jit(solution)/shard_map/all_to_all | solution.py:210
  254.5 10.4 %all-to-all-start.4 = ((f32[2,8,128]{2,1,0:T(8,128)}), f32[2,8,128]{2,1,0:T(8,128)S(1)}, u32[]{:S(2)}, u32[]{:S(2)}) async-start(f32[2,8,128]{2,1,0:T(8,128)} %broadcast_in_dim.10), calls=%async_computation.4 | async-start | bytes 16384 | tf_op jit(solution)/shard_map/all_to_all | solution.py:236
  265.0 19.3 %all-to-all-start.2 = ((f32[4,128,128]{2,1,0:T(8,128)}), f32[4,128,128]{2,1,0:T(8,128)S(1)}, u32[]{:S(2)}, u32[]{:S(2)}) async-start(f32[4,128,128]{2,1,0:T(8,128)} %reduce_sum.55), calls=%async_computation.2 | async-start | bytes 524288 | tf_op jit(solution)/shard_map/all_to_all | solution.py:211
  284.9 8.7 %all-to-all-start.5 = ((f32[16,8,128]{2,1,0:T(8,128)}), f32[16,8,128]{2,1,0:T(8,128)S(1)}, u32[]{:S(2)}, u32[]{:S(2)}) async-start(f32[16,8,128]{2,1,0:T(8,128)} %broadcast_in_dim.11), calls=%async_computation.5 | async-start | bytes 131072 | tf_op jit(solution)/shard_map/all_to_all | solution.py:236
Sparse Core Ops, SparseCore 0:
  11.5 61.4 all-gather.5
  75.2 116.5 all-gather.7

commit v2 on v1

--- a/solution.py
+++ b/solution.py
@@ -35,90 +35,74 @@
     return lax.ppermute(array, "fsdp", perm)
 
 
-def contract_blocks(place, parts, weights, counts):
+def pairs(place, own, plus, minus, two, which):
     x_hi, z_lo = place[0], place[1]
-    sums = [None] * len(counts)
-    for shift in range(4):
-        near = (z_lo + shift) % 4
-        lanes = pl.ds(pl.multiple_of((near % 2) * 128, 128), 128)
-        for other in range(2):
-            row = jnp.bitwise_xor(x_hi, other)
-            for at, which in enumerate(counts):
-                term = lax.dot_general(
-                    parts[which][shift](other),
-                    weights[row, 0, near // 2, at, :, lanes],
-                    NT,
-                    preferred_element_type=F32,
-                )
-                sums[at] = term if sums[at] is None else sums[at] + term
-    return sums
-
-
-def readers(own, plus, minus, two_x, two_g):
-    def full(ref, which):
-        return lambda other: ref[0, other, which]
-
-    def single(ref):
-        return lambda other: ref[0, other]
-
-    return [
-        [full(own, 0), full(plus, 0), single(two_x), full(minus, 0)],
-        [full(own, 1), full(plus, 1), single(two_g), full(minus, 1)],
-    ]
+    found = []
+    for other in range(2):
+        held = [own[0, other, which], plus[0, other, which], two[0, other], minus[0, other, which]]
+        near = []
+        for at in range(4):
+            block = held[0]
+            for shift in range(1, 4):
+                block = jnp.where((z_lo + shift) % 4 == at, held[shift], block)
+            near.append(block)
+        row = jnp.bitwise_xor(x_hi, other)
+        for half in range(2):
+            block = jnp.concatenate([near[2 * half], near[2 * half + 1]], axis=1)
+            found.append((row, half, block))
+    return found
+
+
+def contract(blocks, weights, first, count):
+    total = None
+    for row, half, block in blocks:
+        rows = weights[row, 0, half, first : first + count].reshape(count * 320, 256)
+        term = lax.dot_general(block, rows, NT, preferred_element_type=F32)
+        total = term if total is None else total + term
+    return total
+
+
+def add_up(step, sums, term):
+    @pl.when(step == 0)
+    def _():
+        sums[...] = term
+
+    @pl.when(step > 0)
+    def _():
+        sums[...] += term
 
 
 def primal_kernel(
-    place, own, plus, minus, two_x, two_g, weights, hidden, act_out, factor_out, dh_out, sums
+    place, own, plus, minus, two_x, two_g, weights, hidden, act_out, factor_out, dh_out, by_x, by_g
 ):
     step = pl.program_id(0)
-    terms = contract_blocks(
-        place, readers(own, plus, minus, two_x, two_g), weights, (0, 0, 1)
-    )
-
-    @pl.when(step == 0)
-    def _():
-        for at in range(3):
-            sums[at] = terms[at]
-
-    @pl.when(step > 0)
-    def _():
-        for at in range(3):
-            sums[at] += terms[at]
+    add_up(step, by_x, contract(pairs(place, own, plus, minus, two_x, 0), weights, 0, 2))
+    add_up(step, by_g, contract(pairs(place, own, plus, minus, two_g, 1), weights, 2, 1))
 
     @pl.when(step == pl.num_programs(0) - 1)
     def _():
-        upper = sums[1]
-        act, slope = gelu_value_slope(sums[0])
+        upper = by_x[:, 320:]
+        act, slope = gelu_value_slope(by_x[:, :320])
         hidden[...] = (act * upper).astype(BF16)
         act_out[...] = act
         factor_out[...] = slope * upper
-        dh_out[...] = sums[2]
+        dh_out[...] = by_g[...]
 
 
 def output_kernel(hidden, weights, out):
     for at in range(weights.shape[0]):
         value = jnp.dot(hidden[...], weights[at, 0], preferred_element_type=F32)
-        out[2 * at] = value[:, :128]
-        out[2 * at + 1] = value[:, 128:]
+        for half in range(2):
+            block = 2 * at + half
+            out[block % 4, block // 4, 0] = value[:, half * 128 : (half + 1) * 128]
 
 
 def tangent_kernel(
-    place, own, plus, minus, two_x, two_g, weights, hidden, act, factor, dh, mask, out, sums
+    place, own, plus, minus, two_x, two_g, weights, hidden, act, factor, dh, mask, out, by_x, by_g
 ):
     step = pl.program_id(0)
-    terms = contract_blocks(
-        place, readers(own, plus, minus, two_x, two_g), weights, (0, 0, 0, 0, 1, 1)
-    )
-
-    @pl.when(step == 0)
-    def _():
-        for at in range(6):
-            sums[at] = terms[at]
-
-    @pl.when(step > 0)
-    def _():
-        for at in range(6):
-            sums[at] += terms[at]
+    add_up(step, by_x, contract(pairs(place, own, plus, minus, two_x, 0), weights, 0, 4))
+    add_up(step, by_g, contract(pairs(place, own, plus, minus, two_g, 1), weights, 4, 2))
 
     @pl.when(step == pl.num_programs(0) - 1)
     def _():
@@ -126,8 +110,11 @@
         lanes = lax.broadcasted_iota(jnp.int32, (8, 128), 1)
         total = jnp.zeros((8, 128), F32)
         for k in range(2):
-            tangent = (factor[...] * sums[k] + act[...] * sums[2 + k]).astype(BF16)
-            value = tangent.astype(F32) * dh[...] + hidden[...].astype(F32) * sums[4 + k]
+            gate = by_x[:, k * 320 : (k + 1) * 320]
+            upper = by_x[:, (2 + k) * 320 : (3 + k) * 320]
+            tangent = (factor[...] * gate + act[...] * upper).astype(BF16)
+            value = tangent.astype(F32) * dh[...]
+            value += hidden[...].astype(F32) * by_g[:, k * 320 : (k + 1) * 320]
             value = jnp.sum(value, axis=1, keepdims=True) * mask[...]
             value = jnp.sum(value, axis=0, keepdims=True)
             total = jnp.where((rows == place[2]) & (lanes == k), value, total)
@@ -156,8 +143,8 @@
     place = jnp.stack([fsdp // 16, fsdp % 4, seq * rows // length]).astype(jnp.int32)
 
     stack_w = jnp.stack([w_in0, w_in1, w_out])
-    stack_t = jnp.concatenate([tan_in0, tan_in1, tan_out], axis=0)
-    stack_t, stack_w = lax.optimization_barrier((stack_t, stack_w))
+    stack_w, *tans = lax.optimization_barrier((stack_w, tan_in0, tan_in1, tan_out))
+    stack_t = jnp.concatenate(tans, axis=0)
     full_w = lax.all_gather(stack_w, "seq", axis=0).reshape(2, 4, 2, 3, 320, 256)
     full_t = lax.all_gather(stack_t, "seq", axis=0).reshape(2, 4, 2, 6, 320, 256)
 
@@ -179,7 +166,7 @@
             grid=(4,),
             in_specs=activation_specs() + [weight_spec(3)],
             out_specs=(whole((128, 320)),) * 4,
-            scratch_shapes=[pltpu.VMEM((3, 128, 320), F32)],
+            scratch_shapes=[pltpu.VMEM((128, 640), F32), pltpu.VMEM((128, 320), F32)],
         ),
         compiler_params=pltpu.CompilerParams(vmem_limit_bytes=32 * 2**20),
         cost_estimate=pl.CostEstimate(
@@ -190,13 +177,13 @@
 
     partial = pl.pallas_call(
         output_kernel,
-        out_shape=jax.ShapeDtypeStruct((32, 128, 128), F32),
+        out_shape=jax.ShapeDtypeStruct((4, 4, 2, 128, 128), F32),
         grid=(4,),
         in_specs=[
             pl.BlockSpec((128, 320), lambda s: (0, 0)),
             pl.BlockSpec((4, 1, 320, 256), lambda s: (s, 2, 0, 0)),
         ],
-        out_specs=pl.BlockSpec((8, 128, 128), lambda s: (s, 0, 0)),
+        out_specs=pl.BlockSpec((4, 2, 1, 128, 128), lambda s: (0, s % 2, s // 2, 0, 0)),
         compiler_params=pltpu.CompilerParams(vmem_limit_bytes=32 * 2**20),
         cost_estimate=pl.CostEstimate(
             flops=2 * 128 * 320 * 4096, bytes_accessed=5 * 2**20, transcendentals=0
@@ -204,12 +191,11 @@
         name="block_sums",
     )(hidden, full_w.reshape(16, 3, 320, 256))
 
-    part = partial.reshape(2, 4, 4, 128, 128)
-    part = jnp.sum(lax.all_to_all(part, "fsdp", 0, 0, axis_index_groups=X_PAIRS), axis=0)
-    part = jnp.swapaxes(part, 0, 1)
-    part = jnp.sum(lax.all_to_all(part, "fsdp", 0, 0, axis_index_groups=Z_NEAR), axis=0)
-    part = jnp.sum(lax.all_to_all(part, "fsdp", 0, 0, axis_index_groups=Z_FAR), axis=0)
-    block_out = part.astype(BF16)
+    for groups in (Z_NEAR, Z_FAR, X_PAIRS):
+        partial = lax.all_to_all(partial, "fsdp", 0, 0, axis_index_groups=groups)
+        partial = jnp.sum(partial, axis=0)
+    block_out = partial.astype(BF16)
+    block_out, hidden = lax.optimization_barrier((block_out, hidden))
 
     terms = pl.pallas_call(
         tangent_kernel,
@@ -222,7 +208,7 @@
             + [whole((128, 320))] * 4
             + [whole((128, 1))],
             out_specs=whole((8, 128)),
-            scratch_shapes=[pltpu.VMEM((6, 128, 320), F32)],
+            scratch_shapes=[pltpu.VMEM((128, 1280), F32), pltpu.VMEM((128, 640), F32)],
         ),
         compiler_params=pltpu.CompilerParams(vmem_limit_bytes=40 * 2**20),
         cost_estimate=pl.CostEstimate(

time: 305 us -> 247 us (0.81)
  waiting for transfers between devices: 170 us -> 20.2 us
  blocking collectives: 31.7 us -> 152 us
  starting transfers between devices: 50.6 us -> 22.5 us
    all_to_all x0 -> x5, blocking collectives: none -> 120 us  [the longest x2 83.1 us: shards(): partial = lax.all_to_all(partial, 'fsdp', 0, 0, axis_index_groups=groups)]
    all_gather x1, waiting for transfers between devices: 97.1 us -> 0.01 us  [shards(): lax.all_gather(stack_t, 'seq', axis=0).reshape(2, 4, 2, 6, 320, 256)]
    all_to_all x6 -> x1, waiting for transfers between devices: 57.9 us -> 5.86 us  [shards(): partial = lax.all_to_all(partial, 'fsdp', 0, 0, axis_index_groups=groups)]
    all_to_all x6 -> x1, starting transfers between devices: 32.1 us -> 3.91 us  [shards(): partial = lax.all_to_all(partial, 'fsdp', 0, 0, axis_index_groups=groups)]
  transfers between devices with their start and end apart: 13 -> 8, of which waited for: 9 -> 4; matrix products, arithmetic and copies ran while one was open for 2% -> 3% of each run, Pallas kernels for 6% -> 3%
where the time goes in v2:
time: 247 us; the launch traced here: 243 us
  blocking collectives  152 us (62%)
  starting transfers between devices  22.5 us (9%)
  waiting for transfers between devices  20.2 us (8%)
  Pallas kernels  20.2 us (8%)
  between operations  14.2 us (6%)
  other arithmetic  9.03 us (4%)
  local copies, waits for them, and re-layouts  4.92 us (2%)
    all_to_all x2, blocking collectives, shards(): partial = lax.all_to_all(partial, 'fsdp', 0, 0, axis_index_groups=groups)  83.1 us
    all_to_all x3, blocking collectives, gather_sum(): got = lax.all_to_all(copies, axis, 0, 0, axis_index_groups=groups)  37.1 us
    all_gather x1, blocking collectives, shards(): lax.all_gather(jnp.stack([both, other]), 'fsdp', axis=0, axis_index_group...  31.7 us
    ppermute x4, starting transfers between devices, z_shift(): return lax.ppermute(array, 'fsdp', perm)  13.6 us
    pallas_call x1, Pallas kernels, shards(): pl.pallas_call(tangent_kernel, out_shape=jax.ShapeDtypeStruct((8, 128), F...  12 us
    ppermute x4, waiting for transfers between devices, z_shift(): return lax.ppermute(array, 'fsdp', perm)  11.6 us
    pallas_call x1, Pallas kernels, shards(): pl.pallas_call(primal_kernel, out_shape=(jax.ShapeDtypeStruct((128, 320),...  6.49 us
    all_to_all x1, waiting for transfers between devices, shards(): partial = lax.all_to_all(partial, 'fsdp', 0, 0, axis_index_groups=groups)  5.86 us
  transfers between devices with their start and end apart: 8, of which 4 were waited for; matrix products, arithmetic and copies ran while one was open for 3% of the time, Pallas kernels for 3%

profile of v2, /device:TPU:24, one launch (start us, length us, event | category | flops | bytes accessed | tf_op | source)
XLA Modules:
  0.0 243.0 jit_solution(1157645859002710441)
XLA Ops:
  7.2 0.0 all-gather.6.cloned.1.call-start
  7.2 1.9 pad_maximum_fusion.1
  9.1 0.0 all-gather.6.cloned.1.call-update
  9.1 0.0 all-gather.8.cloned.1.call-start
  9.2 2.2 pad_maximum_fusion
  11.4 0.0 all-gather.8.cloned.1.call-update
  11.4 0.8 fusion
  12.2 4.9 %collective-permute-start = (bf16[2,128,128]{2,1,0:T(8,128)(2,1)S(1)}, bf16[2,128,128]{2,1,0:T(8,128)(2,1)S(1)}, u32[]{:S(2)}, u32[]{:S(2)}) collective-permute-start(bf16[2,128,128]{2,1,0:T(8,128)(2,1)S(1)} %get-tuple-element.27), channel_id=1, source_target_pairs={{0,256},{16,272},{32,288},{48,304},{64,320},{80,336},{96,352},{112... | collective-permute-start | bytes 196616 | tf_op jit(solution)/shard_map/ppermute | solution.py:152
  17.2 2.7 %collective-permute-done = bf16[2,128,128]{2,1,0:T(8,128)(2,1)S(1)} collective-permute-done((bf16[2,128,128]{2,1,0:T(8,128)(2,1)S(1)}, bf16[2,128,128]{2,1,0:T(8,128)(2,1)S(1)}, u32[]{:S(2)}, u32[]{:S(2)}) %collective-permute-start) | collective-permute-done | bytes 65568 | tf_op jit(solution)/shard_map/ppermute | solution.py:152
  19.9 31.7 %all-gather = bf16[8,2,128,128]{3,2,1,0:T(8,128)(2,1)S(1)} all-gather(bf16[2,2,128,128]{3,2,1,0:T(8,128)(2,1)S(1)} %pad_maximum_fusion.2), channel_id=2, replica_groups={{0,64,128,192},{16,80,144,208},{32,96,160,224},{48,112,176,240},{256,32..., dimensions={0}, use_global_device_ids=true | all-gather | bytes 655360 | tf_op jit(solution)/shard_map/all_gather | solution.py:153
  51.6 4.9 %collective-permute-start.1 = (bf16[4,2,2,128,128]{4,3,1,0,2:T(8,128)(2,1)S(1)}, bf16[4,2,2,128,128]{4,3,1,0,2:T(8,128)(2,1)S(1)}, u32[]{:S(2)}, u32[]{:S(2)}) collective-permute-start(bf16[4,2,2,128,128]{4,3,1,0,2:T(8,128)(2,1)S(1)} %bitcast.27), channel_id=1, source_target_pairs={{16,0},{32,16},{48,32},{64,48},{80,64},{96,80},{112,96},{128,112},... | collective-permute-start | bytes 1572872 | tf_op jit(solution)/shard_map/ppermute | solution.py:35
  56.6 1.9 collective-permute-start.2
  58.5 0.8 slice_bitcast_fusion
  59.3 3.4 %collective-permute-start.3 = (bf16[4,2,128,128]{3,2,1,0:T(8,128)(2,1)}, bf16[4,2,128,128]{3,2,1,0:T(8,128)(2,1)S(1)}, u32[]{:S(2)}, u32[]{:S(2)}) collective-permute-start(bf16[4,2,128,128]{3,2,1,0:T(8,128)(2,1)} %get-tuple-element.25), channel_id=1, source_target_pairs={{32,0},{48,16},{64,32},{80,48},{96,64},{112,80},{128,96},{144,112}... | collective-permute-start | bytes 786440 | tf_op jit(solution)/shard_map/ppermute | solution.py:35
  62.6 3.4 %collective-permute-start.4 = (bf16[4,2,128,128]{3,2,1,0:T(8,128)(2,1)S(1)}, bf16[4,2,128,128]{3,2,1,0:T(8,128)(2,1)S(1)}, u32[]{:S(2)}, u32[]{:S(2)}) collective-permute-start(bf16[4,2,128,128]{3,2,1,0:T(8,128)(2,1)S(1)} %get-tuple-element.24), channel_id=1, source_target_pairs={{224,0},{240,16},{0,32},{16,48},{32,64},{48,80},{64,96},{80,112},{... | collective-permute-start | bytes 786440 | tf_op jit(solution)/shard_map/ppermute | solution.py:35
  66.1 0.1 pad_add_fusion.place
  66.1 6.3 %collective-permute-done.1 = bf16[4,2,2,128,128]{4,3,1,0,2:T(8,128)(2,1)S(1)} collective-permute-done((bf16[4,2,2,128,128]{4,3,1,0,2:T(8,128)(2,1)S(1)}, bf16[4,2,2,128,128]{4,3,1,0,2:T(8,128)(2,1)S(1)}, u32[]{:S(2)}, u32[]{:S(2)}) %collective-permute-start.1) | collective-permute-done | bytes 524320 | tf_op jit(solution)/shard_map/ppermute | solution.py:35
  72.5 5.2 %collective-permute-done.2 = bf16[4,2,2,128,128]{4,3,1,0,2:T(8,128)(2,1)S(1)} collective-permute-done((bf16[4,2,2,128,128]{4,3,1,0,2:T(8,128)(2,1)S(1)}, bf16[4,2,2,128,128]{4,3,1,0,2:T(8,128)(2,1)S(1)}, u32[]{:S(2)}, u32[]{:S(2)}) %collective-permute-start.2) | collective-permute-done | bytes 524320 | tf_op jit(solution)/shard_map/ppermute | solution.py:35
  77.8 0.0 collective-permute-done.3.two_x
  77.8 0.0 collective-permute-done.4.two_g
  77.8 0.0 all-gather.6.cloned.1.call-done
  77.9 0.0 copy-start
  77.9 3.2 %copy-done = bf16[48,320,256]{2,1,0:T(8,128)(2,1)S(1)} copy-done((bf16[48,320,256]{2,1,0:T(8,128)(2,1)S(1)}, bf16[48,320,256]{2,1,0:T(8,128)(2,1)}, u32[]{:S(2)}) %copy-start) | copy-done | bytes 7864344
  81.1 0.0 copy-start.1
  81.1 6.5 %primal.1 = (bf16[128,320]{1,0:T(8,128)(2,1)S(1)}, f32[128,320]{1,0:T(8,128)S(1)}, f32[128,320]{1,0:T(8,128)S(1)}, f32[128,320]{1,0:T(8,128)S(1)}) custom-call(s32[3]{0:T(128)S(1)} %pad_add_fusion.place, bf16[4,2,2,128,128]{4,3,2,1,0:T(8,128)(2,1)S(1)} %bitcast.24, bf16[4,2,2,128,128]{4,3,2,1,0:T(8,128)(2,1)S(1)} %copy.29.plus, ...), custom_call_target="tpu_custom_call" | custom-call | flops 1006632960 | bytes 10485760 | tf_op jit(solution)/shard_map/primal/pallas_call | solution.py:161
  87.6 0.0 copy-done.1
  87.6 0.0 copy-start.2
  87.6 1.8 block_sums.1
  89.4 49.5 %all_to_all.30 = f32[4,4,2,128,128]{4,3,2,1,0:T(8,128)} all-to-all(f32[4,4,2,128,128]{4,3,2,1,0:T(8,128)S(1)} %block_sums.1), channel_id=1, replica_groups={{0,16,32,48},{64,80,96,112},{128,144,160,176},{192,208,224,240},{256,27..., dimensions={0} | all-to-all | bytes 4194304 | tf_op jit(solution)/shard_map/all_to_all | solution.py:195
  138.8 2.7 %reduce_sum.54 = f32[4,2,128,128]{3,2,1,0:T(8,128)} reduce(f32[4,4,2,128,128]{4,3,2,1,0:T(8,128)} %all_to_all.30, f32[]{:T(128)} %constant.50.clone.1), dimensions={0}, to_apply=%region_0.1 | reduce | flops 393216 | bytes 2621444 | tf_op jit(solution)/shard_map/reduce_sum | solution.py:196
  141.5 33.6 %all_to_all.31 = f32[4,2,128,128]{3,2,1,0:T(8,128)S(1)} all-to-all(f32[4,2,128,128]{3,2,1,0:T(8,128)} %reduce_sum.54), channel_id=1, replica_groups={{0,64,128,192},{16,80,144,208},{32,96,160,224},{48,112,176,240},{256,32..., dimensions={0} | all-to-all | bytes 1048576 | tf_op jit(solution)/shard_map/all_to_all | solution.py:195
  175.2 0.7 reduce_sum.55
  175.8 3.9 %all-to-all-start.2 = ((f32[2,128,128]{2,1,0:T(8,128)}), f32[2,128,128]{2,1,0:T(8,128)S(1)}, u32[]{:S(2)}, u32[]{:S(2)}) async-start(f32[2,128,128]{2,1,0:T(8,128)} %reduce_sum.55), calls=%async_computation.2 | async-start | bytes 262144 | tf_op jit(solution)/shard_map/all_to_all | solution.py:195
  179.7 0.0 copy-done.2
  179.7 0.1 copy.34.mask
  179.9 5.9 %all-to-all-done.2 = f32[2,128,128]{2,1,0:T(8,128)S(1)} async-done(((f32[2,128,128]{2,1,0:T(8,128)}), f32[2,128,128]{2,1,0:T(8,128)S(1)}, u32[]{:S(2)}, u32[]{:S(2)}) %all-to-all-start.2) | async-done | bytes 131104 | tf_op jit(solution)/shard_map/all_to_all | solution.py:195
  185.7 0.6 reduce_sum.56
  186.3 0.0 all-gather.8.cloned.1.call-done
  186.3 12.0 %tangents.1 = f32[8,128]{1,0:T(8,128)S(1)} custom-call(s32[3]{0:T(128)S(1)} %pad_add_fusion.place, bf16[4,2,2,128,128]{4,3,2,1,0:T(8,128)(2,1)S(1)} %bitcast.25, bf16[4,2,2,128,128]{4,3,2,1,0:T(8,128)(2,1)S(1)} %copy.29.plus, bf16[4,2,2,128,128]{4,3,2,1,0:T(8,128)(2,1)S(1)} %copy.30.minus, bf16[4,2,128,128]{3,2,1,0:T(8,128)(2,1)S(1)} %collective-permute-done.3.two_x, ...), custom_call_target="tpu_custom_call" | custom-call | flops 2013265920 | bytes 18874368 | tf_op jit(solution)/shard_map/tangents/pallas_call | solution.py:200
  198.3 20.7 %all_to_all.32 = f32[16,8,128]{2,1,0:T(8,128)S(1)} all-to-all(f32[16,8,128]{2,1,0:T(8,128)S(1)} %broadcast_in_dim.9), channel_id=1, replica_groups={{0,16,32,48,64,80,96,112,128,144,160,176,192,208,224,240},{256,272,288,..., dimensions={0} | all-to-all | bytes 131072 | tf_op jit(solution)/shard_map/all_to_all | solution.py:222
  219.0 7.7 %all_to_all.33 = f32[2,8,128]{2,1,0:T(8,128)S(1)} all-to-all(f32[2,8,128]{2,1,0:T(8,128)S(1)} %broadcast_in_dim.10), channel_id=1, replica_groups={{0,256},{16,272},{32,288},{48,304},{64,320},{80,336},{96,352},{112,368}..., dimensions={0} | all-to-all | bytes 16384 | tf_op jit(solution)/shard_map/all_to_all | solution.py:222
  226.7 8.8 %all_to_all.34 = f32[16,8,128]{2,1,0:T(8,128)S(1)} all-to-all(f32[16,8,128]{2,1,0:T(8,128)S(1)} %broadcast_in_dim.11), channel_id=1, replica_groups=mesh['fsdp'=32,'seq'=16] {'seq'}, dimensions={0} | all-to-all | bytes 131072 | tf_op jit(solution)/shard_map/all_to_all | solution.py:222
  235.5 0.7 copy.35
  (12 shorter events, 0.2 us)
Async XLA Ops:
  7.2 70.7 %all-gather.6.cloned.1.call-start = ((), (), s32[]{:S(2)}) async-start(), calls=%async_computation.6 | async-start | bytes 8355840 | tf_op jit(solution)/shard_map/all_gather | solution.py:148
  9.1 177.2 %all-gather.8.cloned.1.call-start = ((), (), s32[]{:S(2)}) async-start(), calls=%async_computation.7 | async-start | bytes 16711680 | tf_op jit(solution)/shard_map/all_gather | solution.py:149
  12.2 7.7 %collective-permute-start = (bf16[2,128,128]{2,1,0:T(8,128)(2,1)S(1)}, bf16[2,128,128]{2,1,0:T(8,128)(2,1)S(1)}, u32[]{:S(2)}, u32[]{:S(2)}) collective-permute-start(bf16[2,128,128]{2,1,0:T(8,128)(2,1)S(1)} %get-tuple-element.27), channel_id=1, source_target_pairs={{0,256},{16,272},{32,288},{48,304},{64,320},{80,336},{96,352},{112... | collective-permute-start | bytes 196616 | tf_op jit(solution)/shard_map/ppermute | solution.py:152
  51.6 20.9 %collective-permute-start.1 = (bf16[4,2,2,128,128]{4,3,1,0,2:T(8,128)(2,1)S(1)}, bf16[4,2,2,128,128]{4,3,1,0,2:T(8,128)(2,1)S(1)}, u32[]{:S(2)}, u32[]{:S(2)}) collective-permute-start(bf16[4,2,2,128,128]{4,3,1,0,2:T(8,128)(2,1)S(1)} %bitcast.27), channel_id=1, source_target_pairs={{16,0},{32,16},{48,32},{64,48},{80,64},{96,80},{112,96},{128,112},... | collective-permute-start | bytes 1572872 | tf_op jit(solution)/shard_map/ppermute | solution.py:35
  56.6 21.2 %collective-permute-start.2 = (bf16[4,2,2,128,128]{4,3,1,0,2:T(8,128)(2,1)S(1)}, bf16[4,2,2,128,128]{4,3,1,0,2:T(8,128)(2,1)S(1)}, u32[]{:S(2)}, u32[]{:S(2)}) collective-permute-start(bf16[4,2,2,128,128]{4,3,1,0,2:T(8,128)(2,1)S(1)} %bitcast.28), channel_id=1, source_target_pairs={{240,0},{0,16},{16,32},{32,48},{48,64},{64,80},{80,96},{96,112},{1... | collective-permute-start | bytes 1572872 | tf_op jit(solution)/shard_map/ppermute | solution.py:35
  59.3 18.5 %collective-permute-start.3 = (bf16[4,2,128,128]{3,2,1,0:T(8,128)(2,1)}, bf16[4,2,128,128]{3,2,1,0:T(8,128)(2,1)S(1)}, u32[]{:S(2)}, u32[]{:S(2)}) collective-permute-start(bf16[4,2,128,128]{3,2,1,0:T(8,128)(2,1)} %get-tuple-element.25), channel_id=1, source_target_pairs={{32,0},{48,16},{64,32},{80,48},{96,64},{112,80},{128,96},{144,112}... | collective-permute-start | bytes 786440 | tf_op jit(solution)/shard_map/ppermute | solution.py:35
  62.6 15.2 %collective-permute-start.4 = (bf16[4,2,128,128]{3,2,1,0:T(8,128)(2,1)S(1)}, bf16[4,2,128,128]{3,2,1,0:T(8,128)(2,1)S(1)}, u32[]{:S(2)}, u32[]{:S(2)}) collective-permute-start(bf16[4,2,128,128]{3,2,1,0:T(8,128)(2,1)S(1)} %get-tuple-element.24), channel_id=1, source_target_pairs={{224,0},{240,16},{0,32},{16,48},{32,64},{48,80},{64,96},{80,112},{... | collective-permute-start | bytes 786440 | tf_op jit(solution)/shard_map/ppermute | solution.py:35
  77.9 3.2 %copy-start = (bf16[48,320,256]{2,1,0:T(8,128)(2,1)S(1)}, bf16[48,320,256]{2,1,0:T(8,128)(2,1)}, u32[]{:S(2)}) copy-start(bf16[48,320,256]{2,1,0:T(8,128)(2,1)} %all-gather.6.cloned.1.call-done) | copy-start | bytes 23592964
  81.1 6.5 %copy-start.1 = (bf16[48,320,256]{2,1,0:T(8,128)(2,1)S(1)}, bf16[48,320,256]{2,1,0:T(8,128)(2,1)}, u32[]{:S(2)}) copy-start(bf16[48,320,256]{2,1,0:T(8,128)(2,1)} %all-gather.6.cloned.1.call-done) | copy-start | bytes 23592964
  87.6 92.1 %copy-start.2 = (s32[128]{0:T(128)S(1)}, s32[128]{0:T(128)}, u32[]{:S(2)}) copy-start(s32[128]{0:T(128)} %param.11) | copy-start | bytes 1540
  175.8 9.9 %all-to-all-start.2 = ((f32[2,128,128]{2,1,0:T(8,128)}), f32[2,128,128]{2,1,0:T(8,128)S(1)}, u32[]{:S(2)}, u32[]{:S(2)}) async-start(f32[2,128,128]{2,1,0:T(8,128)} %reduce_sum.55), calls=%async_computation.2 | async-start | bytes 262144 | tf_op jit(solution)/shard_map/all_to_all | solution.py:195
Sparse Core Ops, SparseCore 0:
  10.1 61.4 all-gather.5
  73.8 95.3 all-gather.7

commit v3 on v2

--- a/solution.py
+++ b/solution.py
@@ -13,10 +13,22 @@
 BF16 = jnp.bfloat16
 NT = (((1,), (1,)), ((), ()))
 
-X_PAIRS = [[i, i + 16] for i in range(16)]
-Z_NEAR = [[h * 16 + q * 4 + r for r in range(4)] for h in range(2) for q in range(4)]
 Z_FAR = [[h * 16 + q * 4 + r for q in range(4)] for h in range(2) for r in range(4)]
-Z_ALL = [list(range(16)), list(range(16, 32))]
+
+
+def eights(held):
+    sizes = (2, 4, 4, 4, 2, 2)
+    groups = {}
+    for device in range(512):
+        digits, rest = [], device
+        for size in reversed(sizes):
+            digits.insert(0, rest % size)
+            rest //= size
+        groups.setdefault(tuple(digits[at] for at in held), []).append(device)
+    return [groups[key] for key in sorted(groups)]
+
+
+ALL_BY_EIGHT = [eights((2, 3, 4, 5)), eights((0, 1, 3, 4)), eights((0, 1, 2, 5))]
 
 
 def gelu_value_slope(value):
@@ -57,7 +69,7 @@
     total = None
     for row, half, block in blocks:
         rows = weights[row, 0, half, first : first + count].reshape(count * 320, 256)
-        term = lax.dot_general(block, rows, NT, preferred_element_type=F32)
+        term = lax.dot_general(rows, block, NT, preferred_element_type=F32)
         total = term if total is None else total + term
     return total
 
@@ -73,7 +85,7 @@
 
 
 def primal_kernel(
-    place, own, plus, minus, two_x, two_g, weights, hidden, act_out, factor_out, dh_out, by_x, by_g
+    place, own, plus, minus, two_x, two_g, weights, hidden, across, act_out, factor_out, dh_out, by_x, by_g
 ):
     step = pl.program_id(0)
     add_up(step, by_x, contract(pairs(place, own, plus, minus, two_x, 0), weights, 0, 2))
@@ -81,24 +93,43 @@
 
     @pl.when(step == pl.num_programs(0) - 1)
     def _():
-        upper = by_x[:, 320:]
-        act, slope = gelu_value_slope(by_x[:, :320])
-        hidden[...] = (act * upper).astype(BF16)
+        upper = by_x[320:]
+        act, slope = gelu_value_slope(by_x[:320])
+        product = act * upper
+        hidden[...] = jnp.transpose(product).astype(BF16)
+        across[...] = product.astype(BF16)
         act_out[...] = act
         factor_out[...] = slope * upper
         dh_out[...] = by_g[...]
 
 
-def output_kernel(hidden, weights, out):
-    for at in range(weights.shape[0]):
-        value = jnp.dot(hidden[...], weights[at, 0], preferred_element_type=F32)
-        for half in range(2):
-            block = 2 * at + half
-            out[block % 4, block // 4, 0] = value[:, half * 128 : (half + 1) * 128]
+def output_kernel(place, hidden, weights, own, plus, minus, two_a, two_b):
+    z_lo = place[1]
+    for z_hi in range(4):
+        for shift in range(4):
+            near = (z_lo + shift) % 4
+            lanes = pl.ds(pl.multiple_of((near % 2) * 128, 128), 128)
+            rows = weights[0, z_hi, near // 2, 0, :, lanes]
+            value = jnp.dot(hidden[...], rows, preferred_element_type=F32)
+            if shift == 0:
+                own[0, z_hi] = value
+            elif shift == 1:
+                plus[0, z_hi] = value
+            elif shift == 3:
+                minus[0, z_hi] = value
+            else:
+
+                @pl.when(pl.program_id(0) == 0)
+                def _():
+                    two_a[z_hi] = value
+
+                @pl.when(pl.program_id(0) == 1)
+                def _():
+                    two_b[z_hi] = value
 
 
 def tangent_kernel(
-    place, own, plus, minus, two_x, two_g, weights, hidden, act, factor, dh, mask, out, by_x, by_g
+    place, own, plus, minus, two_x, two_g, weights, across, act, factor, dh, mask, out, by_x, by_g
 ):
     step = pl.program_id(0)
     add_up(step, by_x, contract(pairs(place, own, plus, minus, two_x, 0), weights, 0, 4))
@@ -110,13 +141,13 @@
         lanes = lax.broadcasted_iota(jnp.int32, (8, 128), 1)
         total = jnp.zeros((8, 128), F32)
         for k in range(2):
-            gate = by_x[:, k * 320 : (k + 1) * 320]
-            upper = by_x[:, (2 + k) * 320 : (3 + k) * 320]
+            gate = by_x[k * 320 : (k + 1) * 320]
+            upper = by_x[(2 + k) * 320 : (3 + k) * 320]
             tangent = (factor[...] * gate + act[...] * upper).astype(BF16)
             value = tangent.astype(F32) * dh[...]
-            value += hidden[...].astype(F32) * by_g[:, k * 320 : (k + 1) * 320]
-            value = jnp.sum(value, axis=1, keepdims=True) * mask[...]
-            value = jnp.sum(value, axis=0, keepdims=True)
+            value += across[...].astype(F32) * by_g[k * 320 : (k + 1) * 320]
+            value = jnp.sum(value, axis=0, keepdims=True) * mask[...]
+            value = jnp.sum(value, axis=1, keepdims=True)
             total = jnp.where((rows == place[2]) & (lanes == k), value, total)
         out[...] = total
 
@@ -157,16 +188,22 @@
     two_g = z_shift(own[:, :, 1], -2)
     acts = (own, plus, minus, two_x, two_g)
 
-    flat = jax.ShapeDtypeStruct((128, 320), F32)
-    hidden, act, factor, dh = pl.pallas_call(
+    flat = jax.ShapeDtypeStruct((320, 128), F32)
+    hidden, across, act, factor, dh = pl.pallas_call(
         primal_kernel,
-        out_shape=(jax.ShapeDtypeStruct((128, 320), BF16), flat, flat, flat),
+        out_shape=(
+            jax.ShapeDtypeStruct((128, 320), BF16),
+            jax.ShapeDtypeStruct((320, 128), BF16),
+            flat,
+            flat,
+            flat,
+        ),
         grid_spec=pltpu.PrefetchScalarGridSpec(
             num_scalar_prefetch=1,
             grid=(4,),
             in_specs=activation_specs() + [weight_spec(3)],
-            out_specs=(whole((128, 320)),) * 4,
-            scratch_shapes=[pltpu.VMEM((128, 640), F32), pltpu.VMEM((128, 320), F32)],
+            out_specs=(whole((128, 320)),) + (whole((320, 128)),) * 4,
+            scratch_shapes=[pltpu.VMEM((640, 128), F32), pltpu.VMEM((320, 128), F32)],
         ),
         compiler_params=pltpu.CompilerParams(vmem_limit_bytes=32 * 2**20),
         cost_estimate=pl.CostEstimate(
@@ -175,27 +212,41 @@
         name="primal",
     )(place, *acts, full_w)
 
-    partial = pl.pallas_call(
+    by_x_hi = pl.BlockSpec((1, 4, 128, 128), lambda s, p: (s, 0, 0, 0))
+    half_sums = jax.ShapeDtypeStruct((4, 128, 128), F32)
+    both_sums = jax.ShapeDtypeStruct((2, 4, 128, 128), F32)
+    kept, up, down, two_up, two_down = pl.pallas_call(
         output_kernel,
-        out_shape=jax.ShapeDtypeStruct((4, 4, 2, 128, 128), F32),
-        grid=(4,),
-        in_specs=[
-            pl.BlockSpec((128, 320), lambda s: (0, 0)),
-            pl.BlockSpec((4, 1, 320, 256), lambda s: (s, 2, 0, 0)),
-        ],
-        out_specs=pl.BlockSpec((4, 2, 1, 128, 128), lambda s: (0, s % 2, s // 2, 0, 0)),
+        out_shape=(both_sums, both_sums, both_sums, half_sums, half_sums),
+        grid_spec=pltpu.PrefetchScalarGridSpec(
+            num_scalar_prefetch=1,
+            grid=(2,),
+            in_specs=[
+                whole((128, 320)),
+                pl.BlockSpec(
+                    (1, 4, 2, 1, 320, 256),
+                    lambda s, p: (jnp.bitwise_xor(p[0], s), 0, 0, 2, 0, 0),
+                ),
+            ],
+            out_specs=(by_x_hi, by_x_hi, by_x_hi, whole((4, 128, 128)), whole((4, 128, 128))),
+        ),
         compiler_params=pltpu.CompilerParams(vmem_limit_bytes=32 * 2**20),
         cost_estimate=pl.CostEstimate(
             flops=2 * 128 * 320 * 4096, bytes_accessed=5 * 2**20, transcendentals=0
         ),
         name="block_sums",
-    )(hidden, full_w.reshape(16, 3, 320, 256))
-
-    for groups in (Z_NEAR, Z_FAR, X_PAIRS):
-        partial = lax.all_to_all(partial, "fsdp", 0, 0, axis_index_groups=groups)
-        partial = jnp.sum(partial, axis=0)
+    )(place, hidden, full_w)
+
+    up = z_shift(up, -1)
+    down = z_shift(down, 1)
+    two_up = z_shift(two_up, -2)
+    two_down = z_shift(two_down, 2)
+    away = kept[1] + up[1] + down[1] + two_down
+    away = lax.ppermute(away, "fsdp", [(i, (i + 16) % 32) for i in range(32)])
+    partial = kept[0] + up[0] + down[0] + two_up + away
+    partial = jnp.sum(lax.all_to_all(partial, "fsdp", 0, 0, axis_index_groups=Z_FAR), axis=0)
     block_out = partial.astype(BF16)
-    block_out, hidden = lax.optimization_barrier((block_out, hidden))
+    block_out, across = lax.optimization_barrier((block_out, across))
 
     terms = pl.pallas_call(
         tangent_kernel,
@@ -205,26 +256,22 @@
             grid=(4,),
             in_specs=activation_specs()
             + [weight_spec(6)]
-            + [whole((128, 320))] * 4
-            + [whole((128, 1))],
+            + [whole((320, 128))] * 4
+            + [whole((1, 128))],
             out_specs=whole((8, 128)),
-            scratch_shapes=[pltpu.VMEM((128, 1280), F32), pltpu.VMEM((128, 640), F32)],
+            scratch_shapes=[pltpu.VMEM((1280, 128), F32), pltpu.VMEM((640, 128), F32)],
         ),
         compiler_params=pltpu.CompilerParams(vmem_limit_bytes=40 * 2**20),
         cost_estimate=pl.CostEstimate(
             flops=2 * 6 * 128 * 320 * 4096, bytes_accessed=18 * 2**20, transcendentals=0
         ),
         name="tangents",
-    )(place, *acts, full_t, hidden, act, factor, dh, loss_mask.astype(F32)[:, None])
-
-    def gather_sum(value, axis, groups, size):
-        copies = jnp.broadcast_to(value[None], (size,) + value.shape)
-        got = lax.all_to_all(copies, axis, 0, 0, axis_index_groups=groups)
-        return jnp.sum(got, axis=0)
-
-    terms = gather_sum(terms, "fsdp", Z_ALL, 16)
-    terms = gather_sum(terms, "fsdp", X_PAIRS, 2)
-    terms = gather_sum(terms, "seq", None, 16)
+    )(place, *acts, full_t, across, act, factor, dh, loss_mask.astype(F32)[None])
+
+    for groups in ALL_BY_EIGHT:
+        copies = jnp.broadcast_to(terms[None], (8,) + terms.shape)
+        got = lax.all_to_all(copies, ("fsdp", "seq"), 0, 0, axis_index_groups=groups)
+        terms = jnp.sum(got, axis=0)
     return (block_out, terms[:EXAMPLES, :2])
 
 

time: 247 us -> 241 us (0.976); the launches traced: 243 us -> 239 us
  blocking collectives: 152 us -> 77.3 us
  waiting for transfers between devices: 20.2 us -> 65.5 us
  starting transfers between devices: 22.5 us -> 47.1 us
  local copies, waits for them, and re-layouts: 4.92 us -> 8.01 us
  other arithmetic: 9.03 us -> 6.55 us
    all_to_all x5 -> x3, blocking collectives: 120 us -> 45.7 us  [shards(): lax.all_to_all(copies, ('fsdp', 'seq'), 0, 0, axis_index_groups=groups)]
    ppermute x4 -> x8, starting transfers between devices: 13.6 us -> 29 us  [z_shift(): return lax.ppermute(array, 'fsdp', perm)]
    all_gather x1, waiting for transfers between devices: 0.01 us -> 13.1 us  [shards(): lax.all_gather(stack_t, 'seq', axis=0).reshape(2, 4, 2, 6, 320, 256)]
    ppermute x4 -> x8, waiting for transfers between devices: 11.6 us -> 24.4 us  [z_shift(): return lax.ppermute(array, 'fsdp', perm)]
    ppermute x0 -> x1, waiting for transfers between devices: none -> 10.4 us  [shards(): away = lax.ppermute(away, 'fsdp', [(i, (i + 16) % 32) for i in range(32)])]
    all_to_all x1, waiting for transfers between devices: 5.86 us -> 14.9 us  [shards(): lax.all_to_all(partial, 'fsdp', 0, 0, axis_index_groups=Z_FAR)]
    ppermute x0 -> x1, starting transfers between devices: none -> 4.93 us  [shards(): away = lax.ppermute(away, 'fsdp', [(i, (i + 16) % 32) for i in range(32)])]
    all_to_all x1, starting transfers between devices: 3.91 us -> 8.17 us  [shards(): lax.all_to_all(partial, 'fsdp', 0, 0, axis_index_groups=Z_FAR)]
  transfers between devices with their start and end apart: 8 -> 13, of which waited for: 4 -> 7; matrix products, arithmetic and copies ran while one was open for 3% -> 2% of each run, Pallas kernels for 3% -> 4%
where the time goes in v3:
time: 241 us; the launch traced here: 239 us
  blocking collectives  77.3 us (32%)
  waiting for transfers between devices  65.5 us (27%)
  starting transfers between devices  47.1 us (20%)
  Pallas kernels  20.7 us (9%)
  between operations  14.3 us (6%)
  local copies, waits for them, and re-layouts  8.01 us (3%)
  other arithmetic  6.55 us (3%)
    all_to_all x3, blocking collectives, shards(): lax.all_to_all(copies, ('fsdp', 'seq'), 0, 0, axis_index_groups=groups)  45.7 us
    all_gather x1, blocking collectives, shards(): lax.all_gather(jnp.stack([both, other]), 'fsdp', axis=0, axis_index_group...  31.7 us
    ppermute x8, starting transfers between devices, z_shift(): return lax.ppermute(array, 'fsdp', perm)  29 us
    ppermute x8, waiting for transfers between devices, z_shift(): return lax.ppermute(array, 'fsdp', perm)  24.4 us
    all_to_all x1, waiting for transfers between devices, shards(): lax.all_to_all(partial, 'fsdp', 0, 0, axis_index_groups=Z_FAR)  14.9 us
    all_gather x1, waiting for transfers between devices, shards(): lax.all_gather(stack_t, 'seq', axis=0).reshape(2, 4, 2, 6, 320, 256)  13.1 us
    pallas_call x1, Pallas kernels, shards(): pl.pallas_call(tangent_kernel, out_shape=jax.ShapeDtypeStruct((8, 128), F...  11.4 us
    ppermute x1, waiting for transfers between devices, shards(): away = lax.ppermute(away, 'fsdp', [(i, (i + 16) % 32) for i in range(32)])  10.4 us
  transfers between devices with their start and end apart: 13, of which 7 were waited for; matrix products, arithmetic and copies ran while one was open for 2% of the time, Pallas kernels for 4%

profile of v3, /device:TPU:24, one launch (start us, length us, event | category | flops | bytes accessed | tf_op | source)
XLA Modules:
  0.0 239.5 jit_solution(14529179392444994094)
XLA Ops:
  7.2 0.0 copy-start.2
  7.2 0.0 all-gather.6.cloned.1.call-start
  7.2 2.0 pad_maximum_fusion.1
  9.2 0.0 all-gather.6.cloned.1.call-update
  9.2 0.0 all-gather.8.cloned.1.call-start
  9.3 2.2 pad_maximum_fusion
  11.5 0.0 all-gather.8.cloned.1.call-update
  11.5 0.8 fusion.5
  12.3 4.9 %collective-permute-start = (bf16[2,128,128]{2,1,0:T(8,128)(2,1)S(1)}, bf16[2,128,128]{2,1,0:T(8,128)(2,1)S(1)}, u32[]{:S(2)}, u32[]{:S(2)}) collective-permute-start(bf16[2,128,128]{2,1,0:T(8,128)(2,1)S(1)} %get-tuple-element.39), channel_id=1, source_target_pairs={{0,256},{16,272},{32,288},{48,304},{64,320},{80,336},{96,352},{112... | collective-permute-start | bytes 196616 | tf_op jit(solution)/shard_map/ppermute | solution.py:183
  17.2 2.7 %collective-permute-done = bf16[2,128,128]{2,1,0:T(8,128)(2,1)S(1)} collective-permute-done((bf16[2,128,128]{2,1,0:T(8,128)(2,1)S(1)}, bf16[2,128,128]{2,1,0:T(8,128)(2,1)S(1)}, u32[]{:S(2)}, u32[]{:S(2)}) %collective-permute-start) | collective-permute-done | bytes 65568 | tf_op jit(solution)/shard_map/ppermute | solution.py:183
  20.0 31.7 %all-gather = bf16[8,2,128,128]{3,2,1,0:T(8,128)(2,1)S(1)} all-gather(bf16[2,2,128,128]{3,2,1,0:T(8,128)(2,1)S(1)} %pad_maximum_fusion.2), channel_id=2, replica_groups={{0,64,128,192},{16,80,144,208},{32,96,160,224},{48,112,176,240},{256,32..., dimensions={0}, use_global_device_ids=true | all-gather | bytes 655360 | tf_op jit(solution)/shard_map/all_gather | solution.py:184
  51.7 4.9 %collective-permute-start.1 = (bf16[4,2,2,128,128]{4,3,1,0,2:T(8,128)(2,1)S(1)}, bf16[4,2,2,128,128]{4,3,1,0,2:T(8,128)(2,1)S(1)}, u32[]{:S(2)}, u32[]{:S(2)}) collective-permute-start(bf16[4,2,2,128,128]{4,3,1,0,2:T(8,128)(2,1)S(1)} %bitcast.36), channel_id=1, source_target_pairs={{16,0},{32,16},{48,32},{64,48},{80,64},{96,80},{112,96},{128,112},... | collective-permute-start | bytes 1572872 | tf_op jit(solution)/shard_map/ppermute | solution.py:47
  56.7 1.9 collective-permute-start.2
  58.6 0.8 slice_bitcast_fusion
  59.3 3.4 %collective-permute-start.3 = (bf16[4,2,128,128]{3,2,1,0:T(8,128)(2,1)}, bf16[4,2,128,128]{3,2,1,0:T(8,128)(2,1)S(1)}, u32[]{:S(2)}, u32[]{:S(2)}) collective-permute-start(bf16[4,2,128,128]{3,2,1,0:T(8,128)(2,1)} %get-tuple-element.37), channel_id=1, source_target_pairs={{32,0},{48,16},{64,32},{80,48},{96,64},{112,80},{128,96},{144,112}... | collective-permute-start | bytes 786440 | tf_op jit(solution)/shard_map/ppermute | solution.py:47
  62.7 3.4 %collective-permute-start.4 = (bf16[4,2,128,128]{3,2,1,0:T(8,128)(2,1)S(1)}, bf16[4,2,128,128]{3,2,1,0:T(8,128)(2,1)S(1)}, u32[]{:S(2)}, u32[]{:S(2)}) collective-permute-start(bf16[4,2,128,128]{3,2,1,0:T(8,128)(2,1)S(1)} %get-tuple-element.36), channel_id=1, source_target_pairs={{224,0},{240,16},{0,32},{16,48},{32,64},{48,80},{64,96},{80,112},{... | collective-permute-start | bytes 786440 | tf_op jit(solution)/shard_map/ppermute | solution.py:47
  66.1 0.1 pad_add_fusion.place
  66.2 6.4 %collective-permute-done.1 = bf16[4,2,2,128,128]{4,3,1,0,2:T(8,128)(2,1)S(1)} collective-permute-done((bf16[4,2,2,128,128]{4,3,1,0,2:T(8,128)(2,1)S(1)}, bf16[4,2,2,128,128]{4,3,1,0,2:T(8,128)(2,1)S(1)}, u32[]{:S(2)}, u32[]{:S(2)}) %collective-permute-start.1) | collective-permute-done | bytes 524320 | tf_op jit(solution)/shard_map/ppermute | solution.py:47
  72.6 5.3 %collective-permute-done.2 = bf16[4,2,2,128,128]{4,3,1,0,2:T(8,128)(2,1)S(1)} collective-permute-done((bf16[4,2,2,128,128]{4,3,1,0,2:T(8,128)(2,1)S(1)}, bf16[4,2,2,128,128]{4,3,1,0,2:T(8,128)(2,1)S(1)}, u32[]{:S(2)}, u32[]{:S(2)}) %collective-permute-start.2) | collective-permute-done | bytes 524320 | tf_op jit(solution)/shard_map/ppermute | solution.py:47
  77.9 0.0 collective-permute-done.3.two_x
  77.9 0.0 collective-permute-done.4.two_g
  77.9 0.0 all-gather.6.cloned.1.call-done
  78.0 0.0 copy-start
  78.0 3.2 %copy-done = bf16[48,320,256]{2,1,0:T(8,128)(2,1)S(1)} copy-done((bf16[48,320,256]{2,1,0:T(8,128)(2,1)S(1)}, bf16[48,320,256]{2,1,0:T(8,128)(2,1)}, u32[]{:S(2)}) %copy-start) | copy-done | bytes 7864344
  81.2 6.1 %primal.1 = (bf16[128,320]{1,0:T(8,128)(2,1)S(1)}, bf16[320,128]{1,0:T(8,128)(2,1)S(1)}, f32[320,128]{1,0:T(8,128)S(1)}, f32[320,128]{1,0:T(8,128)S(1)}, f32[320,128]{1,0:T(8,128)S(1)}) custom-call(s32[3]{0:T(128)S(1)} %pad_add_fusion.place, bf16[4,2,2,128,128]{4,3,2,1,0:T(8,128)(2,1)S(1)} %bitcast.33, bf16[4,2,2,128,128]{4,3,2,1,0:T(8,128)(2,1)S(1)} %copy.27.plus, ...), custom_call_target="tpu_custom_call" | custom-call | flops 1006632960 | bytes 10485760 | tf_op jit(solution)/shard_map/primal/pallas_call | solution.py:192
  87.3 0.0 copy-start.1
  87.3 3.2 %copy-done.1 = bf16[48,320,256]{2,1,0:T(8,128)(2,1)S(1)} copy-done((bf16[48,320,256]{2,1,0:T(8,128)(2,1)S(1)}, bf16[48,320,256]{2,1,0:T(8,128)(2,1)}, u32[]{:S(2)}) %copy-start.1) | copy-done | bytes 7864344
  90.6 3.2 %block_sums.1 = (f32[2,4,128,128]{3,2,1,0:T(8,128)S(1)}, f32[2,4,128,128]{3,2,1,0:T(8,128)S(1)}, f32[2,4,128,128]{3,2,1,0:T(8,128)S(1)}, f32[4,128,128]{2,1,0:T(8,128)S(1)}, f32[4,128,128]{2,1,0:T(8,128)S(1)}) custom-call(s32[3]{0:T(128)S(1)} %pad_add_fusion.place, bf16[128,320]{1,0:T(8,128)(2,1)S(1)} %get-tuple-element.19.hidden, ...), custom_call_target="tpu_custom_call" | custom-call | flops 335544320 | bytes 5242880 | tf_op jit(solution)/shard_map/block_sums/pallas_call | solution.py:218
  93.8 6.7 %collective-permute-start.5 = (f32[2,4,128,128]{3,2,1,0:T(8,128)S(1)}, f32[2,4,128,128]{3,2,1,0:T(8,128)S(1)}, u32[]{:S(2)}, u32[]{:S(2)}) collective-permute-start(f32[2,4,128,128]{3,2,1,0:T(8,128)S(1)} %get-tuple-element.21), channel_id=1, source_target_pairs={{240,0},{0,16},{16,32},{32,48},{48,64},{64,80},{80,96},{96,112},{1... | collective-permute-start | bytes 1572872 | tf_op jit(solution)/shard_map/ppermute | solution.py:47
  100.5 1.9 collective-permute-start.6
  102.4 3.5 %collective-permute-start.8 = (f32[4,128,128]{2,1,0:T(8,128)S(1)}, f32[4,128,128]{2,1,0:T(8,128)S(1)}, u32[]{:S(2)}, u32[]{:S(2)}) collective-permute-start(f32[4,128,128]{2,1,0:T(8,128)S(1)} %get-tuple-element.24), channel_id=1, source_target_pairs={{32,0},{48,16},{64,32},{80,48},{96,64},{112,80},{128,96},{144,112}... | collective-permute-start | bytes 786440 | tf_op jit(solution)/shard_map/ppermute | solution.py:47
  105.9 3.2 %collective-permute-start.7 = (f32[4,128,128]{2,1,0:T(8,128)S(1)}, f32[4,128,128]{2,1,0:T(8,128)S(1)}, u32[]{:S(2)}, u32[]{:S(2)}) collective-permute-start(f32[4,128,128]{2,1,0:T(8,128)S(1)} %get-tuple-element.23), channel_id=1, source_target_pairs={{224,0},{240,16},{0,32},{16,48},{32,64},{48,80},{64,96},{80,112},{... | collective-permute-start | bytes 786440 | tf_op jit(solution)/shard_map/ppermute | solution.py:47
  109.2 12.8 %collective-permute-done.8 = f32[4,128,128]{2,1,0:T(8,128)S(1)} collective-permute-done((f32[4,128,128]{2,1,0:T(8,128)S(1)}, f32[4,128,128]{2,1,0:T(8,128)S(1)}, u32[]{:S(2)}, u32[]{:S(2)}) %collective-permute-start.8) | collective-permute-done | bytes 262176 | tf_op jit(solution)/shard_map/ppermute | solution.py:47
  121.9 0.0 collective-permute-done.5
  122.0 0.0 collective-permute-done.6
  122.0 0.1 fusion.1
  122.0 4.9 %collective-permute-start.9 = (f32[4,128,128]{2,1,0:T(8,128)S(1)}, f32[4,128,128]{2,1,0:T(8,128)S(1)}, u32[]{:S(2)}, u32[]{:S(2)}) collective-permute-start(f32[4,128,128]{2,1,0:T(8,128)S(1)} %fusion.1), channel_id=1, source_target_pairs={{0,256},{16,272},{32,288},{48,304},{64,320},{80,336},{96,352},{112... | collective-permute-start | bytes 786440 | tf_op jit(solution)/shard_map/ppermute | solution.py:245
  126.9 0.0 collective-permute-done.7
  127.0 10.4 %collective-permute-done.9 = f32[4,128,128]{2,1,0:T(8,128)S(1)} collective-permute-done((f32[4,128,128]{2,1,0:T(8,128)S(1)}, f32[4,128,128]{2,1,0:T(8,128)S(1)}, u32[]{:S(2)}, u32[]{:S(2)}) %collective-permute-start.9) | collective-permute-done | bytes 262176 | tf_op jit(solution)/shard_map/ppermute | solution.py:245
  137.4 0.8 fusion.4
  138.1 8.2 %all-to-all-start = ((f32[4,128,128]{2,1,0:T(8,128)}), f32[4,128,128]{2,1,0:T(8,128)S(1)}, u32[]{:S(2)}, u32[]{:S(2)}) async-start(f32[4,128,128]{2,1,0:T(8,128)} %fusion.4), calls=%async_computation | async-start | bytes 524288 | tf_op jit(solution)/shard_map/all_to_all | solution.py:247
  146.3 0.0 copy-done.2
  146.3 14.9 %all-to-all-done = f32[4,128,128]{2,1,0:T(8,128)S(1)} async-done(((f32[4,128,128]{2,1,0:T(8,128)}), f32[4,128,128]{2,1,0:T(8,128)S(1)}, u32[]{:S(2)}, u32[]{:S(2)}) %all-to-all-start) | async-done | bytes 262176 | tf_op jit(solution)/shard_map/all_to_all | solution.py:247
  161.2 0.6 reduce_sum.36
  161.8 13.1 %all-gather.8.cloned.1.call-done = bf16[96,320,256]{2,1,0:T(8,128)(2,1)} async-done(((bf16[6,320,256]{2,1,0:T(8,128)(2,1)}), bf16[96,320,256]{2,1,0:T(8,128)(2,1)}) %all-gather.8.cloned.1.call-update) | async-done | bytes 15728656 | tf_op jit(solution)/shard_map/all_gather | solution.py:180
  174.9 11.4 %tangents.1 = f32[8,128]{1,0:T(8,128)S(1)} custom-call(s32[3]{0:T(128)S(1)} %pad_add_fusion.place, bf16[4,2,2,128,128]{4,3,2,1,0:T(8,128)(2,1)S(1)} %bitcast.34, bf16[4,2,2,128,128]{4,3,2,1,0:T(8,128)(2,1)S(1)} %copy.27.plus, bf16[4,2,2,128,128]{4,3,2,1,0:T(8,128)(2,1)S(1)} %copy.28.minus, bf16[4,2,128,128]{3,2,1,0:T(8,128)(2,1)S(1)} %collective-permute-done.3.two_x, ...), custom_call_target="tpu_custom_call" | custom-call | flops 2013265920 | bytes 18874368 | tf_op jit(solution)/shard_map/tangents/pallas_call | solution.py:251
  186.3 29.1 %all_to_all.20 = f32[8,8,128]{2,1,0:T(8,128)S(1)} all-to-all(f32[8,8,128]{2,1,0:T(8,128)S(1)} %broadcast_in_dim.9), channel_id=1, replica_groups={{0,64,128,192,256,320,384,448},{1,65,129,193,257,321,385,449},{2,66,130..., dimensions={0} | all-to-all | bytes 65536 | tf_op jit(solution)/shard_map/all_to_all | solution.py:273
  215.4 8.1 %all_to_all.21 = f32[8,8,128]{2,1,0:T(8,128)S(1)} all-to-all(f32[8,8,128]{2,1,0:T(8,128)S(1)} %broadcast_in_dim.10), channel_id=1, replica_groups={{0,1,16,17,32,33,48,49},{2,3,18,19,34,35,50,51},{4,5,20,21,36,37,52,53}..., dimensions={0} | all-to-all | bytes 65536 | tf_op jit(solution)/shard_map/all_to_all | solution.py:273
  223.5 8.5 %all_to_all.22 = f32[8,8,128]{2,1,0:T(8,128)S(1)} all-to-all(f32[8,8,128]{2,1,0:T(8,128)S(1)} %broadcast_in_dim.11), channel_id=1, replica_groups={{0,2,4,6,8,10,12,14},{1,3,5,7,9,11,13,15},{16,18,20,22,24,26,28,30},{17..., dimensions={0} | all-to-all | bytes 65536 | tf_op jit(solution)/shard_map/all_to_all | solution.py:273
  232.0 0.7 copy.32
  (12 shorter events, 0.2 us)
Async XLA Ops:
  7.2 139.1 %copy-start.2 = (s32[128]{0:T(128)S(1)}, s32[128]{0:T(128)}, u32[]{:S(2)}) copy-start(s32[128]{0:T(128)} %param.11) | copy-start | bytes 1540
  7.2 70.8 %all-gather.6.cloned.1.call-start = ((), (), s32[]{:S(2)}) async-start(), calls=%async_computation.4 | async-start | bytes 8355840 | tf_op jit(solution)/shard_map/all_gather | solution.py:179
  9.2 165.7 %all-gather.8.cloned.1.call-start = ((), (), s32[]{:S(2)}) async-start(), calls=%async_computation.5 | async-start | bytes 16711680 | tf_op jit(solution)/shard_map/all_gather | solution.py:180
  12.3 7.7 %collective-permute-start = (bf16[2,128,128]{2,1,0:T(8,128)(2,1)S(1)}, bf16[2,128,128]{2,1,0:T(8,128)(2,1)S(1)}, u32[]{:S(2)}, u32[]{:S(2)}) collective-permute-start(bf16[2,128,128]{2,1,0:T(8,128)(2,1)S(1)} %get-tuple-element.39), channel_id=1, source_target_pairs={{0,256},{16,272},{32,288},{48,304},{64,320},{80,336},{96,352},{112... | collective-permute-start | bytes 196616 | tf_op jit(solution)/shard_map/ppermute | solution.py:183
  51.7 20.9 %collective-permute-start.1 = (bf16[4,2,2,128,128]{4,3,1,0,2:T(8,128)(2,1)S(1)}, bf16[4,2,2,128,128]{4,3,1,0,2:T(8,128)(2,1)S(1)}, u32[]{:S(2)}, u32[]{:S(2)}) collective-permute-start(bf16[4,2,2,128,128]{4,3,1,0,2:T(8,128)(2,1)S(1)} %bitcast.36), channel_id=1, source_target_pairs={{16,0},{32,16},{48,32},{64,48},{80,64},{96,80},{112,96},{128,112},... | collective-permute-start | bytes 1572872 | tf_op jit(solution)/shard_map/ppermute | solution.py:47
  56.7 21.2 %collective-permute-start.2 = (bf16[4,2,2,128,128]{4,3,1,0,2:T(8,128)(2,1)S(1)}, bf16[4,2,2,128,128]{4,3,1,0,2:T(8,128)(2,1)S(1)}, u32[]{:S(2)}, u32[]{:S(2)}) collective-permute-start(bf16[4,2,2,128,128]{4,3,1,0,2:T(8,128)(2,1)S(1)} %bitcast.37), channel_id=1, source_target_pairs={{240,0},{0,16},{16,32},{32,48},{48,64},{64,80},{80,96},{96,112},{1... | collective-permute-start | bytes 1572872 | tf_op jit(solution)/shard_map/ppermute | solution.py:47
  59.3 18.6 %collective-permute-start.3 = (bf16[4,2,128,128]{3,2,1,0:T(8,128)(2,1)}, bf16[4,2,128,128]{3,2,1,0:T(8,128)(2,1)S(1)}, u32[]{:S(2)}, u32[]{:S(2)}) collective-permute-start(bf16[4,2,128,128]{3,2,1,0:T(8,128)(2,1)} %get-tuple-element.37), channel_id=1, source_target_pairs={{32,0},{48,16},{64,32},{80,48},{96,64},{112,80},{128,96},{144,112}... | collective-permute-start | bytes 786440 | tf_op jit(solution)/shard_map/ppermute | solution.py:47
  62.7 15.2 %collective-permute-start.4 = (bf16[4,2,128,128]{3,2,1,0:T(8,128)(2,1)S(1)}, bf16[4,2,128,128]{3,2,1,0:T(8,128)(2,1)S(1)}, u32[]{:S(2)}, u32[]{:S(2)}) collective-permute-start(bf16[4,2,128,128]{3,2,1,0:T(8,128)(2,1)S(1)} %get-tuple-element.36), channel_id=1, source_target_pairs={{224,0},{240,16},{0,32},{16,48},{32,64},{48,80},{64,96},{80,112},{... | collective-permute-start | bytes 786440 | tf_op jit(solution)/shard_map/ppermute | solution.py:47
  78.0 3.2 %copy-start = (bf16[48,320,256]{2,1,0:T(8,128)(2,1)S(1)}, bf16[48,320,256]{2,1,0:T(8,128)(2,1)}, u32[]{:S(2)}) copy-start(bf16[48,320,256]{2,1,0:T(8,128)(2,1)} %all-gather.6.cloned.1.call-done) | copy-start | bytes 23592964
  87.3 3.2 %copy-start.1 = (bf16[48,320,256]{2,1,0:T(8,128)(2,1)S(1)}, bf16[48,320,256]{2,1,0:T(8,128)(2,1)}, u32[]{:S(2)}) copy-start(bf16[48,320,256]{2,1,0:T(8,128)(2,1)} %all-gather.6.cloned.1.call-done) | copy-start | bytes 23592964
  93.8 28.2 %collective-permute-start.5 = (f32[2,4,128,128]{3,2,1,0:T(8,128)S(1)}, f32[2,4,128,128]{3,2,1,0:T(8,128)S(1)}, u32[]{:S(2)}, u32[]{:S(2)}) collective-permute-start(f32[2,4,128,128]{3,2,1,0:T(8,128)S(1)} %get-tuple-element.21), channel_id=1, source_target_pairs={{240,0},{0,16},{16,32},{32,48},{48,64},{64,80},{80,96},{96,112},{1... | collective-permute-start | bytes 1572872 | tf_op jit(solution)/shard_map/ppermute | solution.py:47
  100.5 21.5 %collective-permute-start.6 = (f32[2,4,128,128]{3,2,1,0:T(8,128)S(1)}, f32[2,4,128,128]{3,2,1,0:T(8,128)S(1)}, u32[]{:S(2)}, u32[]{:S(2)}) collective-permute-start(f32[2,4,128,128]{3,2,1,0:T(8,128)S(1)} %get-tuple-element.22), channel_id=1, source_target_pairs={{16,0},{32,16},{48,32},{64,48},{80,64},{96,80},{112,96},{128,112},... | collective-permute-start | bytes 1572872 | tf_op jit(solution)/shard_map/ppermute | solution.py:47
  102.4 19.5 %collective-permute-start.8 = (f32[4,128,128]{2,1,0:T(8,128)S(1)}, f32[4,128,128]{2,1,0:T(8,128)S(1)}, u32[]{:S(2)}, u32[]{:S(2)}) collective-permute-start(f32[4,128,128]{2,1,0:T(8,128)S(1)} %get-tuple-element.24), channel_id=1, source_target_pairs={{32,0},{48,16},{64,32},{80,48},{96,64},{112,80},{128,96},{144,112}... | collective-permute-start | bytes 786440 | tf_op jit(solution)/shard_map/ppermute | solution.py:47
  105.9 21.0 %collective-permute-start.7 = (f32[4,128,128]{2,1,0:T(8,128)S(1)}, f32[4,128,128]{2,1,0:T(8,128)S(1)}, u32[]{:S(2)}, u32[]{:S(2)}) collective-permute-start(f32[4,128,128]{2,1,0:T(8,128)S(1)} %get-tuple-element.23), channel_id=1, source_target_pairs={{224,0},{240,16},{0,32},{16,48},{32,64},{48,80},{64,96},{80,112},{... | collective-permute-start | bytes 786440 | tf_op jit(solution)/shard_map/ppermute | solution.py:47
  122.0 15.4 %collective-permute-start.9 = (f32[4,128,128]{2,1,0:T(8,128)S(1)}, f32[4,128,128]{2,1,0:T(8,128)S(1)}, u32[]{:S(2)}, u32[]{:S(2)}) collective-permute-start(f32[4,128,128]{2,1,0:T(8,128)S(1)} %fusion.1), channel_id=1, source_target_pairs={{0,256},{16,272},{32,288},{48,304},{64,320},{80,336},{96,352},{112... | collective-permute-start | bytes 786440 | tf_op jit(solution)/shard_map/ppermute | solution.py:245
  138.1 23.0 %all-to-all-start = ((f32[4,128,128]{2,1,0:T(8,128)}), f32[4,128,128]{2,1,0:T(8,128)S(1)}, u32[]{:S(2)}, u32[]{:S(2)}) async-start(f32[4,128,128]{2,1,0:T(8,128)} %fusion.4), calls=%async_computation | async-start | bytes 524288 | tf_op jit(solution)/shard_map/all_to_all | solution.py:247
Sparse Core Ops, SparseCore 0:
  10.1 61.4 all-gather.5
  73.8 100.9 all-gather.7

commit v4 on v3

--- a/solution.py
+++ b/solution.py
@@ -14,21 +14,8 @@
 NT = (((1,), (1,)), ((), ()))
 
 Z_FAR = [[h * 16 + q * 4 + r for q in range(4)] for h in range(2) for r in range(4)]
-
-
-def eights(held):
-    sizes = (2, 4, 4, 4, 2, 2)
-    groups = {}
-    for device in range(512):
-        digits, rest = [], device
-        for size in reversed(sizes):
-            digits.insert(0, rest % size)
-            rest //= size
-        groups.setdefault(tuple(digits[at] for at in held), []).append(device)
-    return [groups[key] for key in sorted(groups)]
-
-
-ALL_BY_EIGHT = [eights((2, 3, 4, 5)), eights((0, 1, 3, 4)), eights((0, 1, 2, 5))]
+Z_ALL = [list(range(16)), list(range(16, 32))]
+X_PAIRS = [[i, i + 16] for i in range(16)]
 
 
 def gelu_value_slope(value):
@@ -45,6 +32,10 @@
 def z_shift(array, step):
     perm = [(h * 16 + (z + step) % 16, h * 16 + z) for h in range(2) for z in range(16)]
     return lax.ppermute(array, "fsdp", perm)
+
+
+def y_shift(array, step):
+    return lax.ppermute(array, "seq", [((i + 4 * step) % 16, i) for i in range(16)])
 
 
 def pairs(place, own, plus, minus, two, which):
@@ -128,12 +119,52 @@
                     two_b[z_hi] = value
 
 
+def by_core(place, blocks, same):
+    first = (place[5] == 0) if same else (place[5] == 1)
+    at = {}
+    for index, (_, half, block) in enumerate(blocks):
+        at[index // 2, half] = block
+    return [jnp.where(first, at[index, 0], at[index, 1]) for index in range(2)]
+
+
+def contract_moved(place, blocks, mine, theirs, first, count):
+    total = None
+    for refs, same in ((mine, True), (theirs, False)):
+        for ref, block in zip(refs, by_core(place, blocks, same)):
+            rows = ref[0, 0, first : first + count].reshape(count * 320, 256)
+            term = lax.dot_general(rows, block, NT, preferred_element_type=F32)
+            total = term if total is None else total + term
+    return total
+
+
 def tangent_kernel(
-    place, own, plus, minus, two_x, two_g, weights, across, act, factor, dh, mask, out, by_x, by_g
+    place,
+    own,
+    plus,
+    minus,
+    two_x,
+    two_g,
+    weights,
+    mine_0,
+    mine_1,
+    theirs_0,
+    theirs_1,
+    across,
+    act,
+    factor,
+    dh,
+    mask,
+    out,
+    by_x,
+    by_g,
 ):
     step = pl.program_id(0)
-    add_up(step, by_x, contract(pairs(place, own, plus, minus, two_x, 0), weights, 0, 4))
-    add_up(step, by_g, contract(pairs(place, own, plus, minus, two_g, 1), weights, 4, 2))
+    of_x = pairs(place, own, plus, minus, two_x, 0)
+    of_g = pairs(place, own, plus, minus, two_g, 1)
+    moved = ((mine_0, mine_1), (theirs_0, theirs_1))
+    add_up(step, by_x.at[:960], contract(of_x, weights, 0, 3))
+    add_up(step, by_x.at[960:], contract_moved(place, of_x, *moved, 0, 1))
+    add_up(step, by_g, contract_moved(place, of_g, *moved, 1, 2))
 
     @pl.when(step == pl.num_programs(0) - 1)
     def _():
@@ -166,20 +197,33 @@
     return pl.BlockSpec((2, 1, 2, count, 320, 256), lambda s, p: (0, s, 0, 0, 0, 0))
 
 
+def moved_spec(other):
+    def index(s, p):
+        y = jnp.bitwise_xor(p[0], other) * 2 + s // 2
+        return ((y - p[3] + 4) % 4, jnp.bitwise_xor(s % 2, p[4]), 0, 0, 0)
+
+    return pl.BlockSpec((1, 1, 3, 320, 256), index)
+
+
 def shards(tokens, out_grad, loss_mask, w_in0, w_in1, w_out, tan_in0, tan_in1, tan_out):
     fsdp = lax.axis_index("fsdp")
     seq = lax.axis_index("seq")
     rows = tokens.shape[0]
     length = rows * lax.axis_size("seq") // EXAMPLES
-    place = jnp.stack([fsdp // 16, fsdp % 4, seq * rows // length]).astype(jnp.int32)
+    place = jnp.stack(
+        [fsdp // 16, fsdp % 4, seq * rows // length, seq // 4, seq // 2 % 2, seq % 2]
+    ).astype(jnp.int32)
 
     stack_w = jnp.stack([w_in0, w_in1, w_out])
-    stack_w, *tans = lax.optimization_barrier((stack_w, tan_in0, tan_in1, tan_out))
-    stack_t = jnp.concatenate(tans, axis=0)
+    both = jnp.stack([tokens, out_grad])
+    _, _, tan_in0, tan_in1, tan_out = lax.optimization_barrier(
+        (stack_w, both, tan_in0, tan_in1, tan_out)
+    )
+    stack_t = jnp.concatenate([tan_in0, tan_in1[:1]], axis=0)
+    moved = jnp.concatenate([tan_in1[1:], tan_out], axis=0)
     full_w = lax.all_gather(stack_w, "seq", axis=0).reshape(2, 4, 2, 3, 320, 256)
-    full_t = lax.all_gather(stack_t, "seq", axis=0).reshape(2, 4, 2, 6, 320, 256)
-
-    both = jnp.stack([tokens, out_grad])
+    full_t = lax.all_gather(stack_t, "seq", axis=0).reshape(2, 4, 2, 3, 320, 256)
+
     other = lax.ppermute(both, "fsdp", [(i, (i + 16) % 32) for i in range(32)])
     own = lax.all_gather(jnp.stack([both, other]), "fsdp", axis=0, axis_index_groups=Z_FAR)
     plus = z_shift(own, 1)
@@ -187,6 +231,11 @@
     two_x = z_shift(own[:, :, 0], 2)
     two_g = z_shift(own[:, :, 1], -2)
     acts = (own, plus, minus, two_x, two_g)
+
+    moved_x = lax.ppermute(moved, "seq", [(i, i ^ 2) for i in range(16)])
+    moved, *_ = lax.optimization_barrier((moved,) + acts)
+    moved = jnp.stack([moved, moved_x])
+    moved_plus, moved_minus = y_shift(moved, 1), y_shift(moved, -1)
 
     flat = jax.ShapeDtypeStruct((320, 128), F32)
     hidden, across, act, factor, dh = pl.pallas_call(
@@ -237,16 +286,21 @@
         name="block_sums",
     )(place, hidden, full_w)
 
+    half_plus, half_minus, _ = lax.optimization_barrier((moved_plus[0], moved_minus[1], kept))
+    half_plus, half_minus = y_shift(half_plus, 1), y_shift(half_minus, -1)
+
     up = z_shift(up, -1)
     down = z_shift(down, 1)
     two_up = z_shift(two_up, -2)
     two_down = z_shift(two_down, 2)
     away = kept[1] + up[1] + down[1] + two_down
+    across, half_plus, half_minus, _ = lax.optimization_barrier(
+        (across, half_plus, half_minus, away)
+    )
+    mine = jnp.stack([moved, moved_plus, jnp.stack([half_plus, half_minus]), moved_minus])
+    theirs = lax.ppermute(mine, "seq", [(i, i ^ 1) for i in range(16)])
     away = lax.ppermute(away, "fsdp", [(i, (i + 16) % 32) for i in range(32)])
     partial = kept[0] + up[0] + down[0] + two_up + away
-    partial = jnp.sum(lax.all_to_all(partial, "fsdp", 0, 0, axis_index_groups=Z_FAR), axis=0)
-    block_out = partial.astype(BF16)
-    block_out, across = lax.optimization_barrier((block_out, across))
 
     terms = pl.pallas_call(
         tangent_kernel,
@@ -255,7 +309,7 @@
             num_scalar_prefetch=1,
             grid=(4,),
             in_specs=activation_specs()
-            + [weight_spec(6)]
+            + [weight_spec(3), moved_spec(0), moved_spec(1), moved_spec(0), moved_spec(1)]
             + [whole((320, 128))] * 4
             + [whole((1, 128))],
             out_specs=whole((8, 128)),
@@ -266,12 +320,20 @@
             flops=2 * 6 * 128 * 320 * 4096, bytes_accessed=18 * 2**20, transcendentals=0
         ),
         name="tangents",
-    )(place, *acts, full_t, across, act, factor, dh, loss_mask.astype(F32)[None])
-
-    for groups in ALL_BY_EIGHT:
-        copies = jnp.broadcast_to(terms[None], (8,) + terms.shape)
-        got = lax.all_to_all(copies, ("fsdp", "seq"), 0, 0, axis_index_groups=groups)
-        terms = jnp.sum(got, axis=0)
+    )(place, *acts, full_t, mine, mine, theirs, theirs, across, act, factor, dh, loss_mask.astype(F32)[None])
+
+    partial, _ = lax.optimization_barrier((partial, terms))
+    z_hi = fsdp // 4 % 4
+    total = lax.dynamic_index_in_dim(partial, z_hi, 0, False)
+    far = [
+        z_shift(lax.dynamic_index_in_dim(partial, (z_hi + 4 - step) % 4, 0, False), 4 * step)
+        for step in range(1, 4)
+    ]
+
+    for axis, size, groups in (("seq", 16, None), ("fsdp", 16, Z_ALL), ("fsdp", 2, X_PAIRS)):
+        copies = jnp.broadcast_to(terms[None], (size,) + terms.shape)
+        terms = jnp.sum(lax.all_to_all(copies, axis, 0, 0, axis_index_groups=groups), axis=0)
+    block_out = (total + far[0] + far[1] + far[2]).astype(BF16)
     return (block_out, terms[:EXAMPLES, :2])
 
 

time: 241 us -> 233 us (0.967)
  starting transfers between devices: 47.1 us -> 98.1 us
  blocking collectives: 77.3 us -> 31.7 us
  waiting for transfers between devices: 65.5 us -> 42.4 us
  other arithmetic: 6.55 us -> 12.2 us
  Pallas kernels: 20.7 us -> 23.2 us
    all_to_all x3 -> x0, blocking collectives: 45.7 us -> none  [shards(): lax.all_to_all(copies, ('fsdp', 'seq'), 0, 0, axis_index_groups=groups)]
    ppermute x8 -> x11, starting transfers between devices: 29 us -> 52.1 us  [z_shift(): return lax.ppermute(array, 'fsdp', perm)]
    ppermute x0 -> x6, starting transfers between devices: none -> 19.4 us  [the longest x4 14.1 us: y_shift(): lax.ppermute(array, 'seq', [((i + 4 * step) % 16, i) for i in range(16)])]
    ppermute x0 -> x6, waiting for transfers between devices: none -> 17.8 us  [the longest x4 14.4 us: y_shift(): lax.ppermute(array, 'seq', [((i + 4 * step) % 16, i) for i in range(16)])]
    all_gather x1, waiting for transfers between devices: 13.1 us -> 0.02 us  [shards(): lax.all_gather(stack_t, 'seq', axis=0).reshape(2, 4, 2, 3, 320, 256)]
    ppermute x1, waiting for transfers between devices: 10.4 us -> 0.01 us  [shards(): away = lax.ppermute(away, 'fsdp', [(i, (i + 16) % 32) for i in range(32)])]
    all_to_all x1 -> x3, waiting for transfers between devices: 14.9 us -> 5.98 us  [shards(): lax.all_to_all(copies, axis, 0, 0, axis_index_groups=groups)]
    all_to_all x1 -> x3, starting transfers between devices: 8.17 us -> 16.8 us  [shards(): lax.all_to_all(copies, axis, 0, 0, axis_index_groups=groups)]
  transfers between devices with their start and end apart: 13 -> 24, of which waited for: 7 -> 9; matrix products, arithmetic and copies ran while one was open for 2% -> 7% of each run, Pallas kernels for 4% -> 10%
where the time goes in v4:
time: 233 us; the launch traced here: 231 us
  starting transfers between devices  98.1 us (42%)
  waiting for transfers between devices  42.4 us (18%)
  blocking collectives  31.7 us (14%)
  Pallas kernels  23.2 us (10%)
  between operations  14.5 us (6%)
  other arithmetic  12.2 us (5%)
  local copies, waits for them, and re-layouts  9.19 us (4%)
    ppermute x11, starting transfers between devices, z_shift(): return lax.ppermute(array, 'fsdp', perm)  52.1 us
    all_gather x1, blocking collectives, shards(): lax.all_gather(jnp.stack([both, other]), 'fsdp', axis=0, axis_index_group...  31.7 us
    all_to_all x3, starting transfers between devices, shards(): lax.all_to_all(copies, axis, 0, 0, axis_index_groups=groups)  16.8 us
    ppermute x11, waiting for transfers between devices, z_shift(): return lax.ppermute(array, 'fsdp', perm)  15.8 us
    ppermute x4, waiting for transfers between devices, y_shift(): lax.ppermute(array, 'seq', [((i + 4 * step) % 16, i) for i in range(16)])  14.4 us
    ppermute x4, starting transfers between devices, y_shift(): lax.ppermute(array, 'seq', [((i + 4 * step) % 16, i) for i in range(16)])  14.1 us
    pallas_call x1, Pallas kernels, shards(): pl.pallas_call(tangent_kernel, out_shape=jax.ShapeDtypeStruct((8, 128), F...  13.8 us
    pallas_call x1, Pallas kernels, shards(): pl.pallas_call(primal_kernel, out_shape=(jax.ShapeDtypeStruct((128, 320),...  6.16 us
  transfers between devices with their start and end apart: 24, of which 9 were waited for; matrix products, arithmetic and copies ran while one was open for 7% of the time, Pallas kernels for 10%

profile of v4, /device:TPU:24, one launch (start us, length us, event | category | flops | bytes accessed | tf_op | source)
XLA Modules:
  0.0 231.2 jit_solution(3517672593794200891)
XLA Ops:
  7.2 0.0 all-gather.6.cloned.1.call-start
  7.2 1.9 pad_maximum_fusion.2
  9.2 0.0 all-gather.6.cloned.1.call-update
  9.2 0.0 all-gather.8.cloned.1.call-start
  9.2 0.8 fusion.8
  10.0 1.0 fusion.10
  11.1 1.8 pad_maximum_fusion.3
  12.8 0.0 all-gather.8.cloned.1.call-update
  12.9 4.9 %collective-permute-start = (bf16[2,128,128]{2,1,0:T(8,128)(2,1)S(1)}, bf16[2,128,128]{2,1,0:T(8,128)(2,1)S(1)}, u32[]{:S(2)}, u32[]{:S(2)}) collective-permute-start(bf16[2,128,128]{2,1,0:T(8,128)(2,1)S(1)} %get-tuple-element.54), channel_id=1, source_target_pairs={{0,256},{16,272},{32,288},{48,304},{64,320},{80,336},{96,352},{112... | collective-permute-start | bytes 196616 | tf_op jit(solution)/shard_map/ppermute | solution.py:227
  17.8 2.7 %collective-permute-done = bf16[2,128,128]{2,1,0:T(8,128)(2,1)S(1)} collective-permute-done((bf16[2,128,128]{2,1,0:T(8,128)(2,1)S(1)}, bf16[2,128,128]{2,1,0:T(8,128)(2,1)S(1)}, u32[]{:S(2)}, u32[]{:S(2)}) %collective-permute-start) | collective-permute-done | bytes 65568 | tf_op jit(solution)/shard_map/ppermute | solution.py:227
  20.6 31.7 %all-gather = bf16[8,2,128,128]{3,2,1,0:T(8,128)(2,1)S(1)} all-gather(bf16[2,2,128,128]{3,2,1,0:T(8,128)(2,1)S(1)} %pad_maximum_fusion.5), channel_id=2, replica_groups={{0,64,128,192},{16,80,144,208},{32,96,160,224},{48,112,176,240},{256,32..., dimensions={0}, use_global_device_ids=true | all-gather | bytes 655360 | tf_op jit(solution)/shard_map/all_gather | solution.py:228
  52.3 4.9 %collective-permute-start.1 = (bf16[4,2,2,128,128]{4,3,1,0,2:T(8,128)(2,1)S(1)}, bf16[4,2,2,128,128]{4,3,1,0,2:T(8,128)(2,1)S(1)}, u32[]{:S(2)}, u32[]{:S(2)}) collective-permute-start(bf16[4,2,2,128,128]{4,3,1,0,2:T(8,128)(2,1)S(1)} %bitcast.67), channel_id=1, source_target_pairs={{16,0},{32,16},{48,32},{64,48},{80,64},{96,80},{112,96},{128,112},... | collective-permute-start | bytes 1572872 | tf_op jit(solution)/shard_map/ppermute | solution.py:34
  57.2 1.9 collective-permute-start.2
  59.2 3.4 %collective-permute-start.10 = (bf16[3,320,256]{2,1,0:T(8,128)(2,1)S(1)}, bf16[3,320,256]{2,1,0:T(8,128)(2,1)S(1)}, u32[]{:S(2)}, u32[]{:S(2)}) collective-permute-start(bf16[3,320,256]{2,1,0:T(8,128)(2,1)S(1)} %pad_maximum_fusion.4), channel_id=1, source_target_pairs={{0,2},{1,3},{2,0},{3,1},{4,6},{5,7},{6,4},{7,5},{8,10},{9,11},{10,... | collective-permute-start | bytes 1474568 | tf_op jit(solution)/shard_map/ppermute | solution.py:235
  62.7 3.4 %collective-permute-start.3 = (bf16[4,2,128,128]{3,2,1,0:T(8,128)(2,1)S(1)}, bf16[4,2,128,128]{3,2,1,0:T(8,128)(2,1)S(1)}, u32[]{:S(2)}, u32[]{:S(2)}) collective-permute-start(bf16[4,2,128,128]{3,2,1,0:T(8,128)(2,1)S(1)} %get-tuple-element.47), channel_id=1, source_target_pairs={{32,0},{48,16},{64,32},{80,48},{96,64},{112,80},{128,96},{144,112}... | collective-permute-start | bytes 786440 | tf_op jit(solution)/shard_map/ppermute | solution.py:34
  66.0 3.4 %collective-permute-start.4 = (bf16[4,2,128,128]{3,2,1,0:T(8,128)(2,1)S(1)}, bf16[4,2,128,128]{3,2,1,0:T(8,128)(2,1)S(1)}, u32[]{:S(2)}, u32[]{:S(2)}) collective-permute-start(bf16[4,2,128,128]{3,2,1,0:T(8,128)(2,1)S(1)} %get-tuple-element.46), channel_id=1, source_target_pairs={{224,0},{240,16},{0,32},{16,48},{32,64},{48,80},{64,96},{80,112},{... | collective-permute-start | bytes 786440 | tf_op jit(solution)/shard_map/ppermute | solution.py:34
  69.4 7.7 %collective-permute-done.3.two_x = bf16[4,2,128,128]{3,2,1,0:T(8,128)(2,1)S(1)} collective-permute-done((bf16[4,2,128,128]{3,2,1,0:T(8,128)(2,1)S(1)}, bf16[4,2,128,128]{3,2,1,0:T(8,128)(2,1)S(1)}, u32[]{:S(2)}, u32[]{:S(2)}) %collective-permute-start.3) | collective-permute-done | bytes 262176 | tf_op jit(solution)/shard_map/ppermute | solution.py:34
  77.1 0.0 collective-permute-done.4.two_g
  77.1 0.0 collective-permute-done.2
  77.1 3.4 %collective-permute-done.10 = bf16[3,320,256]{2,1,0:T(8,128)(2,1)S(1)} collective-permute-done((bf16[3,320,256]{2,1,0:T(8,128)(2,1)S(1)}, bf16[3,320,256]{2,1,0:T(8,128)(2,1)S(1)}, u32[]{:S(2)}, u32[]{:S(2)}) %collective-permute-start.10) | collective-permute-done | bytes 491552 | tf_op jit(solution)/shard_map/ppermute | solution.py:235
  80.5 1.4 fusion.9
  81.9 1.9 collective-permute-start.11
  83.8 5.1 %collective-permute-start.12 = (bf16[2,3,320,256]{3,2,1,0:T(8,128)(2,1)}, bf16[2,3,320,256]{3,2,1,0:T(8,128)(2,1)}, u32[]{:S(2)}, u32[]{:S(2)}) collective-permute-start(bf16[2,3,320,256]{3,2,1,0:T(8,128)(2,1)} %get-tuple-element.45), channel_id=1, source_target_pairs={{12,0},{13,1},{14,2},{15,3},{0,4},{1,5},{2,6},{3,7},{4,8},{5,9},{6... | collective-permute-start | bytes 2949128 | tf_op jit(solution)/shard_map/ppermute | solution.py:38
  89.0 0.1 stack.90.place
  89.2 0.0 all-gather.6.cloned.1.call-done
  89.3 3.2 %copy-done = bf16[48,320,256]{2,1,0:T(8,128)(2,1)S(1)} copy-done((bf16[48,320,256]{2,1,0:T(8,128)(2,1)S(1)}, bf16[48,320,256]{2,1,0:T(8,128)(2,1)}, u32[]{:S(2)}) %copy-start) | copy-done | bytes 7864344
  92.5 6.2 %primal.1 = (bf16[128,320]{1,0:T(8,128)(2,1)S(1)}, bf16[320,128]{1,0:T(8,128)(2,1)S(1)}, f32[320,128]{1,0:T(8,128)S(1)}, f32[320,128]{1,0:T(8,128)S(1)}, f32[320,128]{1,0:T(8,128)S(1)}) custom-call(s32[6]{0:T(128)S(1)} %stack.90.place, bf16[4,2,2,128,128]{4,3,2,1,0:T(8,128)(2,1)S(1)} %bitcast.64, bf16[4,2,2,128,128]{4,3,2,1,0:T(8,128)(2,1)S(1)} %copy.27.plus, ...), custom_call_target="tpu_custom_call" | custom-call | flops 1006632960 | bytes 10485760 | tf_op jit(solution)/shard_map/primal/pallas_call | solution.py:241
  98.7 3.2 %block_sums.1 = (f32[2,4,128,128]{3,2,1,0:T(8,128)S(1)}, f32[2,4,128,128]{3,2,1,0:T(8,128)S(1)}, f32[2,4,128,128]{3,2,1,0:T(8,128)S(1)}, f32[4,128,128]{2,1,0:T(8,128)S(1)}, f32[4,128,128]{2,1,0:T(8,128)S(1)}) custom-call(s32[6]{0:T(128)S(1)} %stack.90.place, bf16[128,320]{1,0:T(8,128)(2,1)S(1)} %get-tuple-element.22.hidden, ...), custom_call_target="tpu_custom_call" | custom-call | flops 335544320 | bytes 5242880 | tf_op jit(solution)/shard_map/block_sums/pallas_call | solution.py:267
  101.8 6.1 %collective-permute-start.6 = (f32[2,4,128,128]{3,2,1,0:T(8,128)S(1)}, f32[2,4,128,128]{3,2,1,0:T(8,128)S(1)}, u32[]{:S(2)}, u32[]{:S(2)}) collective-permute-start(f32[2,4,128,128]{3,2,1,0:T(8,128)S(1)} %get-tuple-element.25), channel_id=1, source_target_pairs={{16,0},{32,16},{48,32},{64,48},{80,64},{96,80},{112,96},{128,112},... | collective-permute-start | bytes 1572872 | tf_op jit(solution)/shard_map/ppermute | solution.py:34
  107.9 1.9 collective-permute-start.5
  109.9 1.1 slice_bitcast_fusion.1
  110.9 4.7 %collective-permute-start.8 = (f32[4,128,128]{2,1,0:T(8,128)S(1)}, f32[4,128,128]{2,1,0:T(8,128)S(1)}, u32[]{:S(2)}, u32[]{:S(2)}) collective-permute-start(f32[4,128,128]{2,1,0:T(8,128)S(1)} %get-tuple-element.27), channel_id=1, source_target_pairs={{32,0},{48,16},{64,32},{80,48},{96,64},{112,80},{128,96},{144,112}... | collective-permute-start | bytes 786440 | tf_op jit(solution)/shard_map/ppermute | solution.py:34
  115.7 1.1 slice_bitcast_fusion
  116.8 1.9 collective-permute-start.13
  118.7 5.1 %collective-permute-start.14 = (bf16[3,320,256]{2,1,0:T(8,128)(2,1)S(1)}, bf16[3,320,256]{2,1,0:T(8,128)(2,1)S(1)}, u32[]{:S(2)}, u32[]{:S(2)}) collective-permute-start(bf16[3,320,256]{2,1,0:T(8,128)(2,1)S(1)} %slice_bitcast_fusion), channel_id=1, source_target_pairs={{12,0},{13,1},{14,2},{15,3},{0,4},{1,5},{2,6},{3,7},{4,8},{5,9},{6... | collective-permute-start | bytes 1474568 | tf_op jit(solution)/shard_map/ppermute | solution.py:38
  123.8 5.3 %collective-permute-done.8 = f32[4,128,128]{2,1,0:T(8,128)S(1)} collective-permute-done((f32[4,128,128]{2,1,0:T(8,128)S(1)}, f32[4,128,128]{2,1,0:T(8,128)S(1)}, u32[]{:S(2)}, u32[]{:S(2)}) %collective-permute-start.8) | collective-permute-done | bytes 262176 | tf_op jit(solution)/shard_map/ppermute | solution.py:34
  129.1 0.9 fusion.1
  130.0 9.0 %collective-permute-done.13 = bf16[3,320,256]{2,1,0:T(8,128)(2,1)S(1)} collective-permute-done((bf16[3,320,256]{2,1,0:T(8,128)(2,1)S(1)}, bf16[3,320,256]{2,1,0:T(8,128)(2,1)S(1)}, u32[]{:S(2)}, u32[]{:S(2)}) %collective-permute-start.13) | collective-permute-done | bytes 491552 | tf_op jit(solution)/shard_map/ppermute | solution.py:38
  139.0 5.4 %collective-permute-done.14 = bf16[3,320,256]{2,1,0:T(8,128)(2,1)S(1)} collective-permute-done((bf16[3,320,256]{2,1,0:T(8,128)(2,1)S(1)}, bf16[3,320,256]{2,1,0:T(8,128)(2,1)S(1)}, u32[]{:S(2)}, u32[]{:S(2)}) %collective-permute-start.14) | collective-permute-done | bytes 491552 | tf_op jit(solution)/shard_map/ppermute | solution.py:38
  144.4 0.1 maximum_bitcast_fusion
  144.5 0.0 copy-start.6
  144.5 3.3 %pad_maximum_fusion.mine_0.mine_1 = bf16[4,2,3,320,256]{4,3,2,1,0:T(8,128)(2,1)} fusion(bf16[1,2,3,320,256]{4,3,2,1,0:T(8,128)(2,1)} %bitcast.30, bf16[1,2,3,320,256]{4,3,2,1,0:T(8,128)(2,1)S(1)} %maximum_bitcast_fusion, bf16[1,2,3,320,256]{4,3,2,1,0:T(8,128)(2,1)} %bitcast.24, bf16[1,2,3,320,256]{4,3,2,1,0:T(8,128)(2,1)S(1)} %copy-done.2), kind=kLoop, calls=%fused_computation | loop fusion | flops 5898240 | bytes 7864320 | tf_op jit(solution)/shard_map/stack | solution.py:300
  147.8 1.9 collective-permute-start.15
  149.7 3.4 %collective-permute-start.7 = (f32[4,128,128]{2,1,0:T(8,128)S(1)}, f32[4,128,128]{2,1,0:T(8,128)}, u32[]{:S(2)}, u32[]{:S(2)}) collective-permute-start(f32[4,128,128]{2,1,0:T(8,128)S(1)} %get-tuple-element.26), channel_id=1, source_target_pairs={{224,0},{240,16},{0,32},{16,48},{32,64},{48,80},{64,96},{80,112},{... | collective-permute-start | bytes 786440 | tf_op jit(solution)/shard_map/ppermute | solution.py:34
  153.2 4.8 %collective-permute-start.9 = (f32[4,128,128]{2,1,0:T(8,128)}, f32[4,128,128]{2,1,0:T(8,128)}, u32[]{:S(2)}, u32[]{:S(2)}) collective-permute-start(f32[4,128,128]{2,1,0:T(8,128)} %fusion.1), channel_id=1, source_target_pairs={{0,256},{16,272},{32,288},{48,304},{64,320},{80,336},{96,352},{112... | collective-permute-start | bytes 786440 | tf_op jit(solution)/shard_map/ppermute | solution.py:302
  158.0 0.0 all-gather.8.cloned.1.call-done
  158.0 13.8 %tangents.1 = f32[8,128]{1,0:T(8,128)S(1)} custom-call(s32[6]{0:T(128)S(1)} %stack.90.place, bf16[4,2,2,128,128]{4,3,2,1,0:T(8,128)(2,1)S(1)} %bitcast.65, bf16[4,2,2,128,128]{4,3,2,1,0:T(8,128)(2,1)S(1)} %copy.27.plus, bf16[4,2,2,128,128]{4,3,2,1,0:T(8,128)(2,1)S(1)} %copy.28.minus, bf16[4,2,128,128]{3,2,1,0:T(8,128)(2,1)S(1)} %collective-permute-done.3.two_x, ...), custom_call_target="tpu_custom_call" | custom-call | flops 2013265920 | bytes 18874368 | tf_op jit(solution)/shard_map/tangents/pallas_call | solution.py:305
  171.9 0.6 broadcast_in_dim.9
  172.5 5.2 %all-to-all-start = ((f32[16,8,128]{2,1,0:T(8,128)}), f32[16,8,128]{2,1,0:T(8,128)S(1)}, u32[]{:S(2)}, u32[]{:S(2)}) async-start(f32[16,8,128]{2,1,0:T(8,128)} %broadcast_in_dim.9), calls=%async_computation | async-start | bytes 131072 | tf_op jit(solution)/shard_map/all_to_all | solution.py:335
  177.7 4.1 %all-to-all-done = f32[16,8,128]{2,1,0:T(8,128)S(1)} async-done(((f32[16,8,128]{2,1,0:T(8,128)}), f32[16,8,128]{2,1,0:T(8,128)S(1)}, u32[]{:S(2)}, u32[]{:S(2)}) %all-to-all-start) | async-done | bytes 65568 | tf_op jit(solution)/shard_map/all_to_all | solution.py:335
  181.8 0.6 broadcast_in_dim.10
  182.5 7.7 %all-to-all-start.1 = ((f32[16,8,128]{2,1,0:T(8,128)}), f32[16,8,128]{2,1,0:T(8,128)S(1)}, u32[]{:S(2)}, u32[]{:S(2)}) async-start(f32[16,8,128]{2,1,0:T(8,128)} %broadcast_in_dim.10), calls=%async_computation.1 | async-start | bytes 131072 | tf_op jit(solution)/shard_map/all_to_all | solution.py:335
  190.2 0.0 collective-permute-done.9
  190.2 1.3 fusion.4
  191.5 7.7 %collective-permute-start.18 = (f32[128,128]{1,0:T(8,128)S(1)}, f32[128,128]{1,0:T(8,128)S(1)}, u32[]{:S(2)}, u32[]{:S(2)}) collective-permute-start(f32[128,128]{1,0:T(8,128)S(1)} %get-tuple-element.51), channel_id=1, source_target_pairs={{192,0},{208,16},{224,32},{240,48},{0,64},{16,80},{32,96},{48,112}... | collective-permute-start | bytes 196616 | tf_op jit(solution)/shard_map/ppermute | solution.py:34
  199.3 7.3 %collective-permute-start.17 = (f32[128,128]{1,0:T(8,128)S(1)}, f32[128,128]{1,0:T(8,128)S(1)}, u32[]{:S(2)}, u32[]{:S(2)}) collective-permute-start(f32[128,128]{1,0:T(8,128)S(1)} %get-tuple-element.52), channel_id=1, source_target_pairs={{128,0},{144,16},{160,32},{176,48},{192,64},{208,80},{224,96},{240... | collective-permute-start | bytes 196616 | tf_op jit(solution)/shard_map/ppermute | solution.py:34
  206.6 7.3 %collective-permute-start.16 = (f32[128,128]{1,0:T(8,128)S(1)}, f32[128,128]{1,0:T(8,128)S(1)}, u32[]{:S(2)}, u32[]{:S(2)}) collective-permute-start(f32[128,128]{1,0:T(8,128)S(1)} %get-tuple-element.50), channel_id=1, source_target_pairs={{64,0},{80,16},{96,32},{112,48},{128,64},{144,80},{160,96},{176,11... | collective-permute-start | bytes 196616 | tf_op jit(solution)/shard_map/ppermute | solution.py:34
  213.8 0.0 all-to-all-done.1
  213.9 0.6 broadcast_in_dim.11
  214.5 3.9 %all-to-all-start.2 = ((f32[2,8,128]{2,1,0:T(8,128)}), f32[2,8,128]{2,1,0:T(8,128)S(1)}, u32[]{:S(2)}, u32[]{:S(2)}) async-start(f32[2,8,128]{2,1,0:T(8,128)} %broadcast_in_dim.11), calls=%async_computation.2 | async-start | bytes 16384 | tf_op jit(solution)/shard_map/all_to_all | solution.py:335
  218.4 2.9 %collective-permute-done.16 = f32[128,128]{1,0:T(8,128)S(1)} collective-permute-done((f32[128,128]{1,0:T(8,128)S(1)}, f32[128,128]{1,0:T(8,128)S(1)}, u32[]{:S(2)}, u32[]{:S(2)}) %collective-permute-start.16) | collective-permute-done | bytes 65568 | tf_op jit(solution)/shard_map/ppermute | solution.py:34
  221.2 0.6 fusion.7
  221.9 1.8 all-to-all-done.2
  223.7 0.7 copy.32
  (33 shorter events, 0.3 us)
Async XLA Ops:
  7.2 52.0 %copy-start.5 = (bf16[2,320,256]{2,1,0:T(8,128)(2,1)S(1)}, bf16[2,320,256]{2,1,0:T(8,128)(2,1)}, u32[]{:S(2)}) copy-start(bf16[2,320,256]{2,1,0:T(8,128)(2,1)} %param.17) | copy-start | bytes 983044
  7.2 82.1 %all-gather.6.cloned.1.call-start = ((), (), s32[]{:S(2)}) async-start(), calls=%async_computation.3 | async-start | bytes 8355840 | tf_op jit(solution)/shard_map/all_gather | solution.py:224
  9.2 148.8 %all-gather.8.cloned.1.call-start = ((), (), s32[]{:S(2)}) async-start(), calls=%async_computation.4 | async-start | bytes 8355840 | tf_op jit(solution)/shard_map/all_gather | solution.py:225
  12.9 7.7 %collective-permute-start = (bf16[2,128,128]{2,1,0:T(8,128)(2,1)S(1)}, bf16[2,128,128]{2,1,0:T(8,128)(2,1)S(1)}, u32[]{:S(2)}, u32[]{:S(2)}) collective-permute-start(bf16[2,128,128]{2,1,0:T(8,128)(2,1)S(1)} %get-tuple-element.54), channel_id=1, source_target_pairs={{0,256},{16,272},{32,288},{48,304},{64,320},{80,336},{96,352},{112... | collective-permute-start | bytes 196616 | tf_op jit(solution)/shard_map/ppermute | solution.py:227
  52.3 24.8 %collective-permute-start.1 = (bf16[4,2,2,128,128]{4,3,1,0,2:T(8,128)(2,1)S(1)}, bf16[4,2,2,128,128]{4,3,1,0,2:T(8,128)(2,1)S(1)}, u32[]{:S(2)}, u32[]{:S(2)}) collective-permute-start(bf16[4,2,2,128,128]{4,3,1,0,2:T(8,128)(2,1)S(1)} %bitcast.67), channel_id=1, source_target_pairs={{16,0},{32,16},{48,32},{64,48},{80,64},{96,80},{112,96},{128,112},... | collective-permute-start | bytes 1572872 | tf_op jit(solution)/shard_map/ppermute | solution.py:34
  57.2 19.9 %collective-permute-start.2 = (bf16[4,2,2,128,128]{4,3,1,0,2:T(8,128)(2,1)S(1)}, bf16[4,2,2,128,128]{4,3,1,0,2:T(8,128)(2,1)S(1)}, u32[]{:S(2)}, u32[]{:S(2)}) collective-permute-start(bf16[4,2,2,128,128]{4,3,1,0,2:T(8,128)(2,1)S(1)} %bitcast.68), channel_id=1, source_target_pairs={{240,0},{0,16},{16,32},{32,48},{48,64},{64,80},{80,96},{96,112},{1... | collective-permute-start | bytes 1572872 | tf_op jit(solution)/shard_map/ppermute | solution.py:34
  59.2 21.3 %collective-permute-start.10 = (bf16[3,320,256]{2,1,0:T(8,128)(2,1)S(1)}, bf16[3,320,256]{2,1,0:T(8,128)(2,1)S(1)}, u32[]{:S(2)}, u32[]{:S(2)}) collective-permute-start(bf16[3,320,256]{2,1,0:T(8,128)(2,1)S(1)} %pad_maximum_fusion.4), channel_id=1, source_target_pairs={{0,2},{1,3},{2,0},{3,1},{4,6},{5,7},{6,4},{7,5},{8,10},{9,11},{10,... | collective-permute-start | bytes 1474568 | tf_op jit(solution)/shard_map/ppermute | solution.py:235
  62.7 14.4 %collective-permute-start.3 = (bf16[4,2,128,128]{3,2,1,0:T(8,128)(2,1)S(1)}, bf16[4,2,128,128]{3,2,1,0:T(8,128)(2,1)S(1)}, u32[]{:S(2)}, u32[]{:S(2)}) collective-permute-start(bf16[4,2,128,128]{3,2,1,0:T(8,128)(2,1)S(1)} %get-tuple-element.47), channel_id=1, source_target_pairs={{32,0},{48,16},{64,32},{80,48},{96,64},{112,80},{128,96},{144,112}... | collective-permute-start | bytes 786440 | tf_op jit(solution)/shard_map/ppermute | solution.py:34
  66.0 11.0 %collective-permute-start.4 = (bf16[4,2,128,128]{3,2,1,0:T(8,128)(2,1)S(1)}, bf16[4,2,128,128]{3,2,1,0:T(8,128)(2,1)S(1)}, u32[]{:S(2)}, u32[]{:S(2)}) collective-permute-start(bf16[4,2,128,128]{3,2,1,0:T(8,128)(2,1)S(1)} %get-tuple-element.46), channel_id=1, source_target_pairs={{224,0},{240,16},{0,32},{16,48},{32,64},{48,80},{64,96},{80,112},{... | collective-permute-start | bytes 786440 | tf_op jit(solution)/shard_map/ppermute | solution.py:34
  81.9 28.0 %collective-permute-start.11 = (bf16[2,3,320,256]{3,2,1,0:T(8,128)(2,1)}, bf16[2,3,320,256]{3,2,1,0:T(8,128)(2,1)}, u32[]{:S(2)}, u32[]{:S(2)}) collective-permute-start(bf16[2,3,320,256]{3,2,1,0:T(8,128)(2,1)} %get-tuple-element.45), channel_id=1, source_target_pairs={{4,0},{5,1},{6,2},{7,3},{8,4},{9,5},{10,6},{11,7},{12,8},{13,9},{1... | collective-permute-start | bytes 2949128 | tf_op jit(solution)/shard_map/ppermute | solution.py:38
  83.8 31.9 %collective-permute-start.12 = (bf16[2,3,320,256]{3,2,1,0:T(8,128)(2,1)}, bf16[2,3,320,256]{3,2,1,0:T(8,128)(2,1)}, u32[]{:S(2)}, u32[]{:S(2)}) collective-permute-start(bf16[2,3,320,256]{3,2,1,0:T(8,128)(2,1)} %get-tuple-element.45), channel_id=1, source_target_pairs={{12,0},{13,1},{14,2},{15,3},{0,4},{1,5},{2,6},{3,7},{4,8},{5,9},{6... | collective-permute-start | bytes 2949128 | tf_op jit(solution)/shard_map/ppermute | solution.py:38
  89.3 3.2 %copy-start = (bf16[48,320,256]{2,1,0:T(8,128)(2,1)S(1)}, bf16[48,320,256]{2,1,0:T(8,128)(2,1)}, u32[]{:S(2)}) copy-start(bf16[48,320,256]{2,1,0:T(8,128)(2,1)} %all-gather.6.cloned.1.call-done) | copy-start | bytes 23592964
  92.5 6.2 %copy-start.1 = (bf16[48,320,256]{2,1,0:T(8,128)(2,1)S(1)}, bf16[48,320,256]{2,1,0:T(8,128)(2,1)}, u32[]{:S(2)}) copy-start(bf16[48,320,256]{2,1,0:T(8,128)(2,1)} %all-gather.6.cloned.1.call-done) | copy-start | bytes 23592964
  101.8 42.6 %copy-start.2 = (bf16[1,2,3,320,256]{4,3,2,1,0:T(8,128)(2,1)S(1)}, bf16[1,2,3,320,256]{4,3,2,1,0:T(8,128)(2,1)}, u32[]{:S(2)}) copy-start(bf16[1,2,3,320,256]{4,3,2,1,0:T(8,128)(2,1)} %get-tuple-element.44) | copy-start | bytes 2949124
  101.8 27.3 %collective-permute-start.6 = (f32[2,4,128,128]{3,2,1,0:T(8,128)S(1)}, f32[2,4,128,128]{3,2,1,0:T(8,128)S(1)}, u32[]{:S(2)}, u32[]{:S(2)}) collective-permute-start(f32[2,4,128,128]{3,2,1,0:T(8,128)S(1)} %get-tuple-element.25), channel_id=1, source_target_pairs={{16,0},{32,16},{48,32},{64,48},{80,64},{96,80},{112,96},{128,112},... | collective-permute-start | bytes 1572872 | tf_op jit(solution)/shard_map/ppermute | solution.py:34
  107.9 21.2 %collective-permute-start.5 = (f32[2,4,128,128]{3,2,1,0:T(8,128)S(1)}, f32[2,4,128,128]{3,2,1,0:T(8,128)S(1)}, u32[]{:S(2)}, u32[]{:S(2)}) collective-permute-start(f32[2,4,128,128]{3,2,1,0:T(8,128)S(1)} %get-tuple-element.24), channel_id=1, source_target_pairs={{240,0},{0,16},{16,32},{32,48},{48,64},{64,80},{80,96},{96,112},{1... | collective-permute-start | bytes 1572872 | tf_op jit(solution)/shard_map/ppermute | solution.py:34
  110.9 18.2 %collective-permute-start.8 = (f32[4,128,128]{2,1,0:T(8,128)S(1)}, f32[4,128,128]{2,1,0:T(8,128)S(1)}, u32[]{:S(2)}, u32[]{:S(2)}) collective-permute-start(f32[4,128,128]{2,1,0:T(8,128)S(1)} %get-tuple-element.27), channel_id=1, source_target_pairs={{32,0},{48,16},{64,32},{80,48},{96,64},{112,80},{128,96},{144,112}... | collective-permute-start | bytes 786440 | tf_op jit(solution)/shard_map/ppermute | solution.py:34
  116.8 22.2 %collective-permute-start.13 = (bf16[3,320,256]{2,1,0:T(8,128)(2,1)S(1)}, bf16[3,320,256]{2,1,0:T(8,128)(2,1)S(1)}, u32[]{:S(2)}, u32[]{:S(2)}) collective-permute-start(bf16[3,320,256]{2,1,0:T(8,128)(2,1)S(1)} %slice_bitcast_fusion.1), channel_id=1, source_target_pairs={{4,0},{5,1},{6,2},{7,3},{8,4},{9,5},{10,6},{11,7},{12,8},{13,9},{1... | collective-permute-start | bytes 1474568 | tf_op jit(solution)/shard_map/ppermute | solution.py:38
  118.7 25.7 %collective-permute-start.14 = (bf16[3,320,256]{2,1,0:T(8,128)(2,1)S(1)}, bf16[3,320,256]{2,1,0:T(8,128)(2,1)S(1)}, u32[]{:S(2)}, u32[]{:S(2)}) collective-permute-start(bf16[3,320,256]{2,1,0:T(8,128)(2,1)S(1)} %slice_bitcast_fusion), channel_id=1, source_target_pairs={{12,0},{13,1},{14,2},{15,3},{0,4},{1,5},{2,6},{3,7},{4,8},{5,9},{6... | collective-permute-start | bytes 1474568 | tf_op jit(solution)/shard_map/ppermute | solution.py:38
  129.1 15.2 %copy-start.3 = (f32[2,4,128,128]{3,2,1,0:T(8,128)}, f32[2,4,128,128]{3,2,1,0:T(8,128)S(1)}, u32[]{:S(2)}) copy-start(f32[2,4,128,128]{3,2,1,0:T(8,128)S(1)} %collective-permute-done.6) | copy-start | bytes 1572868
  129.1 15.2 %copy-start.4 = (f32[2,4,128,128]{3,2,1,0:T(8,128)}, f32[2,4,128,128]{3,2,1,0:T(8,128)S(1)}, u32[]{:S(2)}) copy-start(f32[2,4,128,128]{3,2,1,0:T(8,128)S(1)} %collective-permute-done.5) | copy-start | bytes 1572868
  144.5 13.5 %copy-start.6 = (s32[128]{0:T(128)S(1)}, s32[128]{0:T(128)}, u32[]{:S(2)}) copy-start(s32[128]{0:T(128)} %param.11) | copy-start | bytes 1540
  147.8 10.2 %collective-permute-start.15 = (bf16[4,2,3,320,256]{4,3,2,1,0:T(8,128)(2,1)}, bf16[4,2,3,320,256]{4,3,2,1,0:T(8,128)(2,1)}, u32[]{:S(2)}, u32[]{:S(2)}) collective-permute-start(bf16[4,2,3,320,256]{4,3,2,1,0:T(8,128)(2,1)} %pad_maximum_fusion.mine_0.mine_1), channel_id=1, source_target_pairs={{0,1},{1,0},{2,3},{3,2},{4,5},{5,4},{6,7},{7,6},{8,9},{9,8},{10,11... | collective-permute-start | bytes 11796488 | tf_op jit(solution)/shard_map/ppermute | solution.py:301
  149.7 40.5 %collective-permute-start.7 = (f32[4,128,128]{2,1,0:T(8,128)S(1)}, f32[4,128,128]{2,1,0:T(8,128)}, u32[]{:S(2)}, u32[]{:S(2)}) collective-permute-start(f32[4,128,128]{2,1,0:T(8,128)S(1)} %get-tuple-element.26), channel_id=1, source_target_pairs={{224,0},{240,16},{0,32},{16,48},{32,64},{48,80},{64,96},{80,112},{... | collective-permute-start | bytes 786440 | tf_op jit(solution)/shard_map/ppermute | solution.py:34
  153.2 37.0 %collective-permute-start.9 = (f32[4,128,128]{2,1,0:T(8,128)}, f32[4,128,128]{2,1,0:T(8,128)}, u32[]{:S(2)}, u32[]{:S(2)}) collective-permute-start(f32[4,128,128]{2,1,0:T(8,128)} %fusion.1), channel_id=1, source_target_pairs={{0,256},{16,272},{32,288},{48,304},{64,320},{80,336},{96,352},{112... | collective-permute-start | bytes 786440 | tf_op jit(solution)/shard_map/ppermute | solution.py:302
  172.5 9.3 %all-to-all-start = ((f32[16,8,128]{2,1,0:T(8,128)}), f32[16,8,128]{2,1,0:T(8,128)S(1)}, u32[]{:S(2)}, u32[]{:S(2)}) async-start(f32[16,8,128]{2,1,0:T(8,128)} %broadcast_in_dim.9), calls=%async_computation | async-start | bytes 131072 | tf_op jit(solution)/shard_map/all_to_all | solution.py:335
  182.5 31.4 %all-to-all-start.1 = ((f32[16,8,128]{2,1,0:T(8,128)}), f32[16,8,128]{2,1,0:T(8,128)S(1)}, u32[]{:S(2)}, u32[]{:S(2)}) async-start(f32[16,8,128]{2,1,0:T(8,128)} %broadcast_in_dim.10), calls=%async_computation.1 | async-start | bytes 131072 | tf_op jit(solution)/shard_map/all_to_all | solution.py:335
  191.5 26.9 %collective-permute-start.18 = (f32[128,128]{1,0:T(8,128)S(1)}, f32[128,128]{1,0:T(8,128)S(1)}, u32[]{:S(2)}, u32[]{:S(2)}) collective-permute-start(f32[128,128]{1,0:T(8,128)S(1)} %get-tuple-element.51), channel_id=1, source_target_pairs={{192,0},{208,16},{224,32},{240,48},{0,64},{16,80},{32,96},{48,112}... | collective-permute-start | bytes 196616 | tf_op jit(solution)/shard_map/ppermute | solution.py:34
  199.3 19.1 %collective-permute-start.17 = (f32[128,128]{1,0:T(8,128)S(1)}, f32[128,128]{1,0:T(8,128)S(1)}, u32[]{:S(2)}, u32[]{:S(2)}) collective-permute-start(f32[128,128]{1,0:T(8,128)S(1)} %get-tuple-element.52), channel_id=1, source_target_pairs={{128,0},{144,16},{160,32},{176,48},{192,64},{208,80},{224,96},{240... | collective-permute-start | bytes 196616 | tf_op jit(solution)/shard_map/ppermute | solution.py:34
  206.6 14.7 %collective-permute-start.16 = (f32[128,128]{1,0:T(8,128)S(1)}, f32[128,128]{1,0:T(8,128)S(1)}, u32[]{:S(2)}, u32[]{:S(2)}) collective-permute-start(f32[128,128]{1,0:T(8,128)S(1)} %get-tuple-element.50), channel_id=1, source_target_pairs={{64,0},{80,16},{96,32},{112,48},{128,64},{144,80},{160,96},{176,11... | collective-permute-start | bytes 196616 | tf_op jit(solution)/shard_map/ppermute | solution.py:34
  214.5 9.2 %all-to-all-start.2 = ((f32[2,8,128]{2,1,0:T(8,128)}), f32[2,8,128]{2,1,0:T(8,128)S(1)}, u32[]{:S(2)}, u32[]{:S(2)}) async-start(f32[2,8,128]{2,1,0:T(8,128)} %broadcast_in_dim.11), calls=%async_computation.2 | async-start | bytes 16384 | tf_op jit(solution)/shard_map/all_to_all | solution.py:335
Sparse Core Ops, SparseCore 0:
  10.1 70.3 all-gather.5
  82.7 74.4 all-gather.7

commit v5 on v4

--- a/solution.py
+++ b/solution.py
@@ -225,6 +225,8 @@
     full_t = lax.all_gather(stack_t, "seq", axis=0).reshape(2, 4, 2, 3, 320, 256)
 
     other = lax.ppermute(both, "fsdp", [(i, (i + 16) % 32) for i in range(32)])
+    moved_x = lax.ppermute(moved, "seq", [(i, i ^ 2) for i in range(16)])
+    both, other, moved, moved_x = lax.optimization_barrier((both, other, moved, moved_x))
     own = lax.all_gather(jnp.stack([both, other]), "fsdp", axis=0, axis_index_groups=Z_FAR)
     plus = z_shift(own, 1)
     minus = z_shift(own, -1)
@@ -232,10 +234,12 @@
     two_g = z_shift(own[:, :, 1], -2)
     acts = (own, plus, minus, two_x, two_g)
 
-    moved_x = lax.ppermute(moved, "seq", [(i, i ^ 2) for i in range(16)])
-    moved, *_ = lax.optimization_barrier((moved,) + acts)
     moved = jnp.stack([moved, moved_x])
-    moved_plus, moved_minus = y_shift(moved, 1), y_shift(moved, -1)
+    moved, _ = lax.optimization_barrier((moved, own))
+    moved_plus = y_shift(moved, 1)
+    behind, half_plus, *_ = lax.optimization_barrier((moved, moved_plus[0]) + acts)
+    moved_minus = y_shift(behind, -1)
+    half_plus = y_shift(half_plus, 1)
 
     flat = jax.ShapeDtypeStruct((320, 128), F32)
     hidden, across, act, factor, dh = pl.pallas_call(
@@ -286,8 +290,8 @@
         name="block_sums",
     )(place, hidden, full_w)
 
-    half_plus, half_minus, _ = lax.optimization_barrier((moved_plus[0], moved_minus[1], kept))
-    half_plus, half_minus = y_shift(half_plus, 1), y_shift(half_minus, -1)
+    half_minus, _ = lax.optimization_barrier((moved_minus[1], kept))
+    half_minus = y_shift(half_minus, -1)
 
     up = z_shift(up, -1)
     down = z_shift(down, 1)
@@ -301,6 +305,8 @@
     theirs = lax.ppermute(mine, "seq", [(i, i ^ 1) for i in range(16)])
     away = lax.ppermute(away, "fsdp", [(i, (i + 16) % 32) for i in range(32)])
     partial = kept[0] + up[0] + down[0] + two_up + away
+    partial = jnp.sum(lax.all_to_all(partial, "fsdp", 0, 0, axis_index_groups=Z_FAR), axis=0)
+    block_out = partial.astype(BF16)
 
     terms = pl.pallas_call(
         tangent_kernel,
@@ -322,18 +328,9 @@
         name="tangents",
     )(place, *acts, full_t, mine, mine, theirs, theirs, across, act, factor, dh, loss_mask.astype(F32)[None])
 
-    partial, _ = lax.optimization_barrier((partial, terms))
-    z_hi = fsdp // 4 % 4
-    total = lax.dynamic_index_in_dim(partial, z_hi, 0, False)
-    far = [
-        z_shift(lax.dynamic_index_in_dim(partial, (z_hi + 4 - step) % 4, 0, False), 4 * step)
-        for step in range(1, 4)
-    ]
-
     for axis, size, groups in (("seq", 16, None), ("fsdp", 16, Z_ALL), ("fsdp", 2, X_PAIRS)):
         copies = jnp.broadcast_to(terms[None], (size,) + terms.shape)
         terms = jnp.sum(lax.all_to_all(copies, axis, 0, 0, axis_index_groups=groups), axis=0)
-    block_out = (total + far[0] + far[1] + far[2]).astype(BF16)
     return (block_out, terms[:EXAMPLES, :2])
 
 

time: 233 us -> 261 us (1.12); the launches traced: 231 us -> 256 us
  waiting for transfers between devices: 42.4 us -> 81.3 us
  starting transfers between devices: 98.1 us -> 73.1 us
  blocking collectives: 31.7 us -> 43.5 us
    ppermute x11 -> x8, starting transfers between devices: 52.1 us -> 28.3 us  [z_shift(): return lax.ppermute(array, 'fsdp', perm)]
    ppermute x4, waiting for transfers between devices: 14.4 us -> 32.3 us  [y_shift(): lax.ppermute(array, 'seq', [((i + 4 * step) % 16, i) for i in range(16)])]
    all_to_all x0 -> x1, waiting for transfers between devices: none -> 17.3 us  [shards(): lax.all_to_all(partial, 'fsdp', 0, 0, axis_index_groups=Z_FAR)]
    ppermute x11 -> x8, waiting for transfers between devices: 15.8 us -> 4.05 us  [z_shift(): return lax.ppermute(array, 'fsdp', perm)]
    all_to_all x0 -> x1, blocking collectives: none -> 11 us  [shards(): lax.all_to_all(copies, axis, 0, 0, axis_index_groups=groups)]
    all_to_all x3 -> x2, waiting for transfers between devices: 5.98 us -> 15.7 us  [shards(): lax.all_to_all(copies, axis, 0, 0, axis_index_groups=groups)]
    ppermute x1, waiting for transfers between devices: 2.72 us -> 10.4 us  [shards(): other = lax.ppermute(both, 'fsdp', [(i, (i + 16) % 32) for i in range(32)])]
    all_to_all x0 -> x1, starting transfers between devices: none -> 3.4 us  [shards(): lax.all_to_all(partial, 'fsdp', 0, 0, axis_index_groups=Z_FAR)]
  transfers between devices with their start and end apart: 24 -> 21, of which waited for: 9 -> 12; matrix products, arithmetic and copies ran while one was open for 7% -> 6% of each run, Pallas kernels for 10% -> 9%
where the time goes in v5:
time: 261 us; the launch traced here: 256 us
  waiting for transfers between devices  81.3 us (31%)
  starting transfers between devices  73.1 us (28%)
  blocking collectives  43.5 us (17%)
  Pallas kernels  23.1 us (9%)
  between operations  14.5 us (6%)
  other arithmetic  12.6 us (5%)
  local copies, waits for them, and re-layouts  8.33 us (3%)
    all_gather x1, blocking collectives, shards(): lax.all_gather(jnp.stack([both, other]), 'fsdp', axis=0, axis_index_group...  32.6 us
    ppermute x4, waiting for transfers between devices, y_shift(): lax.ppermute(array, 'seq', [((i + 4 * step) % 16, i) for i in range(16)])  32.3 us
    ppermute x8, starting transfers between devices, z_shift(): return lax.ppermute(array, 'fsdp', perm)  28.3 us
    all_to_all x1, waiting for transfers between devices, shards(): lax.all_to_all(partial, 'fsdp', 0, 0, axis_index_groups=Z_FAR)  17.3 us
    all_to_all x2, waiting for transfers between devices, shards(): lax.all_to_all(copies, axis, 0, 0, axis_index_groups=groups)  15.7 us
    ppermute x4, starting transfers between devices, y_shift(): lax.ppermute(array, 'seq', [((i + 4 * step) % 16, i) for i in range(16)])  14 us
    pallas_call x1, Pallas kernels, shards(): pl.pallas_call(tangent_kernel, out_shape=jax.ShapeDtypeStruct((8, 128), F...  13.8 us
    all_to_all x2, starting transfers between devices, shards(): lax.all_to_all(copies, axis, 0, 0, axis_index_groups=groups)  13.6 us
  transfers between devices with their start and end apart: 21, of which 12 were waited for; matrix products, arithmetic and copies ran while one was open for 6% of the time, Pallas kernels for 9%

profile of v5, /device:TPU:24, one launch (start us, length us, event | category | flops | bytes accessed | tf_op | source)
XLA Modules:
  0.0 256.4 jit_solution(7720390144652935608)
XLA Ops:
  7.2 0.0 all-gather.6.cloned.1.call-start
  7.2 2.0 pad_maximum_fusion.2
  9.2 0.0 all-gather.6.cloned.1.call-update
  9.2 0.0 all-gather.8.cloned.1.call-start
  9.3 0.8 pad_maximum_fusion.6
  10.0 1.0 fusion.5
  11.1 1.8 pad_maximum_fusion.4
  12.9 0.0 all-gather.8.cloned.1.call-update
  13.0 3.4 %collective-permute-start.1 = (bf16[3,320,256]{2,1,0:T(8,128)(2,1)S(1)}, bf16[3,320,256]{2,1,0:T(8,128)(2,1)S(1)}, u32[]{:S(2)}, u32[]{:S(2)}) collective-permute-start(bf16[3,320,256]{2,1,0:T(8,128)(2,1)S(1)} %pad_maximum_fusion.3), channel_id=1, source_target_pairs={{0,2},{1,3},{2,0},{3,1},{4,6},{5,7},{6,4},{7,5},{8,10},{9,11},{10,... | collective-permute-start | bytes 1474568 | tf_op jit(solution)/shard_map/ppermute | solution.py:228
  16.4 4.6 %collective-permute-start = (bf16[2,128,128]{2,1,0:T(8,128)(2,1)S(1)}, bf16[2,128,128]{2,1,0:T(8,128)(2,1)S(1)}, u32[]{:S(2)}, u32[]{:S(2)}) collective-permute-start(bf16[2,128,128]{2,1,0:T(8,128)(2,1)S(1)} %pad_maximum_fusion.6), channel_id=1, source_target_pairs={{0,256},{16,272},{32,288},{48,304},{64,320},{80,336},{96,352},{112... | collective-permute-start | bytes 196616 | tf_op jit(solution)/shard_map/ppermute | solution.py:227
  21.0 10.4 %collective-permute-done = bf16[2,128,128]{2,1,0:T(8,128)(2,1)S(1)} collective-permute-done((bf16[2,128,128]{2,1,0:T(8,128)(2,1)S(1)}, bf16[2,128,128]{2,1,0:T(8,128)(2,1)S(1)}, u32[]{:S(2)}, u32[]{:S(2)}) %collective-permute-start) | collective-permute-done | bytes 65568 | tf_op jit(solution)/shard_map/ppermute | solution.py:227
  31.4 0.0 collective-permute-done.1
  31.4 32.6 %all-gather = bf16[8,2,128,128]{3,2,1,0:T(8,128)(2,1)S(1)} all-gather(bf16[2,2,128,128]{3,2,1,0:T(8,128)(2,1)S(1)} %pad_maximum_fusion.5), channel_id=2, replica_groups={{0,64,128,192},{16,80,144,208},{32,96,160,224},{48,112,176,240},{256,32..., dimensions={0}, use_global_device_ids=true | all-gather | bytes 655360 | tf_op jit(solution)/shard_map/all_gather | solution.py:230
  64.1 1.0 pad_maximum_fusion.1
  65.1 1.9 collective-permute-start.11
  67.0 6.4 %collective-permute-start.2 = (bf16[4,2,2,128,128]{4,3,1,0,2:T(8,128)(2,1)S(1)}, bf16[4,2,2,128,128]{4,3,1,0,2:T(8,128)(2,1)S(1)}, u32[]{:S(2)}, u32[]{:S(2)}) collective-permute-start(bf16[4,2,2,128,128]{4,3,1,0,2:T(8,128)(2,1)S(1)} %bitcast.52), channel_id=1, source_target_pairs={{16,0},{32,16},{48,32},{64,48},{80,64},{96,80},{112,96},{128,112},... | collective-permute-start | bytes 1572872 | tf_op jit(solution)/shard_map/ppermute | solution.py:34
  73.4 1.9 collective-permute-start.3
  75.4 3.8 %collective-permute-start.4 = (bf16[4,2,128,128]{3,2,1,0:T(8,128)(2,1)S(1)}, bf16[4,2,128,128]{3,2,1,0:T(8,128)(2,1)S(1)}, u32[]{:S(2)}, u32[]{:S(2)}) collective-permute-start(bf16[4,2,128,128]{3,2,1,0:T(8,128)(2,1)S(1)} %get-tuple-element.53), channel_id=1, source_target_pairs={{32,0},{48,16},{64,32},{80,48},{96,64},{112,80},{128,96},{144,112}... | collective-permute-start | bytes 786440 | tf_op jit(solution)/shard_map/ppermute | solution.py:34
  79.3 2.9 %collective-permute-start.5 = (bf16[4,2,128,128]{3,2,1,0:T(8,128)(2,1)S(1)}, bf16[4,2,128,128]{3,2,1,0:T(8,128)(2,1)S(1)}, u32[]{:S(2)}, u32[]{:S(2)}) collective-permute-start(bf16[4,2,128,128]{3,2,1,0:T(8,128)(2,1)S(1)} %get-tuple-element.52), channel_id=1, source_target_pairs={{224,0},{240,16},{0,32},{16,48},{32,64},{48,80},{64,96},{80,112},{... | collective-permute-start | bytes 786440 | tf_op jit(solution)/shard_map/ppermute | solution.py:34
  82.2 7.0 %collective-permute-done.11 = bf16[2,3,320,256]{3,2,1,0:T(8,128)(2,1)S(1)} collective-permute-done((bf16[2,3,320,256]{3,2,1,0:T(8,128)(2,1)}, bf16[2,3,320,256]{3,2,1,0:T(8,128)(2,1)S(1)}, u32[]{:S(2)}, u32[]{:S(2)}) %collective-permute-start.11) | collective-permute-done | bytes 983072 | tf_op jit(solution)/shard_map/ppermute | solution.py:38
  89.2 0.9 slice_bitcast_fusion.1
  90.1 1.3 collective-permute-done.4.two_x
  91.4 2.3 collective-permute-done.5.two_g
  93.7 0.0 collective-permute-done.2
  93.7 0.4 collective-permute-done.3
  94.1 4.7 %collective-permute-start.13 = (bf16[2,3,320,256]{3,2,1,0:T(8,128)(2,1)}, bf16[2,3,320,256]{3,2,1,0:T(8,128)(2,1)}, u32[]{:S(2)}, u32[]{:S(2)}) collective-permute-start(bf16[2,3,320,256]{3,2,1,0:T(8,128)(2,1)} %pad_maximum_fusion.1), channel_id=1, source_target_pairs={{12,0},{13,1},{14,2},{15,3},{0,4},{1,5},{2,6},{3,7},{4,8},{5,9},{6... | collective-permute-start | bytes 2949128 | tf_op jit(solution)/shard_map/ppermute | solution.py:38
  98.9 0.1 stack.90.place
  99.1 0.0 all-gather.6.cloned.1.call-done
  99.1 3.2 %copy-done = bf16[48,320,256]{2,1,0:T(8,128)(2,1)S(1)} copy-done((bf16[48,320,256]{2,1,0:T(8,128)(2,1)S(1)}, bf16[48,320,256]{2,1,0:T(8,128)(2,1)}, u32[]{:S(2)}) %copy-start) | copy-done | bytes 7864344
  102.4 6.1 %primal.1 = (bf16[128,320]{1,0:T(8,128)(2,1)S(1)}, bf16[320,128]{1,0:T(8,128)(2,1)S(1)}, f32[320,128]{1,0:T(8,128)S(1)}, f32[320,128]{1,0:T(8,128)S(1)}, f32[320,128]{1,0:T(8,128)S(1)}) custom-call(s32[6]{0:T(128)S(1)} %stack.90.place, bf16[4,2,2,128,128]{4,3,2,1,0:T(8,128)(2,1)S(1)} %bitcast.48, bf16[4,2,2,128,128]{4,3,2,1,0:T(8,128)(2,1)S(1)} %copy.27.plus, ...), custom_call_target="tpu_custom_call" | custom-call | flops 1006632960 | bytes 10485760 | tf_op jit(solution)/shard_map/primal/pallas_call | solution.py:245
  108.5 3.2 %block_sums.1 = (f32[2,4,128,128]{3,2,1,0:T(8,128)S(1)}, f32[2,4,128,128]{3,2,1,0:T(8,128)S(1)}, f32[2,4,128,128]{3,2,1,0:T(8,128)S(1)}, f32[4,128,128]{2,1,0:T(8,128)S(1)}, f32[4,128,128]{2,1,0:T(8,128)S(1)}) custom-call(s32[6]{0:T(128)S(1)} %stack.90.place, bf16[128,320]{1,0:T(8,128)(2,1)S(1)} %get-tuple-element.30.hidden, ...), custom_call_target="tpu_custom_call" | custom-call | flops 335544320 | bytes 5242880 | tf_op jit(solution)/shard_map/block_sums/pallas_call | solution.py:271
  111.7 4.8 %collective-permute-start.7 = (f32[2,4,128,128]{3,2,1,0:T(8,128)S(1)}, f32[2,4,128,128]{3,2,1,0:T(8,128)S(1)}, u32[]{:S(2)}, u32[]{:S(2)}) collective-permute-start(f32[2,4,128,128]{3,2,1,0:T(8,128)S(1)} %get-tuple-element.33), channel_id=1, source_target_pairs={{16,0},{32,16},{48,32},{64,48},{80,64},{96,80},{112,96},{128,112},... | collective-permute-start | bytes 1572872 | tf_op jit(solution)/shard_map/ppermute | solution.py:34
  116.5 3.8 %collective-permute-start.6 = (f32[2,4,128,128]{3,2,1,0:T(8,128)S(1)}, f32[2,4,128,128]{3,2,1,0:T(8,128)S(1)}, u32[]{:S(2)}, u32[]{:S(2)}) collective-permute-start(f32[2,4,128,128]{3,2,1,0:T(8,128)S(1)} %get-tuple-element.32), channel_id=1, source_target_pairs={{240,0},{0,16},{16,32},{32,48},{48,64},{64,80},{80,96},{96,112},{1... | collective-permute-start | bytes 1572872 | tf_op jit(solution)/shard_map/ppermute | solution.py:34
  120.3 1.9 collective-permute-start.12
  122.3 2.8 %collective-permute-start.9 = (f32[4,128,128]{2,1,0:T(8,128)S(1)}, f32[4,128,128]{2,1,0:T(8,128)S(1)}, u32[]{:S(2)}, u32[]{:S(2)}) collective-permute-start(f32[4,128,128]{2,1,0:T(8,128)S(1)} %get-tuple-element.35), channel_id=1, source_target_pairs={{32,0},{48,16},{64,32},{80,48},{96,64},{112,80},{128,96},{144,112}... | collective-permute-start | bytes 786440 | tf_op jit(solution)/shard_map/ppermute | solution.py:34
  125.0 8.9 %collective-permute-done.13 = bf16[2,3,320,256]{3,2,1,0:T(8,128)(2,1)} collective-permute-done((bf16[2,3,320,256]{3,2,1,0:T(8,128)(2,1)}, bf16[2,3,320,256]{3,2,1,0:T(8,128)(2,1)}, u32[]{:S(2)}, u32[]{:S(2)}) %collective-permute-start.13) | collective-permute-done | bytes 983072 | tf_op jit(solution)/shard_map/ppermute | solution.py:38
  133.9 1.1 slice_bitcast_fusion
  135.0 5.4 %collective-permute-start.14 = (bf16[3,320,256]{2,1,0:T(8,128)(2,1)S(1)}, bf16[3,320,256]{2,1,0:T(8,128)(2,1)S(1)}, u32[]{:S(2)}, u32[]{:S(2)}) collective-permute-start(bf16[3,320,256]{2,1,0:T(8,128)(2,1)S(1)} %slice_bitcast_fusion), channel_id=1, source_target_pairs={{12,0},{13,1},{14,2},{15,3},{0,4},{1,5},{2,6},{3,7},{4,8},{5,9},{6... | collective-permute-start | bytes 1474568 | tf_op jit(solution)/shard_map/ppermute | solution.py:38
  140.4 0.0 collective-permute-done.9
  140.4 0.0 collective-permute-done.6
  140.5 0.8 fusion.1
  141.3 0.3 collective-permute-done.12
  141.6 16.1 %collective-permute-done.14 = bf16[3,320,256]{2,1,0:T(8,128)(2,1)S(1)} collective-permute-done((bf16[3,320,256]{2,1,0:T(8,128)(2,1)S(1)}, bf16[3,320,256]{2,1,0:T(8,128)(2,1)S(1)}, u32[]{:S(2)}, u32[]{:S(2)}) %collective-permute-start.14) | collective-permute-done | bytes 491552 | tf_op jit(solution)/shard_map/ppermute | solution.py:38
  157.7 0.1 maximum_bitcast_fusion
  157.8 0.0 copy-start.8
  157.8 3.4 %pad_maximum_fusion.mine_0.mine_1 = bf16[4,2,3,320,256]{4,3,2,1,0:T(8,128)(2,1)} fusion(bf16[1,2,3,320,256]{4,3,2,1,0:T(8,128)(2,1)} %bitcast.30, bf16[1,2,3,320,256]{4,3,2,1,0:T(8,128)(2,1)S(1)} %maximum_bitcast_fusion, bf16[1,2,3,320,256]{4,3,2,1,0:T(8,128)(2,1)S(1)} %bitcast.51, bf16[1,2,3,320,256]{4,3,2,1,0:T(8,128)(2,1)} %bitcast.23), kind=kLoop, calls=%fused_computation | loop fusion | flops 5898240 | bytes 7864320 | tf_op jit(solution)/shard_map/stack | solution.py:304
  161.2 1.9 collective-permute-start.15
  163.1 1.9 collective-permute-start.8
  165.0 3.7 %collective-permute-start.10 = (f32[4,128,128]{2,1,0:T(8,128)}, f32[4,128,128]{2,1,0:T(8,128)}, u32[]{:S(2)}, u32[]{:S(2)}) collective-permute-start(f32[4,128,128]{2,1,0:T(8,128)} %fusion.1), channel_id=1, source_target_pairs={{0,256},{16,272},{32,288},{48,304},{64,320},{80,336},{96,352},{112... | collective-permute-start | bytes 786440 | tf_op jit(solution)/shard_map/ppermute | solution.py:306
  168.8 0.0 all-gather.8.cloned.1.call-done
  168.8 1.4 collective-permute-done.15.theirs_0.theirs_1
  170.2 13.8 %tangents.1 = f32[8,128]{1,0:T(8,128)S(1)} custom-call(s32[6]{0:T(128)S(1)} %stack.90.place, bf16[4,2,2,128,128]{4,3,2,1,0:T(8,128)(2,1)S(1)} %bitcast.49, bf16[4,2,2,128,128]{4,3,2,1,0:T(8,128)(2,1)S(1)} %copy.27.plus, bf16[4,2,2,128,128]{4,3,2,1,0:T(8,128)(2,1)S(1)} %copy.28.minus, bf16[4,2,128,128]{3,2,1,0:T(8,128)(2,1)S(1)} %collective-permute-done.4.two_x, ...), custom_call_target="tpu_custom_call" | custom-call | flops 2013265920 | bytes 18874368 | tf_op jit(solution)/shard_map/tangents/pallas_call | solution.py:311
  184.0 11.0 %all_to_all.20 = f32[16,8,128]{2,1,0:T(8,128)S(1)} all-to-all(f32[16,8,128]{2,1,0:T(8,128)S(1)} %broadcast_in_dim.9), channel_id=1, replica_groups=mesh['fsdp'=32,'seq'=16] {'seq'}, dimensions={0} | all-to-all | bytes 131072 | tf_op jit(solution)/shard_map/all_to_all | solution.py:333
  195.0 0.6 broadcast_in_dim.10
  195.6 9.2 %all-to-all-start.2 = ((f32[16,8,128]{2,1,0:T(8,128)}), f32[16,8,128]{2,1,0:T(8,128)S(1)}, u32[]{:S(2)}, u32[]{:S(2)}) async-start(f32[16,8,128]{2,1,0:T(8,128)} %broadcast_in_dim.10), calls=%async_computation.2 | async-start | bytes 131072 | tf_op jit(solution)/shard_map/all_to_all | solution.py:333
  204.8 1.9 fusion.4
  206.7 11.1 %all-to-all-done.2 = f32[16,8,128]{2,1,0:T(8,128)S(1)} async-done(((f32[16,8,128]{2,1,0:T(8,128)}), f32[16,8,128]{2,1,0:T(8,128)S(1)}, u32[]{:S(2)}, u32[]{:S(2)}) %all-to-all-start.2) | async-done | bytes 65568 | tf_op jit(solution)/shard_map/all_to_all | solution.py:333
  217.8 3.4 %all-to-all-start = ((f32[4,128,128]{2,1,0:T(8,128)}), f32[4,128,128]{2,1,0:T(8,128)S(1)}, u32[]{:S(2)}, u32[]{:S(2)}) async-start(f32[4,128,128]{2,1,0:T(8,128)} %fusion.4), calls=%async_computation | async-start | bytes 524288 | tf_op jit(solution)/shard_map/all_to_all | solution.py:308
  221.2 17.3 %all-to-all-done = f32[4,128,128]{2,1,0:T(8,128)S(1)} async-done(((f32[4,128,128]{2,1,0:T(8,128)}), f32[4,128,128]{2,1,0:T(8,128)S(1)}, u32[]{:S(2)}, u32[]{:S(2)}) %all-to-all-start) | async-done | bytes 262176 | tf_op jit(solution)/shard_map/all_to_all | solution.py:308
  238.5 0.6 broadcast_in_dim.11
  239.1 4.5 %all-to-all-start.3 = ((f32[2,8,128]{2,1,0:T(8,128)}), f32[2,8,128]{2,1,0:T(8,128)S(1)}, u32[]{:S(2)}, u32[]{:S(2)}) async-start(f32[2,8,128]{2,1,0:T(8,128)} %broadcast_in_dim.11), calls=%async_computation.3 | async-start | bytes 16384 | tf_op jit(solution)/shard_map/all_to_all | solution.py:333
  243.6 0.6 reduce_sum.36
  244.2 4.7 %all-to-all-done.3 = f32[2,8,128]{2,1,0:T(8,128)S(1)} async-done(((f32[2,8,128]{2,1,0:T(8,128)}), f32[2,8,128]{2,1,0:T(8,128)S(1)}, u32[]{:S(2)}, u32[]{:S(2)}) %all-to-all-start.3) | async-done | bytes 8224 | tf_op jit(solution)/shard_map/all_to_all | solution.py:333
  248.9 0.7 copy.32
  (31 shorter events, 0.3 us)
Async XLA Ops:
  7.2 5.7 %copy-start.7 = (bf16[2,320,256]{2,1,0:T(8,128)(2,1)S(1)}, bf16[2,320,256]{2,1,0:T(8,128)(2,1)}, u32[]{:S(2)}) copy-start(bf16[2,320,256]{2,1,0:T(8,128)(2,1)} %param.17) | copy-start | bytes 983044
  7.2 92.0 %all-gather.6.cloned.1.call-start = ((), (), s32[]{:S(2)}) async-start(), calls=%async_computation.4 | async-start | bytes 8355840 | tf_op jit(solution)/shard_map/all_gather | solution.py:224
  9.2 159.6 %all-gather.8.cloned.1.call-start = ((), (), s32[]{:S(2)}) async-start(), calls=%async_computation.5 | async-start | bytes 8355840 | tf_op jit(solution)/shard_map/all_gather | solution.py:225
  13.0 18.5 %collective-permute-start.1 = (bf16[3,320,256]{2,1,0:T(8,128)(2,1)S(1)}, bf16[3,320,256]{2,1,0:T(8,128)(2,1)S(1)}, u32[]{:S(2)}, u32[]{:S(2)}) collective-permute-start(bf16[3,320,256]{2,1,0:T(8,128)(2,1)S(1)} %pad_maximum_fusion.3), channel_id=1, source_target_pairs={{0,2},{1,3},{2,0},{3,1},{4,6},{5,7},{6,4},{7,5},{8,10},{9,11},{10,... | collective-permute-start | bytes 1474568 | tf_op jit(solution)/shard_map/ppermute | solution.py:228
  16.4 15.0 %collective-permute-start = (bf16[2,128,128]{2,1,0:T(8,128)(2,1)S(1)}, bf16[2,128,128]{2,1,0:T(8,128)(2,1)S(1)}, u32[]{:S(2)}, u32[]{:S(2)}) collective-permute-start(bf16[2,128,128]{2,1,0:T(8,128)(2,1)S(1)} %pad_maximum_fusion.6), channel_id=1, source_target_pairs={{0,256},{16,272},{32,288},{48,304},{64,320},{80,336},{96,352},{112... | collective-permute-start | bytes 196616 | tf_op jit(solution)/shard_map/ppermute | solution.py:227
  65.1 24.1 %collective-permute-start.11 = (bf16[2,3,320,256]{3,2,1,0:T(8,128)(2,1)}, bf16[2,3,320,256]{3,2,1,0:T(8,128)(2,1)S(1)}, u32[]{:S(2)}, u32[]{:S(2)}) collective-permute-start(bf16[2,3,320,256]{3,2,1,0:T(8,128)(2,1)} %pad_maximum_fusion.1), channel_id=1, source_target_pairs={{4,0},{5,1},{6,2},{7,3},{8,4},{9,5},{10,6},{11,7},{12,8},{13,9},{1... | collective-permute-start | bytes 2949128 | tf_op jit(solution)/shard_map/ppermute | solution.py:38
  67.0 26.7 %collective-permute-start.2 = (bf16[4,2,2,128,128]{4,3,1,0,2:T(8,128)(2,1)S(1)}, bf16[4,2,2,128,128]{4,3,1,0,2:T(8,128)(2,1)S(1)}, u32[]{:S(2)}, u32[]{:S(2)}) collective-permute-start(bf16[4,2,2,128,128]{4,3,1,0,2:T(8,128)(2,1)S(1)} %bitcast.52), channel_id=1, source_target_pairs={{16,0},{32,16},{48,32},{64,48},{80,64},{96,80},{112,96},{128,112},... | collective-permute-start | bytes 1572872 | tf_op jit(solution)/shard_map/ppermute | solution.py:34
  73.4 20.7 %collective-permute-start.3 = (bf16[4,2,2,128,128]{4,3,1,0,2:T(8,128)(2,1)S(1)}, bf16[4,2,2,128,128]{4,3,1,0,2:T(8,128)(2,1)S(1)}, u32[]{:S(2)}, u32[]{:S(2)}) collective-permute-start(bf16[4,2,2,128,128]{4,3,1,0,2:T(8,128)(2,1)S(1)} %bitcast.53), channel_id=1, source_target_pairs={{240,0},{0,16},{16,32},{32,48},{48,64},{64,80},{80,96},{96,112},{1... | collective-permute-start | bytes 1572872 | tf_op jit(solution)/shard_map/ppermute | solution.py:34
  75.4 16.0 %collective-permute-start.4 = (bf16[4,2,128,128]{3,2,1,0:T(8,128)(2,1)S(1)}, bf16[4,2,128,128]{3,2,1,0:T(8,128)(2,1)S(1)}, u32[]{:S(2)}, u32[]{:S(2)}) collective-permute-start(bf16[4,2,128,128]{3,2,1,0:T(8,128)(2,1)S(1)} %get-tuple-element.53), channel_id=1, source_target_pairs={{32,0},{48,16},{64,32},{80,48},{96,64},{112,80},{128,96},{144,112}... | collective-permute-start | bytes 786440 | tf_op jit(solution)/shard_map/ppermute | solution.py:34
  79.3 14.4 %collective-permute-start.5 = (bf16[4,2,128,128]{3,2,1,0:T(8,128)(2,1)S(1)}, bf16[4,2,128,128]{3,2,1,0:T(8,128)(2,1)S(1)}, u32[]{:S(2)}, u32[]{:S(2)}) collective-permute-start(bf16[4,2,128,128]{3,2,1,0:T(8,128)(2,1)S(1)} %get-tuple-element.52), channel_id=1, source_target_pairs={{224,0},{240,16},{0,32},{16,48},{32,64},{48,80},{64,96},{80,112},{... | collective-permute-start | bytes 786440 | tf_op jit(solution)/shard_map/ppermute | solution.py:34
  89.2 9.7 %copy-start.2 = (bf16[2,3,320,256]{3,2,1,0:T(8,128)(2,1)}, bf16[2,3,320,256]{3,2,1,0:T(8,128)(2,1)S(1)}, u32[]{:S(2)}) copy-start(bf16[2,3,320,256]{3,2,1,0:T(8,128)(2,1)S(1)} %collective-permute-done.11) | copy-start | bytes 2949124
  94.1 39.8 %collective-permute-start.13 = (bf16[2,3,320,256]{3,2,1,0:T(8,128)(2,1)}, bf16[2,3,320,256]{3,2,1,0:T(8,128)(2,1)}, u32[]{:S(2)}, u32[]{:S(2)}) collective-permute-start(bf16[2,3,320,256]{3,2,1,0:T(8,128)(2,1)} %pad_maximum_fusion.1), channel_id=1, source_target_pairs={{12,0},{13,1},{14,2},{15,3},{0,4},{1,5},{2,6},{3,7},{4,8},{5,9},{6... | collective-permute-start | bytes 2949128 | tf_op jit(solution)/shard_map/ppermute | solution.py:38
  99.1 3.2 %copy-start = (bf16[48,320,256]{2,1,0:T(8,128)(2,1)S(1)}, bf16[48,320,256]{2,1,0:T(8,128)(2,1)}, u32[]{:S(2)}) copy-start(bf16[48,320,256]{2,1,0:T(8,128)(2,1)} %all-gather.6.cloned.1.call-done) | copy-start | bytes 23592964
  102.4 6.2 %copy-start.1 = (bf16[48,320,256]{2,1,0:T(8,128)(2,1)S(1)}, bf16[48,320,256]{2,1,0:T(8,128)(2,1)}, u32[]{:S(2)}) copy-start(bf16[48,320,256]{2,1,0:T(8,128)(2,1)} %all-gather.6.cloned.1.call-done) | copy-start | bytes 23592964
  108.5 11.8 %copy-start.6 = (bf16[3,320,256]{2,1,0:T(8,128)(2,1)S(1)}, bf16[3,320,256]{2,1,0:T(8,128)(2,1)}, u32[]{:S(2)}) copy-start(bf16[3,320,256]{2,1,0:T(8,128)(2,1)} %slice_bitcast_fusion.1) | copy-start | bytes 1474564
  111.7 46.1 %copy-start.3 = (bf16[2,3,320,256]{3,2,1,0:T(8,128)(2,1)S(1)}, bf16[2,3,320,256]{3,2,1,0:T(8,128)(2,1)}, u32[]{:S(2)}) copy-start(bf16[2,3,320,256]{3,2,1,0:T(8,128)(2,1)} %copy-done.2) | copy-start | bytes 2949124
  111.7 28.7 %collective-permute-start.7 = (f32[2,4,128,128]{3,2,1,0:T(8,128)S(1)}, f32[2,4,128,128]{3,2,1,0:T(8,128)S(1)}, u32[]{:S(2)}, u32[]{:S(2)}) collective-permute-start(f32[2,4,128,128]{3,2,1,0:T(8,128)S(1)} %get-tuple-element.33), channel_id=1, source_target_pairs={{16,0},{32,16},{48,32},{64,48},{80,64},{96,80},{112,96},{128,112},... | collective-permute-start | bytes 1572872 | tf_op jit(solution)/shard_map/ppermute | solution.py:34
  116.5 23.9 %collective-permute-start.6 = (f32[2,4,128,128]{3,2,1,0:T(8,128)S(1)}, f32[2,4,128,128]{3,2,1,0:T(8,128)S(1)}, u32[]{:S(2)}, u32[]{:S(2)}) collective-permute-start(f32[2,4,128,128]{3,2,1,0:T(8,128)S(1)} %get-tuple-element.32), channel_id=1, source_target_pairs={{240,0},{0,16},{16,32},{32,48},{48,64},{64,80},{80,96},{96,112},{1... | collective-permute-start | bytes 1572872 | tf_op jit(solution)/shard_map/ppermute | solution.py:34
  120.3 21.3 %collective-permute-start.12 = (bf16[3,320,256]{2,1,0:T(8,128)(2,1)S(1)}, bf16[3,320,256]{2,1,0:T(8,128)(2,1)S(1)}, u32[]{:S(2)}, u32[]{:S(2)}) collective-permute-start(bf16[3,320,256]{2,1,0:T(8,128)(2,1)S(1)} %copy-done.6), channel_id=1, source_target_pairs={{4,0},{5,1},{6,2},{7,3},{8,4},{9,5},{10,6},{11,7},{12,8},{13,9},{1... | collective-permute-start | bytes 1474568 | tf_op jit(solution)/shard_map/ppermute | solution.py:38
  122.3 18.1 %collective-permute-start.9 = (f32[4,128,128]{2,1,0:T(8,128)S(1)}, f32[4,128,128]{2,1,0:T(8,128)S(1)}, u32[]{:S(2)}, u32[]{:S(2)}) collective-permute-start(f32[4,128,128]{2,1,0:T(8,128)S(1)} %get-tuple-element.35), channel_id=1, source_target_pairs={{32,0},{48,16},{64,32},{80,48},{96,64},{112,80},{128,96},{144,112}... | collective-permute-start | bytes 786440 | tf_op jit(solution)/shard_map/ppermute | solution.py:34
  135.0 22.7 %collective-permute-start.14 = (bf16[3,320,256]{2,1,0:T(8,128)(2,1)S(1)}, bf16[3,320,256]{2,1,0:T(8,128)(2,1)S(1)}, u32[]{:S(2)}, u32[]{:S(2)}) collective-permute-start(bf16[3,320,256]{2,1,0:T(8,128)(2,1)S(1)} %slice_bitcast_fusion), channel_id=1, source_target_pairs={{12,0},{13,1},{14,2},{15,3},{0,4},{1,5},{2,6},{3,7},{4,8},{5,9},{6... | collective-permute-start | bytes 1474568 | tf_op jit(solution)/shard_map/ppermute | solution.py:38
  140.4 24.6 %copy-start.4 = (f32[2,4,128,128]{3,2,1,0:T(8,128)}, f32[2,4,128,128]{3,2,1,0:T(8,128)S(1)}, u32[]{:S(2)}) copy-start(f32[2,4,128,128]{3,2,1,0:T(8,128)S(1)} %collective-permute-done.7) | copy-start | bytes 1572868
  140.5 28.3 %copy-start.5 = (f32[2,4,128,128]{3,2,1,0:T(8,128)}, f32[2,4,128,128]{3,2,1,0:T(8,128)S(1)}, u32[]{:S(2)}) copy-start(f32[2,4,128,128]{3,2,1,0:T(8,128)S(1)} %collective-permute-done.6) | copy-start | bytes 1572868
  157.8 10.9 %copy-start.8 = (s32[128]{0:T(128)S(1)}, s32[128]{0:T(128)}, u32[]{:S(2)}) copy-start(s32[128]{0:T(128)} %param.11) | copy-start | bytes 1540
  161.2 9.0 %collective-permute-start.15 = (bf16[4,2,3,320,256]{4,3,2,1,0:T(8,128)(2,1)}, bf16[4,2,3,320,256]{4,3,2,1,0:T(8,128)(2,1)}, u32[]{:S(2)}, u32[]{:S(2)}) collective-permute-start(bf16[4,2,3,320,256]{4,3,2,1,0:T(8,128)(2,1)} %pad_maximum_fusion.mine_0.mine_1), channel_id=1, source_target_pairs={{0,1},{1,0},{2,3},{3,2},{4,5},{5,4},{6,7},{7,6},{8,9},{9,8},{10,11... | collective-permute-start | bytes 11796488 | tf_op jit(solution)/shard_map/ppermute | solution.py:305
  163.1 41.7 %collective-permute-start.8 = (f32[4,128,128]{2,1,0:T(8,128)S(1)}, f32[4,128,128]{2,1,0:T(8,128)}, u32[]{:S(2)}, u32[]{:S(2)}) collective-permute-start(f32[4,128,128]{2,1,0:T(8,128)S(1)} %get-tuple-element.34), channel_id=1, source_target_pairs={{224,0},{240,16},{0,32},{16,48},{32,64},{48,80},{64,96},{80,112},{... | collective-permute-start | bytes 786440 | tf_op jit(solution)/shard_map/ppermute | solution.py:34
  165.0 39.7 %collective-permute-start.10 = (f32[4,128,128]{2,1,0:T(8,128)}, f32[4,128,128]{2,1,0:T(8,128)}, u32[]{:S(2)}, u32[]{:S(2)}) collective-permute-start(f32[4,128,128]{2,1,0:T(8,128)} %fusion.1), channel_id=1, source_target_pairs={{0,256},{16,272},{32,288},{48,304},{64,320},{80,336},{96,352},{112... | collective-permute-start | bytes 786440 | tf_op jit(solution)/shard_map/ppermute | solution.py:306
  195.6 22.2 %all-to-all-start.2 = ((f32[16,8,128]{2,1,0:T(8,128)}), f32[16,8,128]{2,1,0:T(8,128)S(1)}, u32[]{:S(2)}, u32[]{:S(2)}) async-start(f32[16,8,128]{2,1,0:T(8,128)} %broadcast_in_dim.10), calls=%async_computation.2 | async-start | bytes 131072 | tf_op jit(solution)/shard_map/all_to_all | solution.py:333
  217.8 20.7 %all-to-all-start = ((f32[4,128,128]{2,1,0:T(8,128)}), f32[4,128,128]{2,1,0:T(8,128)S(1)}, u32[]{:S(2)}, u32[]{:S(2)}) async-start(f32[4,128,128]{2,1,0:T(8,128)} %fusion.4), calls=%async_computation | async-start | bytes 524288 | tf_op jit(solution)/shard_map/all_to_all | solution.py:308
  239.1 9.8 %all-to-all-start.3 = ((f32[2,8,128]{2,1,0:T(8,128)}), f32[2,8,128]{2,1,0:T(8,128)S(1)}, u32[]{:S(2)}, u32[]{:S(2)}) async-start(f32[2,8,128]{2,1,0:T(8,128)} %broadcast_in_dim.11), calls=%async_computation.3 | async-start | bytes 16384 | tf_op jit(solution)/shard_map/all_to_all | solution.py:333
Sparse Core Ops, SparseCore 0:
  10.1 61.4 all-gather.5
  73.8 90.0 all-gather.7

commit v6 on v3

--- a/solution.py
+++ b/solution.py
@@ -14,21 +14,8 @@
 NT = (((1,), (1,)), ((), ()))
 
 Z_FAR = [[h * 16 + q * 4 + r for q in range(4)] for h in range(2) for r in range(4)]
-
-
-def eights(held):
-    sizes = (2, 4, 4, 4, 2, 2)
-    groups = {}
-    for device in range(512):
-        digits, rest = [], device
-        for size in reversed(sizes):
-            digits.insert(0, rest % size)
-            rest //= size
-        groups.setdefault(tuple(digits[at] for at in held), []).append(device)
-    return [groups[key] for key in sorted(groups)]
-
-
-ALL_BY_EIGHT = [eights((2, 3, 4, 5)), eights((0, 1, 3, 4)), eights((0, 1, 2, 5))]
+Z_ALL = [list(range(16)), list(range(16, 32))]
+X_PAIRS = [[i, i + 16] for i in range(16)]
 
 
 def gelu_value_slope(value):
@@ -47,16 +34,19 @@
     return lax.ppermute(array, "fsdp", perm)
 
 
-def pairs(place, own, plus, minus, two, which):
+def y_shift(array, step):
+    return lax.ppermute(array, "seq", [((i + 4 * step) % 16, i) for i in range(16)])
+
+
+def pairs(place, acts, which):
     x_hi, z_lo = place[0], place[1]
     found = []
     for other in range(2):
-        held = [own[0, other, which], plus[0, other, which], two[0, other], minus[0, other, which]]
         near = []
         for at in range(4):
-            block = held[0]
+            block = acts[0, other, which, 0]
             for shift in range(1, 4):
-                block = jnp.where((z_lo + shift) % 4 == at, held[shift], block)
+                block = jnp.where((z_lo + shift) % 4 == at, acts[0, other, which, shift], block)
             near.append(block)
         row = jnp.bitwise_xor(x_hi, other)
         for half in range(2):
@@ -85,11 +75,11 @@
 
 
 def primal_kernel(
-    place, own, plus, minus, two_x, two_g, weights, hidden, across, act_out, factor_out, dh_out, by_x, by_g
+    place, acts, weights, hidden, across, act_out, factor_out, dh_out, by_x, by_g
 ):
     step = pl.program_id(0)
-    add_up(step, by_x, contract(pairs(place, own, plus, minus, two_x, 0), weights, 0, 2))
-    add_up(step, by_g, contract(pairs(place, own, plus, minus, two_g, 1), weights, 2, 1))
+    add_up(step, by_x, contract(pairs(place, acts, 0), weights, 0, 2))
+    add_up(step, by_g, contract(pairs(place, acts, 1), weights, 2, 1))
 
     @pl.when(step == pl.num_programs(0) - 1)
     def _():
@@ -128,34 +118,60 @@
                     two_b[z_hi] = value
 
 
-def tangent_kernel(
-    place, own, plus, minus, two_x, two_g, weights, across, act, factor, dh, mask, out, by_x, by_g
+def column_blocks(place, acts, partner, which):
+    own = pairs(place, acts, which)
+    theirs = pairs(place, partner, which)
+    both = [jnp.concatenate([a[2], b[2]], axis=0) for a, b in zip(own, theirs)]
+    found = []
+    for other in range(2):
+        low, high = both[2 * other], both[2 * other + 1]
+        found.append(jnp.where(place[5] == 0, low, high))
+        found.append(jnp.where(place[5] == 0, high, low))
+    return found
+
+
+def column_sums(blocks, rows, first, count):
+    total = None
+    for ref, block in zip(rows, blocks):
+        part = ref[0, first : first + count].reshape(count * 320, 256)
+        term = lax.dot_general(part, block, NT, preferred_element_type=F32)
+        total = term if total is None else total + term
+    return total
+
+
+def column_kernel(
+    place, acts, partner, mine_0, theirs_0, mine_1, theirs_1, kept, away, by_x, by_g
 ):
     step = pl.program_id(0)
-    add_up(step, by_x, contract(pairs(place, own, plus, minus, two_x, 0), weights, 0, 4))
-    add_up(step, by_g, contract(pairs(place, own, plus, minus, two_g, 1), weights, 4, 2))
+    rows = (mine_0, theirs_0, mine_1, theirs_1)
+    add_up(step, by_x, column_sums(column_blocks(place, acts, partner, 0), rows, 0, 4))
+    add_up(step, by_g, column_sums(column_blocks(place, acts, partner, 1), rows, 4, 2))
 
     @pl.when(step == pl.num_programs(0) - 1)
     def _():
-        rows = lax.broadcasted_iota(jnp.int32, (8, 128), 0)
-        lanes = lax.broadcasted_iota(jnp.int32, (8, 128), 1)
-        total = jnp.zeros((8, 128), F32)
-        for k in range(2):
-            gate = by_x[k * 320 : (k + 1) * 320]
-            upper = by_x[(2 + k) * 320 : (3 + k) * 320]
-            tangent = (factor[...] * gate + act[...] * upper).astype(BF16)
-            value = tangent.astype(F32) * dh[...]
-            value += across[...].astype(F32) * by_g[k * 320 : (k + 1) * 320]
-            value = jnp.sum(value, axis=0, keepdims=True) * mask[...]
-            value = jnp.sum(value, axis=1, keepdims=True)
-            total = jnp.where((rows == place[2]) & (lanes == k), value, total)
-        out[...] = total
-
-
-def activation_specs():
-    full = pl.BlockSpec((1, 2, 2, 128, 128), lambda s, p: (s, 0, 0, 0, 0))
-    single = pl.BlockSpec((1, 2, 128, 128), lambda s, p: (s, 0, 0, 0))
-    return [full, full, full, single, single]
+        kept[:1280] = by_x[:, :128]
+        kept[1280:] = by_g[:, :128]
+        away[:1280] = by_x[:, 128:]
+        away[1280:] = by_g[:, 128:]
+
+
+def term_kernel(example, kept, got, across, act, factor, dh, mask, out):
+    rows = lax.broadcasted_iota(jnp.int32, (8, 128), 0)
+    lanes = lax.broadcasted_iota(jnp.int32, (8, 128), 1)
+    total = jnp.zeros((8, 128), F32)
+    for k in range(2):
+
+        def summed(at):
+            part = slice(at * 320, (at + 1) * 320)
+            return kept[part] + got[part]
+
+        tangent = (factor[...] * summed(k) + act[...] * summed(2 + k)).astype(BF16)
+        value = tangent.astype(F32) * dh[...]
+        value += across[...].astype(F32) * summed(4 + k)
+        value = jnp.sum(value, axis=0, keepdims=True) * mask[...]
+        value = jnp.sum(value, axis=1, keepdims=True)
+        total = jnp.where((rows == example[0]) & (lanes == k), value, total)
+    out[...] = total
 
 
 def whole(shape):
@@ -164,6 +180,13 @@
 
 def weight_spec(count):
     return pl.BlockSpec((2, 1, 2, count, 320, 256), lambda s, p: (0, s, 0, 0, 0, 0))
+
+
+def column_spec(other):
+    def index(s, p):
+        return ((jnp.bitwise_xor(p[0], other) * 2 + s - p[3] + 4) % 4, 0, 0, 0)
+
+    return pl.BlockSpec((1, 6, 320, 256), index)
 
 
 def shards(tokens, out_grad, loss_mask, w_in0, w_in1, w_out, tan_in0, tan_in1, tan_out):
@@ -171,22 +194,42 @@
     seq = lax.axis_index("seq")
     rows = tokens.shape[0]
     length = rows * lax.axis_size("seq") // EXAMPLES
-    place = jnp.stack([fsdp // 16, fsdp % 4, seq * rows // length]).astype(jnp.int32)
+    place = jnp.stack(
+        [fsdp // 16, fsdp % 4, seq * rows // length, seq // 4, seq // 2 % 2, seq % 2]
+    ).astype(jnp.int32)
 
     stack_w = jnp.stack([w_in0, w_in1, w_out])
-    stack_w, *tans = lax.optimization_barrier((stack_w, tan_in0, tan_in1, tan_out))
-    stack_t = jnp.concatenate(tans, axis=0)
-    full_w = lax.all_gather(stack_w, "seq", axis=0).reshape(2, 4, 2, 3, 320, 256)
-    full_t = lax.all_gather(stack_t, "seq", axis=0).reshape(2, 4, 2, 6, 320, 256)
-
     both = jnp.stack([tokens, out_grad])
     other = lax.ppermute(both, "fsdp", [(i, (i + 16) % 32) for i in range(32)])
-    own = lax.all_gather(jnp.stack([both, other]), "fsdp", axis=0, axis_index_groups=Z_FAR)
+    _, _, tan_in0, tan_in1, tan_out = lax.optimization_barrier(
+        (stack_w, other, tan_in0, tan_in1, tan_out)
+    )
+    stack_t = jnp.concatenate([tan_in0, tan_in1, tan_out], axis=0)
+    full_w = lax.all_gather(stack_w, "seq", axis=0).reshape(2, 4, 2, 3, 320, 256)
+
+    t_plus, t_minus = y_shift(stack_t, 1), y_shift(stack_t, -1)
+
+    both = jnp.stack([both, other])
+    far = [both] + [z_shift(both, step) for step in (4, 8, 12)]
+    z_hi = fsdp // 4 % 4
+    own = lax.dynamic_slice_in_dim(jnp.stack(far + far[:3]), (4 - z_hi) % 4, 4, axis=0)
     plus = z_shift(own, 1)
     minus = z_shift(own, -1)
     two_x = z_shift(own[:, :, 0], 2)
     two_g = z_shift(own[:, :, 1], -2)
-    acts = (own, plus, minus, two_x, two_g)
+    acts = jnp.stack([own, plus, jnp.stack([two_x, two_g], axis=2), minus], axis=3)
+
+    half_plus, half_minus, _ = lax.optimization_barrier((t_plus[:3], t_minus[3:], own))
+    half_plus, half_minus = y_shift(half_plus, 1), y_shift(half_minus, -1)
+    half_plus, half_minus, _ = lax.optimization_barrier((half_plus, half_minus, acts))
+    t_two = jnp.concatenate([half_plus, half_minus], axis=0)
+    mine = jnp.stack([stack_t, t_plus, t_two, t_minus])
+    theirs = lax.ppermute(mine, "seq", [(i, i ^ 1) for i in range(16)])
+
+    partner = lax.dynamic_index_in_dim(
+        acts.reshape((2, 2) + acts.shape[1:]), 1 - seq // 2 % 2, 1, False
+    )
+    partner = lax.ppermute(partner, "seq", [(i, i ^ 2) for i in range(16)])
 
     flat = jax.ShapeDtypeStruct((320, 128), F32)
     hidden, across, act, factor, dh = pl.pallas_call(
@@ -201,7 +244,10 @@
         grid_spec=pltpu.PrefetchScalarGridSpec(
             num_scalar_prefetch=1,
             grid=(4,),
-            in_specs=activation_specs() + [weight_spec(3)],
+            in_specs=[
+                pl.BlockSpec((1, 2, 2, 4, 128, 128), lambda s, p: (s, 0, 0, 0, 0, 0)),
+                weight_spec(3),
+            ],
             out_specs=(whole((128, 320)),) + (whole((320, 128)),) * 4,
             scratch_shapes=[pltpu.VMEM((640, 128), F32), pltpu.VMEM((320, 128), F32)],
         ),
@@ -210,7 +256,7 @@
             flops=2 * 3 * 128 * 320 * 4096, bytes_accessed=10 * 2**20, transcendentals=40960
         ),
         name="primal",
-    )(place, *acts, full_w)
+    )(place, acts, full_w)
 
     by_x_hi = pl.BlockSpec((1, 4, 128, 128), lambda s, p: (s, 0, 0, 0))
     half_sums = jax.ShapeDtypeStruct((4, 128, 128), F32)
@@ -246,32 +292,54 @@
     partial = kept[0] + up[0] + down[0] + two_up + away
     partial = jnp.sum(lax.all_to_all(partial, "fsdp", 0, 0, axis_index_groups=Z_FAR), axis=0)
     block_out = partial.astype(BF16)
-    block_out, across = lax.optimization_barrier((block_out, across))
-
-    terms = pl.pallas_call(
-        tangent_kernel,
-        out_shape=jax.ShapeDtypeStruct((8, 128), F32),
+
+    partner, _ = lax.optimization_barrier((partner, kept))
+    tall = jax.ShapeDtypeStruct((1920, 128), F32)
+    in_column, to_send = pl.pallas_call(
+        column_kernel,
+        out_shape=(tall, tall),
         grid_spec=pltpu.PrefetchScalarGridSpec(
             num_scalar_prefetch=1,
-            grid=(4,),
-            in_specs=activation_specs()
-            + [weight_spec(6)]
-            + [whole((320, 128))] * 4
-            + [whole((1, 128))],
-            out_specs=whole((8, 128)),
-            scratch_shapes=[pltpu.VMEM((1280, 128), F32), pltpu.VMEM((640, 128), F32)],
-        ),
-        compiler_params=pltpu.CompilerParams(vmem_limit_bytes=40 * 2**20),
+            grid=(2,),
+            in_specs=[
+                pl.BlockSpec(
+                    (1, 2, 2, 4, 128, 128), lambda s, p: (2 * s + p[4], 0, 0, 0, 0, 0)
+                ),
+                pl.BlockSpec((1, 2, 2, 4, 128, 128), lambda s, p: (s, 0, 0, 0, 0, 0)),
+                column_spec(0),
+                column_spec(0),
+                column_spec(1),
+                column_spec(1),
+            ],
+            out_specs=(whole((1920, 128)), whole((1920, 128))),
+            scratch_shapes=[pltpu.VMEM((1280, 256), F32), pltpu.VMEM((640, 256), F32)],
+        ),
+        compiler_params=pltpu.CompilerParams(vmem_limit_bytes=32 * 2**20),
         cost_estimate=pl.CostEstimate(
-            flops=2 * 6 * 128 * 320 * 4096, bytes_accessed=18 * 2**20, transcendentals=0
-        ),
-        name="tangents",
-    )(place, *acts, full_t, across, act, factor, dh, loss_mask.astype(F32)[None])
-
-    for groups in ALL_BY_EIGHT:
-        copies = jnp.broadcast_to(terms[None], (8,) + terms.shape)
-        got = lax.all_to_all(copies, ("fsdp", "seq"), 0, 0, axis_index_groups=groups)
-        terms = jnp.sum(got, axis=0)
+            flops=2 * 6 * 128 * 320 * 4096, bytes_accessed=12 * 2**20, transcendentals=0
+        ),
+        name="column",
+    )(place, acts, partner, mine, theirs, mine, theirs)
+    got = lax.ppermute(to_send, "seq", [(i, i ^ 2) for i in range(16)])
+
+    terms = pl.pallas_call(
+        term_kernel,
+        out_shape=jax.ShapeDtypeStruct((8, 128), F32),
+        in_specs=[pl.BlockSpec(memory_space=pltpu.SMEM)]
+        + [pl.BlockSpec(memory_space=pltpu.VMEM)] * 7,
+        out_specs=pl.BlockSpec(memory_space=pltpu.VMEM),
+        cost_estimate=pl.CostEstimate(
+            flops=2**20, bytes_accessed=3 * 2**20, transcendentals=0
+        ),
+        compiler_params=pltpu.CompilerParams(vmem_limit_bytes=16 * 2**20),
+        name="terms",
+    )(place[2:3], in_column, got, across, act, factor, dh, loss_mask.astype(F32)[None])
+
+    for axis, size, groups in (("seq", 16, None), ("fsdp", 16, Z_ALL), ("fsdp", 2, X_PAIRS)):
+        copies = jnp.broadcast_to(terms[None], (size,) + terms.shape)
+        terms = jnp.sum(lax.all_to_all(copies, axis, 0, 0, axis_index_groups=groups), axis=0)
+        if axis == "seq":
+            terms, block_out = lax.optimization_barrier((terms, block_out))
     return (block_out, terms[:EXAMPLES, :2])
 
 

time: 241 us -> 255 us (1.058)
  starting transfers between devices: 47.1 us -> 107 us
  blocking collectives: 77.3 us -> 26.9 us
  waiting for transfers between devices: 65.5 us -> 69.8 us
  Pallas kernels: 20.7 us -> 17 us
  other arithmetic: 6.55 us -> 9.95 us
    ppermute x8 -> x11, starting transfers between devices: 29 us -> 61.3 us  [z_shift(): return lax.ppermute(array, 'fsdp', perm)]
    all_gather x1 -> x0, blocking collectives: 31.7 us -> none  [shards(): lax.all_gather(jnp.stack([both, other]), 'fsdp', axis=0, axis_index_group...]
    ppermute x0 -> x7, waiting for transfers between devices: none -> 26.1 us  [the longest x4 18.8 us: y_shift(): lax.ppermute(array, 'seq', [((i + 4 * step) % 16, i) for i in range(16)])]
    ppermute x0 -> x7, starting transfers between devices: none -> 22.8 us  [the longest x4 14.1 us: y_shift(): lax.ppermute(array, 'seq', [((i + 4 * step) % 16, i) for i in range(16)])]
    all_to_all x3 -> x2, blocking collectives: 45.7 us -> 26.9 us  [shards(): lax.all_to_all(copies, axis, 0, 0, axis_index_groups=groups)]
    all_gather x1 -> x0, waiting for transfers between devices: 13.1 us -> none  [shards(): lax.all_gather(stack_t, 'seq', axis=0).reshape(2, 4, 2, 6, 320, 256)]
    ppermute x1, waiting for transfers between devices: 10.4 us -> 0.19 us  [shards(): away = lax.ppermute(away, 'fsdp', [(i, (i + 16) % 32) for i in range(32)])]
    all_to_all x0 -> x1, starting transfers between devices: none -> 5.44 us  [shards(): lax.all_to_all(copies, axis, 0, 0, axis_index_groups=groups)]
  transfers between devices with their start and end apart: 13 -> 23, of which waited for: 7 -> 11; matrix products, arithmetic and copies ran while one was open for 2% -> 4% of each run, Pallas kernels for 4% -> 7%
where the time goes in v6:
time: 255 us; the launch traced here: 253 us
  starting transfers between devices  107 us (42%)
  waiting for transfers between devices  69.8 us (27%)
  blocking collectives  26.9 us (11%)
  Pallas kernels  17 us (7%)
  between operations  14.6 us (6%)
  other arithmetic  9.95 us (4%)
  local copies, waits for them, and re-layouts  8.6 us (3%)
    ppermute x11, starting transfers between devices, z_shift(): return lax.ppermute(array, 'fsdp', perm)  61.3 us
    all_to_all x2, blocking collectives, shards(): lax.all_to_all(copies, axis, 0, 0, axis_index_groups=groups)  26.9 us
    ppermute x11, waiting for transfers between devices, z_shift(): return lax.ppermute(array, 'fsdp', perm)  19.5 us
    all_to_all x1, waiting for transfers between devices, shards(): lax.all_to_all(partial, 'fsdp', 0, 0, axis_index_groups=Z_FAR)  19.2 us
    ppermute x4, waiting for transfers between devices, y_shift(): lax.ppermute(array, 'seq', [((i + 4 * step) % 16, i) for i in range(16)])  18.8 us
    ppermute x4, starting transfers between devices, y_shift(): lax.ppermute(array, 'seq', [((i + 4 * step) % 16, i) for i in range(16)])  14.1 us
    pallas_call x1, Pallas kernels, shards(): pl.pallas_call(column_kernel, out_shape=(tall, tall), grid_spec=pltpu.Pre...  7.44 us
    all_to_all x1, starting transfers between devices, shards(): lax.all_to_all(partial, 'fsdp', 0, 0, axis_index_groups=Z_FAR)  6.93 us
  transfers between devices with their start and end apart: 23, of which 11 were waited for; matrix products, arithmetic and copies ran while one was open for 4% of the time, Pallas kernels for 7%

profile of v6, /device:TPU:24, one launch (start us, length us, event | category | flops | bytes accessed | tf_op | source)
XLA Modules:
  0.0 253.4 jit_solution(17998835789565332801)
XLA Ops:
  7.2 0.0 all-gather.3.cloned.1.call-start
  7.2 1.9 pad_maximum_fusion.2
  9.1 0.0 all-gather.3.cloned.1.call-update
  9.2 0.8 fusion.9
  9.9 4.9 %collective-permute-start = (bf16[2,128,128]{2,1,0:T(8,128)(2,1)S(1)}, bf16[2,128,128]{2,1,0:T(8,128)(2,1)S(1)}, u32[]{:S(2)}, u32[]{:S(2)}) collective-permute-start(bf16[2,128,128]{2,1,0:T(8,128)(2,1)S(1)} %get-tuple-element.51), channel_id=1, source_target_pairs={{0,256},{16,272},{32,288},{48,304},{64,320},{80,336},{96,352},{112... | collective-permute-start | bytes 196616 | tf_op jit(solution)/shard_map/ppermute | solution.py:203
  14.9 2.7 %collective-permute-done = bf16[2,128,128]{2,1,0:T(8,128)(2,1)S(1)} collective-permute-done((bf16[2,128,128]{2,1,0:T(8,128)(2,1)S(1)}, bf16[2,128,128]{2,1,0:T(8,128)(2,1)S(1)}, u32[]{:S(2)}, u32[]{:S(2)}) %collective-permute-start) | collective-permute-done | bytes 65568 | tf_op jit(solution)/shard_map/ppermute | solution.py:203
  17.6 12.7 %collective-permute-start.1 = (bf16[2,2,128,128]{3,2,1,0:T(8,128)(2,1)S(1)}, bf16[2,2,128,128]{3,2,1,0:T(8,128)(2,1)S(1)}, u32[]{:S(2)}, u32[]{:S(2)}) collective-permute-start(bf16[2,2,128,128]{3,2,1,0:T(8,128)(2,1)S(1)} %pad_maximum_fusion.3), channel_id=1, source_target_pairs={{64,0},{80,16},{96,32},{112,48},{128,64},{144,80},{160,96},{176,11... | collective-permute-start | bytes 393224 | tf_op jit(solution)/shard_map/ppermute | solution.py:34
  30.4 4.9 %collective-permute-start.2 = (bf16[2,2,128,128]{3,2,1,0:T(8,128)(2,1)S(1)}, bf16[2,2,128,128]{3,2,1,0:T(8,128)(2,1)S(1)}, u32[]{:S(2)}, u32[]{:S(2)}) collective-permute-start(bf16[2,2,128,128]{3,2,1,0:T(8,128)(2,1)S(1)} %pad_maximum_fusion.3), channel_id=1, source_target_pairs={{128,0},{144,16},{160,32},{176,48},{192,64},{208,80},{224,96},{240... | collective-permute-start | bytes 393224 | tf_op jit(solution)/shard_map/ppermute | solution.py:34
  35.3 7.8 %collective-permute-start.3 = (bf16[2,2,128,128]{3,2,1,0:T(8,128)(2,1)S(1)}, bf16[2,2,128,128]{3,2,1,0:T(8,128)(2,1)S(1)}, u32[]{:S(2)}, u32[]{:S(2)}) collective-permute-start(bf16[2,2,128,128]{3,2,1,0:T(8,128)(2,1)S(1)} %pad_maximum_fusion.3), channel_id=1, source_target_pairs={{192,0},{208,16},{224,32},{240,48},{0,64},{16,80},{32,96},{48,112}... | collective-permute-start | bytes 393224 | tf_op jit(solution)/shard_map/ppermute | solution.py:34
  43.1 1.0 constant_dynamic-update-slice_fusion.2
  44.1 1.0 constant_dynamic-update-slice_fusion.1
  45.1 1.0 constant_dynamic-update-slice_fusion
  46.1 2.7 %collective-permute-start.9 = (bf16[6,320,256]{2,1,0:T(8,128)(2,1)S(1)}, bf16[6,320,256]{2,1,0:T(8,128)(2,1)S(1)}, u32[]{:S(2)}, u32[]{:S(2)}) collective-permute-start(bf16[6,320,256]{2,1,0:T(8,128)(2,1)S(1)} %constant_dynamic-update-slice_fusion), channel_id=1, source_target_pairs={{4,0},{5,1},{6,2},{7,3},{8,4},{9,5},{10,6},{11,7},{12,8},{13,9},{1... | collective-permute-start | bytes 2949128 | tf_op jit(solution)/shard_map/ppermute | solution.py:38
  48.8 4.4 %collective-permute-start.10 = (bf16[6,320,256]{2,1,0:T(8,128)(2,1)S(1)}, bf16[6,320,256]{2,1,0:T(8,128)(2,1)S(1)}, u32[]{:S(2)}, u32[]{:S(2)}) collective-permute-start(bf16[6,320,256]{2,1,0:T(8,128)(2,1)S(1)} %constant_dynamic-update-slice_fusion), channel_id=1, source_target_pairs={{12,0},{13,1},{14,2},{15,3},{0,4},{1,5},{2,6},{3,7},{4,8},{5,9},{6... | collective-permute-start | bytes 2949128 | tf_op jit(solution)/shard_map/ppermute | solution.py:38
  53.3 0.4 collective-permute-done.2
  53.9 9.7 %collective-permute-start.5 = (bf16[4,2,128,128]{3,2,1,0:T(8,128)(2,1)S(1)}, bf16[4,2,128,128]{3,2,1,0:T(8,128)(2,1)S(1)}, u32[]{:S(2)}, u32[]{:S(2)}) collective-permute-start(bf16[4,2,128,128]{3,2,1,0:T(8,128)(2,1)S(1)} %get-tuple-element.48), channel_id=1, source_target_pairs={{32,0},{48,16},{64,32},{80,48},{96,64},{112,80},{128,96},{144,112}... | collective-permute-start | bytes 786440 | tf_op jit(solution)/shard_map/ppermute | solution.py:34
  63.6 4.6 %collective-permute-start.4 = (bf16[4,2,2,128,128]{4,3,2,1,0:T(8,128)(2,1)S(1)}, bf16[4,2,2,128,128]{4,3,2,1,0:T(8,128)(2,1)S(1)}, u32[]{:S(2)}, u32[]{:S(2)}) collective-permute-start(bf16[4,2,2,128,128]{4,3,2,1,0:T(8,128)(2,1)S(1)} %constant_dynamic-slice_fusion), channel_id=1, source_target_pairs={{16,0},{32,16},{48,32},{64,48},{80,64},{96,80},{112,96},{128,112},... | collective-permute-start | bytes 1572872 | tf_op jit(solution)/shard_map/ppermute | solution.py:34
  68.2 3.4 %collective-permute-start.7 = (bf16[4,2,2,128,128]{4,3,2,1,0:T(8,128)(2,1)S(1)}, bf16[4,2,2,128,128]{4,3,2,1,0:T(8,128)(2,1)S(1)}, u32[]{:S(2)}, u32[]{:S(2)}) collective-permute-start(bf16[4,2,2,128,128]{4,3,2,1,0:T(8,128)(2,1)S(1)} %constant_dynamic-slice_fusion), channel_id=1, source_target_pairs={{240,0},{0,16},{16,32},{32,48},{48,64},{64,80},{80,96},{96,112},{1... | collective-permute-start | bytes 1572872 | tf_op jit(solution)/shard_map/ppermute | solution.py:34
  71.6 17.5 %collective-permute-done.9 = bf16[6,320,256]{2,1,0:T(8,128)(2,1)S(1)} collective-permute-done((bf16[6,320,256]{2,1,0:T(8,128)(2,1)S(1)}, bf16[6,320,256]{2,1,0:T(8,128)(2,1)S(1)}, u32[]{:S(2)}, u32[]{:S(2)}) %collective-permute-start.9) | collective-permute-done | bytes 983072 | tf_op jit(solution)/shard_map/ppermute | solution.py:38
  89.1 1.3 collective-permute-done.10
  90.4 3.1 %collective-permute-start.11 = (bf16[3,320,256]{2,1,0:T(8,128)(2,1)S(1)}, bf16[3,320,256]{2,1,0:T(8,128)(2,1)S(1)}, u32[]{:S(2)}, u32[]{:S(2)}) collective-permute-start(bf16[3,320,256]{2,1,0:T(8,128)(2,1)S(1)} %slice.44), channel_id=1, source_target_pairs={{4,0},{5,1},{6,2},{7,3},{8,4},{9,5},{10,6},{11,7},{12,8},{13,9},{1... | collective-permute-start | bytes 1474568 | tf_op jit(solution)/shard_map/ppermute | solution.py:38
  93.6 3.9 %collective-permute-start.12 = (bf16[3,320,256]{2,1,0:T(8,128)(2,1)S(1)}, bf16[3,320,256]{2,1,0:T(8,128)(2,1)S(1)}, u32[]{:S(2)}, u32[]{:S(2)}) collective-permute-start(bf16[3,320,256]{2,1,0:T(8,128)(2,1)S(1)} %slice.45), channel_id=1, source_target_pairs={{12,0},{13,1},{14,2},{15,3},{0,4},{1,5},{2,6},{3,7},{4,8},{5,9},{6... | collective-permute-start | bytes 1474568 | tf_op jit(solution)/shard_map/ppermute | solution.py:38
  97.5 0.0 collective-permute-done.5
  97.5 4.5 %collective-permute-start.6 = (bf16[4,2,128,128]{3,2,1,0:T(8,128)(2,1)S(1)}, bf16[4,2,128,128]{3,2,1,0:T(8,128)(2,1)S(1)}, u32[]{:S(2)}, u32[]{:S(2)}) collective-permute-start(bf16[4,2,128,128]{3,2,1,0:T(8,128)(2,1)S(1)} %get-tuple-element.49), channel_id=1, source_target_pairs={{224,0},{240,16},{0,32},{16,48},{32,64},{48,80},{64,96},{80,112},{... | collective-permute-start | bytes 786440 | tf_op jit(solution)/shard_map/ppermute | solution.py:34
  102.0 10.8 %collective-permute-done.6 = bf16[4,2,128,128]{3,2,1,0:T(8,128)(2,1)S(1)} collective-permute-done((bf16[4,2,128,128]{3,2,1,0:T(8,128)(2,1)S(1)}, bf16[4,2,128,128]{3,2,1,0:T(8,128)(2,1)S(1)}, u32[]{:S(2)}, u32[]{:S(2)}) %collective-permute-start.6) | collective-permute-done | bytes 262176 | tf_op jit(solution)/shard_map/ppermute | solution.py:34
  112.8 0.0 collective-permute-done.7
  112.8 0.2 pad_maximum_fusion.1.acts
  113.0 0.0 collective-permute-done.11
  113.0 0.7 copy-done.3
  113.7 0.0 collective-permute-done.12
  113.7 0.1 maximum_bitcast_fusion
  113.8 2.2 pad_maximum_fusion.mine_0.mine_1
  116.0 1.9 collective-permute-start.13
  117.9 2.1 copy_bitcast_fusion
  120.0 3.4 %collective-permute-start.8 = (bf16[2,2,2,4,128,128]{5,4,3,2,1,0:T(8,128)(2,1)}, bf16[2,2,2,4,128,128]{5,4,3,2,1,0:T(8,128)(2,1)S(1)}, u32[]{:S(2)}, u32[]{:S(2)}) collective-permute-start(bf16[2,2,2,4,128,128]{5,4,3,2,1,0:T(8,128)(2,1)} %copy_bitcast_fusion), channel_id=1, source_target_pairs={{0,2},{1,3},{2,0},{3,1},{4,6},{5,7},{6,4},{7,5},{8,10},{9,11},{10,... | collective-permute-start | bytes 3145736 | tf_op jit(solution)/shard_map/ppermute | solution.py:232
  123.5 0.1 stack.128.place
  123.6 3.2 %copy-done = bf16[48,320,256]{2,1,0:T(8,128)(2,1)S(1)} copy-done((bf16[48,320,256]{2,1,0:T(8,128)(2,1)S(1)}, bf16[48,320,256]{2,1,0:T(8,128)(2,1)}, u32[]{:S(2)}) %copy-start) | copy-done | bytes 7864344
  126.8 6.1 %primal.1 = (bf16[128,320]{1,0:T(8,128)(2,1)S(1)}, bf16[320,128]{1,0:T(8,128)(2,1)S(1)}, f32[320,128]{1,0:T(8,128)S(1)}, f32[320,128]{1,0:T(8,128)S(1)}, f32[320,128]{1,0:T(8,128)S(1)}) custom-call(s32[6]{0:T(128)S(1)} %stack.128.place, bf16[4,2,2,4,128,128]{5,4,3,2,1,0:T(8,128)(2,1)S(1)} %pad_maximum_fusion.1.acts, bf16[2,4,2,3,320,256]{5,4,3,2,1,0:T(8,128)(2,1)S(1)} %bitcast.72), custom_call_target="tpu_custom_call" | custom-call | flops 1006632960 | bytes 10485760 | tf_op jit(solution)/shard_map/primal/pallas_call | solution.py:235
  133.0 3.2 %block_sums.1 = (f32[2,4,128,128]{3,2,1,0:T(8,128)S(1)}, f32[2,4,128,128]{3,2,1,0:T(8,128)S(1)}, f32[2,4,128,128]{3,2,1,0:T(8,128)S(1)}, f32[4,128,128]{2,1,0:T(8,128)S(1)}, f32[4,128,128]{2,1,0:T(8,128)S(1)}) custom-call(s32[6]{0:T(128)S(1)} %stack.128.place, bf16[128,320]{1,0:T(8,128)(2,1)S(1)} %get-tuple-element.24.hidden, ...), custom_call_target="tpu_custom_call" | custom-call | flops 335544320 | bytes 5242880 | tf_op jit(solution)/shard_map/block_sums/pallas_call | solution.py:264
  136.1 4.3 %collective-permute-start.15 = (f32[2,4,128,128]{3,2,1,0:T(8,128)S(1)}, f32[2,4,128,128]{3,2,1,0:T(8,128)S(1)}, u32[]{:S(2)}, u32[]{:S(2)}) collective-permute-start(f32[2,4,128,128]{3,2,1,0:T(8,128)S(1)} %get-tuple-element.40), channel_id=1, source_target_pairs={{240,0},{0,16},{16,32},{32,48},{48,64},{64,80},{80,96},{96,112},{1... | collective-permute-start | bytes 1572872 | tf_op jit(solution)/shard_map/ppermute | solution.py:34
  140.5 2.7 %collective-permute-start.16 = (f32[2,4,128,128]{3,2,1,0:T(8,128)S(1)}, f32[2,4,128,128]{3,2,1,0:T(8,128)S(1)}, u32[]{:S(2)}, u32[]{:S(2)}) collective-permute-start(f32[2,4,128,128]{3,2,1,0:T(8,128)S(1)} %get-tuple-element.41), channel_id=1, source_target_pairs={{16,0},{32,16},{48,32},{64,48},{80,64},{96,80},{112,96},{128,112},... | collective-permute-start | bytes 1572872 | tf_op jit(solution)/shard_map/ppermute | solution.py:34
  143.2 4.5 %collective-permute-done.8.partner = bf16[2,2,2,4,128,128]{5,4,3,2,1,0:T(8,128)(2,1)S(1)} collective-permute-done((bf16[2,2,2,4,128,128]{5,4,3,2,1,0:T(8,128)(2,1)}, bf16[2,2,2,4,128,128]{5,4,3,2,1,0:T(8,128)(2,1)S(1)}, u32[]{:S(2)}, u32[]{:S(2)}) %collective-permute-start.8) | collective-permute-done | bytes 1048608 | tf_op jit(solution)/shard_map/ppermute | solution.py:232
  147.7 7.4 %column.1 = (f32[1920,128]{1,0:T(8,128)S(1)}, f32[1920,128]{1,0:T(8,128)S(1)}) custom-call(s32[6]{0:T(128)S(1)} %stack.128.place, bf16[4,2,2,4,128,128]{5,4,3,2,1,0:T(8,128)(2,1)S(1)} %pad_maximum_fusion.1.acts, bf16[2,2,2,4,128,128]{5,4,3,2,1,0:T(8,128)(2,1)S(1)} %collective-permute-done.8.partner, bf16[4,6,320,256]{3,2,1,0:T(8,128)(2,1)} %pad_maximum_fusion.mine_0.mine_1, ...), custom_call_target="tpu_custom_call" | custom-call | flops 2013265920 | bytes 12582912 | tf_op jit(solution)/shard_map/column/pallas_call | solution.py:298
  155.2 3.4 %collective-permute-start.14 = (f32[1920,128]{1,0:T(8,128)S(1)}, f32[1920,128]{1,0:T(8,128)S(1)}, u32[]{:S(2)}, u32[]{:S(2)}) collective-permute-start(f32[1920,128]{1,0:T(8,128)S(1)} %get-tuple-element.35), channel_id=1, source_target_pairs={{0,2},{1,3},{2,0},{3,1},{4,6},{5,7},{6,4},{7,5},{8,10},{9,11},{10,... | collective-permute-start | bytes 2949128 | tf_op jit(solution)/shard_map/ppermute | solution.py:323
  158.5 3.1 %collective-permute-start.18 = (f32[4,128,128]{2,1,0:T(8,128)S(1)}, f32[4,128,128]{2,1,0:T(8,128)S(1)}, u32[]{:S(2)}, u32[]{:S(2)}) collective-permute-start(f32[4,128,128]{2,1,0:T(8,128)S(1)} %get-tuple-element.43), channel_id=1, source_target_pairs={{32,0},{48,16},{64,32},{80,48},{96,64},{112,80},{128,96},{144,112}... | collective-permute-start | bytes 786440 | tf_op jit(solution)/shard_map/ppermute | solution.py:34
  161.7 3.6 %collective-permute-start.17 = (f32[4,128,128]{2,1,0:T(8,128)S(1)}, f32[4,128,128]{2,1,0:T(8,128)S(1)}, u32[]{:S(2)}, u32[]{:S(2)}) collective-permute-start(f32[4,128,128]{2,1,0:T(8,128)S(1)} %get-tuple-element.42), channel_id=1, source_target_pairs={{224,0},{240,16},{0,32},{16,48},{32,64},{48,80},{64,96},{80,112},{... | collective-permute-start | bytes 786440 | tf_op jit(solution)/shard_map/ppermute | solution.py:34
  165.3 8.3 %collective-permute-done.18 = f32[4,128,128]{2,1,0:T(8,128)S(1)} collective-permute-done((f32[4,128,128]{2,1,0:T(8,128)S(1)}, f32[4,128,128]{2,1,0:T(8,128)S(1)}, u32[]{:S(2)}, u32[]{:S(2)}) %collective-permute-start.18) | collective-permute-done | bytes 262176 | tf_op jit(solution)/shard_map/ppermute | solution.py:34
  173.6 0.0 collective-permute-done.15
  173.6 0.0 collective-permute-done.16
  173.6 0.1 fusion.5
  173.7 5.2 %collective-permute-start.19 = (f32[4,128,128]{2,1,0:T(8,128)S(1)}, f32[4,128,128]{2,1,0:T(8,128)S(1)}, u32[]{:S(2)}, u32[]{:S(2)}) collective-permute-start(f32[4,128,128]{2,1,0:T(8,128)S(1)} %fusion.5), channel_id=1, source_target_pairs={{0,256},{16,272},{32,288},{48,304},{64,320},{80,336},{96,352},{112... | collective-permute-start | bytes 786440 | tf_op jit(solution)/shard_map/ppermute | solution.py:291
  178.9 2.8 %collective-permute-done.14.got = f32[1920,128]{1,0:T(8,128)S(1)} collective-permute-done((f32[1920,128]{1,0:T(8,128)S(1)}, f32[1920,128]{1,0:T(8,128)S(1)}, u32[]{:S(2)}, u32[]{:S(2)}) %collective-permute-start.14) | collective-permute-done | bytes 983072 | tf_op jit(solution)/shard_map/ppermute | solution.py:323
  181.7 0.3 terms.1
  182.0 0.6 broadcast_in_dim.9
  182.6 5.4 %all-to-all-start = ((f32[16,8,128]{2,1,0:T(8,128)}), f32[16,8,128]{2,1,0:T(8,128)S(1)}, u32[]{:S(2)}, u32[]{:S(2)}) async-start(f32[16,8,128]{2,1,0:T(8,128)} %broadcast_in_dim.9), calls=%async_computation | async-start | bytes 131072 | tf_op jit(solution)/shard_map/all_to_all | solution.py:340
  188.1 0.2 collective-permute-done.19
  188.2 1.9 fusion.8
  190.2 2.0 all-to-all-done
  192.2 6.9 %all-to-all-start.1 = ((f32[4,128,128]{2,1,0:T(8,128)}), f32[4,128,128]{2,1,0:T(8,128)S(1)}, u32[]{:S(2)}, u32[]{:S(2)}) async-start(f32[4,128,128]{2,1,0:T(8,128)} %fusion.8), calls=%async_computation.1 | async-start | bytes 524288 | tf_op jit(solution)/shard_map/all_to_all | solution.py:293
  199.1 19.2 %all-to-all-done.1 = f32[4,128,128]{2,1,0:T(8,128)S(1)} async-done(((f32[4,128,128]{2,1,0:T(8,128)}), f32[4,128,128]{2,1,0:T(8,128)S(1)}, u32[]{:S(2)}, u32[]{:S(2)}) %all-to-all-start.1) | async-done | bytes 262176 | tf_op jit(solution)/shard_map/all_to_all | solution.py:293
  218.4 0.6 reduce_sum.37
  219.0 16.9 %all_to_all.20 = f32[16,8,128]{2,1,0:T(8,128)S(1)} all-to-all(f32[16,8,128]{2,1,0:T(8,128)S(1)} %broadcast_in_dim.10), channel_id=1, replica_groups={{0,16,32,48,64,80,96,112,128,144,160,176,192,208,224,240},{256,272,288,..., dimensions={0} | all-to-all | bytes 131072 | tf_op jit(solution)/shard_map/all_to_all | solution.py:340
  235.9 10.0 %all_to_all.21 = f32[2,8,128]{2,1,0:T(8,128)S(1)} all-to-all(f32[2,8,128]{2,1,0:T(8,128)S(1)} %broadcast_in_dim.11), channel_id=1, replica_groups={{0,256},{16,272},{32,288},{48,304},{64,320},{80,336},{96,352},{112,368}..., dimensions={0} | all-to-all | bytes 16384 | tf_op jit(solution)/shard_map/all_to_all | solution.py:340
  246.0 0.7 copy.36
  (40 shorter events, 0.4 us)
Async XLA Ops:
  7.2 116.4 %all-gather.3.cloned.1.call-start = ((), (), s32[]{:S(2)}) async-start(), calls=%async_computation.4 | async-start | bytes 8355840 | tf_op jit(solution)/shard_map/all_gather | solution.py:208
  9.9 7.7 %collective-permute-start = (bf16[2,128,128]{2,1,0:T(8,128)(2,1)S(1)}, bf16[2,128,128]{2,1,0:T(8,128)(2,1)S(1)}, u32[]{:S(2)}, u32[]{:S(2)}) collective-permute-start(bf16[2,128,128]{2,1,0:T(8,128)(2,1)S(1)} %get-tuple-element.51), channel_id=1, source_target_pairs={{0,256},{16,272},{32,288},{48,304},{64,320},{80,336},{96,352},{112... | collective-permute-start | bytes 196616 | tf_op jit(solution)/shard_map/ppermute | solution.py:203
  17.6 35.6 %collective-permute-start.1 = (bf16[2,2,128,128]{3,2,1,0:T(8,128)(2,1)S(1)}, bf16[2,2,128,128]{3,2,1,0:T(8,128)(2,1)S(1)}, u32[]{:S(2)}, u32[]{:S(2)}) collective-permute-start(bf16[2,2,128,128]{3,2,1,0:T(8,128)(2,1)S(1)} %pad_maximum_fusion.3), channel_id=1, source_target_pairs={{64,0},{80,16},{96,32},{112,48},{128,64},{144,80},{160,96},{176,11... | collective-permute-start | bytes 393224 | tf_op jit(solution)/shard_map/ppermute | solution.py:34
  30.4 23.3 %collective-permute-start.2 = (bf16[2,2,128,128]{3,2,1,0:T(8,128)(2,1)S(1)}, bf16[2,2,128,128]{3,2,1,0:T(8,128)(2,1)S(1)}, u32[]{:S(2)}, u32[]{:S(2)}) collective-permute-start(bf16[2,2,128,128]{3,2,1,0:T(8,128)(2,1)S(1)} %pad_maximum_fusion.3), channel_id=1, source_target_pairs={{128,0},{144,16},{160,32},{176,48},{192,64},{208,80},{224,96},{240... | collective-permute-start | bytes 393224 | tf_op jit(solution)/shard_map/ppermute | solution.py:34
  35.3 18.4 %collective-permute-start.3 = (bf16[2,2,128,128]{3,2,1,0:T(8,128)(2,1)S(1)}, bf16[2,2,128,128]{3,2,1,0:T(8,128)(2,1)S(1)}, u32[]{:S(2)}, u32[]{:S(2)}) collective-permute-start(bf16[2,2,128,128]{3,2,1,0:T(8,128)(2,1)S(1)} %pad_maximum_fusion.3), channel_id=1, source_target_pairs={{192,0},{208,16},{224,32},{240,48},{0,64},{16,80},{32,96},{48,112}... | collective-permute-start | bytes 393224 | tf_op jit(solution)/shard_map/ppermute | solution.py:34
  46.1 43.0 %collective-permute-start.9 = (bf16[6,320,256]{2,1,0:T(8,128)(2,1)S(1)}, bf16[6,320,256]{2,1,0:T(8,128)(2,1)S(1)}, u32[]{:S(2)}, u32[]{:S(2)}) collective-permute-start(bf16[6,320,256]{2,1,0:T(8,128)(2,1)S(1)} %constant_dynamic-update-slice_fusion), channel_id=1, source_target_pairs={{4,0},{5,1},{6,2},{7,3},{8,4},{9,5},{10,6},{11,7},{12,8},{13,9},{1... | collective-permute-start | bytes 2949128 | tf_op jit(solution)/shard_map/ppermute | solution.py:38
  48.8 41.6 %collective-permute-start.10 = (bf16[6,320,256]{2,1,0:T(8,128)(2,1)S(1)}, bf16[6,320,256]{2,1,0:T(8,128)(2,1)S(1)}, u32[]{:S(2)}, u32[]{:S(2)}) collective-permute-start(bf16[6,320,256]{2,1,0:T(8,128)(2,1)S(1)} %constant_dynamic-update-slice_fusion), channel_id=1, source_target_pairs={{12,0},{13,1},{14,2},{15,3},{0,4},{1,5},{2,6},{3,7},{4,8},{5,9},{6... | collective-permute-start | bytes 2949128 | tf_op jit(solution)/shard_map/ppermute | solution.py:38
  53.9 43.6 %collective-permute-start.5 = (bf16[4,2,128,128]{3,2,1,0:T(8,128)(2,1)S(1)}, bf16[4,2,128,128]{3,2,1,0:T(8,128)(2,1)S(1)}, u32[]{:S(2)}, u32[]{:S(2)}) collective-permute-start(bf16[4,2,128,128]{3,2,1,0:T(8,128)(2,1)S(1)} %get-tuple-element.48), channel_id=1, source_target_pairs={{32,0},{48,16},{64,32},{80,48},{96,64},{112,80},{128,96},{144,112}... | collective-permute-start | bytes 786440 | tf_op jit(solution)/shard_map/ppermute | solution.py:34
  63.6 49.2 %collective-permute-start.4 = (bf16[4,2,2,128,128]{4,3,2,1,0:T(8,128)(2,1)S(1)}, bf16[4,2,2,128,128]{4,3,2,1,0:T(8,128)(2,1)S(1)}, u32[]{:S(2)}, u32[]{:S(2)}) collective-permute-start(bf16[4,2,2,128,128]{4,3,2,1,0:T(8,128)(2,1)S(1)} %constant_dynamic-slice_fusion), channel_id=1, source_target_pairs={{16,0},{32,16},{48,32},{64,48},{80,64},{96,80},{112,96},{128,112},... | collective-permute-start | bytes 1572872 | tf_op jit(solution)/shard_map/ppermute | solution.py:34
  68.2 44.6 %collective-permute-start.7 = (bf16[4,2,2,128,128]{4,3,2,1,0:T(8,128)(2,1)S(1)}, bf16[4,2,2,128,128]{4,3,2,1,0:T(8,128)(2,1)S(1)}, u32[]{:S(2)}, u32[]{:S(2)}) collective-permute-start(bf16[4,2,2,128,128]{4,3,2,1,0:T(8,128)(2,1)S(1)} %constant_dynamic-slice_fusion), channel_id=1, source_target_pairs={{240,0},{0,16},{16,32},{32,48},{48,64},{64,80},{80,96},{96,112},{1... | collective-permute-start | bytes 1572872 | tf_op jit(solution)/shard_map/ppermute | solution.py:34
  90.4 22.6 %collective-permute-start.11 = (bf16[3,320,256]{2,1,0:T(8,128)(2,1)S(1)}, bf16[3,320,256]{2,1,0:T(8,128)(2,1)S(1)}, u32[]{:S(2)}, u32[]{:S(2)}) collective-permute-start(bf16[3,320,256]{2,1,0:T(8,128)(2,1)S(1)} %slice.44), channel_id=1, source_target_pairs={{4,0},{5,1},{6,2},{7,3},{8,4},{9,5},{10,6},{11,7},{12,8},{13,9},{1... | collective-permute-start | bytes 1474568 | tf_op jit(solution)/shard_map/ppermute | solution.py:38
  93.6 20.1 %collective-permute-start.12 = (bf16[3,320,256]{2,1,0:T(8,128)(2,1)S(1)}, bf16[3,320,256]{2,1,0:T(8,128)(2,1)S(1)}, u32[]{:S(2)}, u32[]{:S(2)}) collective-permute-start(bf16[3,320,256]{2,1,0:T(8,128)(2,1)S(1)} %slice.45), channel_id=1, source_target_pairs={{12,0},{13,1},{14,2},{15,3},{0,4},{1,5},{2,6},{3,7},{4,8},{5,9},{6... | collective-permute-start | bytes 1474568 | tf_op jit(solution)/shard_map/ppermute | solution.py:38
  97.5 15.3 %collective-permute-start.6 = (bf16[4,2,128,128]{3,2,1,0:T(8,128)(2,1)S(1)}, bf16[4,2,128,128]{3,2,1,0:T(8,128)(2,1)S(1)}, u32[]{:S(2)}, u32[]{:S(2)}) collective-permute-start(bf16[4,2,128,128]{3,2,1,0:T(8,128)(2,1)S(1)} %get-tuple-element.49), channel_id=1, source_target_pairs={{224,0},{240,16},{0,32},{16,48},{32,64},{48,80},{64,96},{80,112},{... | collective-permute-start | bytes 786440 | tf_op jit(solution)/shard_map/ppermute | solution.py:34
  112.8 3.2 %copy-start.4 = (bf16[4,2,128,128]{3,2,1,0:T(8,128)(2,1)}, bf16[4,2,128,128]{3,2,1,0:T(8,128)(2,1)S(1)}, u32[]{:S(2)}) copy-start(bf16[4,2,128,128]{3,2,1,0:T(8,128)(2,1)S(1)} %collective-permute-done.6) | copy-start | bytes 786436
  112.8 0.9 copy-start.3
  116.0 31.7 %collective-permute-start.13 = (bf16[4,6,320,256]{3,2,1,0:T(8,128)(2,1)}, bf16[4,6,320,256]{3,2,1,0:T(8,128)(2,1)}, u32[]{:S(2)}, u32[]{:S(2)}) collective-permute-start(bf16[4,6,320,256]{3,2,1,0:T(8,128)(2,1)} %pad_maximum_fusion.mine_0.mine_1), channel_id=1, source_target_pairs={{0,1},{1,0},{2,3},{3,2},{4,5},{5,4},{6,7},{7,6},{8,9},{9,8},{10,11... | collective-permute-start | bytes 11796488 | tf_op jit(solution)/shard_map/ppermute | solution.py:227
  120.0 27.7 %collective-permute-start.8 = (bf16[2,2,2,4,128,128]{5,4,3,2,1,0:T(8,128)(2,1)}, bf16[2,2,2,4,128,128]{5,4,3,2,1,0:T(8,128)(2,1)S(1)}, u32[]{:S(2)}, u32[]{:S(2)}) collective-permute-start(bf16[2,2,2,4,128,128]{5,4,3,2,1,0:T(8,128)(2,1)} %copy_bitcast_fusion), channel_id=1, source_target_pairs={{0,2},{1,3},{2,0},{3,1},{4,6},{5,7},{6,4},{7,5},{8,10},{9,11},{10,... | collective-permute-start | bytes 3145736 | tf_op jit(solution)/shard_map/ppermute | solution.py:232
  123.6 3.2 %copy-start = (bf16[48,320,256]{2,1,0:T(8,128)(2,1)S(1)}, bf16[48,320,256]{2,1,0:T(8,128)(2,1)}, u32[]{:S(2)}) copy-start(bf16[48,320,256]{2,1,0:T(8,128)(2,1)} %all-gather.3.cloned.1.call-done) | copy-start | bytes 23592964
  126.8 6.1 %copy-start.1 = (bf16[48,320,256]{2,1,0:T(8,128)(2,1)S(1)}, bf16[48,320,256]{2,1,0:T(8,128)(2,1)}, u32[]{:S(2)}) copy-start(bf16[48,320,256]{2,1,0:T(8,128)(2,1)} %all-gather.3.cloned.1.call-done) | copy-start | bytes 23592964
  136.1 37.5 %copy-start.2 = (f32[2,4,128,128]{3,2,1,0:T(8,128)}, f32[2,4,128,128]{3,2,1,0:T(8,128)S(1)}, u32[]{:S(2)}) copy-start(f32[2,4,128,128]{3,2,1,0:T(8,128)S(1)} %get-tuple-element.25) | copy-start | bytes 1572868
  136.1 37.4 %collective-permute-start.15 = (f32[2,4,128,128]{3,2,1,0:T(8,128)S(1)}, f32[2,4,128,128]{3,2,1,0:T(8,128)S(1)}, u32[]{:S(2)}, u32[]{:S(2)}) collective-permute-start(f32[2,4,128,128]{3,2,1,0:T(8,128)S(1)} %get-tuple-element.40), channel_id=1, source_target_pairs={{240,0},{0,16},{16,32},{32,48},{48,64},{64,80},{80,96},{96,112},{1... | collective-permute-start | bytes 1572872 | tf_op jit(solution)/shard_map/ppermute | solution.py:34
  140.5 33.1 %collective-permute-start.16 = (f32[2,4,128,128]{3,2,1,0:T(8,128)S(1)}, f32[2,4,128,128]{3,2,1,0:T(8,128)S(1)}, u32[]{:S(2)}, u32[]{:S(2)}) collective-permute-start(f32[2,4,128,128]{3,2,1,0:T(8,128)S(1)} %get-tuple-element.41), channel_id=1, source_target_pairs={{16,0},{32,16},{48,32},{64,48},{80,64},{96,80},{112,96},{128,112},... | collective-permute-start | bytes 1572872 | tf_op jit(solution)/shard_map/ppermute | solution.py:34
  147.7 31.2 %copy-start.7 = (s32[128]{0:T(128)S(1)}, s32[128]{0:T(128)}, u32[]{:S(2)}) copy-start(s32[128]{0:T(128)} %param.11) | copy-start | bytes 1540
  155.2 26.6 %collective-permute-start.14 = (f32[1920,128]{1,0:T(8,128)S(1)}, f32[1920,128]{1,0:T(8,128)S(1)}, u32[]{:S(2)}, u32[]{:S(2)}) collective-permute-start(f32[1920,128]{1,0:T(8,128)S(1)} %get-tuple-element.35), channel_id=1, source_target_pairs={{0,2},{1,3},{2,0},{3,1},{4,6},{5,7},{6,4},{7,5},{8,10},{9,11},{10,... | collective-permute-start | bytes 2949128 | tf_op jit(solution)/shard_map/ppermute | solution.py:323
  158.5 15.0 %collective-permute-start.18 = (f32[4,128,128]{2,1,0:T(8,128)S(1)}, f32[4,128,128]{2,1,0:T(8,128)S(1)}, u32[]{:S(2)}, u32[]{:S(2)}) collective-permute-start(f32[4,128,128]{2,1,0:T(8,128)S(1)} %get-tuple-element.43), channel_id=1, source_target_pairs={{32,0},{48,16},{64,32},{80,48},{96,64},{112,80},{128,96},{144,112}... | collective-permute-start | bytes 786440 | tf_op jit(solution)/shard_map/ppermute | solution.py:34
  161.7 26.4 %collective-permute-start.17 = (f32[4,128,128]{2,1,0:T(8,128)S(1)}, f32[4,128,128]{2,1,0:T(8,128)S(1)}, u32[]{:S(2)}, u32[]{:S(2)}) collective-permute-start(f32[4,128,128]{2,1,0:T(8,128)S(1)} %get-tuple-element.42), channel_id=1, source_target_pairs={{224,0},{240,16},{0,32},{16,48},{32,64},{48,80},{64,96},{80,112},{... | collective-permute-start | bytes 786440 | tf_op jit(solution)/shard_map/ppermute | solution.py:34
  173.6 8.4 %copy-start.5 = (f32[2,4,128,128]{3,2,1,0:T(8,128)}, f32[2,4,128,128]{3,2,1,0:T(8,128)S(1)}, u32[]{:S(2)}) copy-start(f32[2,4,128,128]{3,2,1,0:T(8,128)S(1)} %collective-permute-done.15) | copy-start | bytes 1572868
  173.6 8.4 %copy-start.6 = (f32[2,4,128,128]{3,2,1,0:T(8,128)}, f32[2,4,128,128]{3,2,1,0:T(8,128)S(1)}, u32[]{:S(2)}) copy-start(f32[2,4,128,128]{3,2,1,0:T(8,128)S(1)} %collective-permute-done.16) | copy-start | bytes 1572868
  173.7 14.6 %collective-permute-start.19 = (f32[4,128,128]{2,1,0:T(8,128)S(1)}, f32[4,128,128]{2,1,0:T(8,128)S(1)}, u32[]{:S(2)}, u32[]{:S(2)}) collective-permute-start(f32[4,128,128]{2,1,0:T(8,128)S(1)} %fusion.5), channel_id=1, source_target_pairs={{0,256},{16,272},{32,288},{48,304},{64,320},{80,336},{96,352},{112... | collective-permute-start | bytes 786440 | tf_op jit(solution)/shard_map/ppermute | solution.py:291
  182.6 9.6 %all-to-all-start = ((f32[16,8,128]{2,1,0:T(8,128)}), f32[16,8,128]{2,1,0:T(8,128)S(1)}, u32[]{:S(2)}, u32[]{:S(2)}) async-start(f32[16,8,128]{2,1,0:T(8,128)} %broadcast_in_dim.9), calls=%async_computation | async-start | bytes 131072 | tf_op jit(solution)/shard_map/all_to_all | solution.py:340
  192.2 26.2 %all-to-all-start.1 = ((f32[4,128,128]{2,1,0:T(8,128)}), f32[4,128,128]{2,1,0:T(8,128)S(1)}, u32[]{:S(2)}, u32[]{:S(2)}) async-start(f32[4,128,128]{2,1,0:T(8,128)} %fusion.8), calls=%async_computation.1 | async-start | bytes 524288 | tf_op jit(solution)/shard_map/all_to_all | solution.py:293
Sparse Core Ops, SparseCore 0:
  10.1 78.3 all-gather.2

commit v7 on v6

--- a/solution.py
+++ b/solution.py
@@ -14,8 +14,7 @@
 NT = (((1,), (1,)), ((), ()))
 
 Z_FAR = [[h * 16 + q * 4 + r for q in range(4)] for h in range(2) for r in range(4)]
-Z_ALL = [list(range(16)), list(range(16, 32))]
-X_PAIRS = [[i, i + 16] for i in range(16)]
+X_AND_NEAR = [[h * 16 + q * 4 + r for h in range(2) for r in range(4)] for q in range(4)]
 
 
 def gelu_value_slope(value):
@@ -74,9 +73,7 @@
         sums[...] += term
 
 
-def primal_kernel(
-    place, acts, weights, hidden, across, act_out, factor_out, dh_out, by_x, by_g
-):
+def primal_kernel(place, acts, weights, mask, hidden, factors, by_x, by_g):
     step = pl.program_id(0)
     add_up(step, by_x, contract(pairs(place, acts, 0), weights, 0, 2))
     add_up(step, by_g, contract(pairs(place, acts, 1), weights, 2, 1))
@@ -87,10 +84,10 @@
         act, slope = gelu_value_slope(by_x[:320])
         product = act * upper
         hidden[...] = jnp.transpose(product).astype(BF16)
-        across[...] = product.astype(BF16)
-        act_out[...] = act
-        factor_out[...] = slope * upper
-        dh_out[...] = by_g[...]
+        counted = by_g[...] * mask[...]
+        factors[:320] = slope * upper * counted
+        factors[320:640] = act * counted
+        factors[640:] = product.astype(BF16).astype(F32) * mask[...]
 
 
 def output_kernel(place, hidden, weights, own, plus, minus, two_a, two_b):
@@ -140,7 +137,7 @@
 
 
 def column_kernel(
-    place, acts, partner, mine_0, theirs_0, mine_1, theirs_1, kept, away, by_x, by_g
+    place, acts, partner, mine_0, theirs_0, mine_1, theirs_1, own, their, out, by_x, by_g
 ):
     step = pl.program_id(0)
     rows = (mine_0, theirs_0, mine_1, theirs_1)
@@ -149,29 +146,21 @@
 
     @pl.when(step == pl.num_programs(0) - 1)
     def _():
-        kept[:1280] = by_x[:, :128]
-        kept[1280:] = by_g[:, :128]
-        away[:1280] = by_x[:, 128:]
-        away[1280:] = by_g[:, 128:]
-
-
-def term_kernel(example, kept, got, across, act, factor, dh, mask, out):
-    rows = lax.broadcasted_iota(jnp.int32, (8, 128), 0)
-    lanes = lax.broadcasted_iota(jnp.int32, (8, 128), 1)
-    total = jnp.zeros((8, 128), F32)
-    for k in range(2):
-
-        def summed(at):
-            part = slice(at * 320, (at + 1) * 320)
-            return kept[part] + got[part]
-
-        tangent = (factor[...] * summed(k) + act[...] * summed(2 + k)).astype(BF16)
-        value = tangent.astype(F32) * dh[...]
-        value += across[...].astype(F32) * summed(4 + k)
-        value = jnp.sum(value, axis=0, keepdims=True) * mask[...]
-        value = jnp.sum(value, axis=1, keepdims=True)
-        total = jnp.where((rows == example[0]) & (lanes == k), value, total)
-    out[...] = total
+        sublanes = lax.broadcasted_iota(jnp.int32, (8, 128), 0)
+        lanes = lax.broadcasted_iota(jnp.int32, (8, 128), 1)
+        total = jnp.zeros((8, 128), F32)
+        for k in range(2):
+            value = jnp.zeros((320, 128), F32)
+            for factors, at in ((own, 0), (their, 128)):
+                tokens = slice(at, at + 128)
+                gate = by_x[k * 320 : (k + 1) * 320, tokens]
+                upper = by_x[(2 + k) * 320 : (3 + k) * 320, tokens]
+                value += factors[:320] * gate + factors[320:640] * upper
+                value += factors[640:] * by_g[k * 320 : (k + 1) * 320, tokens]
+            value = jnp.sum(value, axis=0, keepdims=True)
+            value = jnp.sum(value, axis=1, keepdims=True)
+            total = jnp.where((sublanes == place[2]) & (lanes == k), value, total)
+        out[...] = total
 
 
 def whole(shape):
@@ -219,27 +208,19 @@
     two_g = z_shift(own[:, :, 1], -2)
     acts = jnp.stack([own, plus, jnp.stack([two_x, two_g], axis=2), minus], axis=3)
 
-    half_plus, half_minus, _ = lax.optimization_barrier((t_plus[:3], t_minus[3:], own))
+    half_plus, half_minus, _ = lax.optimization_barrier((t_plus[:3], t_minus[3:], acts))
     half_plus, half_minus = y_shift(half_plus, 1), y_shift(half_minus, -1)
-    half_plus, half_minus, _ = lax.optimization_barrier((half_plus, half_minus, acts))
-    t_two = jnp.concatenate([half_plus, half_minus], axis=0)
-    mine = jnp.stack([stack_t, t_plus, t_two, t_minus])
-    theirs = lax.ppermute(mine, "seq", [(i, i ^ 1) for i in range(16)])
 
     partner = lax.dynamic_index_in_dim(
         acts.reshape((2, 2) + acts.shape[1:]), 1 - seq // 2 % 2, 1, False
     )
     partner = lax.ppermute(partner, "seq", [(i, i ^ 2) for i in range(16)])
 
-    flat = jax.ShapeDtypeStruct((320, 128), F32)
-    hidden, across, act, factor, dh = pl.pallas_call(
+    hidden, factors = pl.pallas_call(
         primal_kernel,
         out_shape=(
             jax.ShapeDtypeStruct((128, 320), BF16),
-            jax.ShapeDtypeStruct((320, 128), BF16),
-            flat,
-            flat,
-            flat,
+            jax.ShapeDtypeStruct((960, 128), F32),
         ),
         grid_spec=pltpu.PrefetchScalarGridSpec(
             num_scalar_prefetch=1,
@@ -247,8 +228,9 @@
             in_specs=[
                 pl.BlockSpec((1, 2, 2, 4, 128, 128), lambda s, p: (s, 0, 0, 0, 0, 0)),
                 weight_spec(3),
+                whole((1, 128)),
             ],
-            out_specs=(whole((128, 320)),) + (whole((320, 128)),) * 4,
+            out_specs=(whole((128, 320)), whole((960, 128))),
             scratch_shapes=[pltpu.VMEM((640, 128), F32), pltpu.VMEM((320, 128), F32)],
         ),
         compiler_params=pltpu.CompilerParams(vmem_limit_bytes=32 * 2**20),
@@ -256,7 +238,8 @@
             flops=2 * 3 * 128 * 320 * 4096, bytes_accessed=10 * 2**20, transcendentals=40960
         ),
         name="primal",
-    )(place, acts, full_w)
+    )(place, acts, full_w, loss_mask.astype(F32)[None])
+    their = lax.ppermute(factors, "seq", [(i, i ^ 2) for i in range(16)])
 
     by_x_hi = pl.BlockSpec((1, 4, 128, 128), lambda s, p: (s, 0, 0, 0))
     half_sums = jax.ShapeDtypeStruct((4, 128, 128), F32)
@@ -283,21 +266,23 @@
         name="block_sums",
     )(place, hidden, full_w)
 
+    half_plus, half_minus, _ = lax.optimization_barrier((half_plus, half_minus, kept))
+    t_two = jnp.concatenate([half_plus, half_minus], axis=0)
+    mine = jnp.stack([stack_t, t_plus, t_two, t_minus])
+    theirs = lax.ppermute(mine, "seq", [(i, i ^ 1) for i in range(16)])
+
     up = z_shift(up, -1)
     down = z_shift(down, 1)
     two_up = z_shift(two_up, -2)
     two_down = z_shift(two_down, 2)
     away = kept[1] + up[1] + down[1] + two_down
+    partner, _ = lax.optimization_barrier((partner, away))
     away = lax.ppermute(away, "fsdp", [(i, (i + 16) % 32) for i in range(32)])
     partial = kept[0] + up[0] + down[0] + two_up + away
-    partial = jnp.sum(lax.all_to_all(partial, "fsdp", 0, 0, axis_index_groups=Z_FAR), axis=0)
-    block_out = partial.astype(BF16)
-
-    partner, _ = lax.optimization_barrier((partner, kept))
-    tall = jax.ShapeDtypeStruct((1920, 128), F32)
-    in_column, to_send = pl.pallas_call(
+
+    terms = pl.pallas_call(
         column_kernel,
-        out_shape=(tall, tall),
+        out_shape=jax.ShapeDtypeStruct((8, 128), F32),
         grid_spec=pltpu.PrefetchScalarGridSpec(
             num_scalar_prefetch=1,
             grid=(2,),
@@ -310,8 +295,10 @@
                 column_spec(0),
                 column_spec(1),
                 column_spec(1),
+                whole((960, 128)),
+                whole((960, 128)),
             ],
-            out_specs=(whole((1920, 128)), whole((1920, 128))),
+            out_specs=whole((8, 128)),
             scratch_shapes=[pltpu.VMEM((1280, 256), F32), pltpu.VMEM((640, 256), F32)],
         ),
         compiler_params=pltpu.CompilerParams(vmem_limit_bytes=32 * 2**20),
@@ -319,27 +306,16 @@
             flops=2 * 6 * 128 * 320 * 4096, bytes_accessed=12 * 2**20, transcendentals=0
         ),
         name="column",
-    )(place, acts, partner, mine, theirs, mine, theirs)
-    got = lax.ppermute(to_send, "seq", [(i, i ^ 2) for i in range(16)])
-
-    terms = pl.pallas_call(
-        term_kernel,
-        out_shape=jax.ShapeDtypeStruct((8, 128), F32),
-        in_specs=[pl.BlockSpec(memory_space=pltpu.SMEM)]
-        + [pl.BlockSpec(memory_space=pltpu.VMEM)] * 7,
-        out_specs=pl.BlockSpec(memory_space=pltpu.VMEM),
-        cost_estimate=pl.CostEstimate(
-            flops=2**20, bytes_accessed=3 * 2**20, transcendentals=0
-        ),
-        compiler_params=pltpu.CompilerParams(vmem_limit_bytes=16 * 2**20),
-        name="terms",
-    )(place[2:3], in_column, got, across, act, factor, dh, loss_mask.astype(F32)[None])
-
-    for axis, size, groups in (("seq", 16, None), ("fsdp", 16, Z_ALL), ("fsdp", 2, X_PAIRS)):
-        copies = jnp.broadcast_to(terms[None], (size,) + terms.shape)
-        terms = jnp.sum(lax.all_to_all(copies, axis, 0, 0, axis_index_groups=groups), axis=0)
-        if axis == "seq":
-            terms, block_out = lax.optimization_barrier((terms, block_out))
+    )(place, acts, partner, mine, theirs, mine, theirs, factors, their)
+
+    def sum_over(copies, axis, groups):
+        return jnp.sum(lax.all_to_all(copies, axis, 0, 0, axis_index_groups=groups), axis=0)
+
+    terms = sum_over(jnp.broadcast_to(terms[None], (16, 8, 128)), "seq", None)
+    copies = jnp.broadcast_to(terms[None], (4, 8, 128))
+    both = sum_over(jnp.concatenate([partial, copies], axis=1), "fsdp", Z_FAR)
+    block_out = both[:128].astype(BF16)
+    terms = sum_over(jnp.broadcast_to(both[None, 128:], (8, 8, 128)), "fsdp", X_AND_NEAR)
     return (block_out, terms[:EXAMPLES, :2])
 
 

time: 255 us -> 242 us (0.949)
  waiting for transfers between devices: 69.8 us -> 49.2 us
  local copies, waits for them, and re-layouts: 8.6 us -> 12 us
    ppermute x4, waiting for transfers between devices: 18.8 us -> 0.01 us  [y_shift(): lax.ppermute(array, 'seq', [((i + 4 * step) % 16, i) for i in range(16)])]
    ppermute x11, waiting for transfers between devices: 19.5 us -> 35.3 us  [z_shift(): return lax.ppermute(array, 'fsdp', perm)]
    all_to_all x2, waiting for transfers between devices: 21.3 us -> 10.5 us  [sum_over(): lax.all_to_all(copies, axis, 0, 0, axis_index_groups=groups)]
    ppermute x1, waiting for transfers between devices: 4.49 us -> 0.01 us  [shards(): partner = lax.ppermute(partner, 'seq', [(i, i ^ 2) for i in range(16)])]
    ppermute x11, starting transfers between devices: 61.3 us -> 64.7 us  [z_shift(): return lax.ppermute(array, 'fsdp', perm)]
    all_to_all x2 -> x1, blocking collectives: 26.9 us -> 28.7 us  [sum_over(): lax.all_to_all(copies, axis, 0, 0, axis_index_groups=groups)]
    unnamed x23 -> x45, local copies, waits for them, and re-layouts: 6.65 us -> 7.02 us
    pallas_call x2 -> x1, Pallas kernels: 7.7 us -> 7.61 us  [shards(): pl.pallas_call(column_kernel, out_shape=jax.ShapeDtypeStruct((8, 128), F3...]
  transfers between devices with their start and end apart: 23 -> 23, of which waited for: 11 -> 7; matrix products, arithmetic and copies ran while one was open for 4% -> 5% of each run, Pallas kernels for 7% -> 7%
where the time goes in v7:
time: 242 us; the launch traced here: 240 us
  starting transfers between devices  108 us (45%)
  waiting for transfers between devices  49.2 us (20%)
  blocking collectives  28.7 us (12%)
  Pallas kernels  16.9 us (7%)
  between operations  14.8 us (6%)
  local copies, waits for them, and re-layouts  12 us (5%)
  other arithmetic  10.3 us (4%)
    ppermute x11, starting transfers between devices, z_shift(): return lax.ppermute(array, 'fsdp', perm)  64.7 us
    ppermute x11, waiting for transfers between devices, z_shift(): return lax.ppermute(array, 'fsdp', perm)  35.3 us
    all_to_all x1, blocking collectives, sum_over(): lax.all_to_all(copies, axis, 0, 0, axis_index_groups=groups)  28.7 us
    ppermute x4, starting transfers between devices, y_shift(): lax.ppermute(array, 'seq', [((i + 4 * step) % 16, i) for i in range(16)])  12.9 us
    all_to_all x2, starting transfers between devices, sum_over(): lax.all_to_all(copies, axis, 0, 0, axis_index_groups=groups)  12.8 us
    all_to_all x2, waiting for transfers between devices, sum_over(): lax.all_to_all(copies, axis, 0, 0, axis_index_groups=groups)  10.5 us
    pallas_call x1, Pallas kernels, shards(): pl.pallas_call(column_kernel, out_shape=jax.ShapeDtypeStruct((8, 128), F3...  7.61 us
    unnamed x45, local copies, waits for them, and re-layouts  7.02 us
  transfers between devices with their start and end apart: 23, of which 7 were waited for; matrix products, arithmetic and copies ran while one was open for 5% of the time, Pallas kernels for 7%

profile of v7, /device:TPU:24, one launch (start us, length us, event | category | flops | bytes accessed | tf_op | source)
XLA Modules:
  0.0 240.0 jit_solution(5641213929020351316)
XLA Ops:
  7.2 0.0 all-gather.3.cloned.1.call-start
  7.2 1.9 pad_maximum_fusion.2
  9.1 0.0 all-gather.3.cloned.1.call-update
  9.2 0.8 fusion.9
  10.0 4.9 %collective-permute-start = (bf16[2,128,128]{2,1,0:T(8,128)(2,1)S(1)}, bf16[2,128,128]{2,1,0:T(8,128)(2,1)S(1)}, u32[]{:S(2)}, u32[]{:S(2)}) collective-permute-start(bf16[2,128,128]{2,1,0:T(8,128)(2,1)S(1)} %get-tuple-element.37), channel_id=1, source_target_pairs={{0,256},{16,272},{32,288},{48,304},{64,320},{80,336},{96,352},{112... | collective-permute-start | bytes 196616 | tf_op jit(solution)/shard_map/ppermute | solution.py:192
  15.0 2.7 %collective-permute-done = bf16[2,128,128]{2,1,0:T(8,128)(2,1)S(1)} collective-permute-done((bf16[2,128,128]{2,1,0:T(8,128)(2,1)S(1)}, bf16[2,128,128]{2,1,0:T(8,128)(2,1)S(1)}, u32[]{:S(2)}, u32[]{:S(2)}) %collective-permute-start) | collective-permute-done | bytes 65568 | tf_op jit(solution)/shard_map/ppermute | solution.py:192
  17.6 12.7 %collective-permute-start.1 = (bf16[2,2,128,128]{3,2,1,0:T(8,128)(2,1)S(1)}, bf16[2,2,128,128]{3,2,1,0:T(8,128)(2,1)S(1)}, u32[]{:S(2)}, u32[]{:S(2)}) collective-permute-start(bf16[2,2,128,128]{3,2,1,0:T(8,128)(2,1)S(1)} %pad_maximum_fusion.4), channel_id=1, source_target_pairs={{64,0},{80,16},{96,32},{112,48},{128,64},{144,80},{160,96},{176,11... | collective-permute-start | bytes 393224 | tf_op jit(solution)/shard_map/ppermute | solution.py:33
  30.4 4.9 %collective-permute-start.2 = (bf16[2,2,128,128]{3,2,1,0:T(8,128)(2,1)S(1)}, bf16[2,2,128,128]{3,2,1,0:T(8,128)(2,1)S(1)}, u32[]{:S(2)}, u32[]{:S(2)}) collective-permute-start(bf16[2,2,128,128]{3,2,1,0:T(8,128)(2,1)S(1)} %pad_maximum_fusion.4), channel_id=1, source_target_pairs={{128,0},{144,16},{160,32},{176,48},{192,64},{208,80},{224,96},{240... | collective-permute-start | bytes 393224 | tf_op jit(solution)/shard_map/ppermute | solution.py:33
  35.3 7.8 %collective-permute-start.3 = (bf16[2,2,128,128]{3,2,1,0:T(8,128)(2,1)S(1)}, bf16[2,2,128,128]{3,2,1,0:T(8,128)(2,1)S(1)}, u32[]{:S(2)}, u32[]{:S(2)}) collective-permute-start(bf16[2,2,128,128]{3,2,1,0:T(8,128)(2,1)S(1)} %pad_maximum_fusion.4), channel_id=1, source_target_pairs={{192,0},{208,16},{224,32},{240,48},{0,64},{16,80},{32,96},{48,112}... | collective-permute-start | bytes 393224 | tf_op jit(solution)/shard_map/ppermute | solution.py:33
  43.1 1.0 constant_dynamic-update-slice_fusion.2
  44.1 1.0 constant_dynamic-update-slice_fusion.1
  45.1 1.0 constant_dynamic-update-slice_fusion
  46.2 2.1 collective-permute-start.15
  48.3 3.7 %collective-permute-start.14 = (bf16[6,320,256]{2,1,0:T(8,128)(2,1)S(1)}, bf16[6,320,256]{2,1,0:T(8,128)(2,1)S(1)}, u32[]{:S(2)}, u32[]{:S(2)}) collective-permute-start(bf16[6,320,256]{2,1,0:T(8,128)(2,1)S(1)} %constant_dynamic-update-slice_fusion), channel_id=1, source_target_pairs={{4,0},{5,1},{6,2},{7,3},{8,4},{9,5},{10,6},{11,7},{12,8},{13,9},{1... | collective-permute-start | bytes 2949128 | tf_op jit(solution)/shard_map/ppermute | solution.py:37
  52.1 1.6 collective-permute-done.2
  53.9 7.8 %collective-permute-start.6 = (bf16[4,2,128,128]{3,2,1,0:T(8,128)(2,1)S(1)}, bf16[4,2,128,128]{3,2,1,0:T(8,128)(2,1)S(1)}, u32[]{:S(2)}, u32[]{:S(2)}) collective-permute-start(bf16[4,2,128,128]{3,2,1,0:T(8,128)(2,1)S(1)} %get-tuple-element.35), channel_id=1, source_target_pairs={{224,0},{240,16},{0,32},{16,48},{32,64},{48,80},{64,96},{80,112},{... | collective-permute-start | bytes 786440 | tf_op jit(solution)/shard_map/ppermute | solution.py:33
  61.8 0.0 copy-start.18
  61.8 4.2 %collective-permute-start.7 = (bf16[4,2,2,128,128]{4,3,2,1,0:T(8,128)(2,1)S(1)}, bf16[4,2,2,128,128]{4,3,2,1,0:T(8,128)(2,1)S(1)}, u32[]{:S(2)}, u32[]{:S(2)}) collective-permute-start(bf16[4,2,2,128,128]{4,3,2,1,0:T(8,128)(2,1)S(1)} %constant_dynamic-slice_fusion), channel_id=1, source_target_pairs={{240,0},{0,16},{16,32},{32,48},{48,64},{64,80},{80,96},{96,112},{1... | collective-permute-start | bytes 1572872 | tf_op jit(solution)/shard_map/ppermute | solution.py:33
  66.0 4.3 %collective-permute-start.4 = (bf16[4,2,2,128,128]{4,3,2,1,0:T(8,128)(2,1)S(1)}, bf16[4,2,2,128,128]{4,3,2,1,0:T(8,128)(2,1)S(1)}, u32[]{:S(2)}, u32[]{:S(2)}) collective-permute-start(bf16[4,2,2,128,128]{4,3,2,1,0:T(8,128)(2,1)S(1)} %constant_dynamic-slice_fusion), channel_id=1, source_target_pairs={{16,0},{32,16},{48,32},{64,48},{80,64},{96,80},{112,96},{128,112},... | collective-permute-start | bytes 1572872 | tf_op jit(solution)/shard_map/ppermute | solution.py:33
  70.3 0.0 collective-permute-done.6
  70.4 4.8 %collective-permute-start.5 = (bf16[4,2,128,128]{3,2,1,0:T(8,128)(2,1)S(1)}, bf16[4,2,128,128]{3,2,1,0:T(8,128)(2,1)S(1)}, u32[]{:S(2)}, u32[]{:S(2)}) collective-permute-start(bf16[4,2,128,128]{3,2,1,0:T(8,128)(2,1)S(1)} %get-tuple-element.34), channel_id=1, source_target_pairs={{32,0},{48,16},{64,32},{80,48},{96,64},{112,80},{128,96},{144,112}... | collective-permute-start | bytes 786440 | tf_op jit(solution)/shard_map/ppermute | solution.py:33
  75.2 17.6 %collective-permute-done.5 = bf16[4,2,128,128]{3,2,1,0:T(8,128)(2,1)S(1)} collective-permute-done((bf16[4,2,128,128]{3,2,1,0:T(8,128)(2,1)S(1)}, bf16[4,2,128,128]{3,2,1,0:T(8,128)(2,1)S(1)}, u32[]{:S(2)}, u32[]{:S(2)}) %collective-permute-start.5) | collective-permute-done | bytes 262176 | tf_op jit(solution)/shard_map/ppermute | solution.py:33
  92.9 0.0 collective-permute-done.7
  92.9 0.0 collective-permute-done.4
  92.9 0.1 pad_maximum_fusion.1.acts
  93.1 1.0 slice.57
  94.1 0.0 collective-permute-done.15
  94.1 1.0 copy-done.5
  95.1 0.8 slice.58
  95.9 2.6 %collective-permute-start.16 = (bf16[3,320,256]{2,1,0:T(8,128)(2,1)}, bf16[3,320,256]{2,1,0:T(8,128)(2,1)}, u32[]{:S(2)}, u32[]{:S(2)}) collective-permute-start(bf16[3,320,256]{2,1,0:T(8,128)(2,1)} %slice.57), channel_id=1, source_target_pairs={{4,0},{5,1},{6,2},{7,3},{8,4},{9,5},{10,6},{11,7},{12,8},{13,9},{1... | collective-permute-start | bytes 1474568 | tf_op jit(solution)/shard_map/ppermute | solution.py:37
  98.6 4.4 %collective-permute-start.17 = (bf16[3,320,256]{2,1,0:T(8,128)(2,1)}, bf16[3,320,256]{2,1,0:T(8,128)(2,1)}, u32[]{:S(2)}, u32[]{:S(2)}) collective-permute-start(bf16[3,320,256]{2,1,0:T(8,128)(2,1)} %slice.58), channel_id=1, source_target_pairs={{12,0},{13,1},{14,2},{15,3},{0,4},{1,5},{2,6},{3,7},{4,8},{5,9},{6... | collective-permute-start | bytes 1474568 | tf_op jit(solution)/shard_map/ppermute | solution.py:37
  103.1 0.1 stack.128.place
  103.2 0.0 all-gather.3.cloned.1.call-done
  103.2 3.2 %copy-done = bf16[48,320,256]{2,1,0:T(8,128)(2,1)S(1)} copy-done((bf16[48,320,256]{2,1,0:T(8,128)(2,1)S(1)}, bf16[48,320,256]{2,1,0:T(8,128)(2,1)}, u32[]{:S(2)}) %copy-start) | copy-done | bytes 7864344
  106.5 6.2 %primal.1 = (bf16[128,320]{1,0:T(8,128)(2,1)S(1)}, f32[960,128]{1,0:T(8,128)S(1)}) custom-call(s32[6]{0:T(128)S(1)} %stack.128.place, bf16[4,2,2,4,128,128]{5,4,3,2,1,0:T(8,128)(2,1)S(1)} %pad_maximum_fusion.1.acts, bf16[2,4,2,3,320,256]{5,4,3,2,1,0:T(8,128)(2,1)S(1)} %bitcast.72, f32[1,128]{1,0:T(1,128)S(1)} %convert_bitcast_fusion.mask), custom_call_target="tpu_custom_call" | custom-call | flops 1006632960 | bytes 10485760 | tf_op jit(solution)/shard_map/primal/pallas_call | solution.py:219
  112.7 3.2 %block_sums.1 = (f32[2,4,128,128]{3,2,1,0:T(8,128)S(1)}, f32[2,4,128,128]{3,2,1,0:T(8,128)S(1)}, f32[2,4,128,128]{3,2,1,0:T(8,128)S(1)}, f32[4,128,128]{2,1,0:T(8,128)S(1)}, f32[4,128,128]{2,1,0:T(8,128)S(1)}) custom-call(s32[6]{0:T(128)S(1)} %stack.128.place, bf16[128,320]{1,0:T(8,128)(2,1)S(1)} %get-tuple-element.17.hidden, ...), custom_call_target="tpu_custom_call" | custom-call | flops 335544320 | bytes 5242880 | tf_op jit(solution)/shard_map/block_sums/pallas_call | solution.py:247
  115.9 1.7 maximum_bitcast_fusion
  117.6 2.2 pad_maximum_fusion.mine_0.mine_1
  119.8 1.9 collective-permute-start.18
  121.8 1.3 copy_bitcast_fusion
  123.0 3.4 %collective-permute-start.13 = (bf16[2,2,2,4,128,128]{5,4,3,2,1,0:T(8,128)(2,1)S(1)}, bf16[2,2,2,4,128,128]{5,4,3,2,1,0:T(8,128)(2,1)S(1)}, u32[]{:S(2)}, u32[]{:S(2)}) collective-permute-start(bf16[2,2,2,4,128,128]{5,4,3,2,1,0:T(8,128)(2,1)S(1)} %copy_bitcast_fusion), channel_id=1, source_target_pairs={{0,2},{1,3},{2,0},{3,1},{4,6},{5,7},{6,4},{7,5},{8,10},{9,11},{10,... | collective-permute-start | bytes 3145736 | tf_op jit(solution)/shard_map/ppermute | solution.py:217
  126.5 4.2 %collective-permute-start.9 = (f32[2,4,128,128]{3,2,1,0:T(8,128)}, f32[2,4,128,128]{3,2,1,0:T(8,128)S(1)}, u32[]{:S(2)}, u32[]{:S(2)}) collective-permute-start(f32[2,4,128,128]{3,2,1,0:T(8,128)} %copy-done.3), channel_id=1, source_target_pairs={{16,0},{32,16},{48,32},{64,48},{80,64},{96,80},{112,96},{128,112},... | collective-permute-start | bytes 1572872 | tf_op jit(solution)/shard_map/ppermute | solution.py:33
  130.7 1.9 collective-permute-start.8
  132.6 6.2 %collective-permute-start.11 = (f32[4,128,128]{2,1,0:T(8,128)}, f32[4,128,128]{2,1,0:T(8,128)S(1)}, u32[]{:S(2)}, u32[]{:S(2)}) collective-permute-start(f32[4,128,128]{2,1,0:T(8,128)} %copy-done.4), channel_id=1, source_target_pairs={{32,0},{48,16},{64,32},{80,48},{96,64},{112,80},{128,96},{144,112}... | collective-permute-start | bytes 786440 | tf_op jit(solution)/shard_map/ppermute | solution.py:33
  138.8 16.0 %collective-permute-done.11 = f32[4,128,128]{2,1,0:T(8,128)S(1)} collective-permute-done((f32[4,128,128]{2,1,0:T(8,128)}, f32[4,128,128]{2,1,0:T(8,128)S(1)}, u32[]{:S(2)}, u32[]{:S(2)}) %collective-permute-start.11) | collective-permute-done | bytes 262176 | tf_op jit(solution)/shard_map/ppermute | solution.py:33
  154.8 2.4 %collective-permute-start.19 = (f32[960,128]{1,0:T(8,128)S(1)}, f32[960,128]{1,0:T(8,128)S(1)}, u32[]{:S(2)}, u32[]{:S(2)}) collective-permute-start(f32[960,128]{1,0:T(8,128)S(1)} %get-tuple-element.31.own), channel_id=1, source_target_pairs={{0,2},{1,3},{2,0},{3,1},{4,6},{5,7},{6,4},{7,5},{8,10},{9,11},{10,... | collective-permute-start | bytes 1474568 | tf_op jit(solution)/shard_map/ppermute | solution.py:242
  157.3 0.0 collective-permute-done.9
  157.3 5.8 %collective-permute-start.10 = (f32[4,128,128]{2,1,0:T(8,128)S(1)}, f32[4,128,128]{2,1,0:T(8,128)}, u32[]{:S(2)}, u32[]{:S(2)}) collective-permute-start(f32[4,128,128]{2,1,0:T(8,128)S(1)} %get-tuple-element.21), channel_id=1, source_target_pairs={{224,0},{240,16},{0,32},{16,48},{32,64},{48,80},{64,96},{80,112},{... | collective-permute-start | bytes 786440 | tf_op jit(solution)/shard_map/ppermute | solution.py:33
  163.1 0.9 fusion.5
  164.0 4.9 %collective-permute-start.12 = (f32[4,128,128]{2,1,0:T(8,128)}, f32[4,128,128]{2,1,0:T(8,128)}, u32[]{:S(2)}, u32[]{:S(2)}) collective-permute-start(f32[4,128,128]{2,1,0:T(8,128)} %fusion.5), channel_id=1, source_target_pairs={{0,256},{16,272},{32,288},{48,304},{64,320},{80,336},{96,352},{112... | collective-permute-start | bytes 786440 | tf_op jit(solution)/shard_map/ppermute | solution.py:280
  168.9 0.0 collective-permute-done.13.partner
  168.9 0.7 collective-permute-done.19.their
  169.6 7.6 %column.1 = f32[8,128]{1,0:T(8,128)S(1)} custom-call(s32[6]{0:T(128)S(1)} %stack.128.place, bf16[4,2,2,4,128,128]{5,4,3,2,1,0:T(8,128)(2,1)S(1)} %pad_maximum_fusion.1.acts, bf16[2,2,2,4,128,128]{5,4,3,2,1,0:T(8,128)(2,1)S(1)} %collective-permute-done.13.partner, bf16[4,6,320,256]{3,2,1,0:T(8,128)(2,1)} %pad_maximum_fusion.mine_0.mine_1, ...), custom_call_target="tpu_custom_call" | custom-call | flops 2013265920 | bytes 12582912 | tf_op jit(solution)/shard_map/column/pallas_call | solution.py:283
  177.2 0.6 broadcast_in_dim.9
  177.9 4.5 %all-to-all-start = ((f32[16,8,128]{2,1,0:T(8,128)}), f32[16,8,128]{2,1,0:T(8,128)S(1)}, u32[]{:S(2)}, u32[]{:S(2)}) async-start(f32[16,8,128]{2,1,0:T(8,128)} %broadcast_in_dim.9), calls=%async_computation | async-start | bytes 131072 | tf_op jit(solution)/shard_map/all_to_all | solution.py:312
  182.4 0.0 collective-permute-done.10
  182.4 1.3 fusion.8
  183.7 2.9 %all-to-all-done = f32[16,8,128]{2,1,0:T(8,128)S(1)} async-done(((f32[16,8,128]{2,1,0:T(8,128)}), f32[16,8,128]{2,1,0:T(8,128)S(1)}, u32[]{:S(2)}, u32[]{:S(2)}) %all-to-all-start) | async-done | bytes 65568 | tf_op jit(solution)/shard_map/all_to_all | solution.py:312
  186.6 28.7 %all_to_all.15 = f32[4,136,128]{2,1,0:T(8,128)S(1)} all-to-all(f32[4,136,128]{2,1,0:T(8,128)S(1)} %pad_maximum_fusion.3), channel_id=1, replica_groups={{0,64,128,192},{16,80,144,208},{32,96,160,224},{48,112,176,240},{256,32..., dimensions={0} | all-to-all | bytes 557056 | tf_op jit(solution)/shard_map/all_to_all | solution.py:312
  215.4 0.6 broadcast_in_dim.11
  216.0 8.3 %all-to-all-start.2 = ((f32[8,8,128]{2,1,0:T(8,128)}), f32[8,8,128]{2,1,0:T(8,128)S(1)}, u32[]{:S(2)}, u32[]{:S(2)}) async-start(f32[8,8,128]{2,1,0:T(8,128)} %broadcast_in_dim.11), calls=%async_computation.2 | async-start | bytes 65536 | tf_op jit(solution)/shard_map/all_to_all | solution.py:312
  224.2 0.6 slice.82
  224.8 7.6 %all-to-all-done.2 = f32[8,8,128]{2,1,0:T(8,128)S(1)} async-done(((f32[8,8,128]{2,1,0:T(8,128)}), f32[8,8,128]{2,1,0:T(8,128)S(1)}, u32[]{:S(2)}, u32[]{:S(2)}) %all-to-all-start.2) | async-done | bytes 32800 | tf_op jit(solution)/shard_map/all_to_all | solution.py:312
  232.5 0.7 copy.36
  (62 shorter events, 0.5 us)
Async XLA Ops:
  7.2 96.1 %all-gather.3.cloned.1.call-start = ((), (), s32[]{:S(2)}) async-start(), calls=%async_computation.3 | async-start | bytes 8355840 | tf_op jit(solution)/shard_map/all_gather | solution.py:197
  10.0 7.7 %collective-permute-start = (bf16[2,128,128]{2,1,0:T(8,128)(2,1)S(1)}, bf16[2,128,128]{2,1,0:T(8,128)(2,1)S(1)}, u32[]{:S(2)}, u32[]{:S(2)}) collective-permute-start(bf16[2,128,128]{2,1,0:T(8,128)(2,1)S(1)} %get-tuple-element.37), channel_id=1, source_target_pairs={{0,256},{16,272},{32,288},{48,304},{64,320},{80,336},{96,352},{112... | collective-permute-start | bytes 196616 | tf_op jit(solution)/shard_map/ppermute | solution.py:192
  17.6 34.4 %collective-permute-start.1 = (bf16[2,2,128,128]{3,2,1,0:T(8,128)(2,1)S(1)}, bf16[2,2,128,128]{3,2,1,0:T(8,128)(2,1)S(1)}, u32[]{:S(2)}, u32[]{:S(2)}) collective-permute-start(bf16[2,2,128,128]{3,2,1,0:T(8,128)(2,1)S(1)} %pad_maximum_fusion.4), channel_id=1, source_target_pairs={{64,0},{80,16},{96,32},{112,48},{128,64},{144,80},{160,96},{176,11... | collective-permute-start | bytes 393224 | tf_op jit(solution)/shard_map/ppermute | solution.py:33
  30.4 23.3 %collective-permute-start.2 = (bf16[2,2,128,128]{3,2,1,0:T(8,128)(2,1)S(1)}, bf16[2,2,128,128]{3,2,1,0:T(8,128)(2,1)S(1)}, u32[]{:S(2)}, u32[]{:S(2)}) collective-permute-start(bf16[2,2,128,128]{3,2,1,0:T(8,128)(2,1)S(1)} %pad_maximum_fusion.4), channel_id=1, source_target_pairs={{128,0},{144,16},{160,32},{176,48},{192,64},{208,80},{224,96},{240... | collective-permute-start | bytes 393224 | tf_op jit(solution)/shard_map/ppermute | solution.py:33
  35.3 18.4 %collective-permute-start.3 = (bf16[2,2,128,128]{3,2,1,0:T(8,128)(2,1)S(1)}, bf16[2,2,128,128]{3,2,1,0:T(8,128)(2,1)S(1)}, u32[]{:S(2)}, u32[]{:S(2)}) collective-permute-start(bf16[2,2,128,128]{3,2,1,0:T(8,128)(2,1)S(1)} %pad_maximum_fusion.4), channel_id=1, source_target_pairs={{192,0},{208,16},{224,32},{240,48},{0,64},{16,80},{32,96},{48,112}... | collective-permute-start | bytes 393224 | tf_op jit(solution)/shard_map/ppermute | solution.py:33
  46.1 46.9 %copy-start.12 = (bf16[6,320,256]{2,1,0:T(8,128)(2,1)}, bf16[6,320,256]{2,1,0:T(8,128)(2,1)S(1)}, u32[]{:S(2)}) copy-start(bf16[6,320,256]{2,1,0:T(8,128)(2,1)S(1)} %constant_dynamic-update-slice_fusion) | copy-start | bytes 2949124
  46.2 47.9 %collective-permute-start.15 = (bf16[6,320,256]{2,1,0:T(8,128)(2,1)S(1)}, bf16[6,320,256]{2,1,0:T(8,128)(2,1)S(1)}, u32[]{:S(2)}, u32[]{:S(2)}) collective-permute-start(bf16[6,320,256]{2,1,0:T(8,128)(2,1)S(1)} %constant_dynamic-update-slice_fusion), channel_id=1, source_target_pairs={{12,0},{13,1},{14,2},{15,3},{0,4},{1,5},{2,6},{3,7},{4,8},{5,9},{6... | collective-permute-start | bytes 2949128 | tf_op jit(solution)/shard_map/ppermute | solution.py:37
  48.3 44.8 %collective-permute-start.14 = (bf16[6,320,256]{2,1,0:T(8,128)(2,1)S(1)}, bf16[6,320,256]{2,1,0:T(8,128)(2,1)S(1)}, u32[]{:S(2)}, u32[]{:S(2)}) collective-permute-start(bf16[6,320,256]{2,1,0:T(8,128)(2,1)S(1)} %constant_dynamic-update-slice_fusion), channel_id=1, source_target_pairs={{4,0},{5,1},{6,2},{7,3},{8,4},{9,5},{10,6},{11,7},{12,8},{13,9},{1... | collective-permute-start | bytes 2949128 | tf_op jit(solution)/shard_map/ppermute | solution.py:37
  53.9 16.4 %collective-permute-start.6 = (bf16[4,2,128,128]{3,2,1,0:T(8,128)(2,1)S(1)}, bf16[4,2,128,128]{3,2,1,0:T(8,128)(2,1)S(1)}, u32[]{:S(2)}, u32[]{:S(2)}) collective-permute-start(bf16[4,2,128,128]{3,2,1,0:T(8,128)(2,1)S(1)} %get-tuple-element.35), channel_id=1, source_target_pairs={{224,0},{240,16},{0,32},{16,48},{32,64},{48,80},{64,96},{80,112},{... | collective-permute-start | bytes 786440 | tf_op jit(solution)/shard_map/ppermute | solution.py:33
  61.7 31.1 %copy-start.9 = (bf16[4,2,2,128,128]{4,3,2,1,0:T(8,128)(2,1)}, bf16[4,2,2,128,128]{4,3,2,1,0:T(8,128)(2,1)S(1)}, u32[]{:S(2)}) copy-start(bf16[4,2,2,128,128]{4,3,2,1,0:T(8,128)(2,1)S(1)} %constant_dynamic-slice_fusion) | copy-start | bytes 1572868
  61.8 41.5 %copy-start.18 = (s32[128]{0:T(128)S(1)}, s32[128]{0:T(128)}, u32[]{:S(2)}) copy-start(s32[128]{0:T(128)} %param.11) | copy-start | bytes 1540
  61.8 31.1 %collective-permute-start.7 = (bf16[4,2,2,128,128]{4,3,2,1,0:T(8,128)(2,1)S(1)}, bf16[4,2,2,128,128]{4,3,2,1,0:T(8,128)(2,1)S(1)}, u32[]{:S(2)}, u32[]{:S(2)}) collective-permute-start(bf16[4,2,2,128,128]{4,3,2,1,0:T(8,128)(2,1)S(1)} %constant_dynamic-slice_fusion), channel_id=1, source_target_pairs={{240,0},{0,16},{16,32},{32,48},{48,64},{64,80},{80,96},{96,112},{1... | collective-permute-start | bytes 1572872 | tf_op jit(solution)/shard_map/ppermute | solution.py:33
  66.0 26.9 %collective-permute-start.4 = (bf16[4,2,2,128,128]{4,3,2,1,0:T(8,128)(2,1)S(1)}, bf16[4,2,2,128,128]{4,3,2,1,0:T(8,128)(2,1)S(1)}, u32[]{:S(2)}, u32[]{:S(2)}) collective-permute-start(bf16[4,2,2,128,128]{4,3,2,1,0:T(8,128)(2,1)S(1)} %constant_dynamic-slice_fusion), channel_id=1, source_target_pairs={{16,0},{32,16},{48,32},{64,48},{80,64},{96,80},{112,96},{128,112},... | collective-permute-start | bytes 1572872 | tf_op jit(solution)/shard_map/ppermute | solution.py:33
  70.3 28.2 %copy-start.14 = (bf16[4,2,128,128]{3,2,1,0:T(8,128)(2,1)}, bf16[4,2,128,128]{3,2,1,0:T(8,128)(2,1)S(1)}, u32[]{:S(2)}) copy-start(bf16[4,2,128,128]{3,2,1,0:T(8,128)(2,1)S(1)} %collective-permute-done.6) | copy-start | bytes 786436
  70.4 22.5 %collective-permute-start.5 = (bf16[4,2,128,128]{3,2,1,0:T(8,128)(2,1)S(1)}, bf16[4,2,128,128]{3,2,1,0:T(8,128)(2,1)S(1)}, u32[]{:S(2)}, u32[]{:S(2)}) collective-permute-start(bf16[4,2,128,128]{3,2,1,0:T(8,128)(2,1)S(1)} %get-tuple-element.34), channel_id=1, source_target_pairs={{32,0},{48,16},{64,32},{80,48},{96,64},{112,80},{128,96},{144,112}... | collective-permute-start | bytes 786440 | tf_op jit(solution)/shard_map/ppermute | solution.py:33
  92.9 5.7 %copy-start.15 = (bf16[4,2,128,128]{3,2,1,0:T(8,128)(2,1)}, bf16[4,2,128,128]{3,2,1,0:T(8,128)(2,1)S(1)}, u32[]{:S(2)}) copy-start(bf16[4,2,128,128]{3,2,1,0:T(8,128)(2,1)S(1)} %collective-permute-done.5) | copy-start | bytes 786436
  92.9 5.7 %copy-start.10 = (bf16[4,2,2,128,128]{4,3,2,1,0:T(8,128)(2,1)}, bf16[4,2,2,128,128]{4,3,2,1,0:T(8,128)(2,1)S(1)}, u32[]{:S(2)}) copy-start(bf16[4,2,2,128,128]{4,3,2,1,0:T(8,128)(2,1)S(1)} %collective-permute-done.7) | copy-start | bytes 1572868
  92.9 5.7 %copy-start.11 = (bf16[4,2,2,128,128]{4,3,2,1,0:T(8,128)(2,1)}, bf16[4,2,2,128,128]{4,3,2,1,0:T(8,128)(2,1)S(1)}, u32[]{:S(2)}) copy-start(bf16[4,2,2,128,128]{4,3,2,1,0:T(8,128)(2,1)S(1)} %collective-permute-done.4) | copy-start | bytes 1572868
  93.1 2.9 %copy-start.7 = (bf16[6,320,256]{2,1,0:T(8,128)(2,1)}, bf16[6,320,256]{2,1,0:T(8,128)(2,1)S(1)}, u32[]{:S(2)}) copy-start(bf16[6,320,256]{2,1,0:T(8,128)(2,1)S(1)} %collective-permute-done.14) | copy-start | bytes 2949124
  94.1 1.0 copy-start.5
  95.9 19.9 %collective-permute-start.16 = (bf16[3,320,256]{2,1,0:T(8,128)(2,1)}, bf16[3,320,256]{2,1,0:T(8,128)(2,1)}, u32[]{:S(2)}, u32[]{:S(2)}) collective-permute-start(bf16[3,320,256]{2,1,0:T(8,128)(2,1)} %slice.57), channel_id=1, source_target_pairs={{4,0},{5,1},{6,2},{7,3},{8,4},{9,5},{10,6},{11,7},{12,8},{13,9},{1... | collective-permute-start | bytes 1474568 | tf_op jit(solution)/shard_map/ppermute | solution.py:37
  98.6 17.3 %collective-permute-start.17 = (bf16[3,320,256]{2,1,0:T(8,128)(2,1)}, bf16[3,320,256]{2,1,0:T(8,128)(2,1)}, u32[]{:S(2)}, u32[]{:S(2)}) collective-permute-start(bf16[3,320,256]{2,1,0:T(8,128)(2,1)} %slice.58), channel_id=1, source_target_pairs={{12,0},{13,1},{14,2},{15,3},{0,4},{1,5},{2,6},{3,7},{4,8},{5,9},{6... | collective-permute-start | bytes 1474568 | tf_op jit(solution)/shard_map/ppermute | solution.py:37
  103.2 3.2 %copy-start = (bf16[48,320,256]{2,1,0:T(8,128)(2,1)S(1)}, bf16[48,320,256]{2,1,0:T(8,128)(2,1)}, u32[]{:S(2)}) copy-start(bf16[48,320,256]{2,1,0:T(8,128)(2,1)} %all-gather.3.cloned.1.call-done) | copy-start | bytes 23592964
  106.5 6.2 %copy-start.1 = (bf16[48,320,256]{2,1,0:T(8,128)(2,1)S(1)}, bf16[48,320,256]{2,1,0:T(8,128)(2,1)}, u32[]{:S(2)}) copy-start(bf16[48,320,256]{2,1,0:T(8,128)(2,1)} %all-gather.3.cloned.1.call-done) | copy-start | bytes 23592964
  112.7 5.0 %copy-start.6 = (bf16[6,320,256]{2,1,0:T(8,128)(2,1)S(1)}, bf16[6,320,256]{2,1,0:T(8,128)(2,1)}, u32[]{:S(2)}) copy-start(bf16[6,320,256]{2,1,0:T(8,128)(2,1)} %copy-done.5) | copy-start | bytes 2949124
  112.7 5.0 %copy-start.8 = (bf16[6,320,256]{2,1,0:T(8,128)(2,1)S(1)}, bf16[6,320,256]{2,1,0:T(8,128)(2,1)}, u32[]{:S(2)}) copy-start(bf16[6,320,256]{2,1,0:T(8,128)(2,1)} %copy-done.7) | copy-start | bytes 2949124
  112.7 5.0 %copy-start.13 = (bf16[6,320,256]{2,1,0:T(8,128)(2,1)S(1)}, bf16[6,320,256]{2,1,0:T(8,128)(2,1)}, u32[]{:S(2)}) copy-start(bf16[6,320,256]{2,1,0:T(8,128)(2,1)} %copy-done.12) | copy-start | bytes 2949124
  115.9 4.0 %copy-start.2 = (f32[2,4,128,128]{3,2,1,0:T(8,128)}, f32[2,4,128,128]{3,2,1,0:T(8,128)S(1)}, u32[]{:S(2)}) copy-start(f32[2,4,128,128]{3,2,1,0:T(8,128)S(1)} %get-tuple-element.19) | copy-start | bytes 1572868
  115.9 4.0 %copy-start.3 = (f32[2,4,128,128]{3,2,1,0:T(8,128)}, f32[2,4,128,128]{3,2,1,0:T(8,128)S(1)}, u32[]{:S(2)}) copy-start(f32[2,4,128,128]{3,2,1,0:T(8,128)S(1)} %get-tuple-element.20) | copy-start | bytes 1572868
  115.9 4.0 %copy-start.4 = (f32[4,128,128]{2,1,0:T(8,128)}, f32[4,128,128]{2,1,0:T(8,128)S(1)}, u32[]{:S(2)}) copy-start(f32[4,128,128]{2,1,0:T(8,128)S(1)} %get-tuple-element.22) | copy-start | bytes 786436
  119.8 49.8 %collective-permute-start.18 = (bf16[4,6,320,256]{3,2,1,0:T(8,128)(2,1)}, bf16[4,6,320,256]{3,2,1,0:T(8,128)(2,1)}, u32[]{:S(2)}, u32[]{:S(2)}) collective-permute-start(bf16[4,6,320,256]{3,2,1,0:T(8,128)(2,1)} %pad_maximum_fusion.mine_0.mine_1), channel_id=1, source_target_pairs={{0,1},{1,0},{2,3},{3,2},{4,5},{5,4},{6,7},{7,6},{8,9},{9,8},{10,11... | collective-permute-start | bytes 11796488 | tf_op jit(solution)/shard_map/ppermute | solution.py:272
  123.0 45.8 %collective-permute-start.13 = (bf16[2,2,2,4,128,128]{5,4,3,2,1,0:T(8,128)(2,1)S(1)}, bf16[2,2,2,4,128,128]{5,4,3,2,1,0:T(8,128)(2,1)S(1)}, u32[]{:S(2)}, u32[]{:S(2)}) collective-permute-start(bf16[2,2,2,4,128,128]{5,4,3,2,1,0:T(8,128)(2,1)S(1)} %copy_bitcast_fusion), channel_id=1, source_target_pairs={{0,2},{1,3},{2,0},{3,1},{4,6},{5,7},{6,4},{7,5},{8,10},{9,11},{10,... | collective-permute-start | bytes 3145736 | tf_op jit(solution)/shard_map/ppermute | solution.py:217
  126.5 30.8 %collective-permute-start.9 = (f32[2,4,128,128]{3,2,1,0:T(8,128)}, f32[2,4,128,128]{3,2,1,0:T(8,128)S(1)}, u32[]{:S(2)}, u32[]{:S(2)}) collective-permute-start(f32[2,4,128,128]{3,2,1,0:T(8,128)} %copy-done.3), channel_id=1, source_target_pairs={{16,0},{32,16},{48,32},{64,48},{80,64},{96,80},{112,96},{128,112},... | collective-permute-start | bytes 1572872 | tf_op jit(solution)/shard_map/ppermute | solution.py:33
  130.7 32.4 %collective-permute-start.8 = (f32[2,4,128,128]{3,2,1,0:T(8,128)}, f32[2,4,128,128]{3,2,1,0:T(8,128)S(1)}, u32[]{:S(2)}, u32[]{:S(2)}) collective-permute-start(f32[2,4,128,128]{3,2,1,0:T(8,128)} %copy-done.2), channel_id=1, source_target_pairs={{240,0},{0,16},{16,32},{32,48},{48,64},{64,80},{80,96},{96,112},{1... | collective-permute-start | bytes 1572872 | tf_op jit(solution)/shard_map/ppermute | solution.py:33
  132.6 22.2 %collective-permute-start.11 = (f32[4,128,128]{2,1,0:T(8,128)}, f32[4,128,128]{2,1,0:T(8,128)S(1)}, u32[]{:S(2)}, u32[]{:S(2)}) collective-permute-start(f32[4,128,128]{2,1,0:T(8,128)} %copy-done.4), channel_id=1, source_target_pairs={{32,0},{48,16},{64,32},{80,48},{96,64},{112,80},{128,96},{144,112}... | collective-permute-start | bytes 786440 | tf_op jit(solution)/shard_map/ppermute | solution.py:33
  154.8 14.8 %collective-permute-start.19 = (f32[960,128]{1,0:T(8,128)S(1)}, f32[960,128]{1,0:T(8,128)S(1)}, u32[]{:S(2)}, u32[]{:S(2)}) collective-permute-start(f32[960,128]{1,0:T(8,128)S(1)} %get-tuple-element.31.own), channel_id=1, source_target_pairs={{0,2},{1,3},{2,0},{3,1},{4,6},{5,7},{6,4},{7,5},{8,10},{9,11},{10,... | collective-permute-start | bytes 1474568 | tf_op jit(solution)/shard_map/ppermute | solution.py:242
  157.3 12.4 %copy-start.16 = (f32[2,4,128,128]{3,2,1,0:T(8,128)}, f32[2,4,128,128]{3,2,1,0:T(8,128)S(1)}, u32[]{:S(2)}) copy-start(f32[2,4,128,128]{3,2,1,0:T(8,128)S(1)} %collective-permute-done.9) | copy-start | bytes 1572868
  157.3 25.1 %collective-permute-start.10 = (f32[4,128,128]{2,1,0:T(8,128)S(1)}, f32[4,128,128]{2,1,0:T(8,128)}, u32[]{:S(2)}, u32[]{:S(2)}) collective-permute-start(f32[4,128,128]{2,1,0:T(8,128)S(1)} %get-tuple-element.21), channel_id=1, source_target_pairs={{224,0},{240,16},{0,32},{16,48},{32,64},{48,80},{64,96},{80,112},{... | collective-permute-start | bytes 786440 | tf_op jit(solution)/shard_map/ppermute | solution.py:33
  163.1 6.6 %copy-start.17 = (f32[2,4,128,128]{3,2,1,0:T(8,128)}, f32[2,4,128,128]{3,2,1,0:T(8,128)S(1)}, u32[]{:S(2)}) copy-start(f32[2,4,128,128]{3,2,1,0:T(8,128)S(1)} %collective-permute-done.8) | copy-start | bytes 1572868
  164.0 18.5 %collective-permute-start.12 = (f32[4,128,128]{2,1,0:T(8,128)}, f32[4,128,128]{2,1,0:T(8,128)}, u32[]{:S(2)}, u32[]{:S(2)}) collective-permute-start(f32[4,128,128]{2,1,0:T(8,128)} %fusion.5), channel_id=1, source_target_pairs={{0,256},{16,272},{32,288},{48,304},{64,320},{80,336},{96,352},{112... | collective-permute-start | bytes 786440 | tf_op jit(solution)/shard_map/ppermute | solution.py:280
  177.9 8.7 %all-to-all-start = ((f32[16,8,128]{2,1,0:T(8,128)}), f32[16,8,128]{2,1,0:T(8,128)S(1)}, u32[]{:S(2)}, u32[]{:S(2)}) async-start(f32[16,8,128]{2,1,0:T(8,128)} %broadcast_in_dim.9), calls=%async_computation | async-start | bytes 131072 | tf_op jit(solution)/shard_map/all_to_all | solution.py:312
  216.0 16.5 %all-to-all-start.2 = ((f32[8,8,128]{2,1,0:T(8,128)}), f32[8,8,128]{2,1,0:T(8,128)S(1)}, u32[]{:S(2)}, u32[]{:S(2)}) async-start(f32[8,8,128]{2,1,0:T(8,128)} %broadcast_in_dim.11), calls=%async_computation.2 | async-start | bytes 65536 | tf_op jit(solution)/shard_map/all_to_all | solution.py:312
Sparse Core Ops, SparseCore 0:
  10.1 80.8 all-gather.2

commit v8 on v7

--- a/solution.py
+++ b/solution.py
@@ -188,28 +188,26 @@
     ).astype(jnp.int32)
 
     stack_w = jnp.stack([w_in0, w_in1, w_out])
+    _, tan_in0, tan_in1, tan_out = lax.optimization_barrier(
+        (stack_w, tan_in0, tan_in1, tan_out)
+    )
+    stack_t = jnp.concatenate([tan_in0, tan_in1, tan_out], axis=0)
     both = jnp.stack([tokens, out_grad])
+    both, _ = lax.optimization_barrier((both, stack_t))
     other = lax.ppermute(both, "fsdp", [(i, (i + 16) % 32) for i in range(32)])
-    _, _, tan_in0, tan_in1, tan_out = lax.optimization_barrier(
-        (stack_w, other, tan_in0, tan_in1, tan_out)
-    )
-    stack_t = jnp.concatenate([tan_in0, tan_in1, tan_out], axis=0)
     full_w = lax.all_gather(stack_w, "seq", axis=0).reshape(2, 4, 2, 3, 320, 256)
 
     t_plus, t_minus = y_shift(stack_t, 1), y_shift(stack_t, -1)
 
-    both = jnp.stack([both, other])
-    far = [both] + [z_shift(both, step) for step in (4, 8, 12)]
-    z_hi = fsdp // 4 % 4
-    own = lax.dynamic_slice_in_dim(jnp.stack(far + far[:3]), (4 - z_hi) % 4, 4, axis=0)
+    own = lax.all_gather(jnp.stack([both, other]), "fsdp", axis=0, axis_index_groups=Z_FAR)
     plus = z_shift(own, 1)
     minus = z_shift(own, -1)
     two_x = z_shift(own[:, :, 0], 2)
     two_g = z_shift(own[:, :, 1], -2)
     acts = jnp.stack([own, plus, jnp.stack([two_x, two_g], axis=2), minus], axis=3)
 
-    half_plus, half_minus, _ = lax.optimization_barrier((t_plus[:3], t_minus[3:], acts))
-    half_plus, half_minus = y_shift(half_plus, 1), y_shift(half_minus, -1)
+    t_plus, t_minus, _ = lax.optimization_barrier((t_plus, t_minus, own))
+    half_plus, half_minus = y_shift(t_plus[:3], 1), y_shift(t_minus[3:], -1)
 
     partner = lax.dynamic_index_in_dim(
         acts.reshape((2, 2) + acts.shape[1:]), 1 - seq // 2 % 2, 1, False
@@ -266,7 +264,9 @@
         name="block_sums",
     )(place, hidden, full_w)
 
-    half_plus, half_minus, _ = lax.optimization_barrier((half_plus, half_minus, kept))
+    half_plus, half_minus, *_ = lax.optimization_barrier(
+        (half_plus, half_minus, plus, minus, two_x, two_g)
+    )
     t_two = jnp.concatenate([half_plus, half_minus], axis=0)
     mine = jnp.stack([stack_t, t_plus, t_two, t_minus])
     theirs = lax.ppermute(mine, "seq", [(i, i ^ 1) for i in range(16)])

time: 242 us -> 233 us (0.963)
  blocking collectives: 28.7 us -> 65.3 us
  starting transfers between devices: 108 us -> 75.2 us
  waiting for transfers between devices: 49.2 us -> 41.2 us
  local copies, waits for them, and re-layouts: 12 us -> 8.35 us
    ppermute x11 -> x8, starting transfers between devices: 64.7 us -> 30.5 us  [z_shift(): return lax.ppermute(array, 'fsdp', perm)]
    all_gather x0 -> x1, blocking collectives: none -> 31.5 us  [shards(): lax.all_gather(jnp.stack([both, other]), 'fsdp', axis=0, axis_index_group...]
    ppermute x11 -> x8, waiting for transfers between devices: 35.3 us -> 25.4 us  [z_shift(): return lax.ppermute(array, 'fsdp', perm)]
    all_to_all x1 -> x2, blocking collectives: 28.7 us -> 33.8 us  [sum_over(): lax.all_to_all(copies, axis, 0, 0, axis_index_groups=groups)]
    ppermute x4, starting transfers between devices: 12.9 us -> 16.5 us  [y_shift(): lax.ppermute(array, 'seq', [((i + 4 * step) % 16, i) for i in range(16)])]
    all_to_all x2 -> x1, starting transfers between devices: 12.8 us -> 9.69 us  [sum_over(): lax.all_to_all(copies, axis, 0, 0, axis_index_groups=groups)]
    all_to_all x2 -> x1, waiting for transfers between devices: 10.5 us -> 7.61 us  [sum_over(): lax.all_to_all(copies, axis, 0, 0, axis_index_groups=groups)]
    ppermute x1, waiting for transfers between devices: 2.67 us -> 5.1 us  [shards(): other = lax.ppermute(both, 'fsdp', [(i, (i + 16) % 32) for i in range(32)])]
  transfers between devices with their start and end apart: 23 -> 19, of which waited for: 7 -> 5; matrix products, arithmetic and copies ran while one was open for 5% -> 4% of each run, Pallas kernels for 7% -> 7%
where the time goes in v8:
time: 233 us; the launch traced here: 231 us
  starting transfers between devices  75.2 us (32%)
  blocking collectives  65.3 us (28%)
  waiting for transfers between devices  41.2 us (18%)
  Pallas kernels  16.9 us (7%)
  between operations  14.5 us (6%)
  other arithmetic  9.88 us (4%)
  local copies, waits for them, and re-layouts  8.35 us (4%)
    all_to_all x2, blocking collectives, sum_over(): lax.all_to_all(copies, axis, 0, 0, axis_index_groups=groups)  33.8 us
    all_gather x1, blocking collectives, shards(): lax.all_gather(jnp.stack([both, other]), 'fsdp', axis=0, axis_index_group...  31.5 us
    ppermute x8, starting transfers between devices, z_shift(): return lax.ppermute(array, 'fsdp', perm)  30.5 us
    ppermute x8, waiting for transfers between devices, z_shift(): return lax.ppermute(array, 'fsdp', perm)  25.4 us
    ppermute x4, starting transfers between devices, y_shift(): lax.ppermute(array, 'seq', [((i + 4 * step) % 16, i) for i in range(16)])  16.5 us
    all_to_all x1, starting transfers between devices, sum_over(): lax.all_to_all(copies, axis, 0, 0, axis_index_groups=groups)  9.69 us
    all_to_all x1, waiting for transfers between devices, sum_over(): lax.all_to_all(copies, axis, 0, 0, axis_index_groups=groups)  7.61 us
    pallas_call x1, Pallas kernels, shards(): pl.pallas_call(column_kernel, out_shape=jax.ShapeDtypeStruct((8, 128), F3...  7.56 us
  transfers between devices with their start and end apart: 19, of which 5 were waited for; matrix products, arithmetic and copies ran while one was open for 4% of the time, Pallas kernels for 7%

profile of v8, /device:TPU:24, one launch (start us, length us, event | category | flops | bytes accessed | tf_op | source)
XLA Modules:
  0.0 231.4 jit_solution(203188323943483282)
XLA Ops:
  7.2 0.0 all-gather.4.cloned.1.call-start
  7.2 1.9 pad_maximum_fusion.3
  9.1 0.0 all-gather.4.cloned.1.call-update
  9.1 1.0 constant_dynamic-update-slice_fusion.2
  10.1 1.0 constant_dynamic-update-slice_fusion.1
  11.1 1.0 constant_dynamic-update-slice_fusion
  12.1 2.7 %collective-permute-start.11 = (bf16[6,320,256]{2,1,0:T(8,128)(2,1)S(1)}, bf16[6,320,256]{2,1,0:T(8,128)(2,1)S(1)}, u32[]{:S(2)}, u32[]{:S(2)}) collective-permute-start(bf16[6,320,256]{2,1,0:T(8,128)(2,1)S(1)} %constant_dynamic-update-slice_fusion), channel_id=1, source_target_pairs={{4,0},{5,1},{6,2},{7,3},{8,4},{9,5},{10,6},{11,7},{12,8},{13,9},{1... | collective-permute-start | bytes 2949128 | tf_op jit(solution)/shard_map/ppermute | solution.py:37
  14.8 6.8 %collective-permute-start.12 = (bf16[6,320,256]{2,1,0:T(8,128)(2,1)S(1)}, bf16[6,320,256]{2,1,0:T(8,128)(2,1)S(1)}, u32[]{:S(2)}, u32[]{:S(2)}) collective-permute-start(bf16[6,320,256]{2,1,0:T(8,128)(2,1)S(1)} %constant_dynamic-update-slice_fusion), channel_id=1, source_target_pairs={{12,0},{13,1},{14,2},{15,3},{0,4},{1,5},{2,6},{3,7},{4,8},{5,9},{6... | collective-permute-start | bytes 2949128 | tf_op jit(solution)/shard_map/ppermute | solution.py:37
  21.6 0.8 pad_maximum_fusion.6
  22.4 2.5 %collective-permute-start = (bf16[2,128,128]{2,1,0:T(8,128)(2,1)S(1)}, bf16[2,128,128]{2,1,0:T(8,128)(2,1)S(1)}, u32[]{:S(2)}, u32[]{:S(2)}) collective-permute-start(bf16[2,128,128]{2,1,0:T(8,128)(2,1)S(1)} %pad_maximum_fusion.6), channel_id=1, source_target_pairs={{0,256},{16,272},{32,288},{48,304},{64,320},{80,336},{96,352},{112... | collective-permute-start | bytes 196616 | tf_op jit(solution)/shard_map/ppermute | solution.py:197
  24.9 5.1 %collective-permute-done = bf16[2,128,128]{2,1,0:T(8,128)(2,1)S(1)} collective-permute-done((bf16[2,128,128]{2,1,0:T(8,128)(2,1)S(1)}, bf16[2,128,128]{2,1,0:T(8,128)(2,1)S(1)}, u32[]{:S(2)}, u32[]{:S(2)}) %collective-permute-start) | collective-permute-done | bytes 65568 | tf_op jit(solution)/shard_map/ppermute | solution.py:197
  30.0 31.5 %all-gather = bf16[8,2,128,128]{3,2,1,0:T(8,128)(2,1)S(1)} all-gather(bf16[2,2,128,128]{3,2,1,0:T(8,128)(2,1)S(1)} %pad_maximum_fusion.5), channel_id=2, replica_groups={{0,64,128,192},{16,80,144,208},{32,96,160,224},{48,112,176,240},{256,32..., dimensions={0}, use_global_device_ids=true | all-gather | bytes 655360 | tf_op jit(solution)/shard_map/all_gather | solution.py:202
  61.6 1.9 collective-permute-start.2
  63.5 2.2 collective-permute-start.1
  65.7 3.7 %collective-permute-start.4 = (bf16[4,2,2,128,128]{4,3,2,1,0:T(8,128)(2,1)S(1)}, bf16[4,2,2,128,128]{4,3,2,1,0:T(8,128)(2,1)S(1)}, u32[]{:S(2)}, u32[]{:S(2)}) collective-permute-start(bf16[4,2,2,128,128]{4,3,2,1,0:T(8,128)(2,1)S(1)} %bitcast.60), channel_id=1, source_target_pairs={{240,0},{0,16},{16,32},{32,48},{48,64},{64,80},{80,96},{96,112},{1... | collective-permute-start | bytes 1572872 | tf_op jit(solution)/shard_map/ppermute | solution.py:33
  69.4 0.0 collective-permute-done.11
  69.4 0.0 collective-permute-done.12
  69.5 2.2 collective-permute-start.13
  71.7 4.8 %collective-permute-start.14 = (bf16[3,320,256]{2,1,0:T(8,128)(2,1)S(1)}, bf16[3,320,256]{2,1,0:T(8,128)(2,1)S(1)}, u32[]{:S(2)}, u32[]{:S(2)}) collective-permute-start(bf16[3,320,256]{2,1,0:T(8,128)(2,1)S(1)} %slice.49), channel_id=1, source_target_pairs={{12,0},{13,1},{14,2},{15,3},{0,4},{1,5},{2,6},{3,7},{4,8},{5,9},{6... | collective-permute-start | bytes 1474568 | tf_op jit(solution)/shard_map/ppermute | solution.py:37
  76.6 0.0 collective-permute-done.2
  76.6 4.8 %collective-permute-start.3 = (bf16[4,2,128,128]{3,2,1,0:T(8,128)(2,1)S(1)}, bf16[4,2,128,128]{3,2,1,0:T(8,128)(2,1)S(1)}, u32[]{:S(2)}, u32[]{:S(2)}) collective-permute-start(bf16[4,2,128,128]{3,2,1,0:T(8,128)(2,1)S(1)} %get-tuple-element.37), channel_id=1, source_target_pairs={{224,0},{240,16},{0,32},{16,48},{32,64},{48,80},{64,96},{80,112},{... | collective-permute-start | bytes 786440 | tf_op jit(solution)/shard_map/ppermute | solution.py:33
  81.4 7.0 %collective-permute-done.3 = bf16[4,2,128,128]{3,2,1,0:T(8,128)(2,1)S(1)} collective-permute-done((bf16[4,2,128,128]{3,2,1,0:T(8,128)(2,1)S(1)}, bf16[4,2,128,128]{3,2,1,0:T(8,128)(2,1)S(1)}, u32[]{:S(2)}, u32[]{:S(2)}) %collective-permute-start.3) | collective-permute-done | bytes 262176 | tf_op jit(solution)/shard_map/ppermute | solution.py:33
  88.4 0.0 collective-permute-done.1
  88.4 0.0 collective-permute-done.4
  88.4 0.0 collective-permute-done.13
  88.4 0.0 collective-permute-done.14
  88.4 0.1 maximum_bitcast_fusion
  88.5 0.0 copy-start.9
  88.5 2.2 pad_maximum_fusion.mine_0.mine_1
  90.7 1.9 collective-permute-start.15
  92.7 0.1 stack.110.place
  92.8 1.1 fusion.3
  93.9 5.6 %collective-permute-start.10 = (bf16[2,2,2,4,128,128]{5,4,3,2,1,0:T(8,128)(2,1)}, bf16[2,2,2,4,128,128]{5,4,3,2,1,0:T(8,128)(2,1)S(1)}, u32[]{:S(2)}, u32[]{:S(2)}) collective-permute-start(bf16[2,2,2,4,128,128]{5,4,3,2,1,0:T(8,128)(2,1)} %fusion.3), channel_id=1, source_target_pairs={{0,2},{1,3},{2,0},{3,1},{4,6},{5,7},{6,4},{7,5},{8,10},{9,11},{10,... | collective-permute-start | bytes 3145736 | tf_op jit(solution)/shard_map/ppermute | solution.py:215
  99.5 1.6 pad_maximum_fusion.1.acts
  101.1 0.0 all-gather.4.cloned.1.call-done
  101.1 3.2 %copy-done = bf16[48,320,256]{2,1,0:T(8,128)(2,1)S(1)} copy-done((bf16[48,320,256]{2,1,0:T(8,128)(2,1)S(1)}, bf16[48,320,256]{2,1,0:T(8,128)(2,1)}, u32[]{:S(2)}) %copy-start) | copy-done | bytes 7864344
  104.3 6.2 %primal.1 = (bf16[128,320]{1,0:T(8,128)(2,1)S(1)}, f32[960,128]{1,0:T(8,128)S(1)}) custom-call(s32[6]{0:T(128)S(1)} %stack.110.place, bf16[4,2,2,4,128,128]{5,4,3,2,1,0:T(8,128)(2,1)S(1)} %pad_maximum_fusion.1.acts, bf16[2,4,2,3,320,256]{5,4,3,2,1,0:T(8,128)(2,1)S(1)} %bitcast.56, f32[1,128]{1,0:T(1,128)S(1)} %convert_bitcast_fusion.mask), custom_call_target="tpu_custom_call" | custom-call | flops 1006632960 | bytes 10485760 | tf_op jit(solution)/shard_map/primal/pallas_call | solution.py:217
  110.5 3.2 %block_sums.1 = (f32[2,4,128,128]{3,2,1,0:T(8,128)S(1)}, f32[2,4,128,128]{3,2,1,0:T(8,128)S(1)}, f32[2,4,128,128]{3,2,1,0:T(8,128)S(1)}, f32[4,128,128]{2,1,0:T(8,128)S(1)}, f32[4,128,128]{2,1,0:T(8,128)S(1)}) custom-call(s32[6]{0:T(128)S(1)} %stack.110.place, bf16[128,320]{1,0:T(8,128)(2,1)S(1)} %get-tuple-element.22.hidden, ...), custom_call_target="tpu_custom_call" | custom-call | flops 335544320 | bytes 5242880 | tf_op jit(solution)/shard_map/block_sums/pallas_call | solution.py:245
  113.7 3.5 %collective-permute-start.5 = (f32[2,4,128,128]{3,2,1,0:T(8,128)S(1)}, f32[2,4,128,128]{3,2,1,0:T(8,128)S(1)}, u32[]{:S(2)}, u32[]{:S(2)}) collective-permute-start(f32[2,4,128,128]{3,2,1,0:T(8,128)S(1)} %get-tuple-element.24), channel_id=1, source_target_pairs={{240,0},{0,16},{16,32},{32,48},{48,64},{64,80},{80,96},{96,112},{1... | collective-permute-start | bytes 1572872 | tf_op jit(solution)/shard_map/ppermute | solution.py:33
  117.2 6.5 %collective-permute-start.6 = (f32[2,4,128,128]{3,2,1,0:T(8,128)S(1)}, f32[2,4,128,128]{3,2,1,0:T(8,128)S(1)}, u32[]{:S(2)}, u32[]{:S(2)}) collective-permute-start(f32[2,4,128,128]{3,2,1,0:T(8,128)S(1)} %get-tuple-element.25), channel_id=1, source_target_pairs={{16,0},{32,16},{48,32},{64,48},{80,64},{96,80},{112,96},{128,112},... | collective-permute-start | bytes 1572872 | tf_op jit(solution)/shard_map/ppermute | solution.py:33
  123.7 4.4 %collective-permute-start.8 = (f32[4,128,128]{2,1,0:T(8,128)S(1)}, f32[4,128,128]{2,1,0:T(8,128)S(1)}, u32[]{:S(2)}, u32[]{:S(2)}) collective-permute-start(f32[4,128,128]{2,1,0:T(8,128)S(1)} %get-tuple-element.27), channel_id=1, source_target_pairs={{32,0},{48,16},{64,32},{80,48},{96,64},{112,80},{128,96},{144,112}... | collective-permute-start | bytes 786440 | tf_op jit(solution)/shard_map/ppermute | solution.py:33
  128.1 18.4 %collective-permute-done.8 = f32[4,128,128]{2,1,0:T(8,128)S(1)} collective-permute-done((f32[4,128,128]{2,1,0:T(8,128)S(1)}, f32[4,128,128]{2,1,0:T(8,128)S(1)}, u32[]{:S(2)}, u32[]{:S(2)}) %collective-permute-start.8) | collective-permute-done | bytes 262176 | tf_op jit(solution)/shard_map/ppermute | solution.py:33
  146.5 2.4 %collective-permute-start.16 = (f32[960,128]{1,0:T(8,128)S(1)}, f32[960,128]{1,0:T(8,128)S(1)}, u32[]{:S(2)}, u32[]{:S(2)}) collective-permute-start(f32[960,128]{1,0:T(8,128)S(1)} %get-tuple-element.33.own), channel_id=1, source_target_pairs={{0,2},{1,3},{2,0},{3,1},{4,6},{5,7},{6,4},{7,5},{8,10},{9,11},{10,... | collective-permute-start | bytes 1474568 | tf_op jit(solution)/shard_map/ppermute | solution.py:240
  148.9 0.0 collective-permute-done.5
  148.9 0.0 copy-start.7
  149.0 3.6 %collective-permute-start.7 = (f32[4,128,128]{2,1,0:T(8,128)S(1)}, f32[4,128,128]{2,1,0:T(8,128)}, u32[]{:S(2)}, u32[]{:S(2)}) collective-permute-start(f32[4,128,128]{2,1,0:T(8,128)S(1)} %get-tuple-element.26), channel_id=1, source_target_pairs={{224,0},{240,16},{0,32},{16,48},{32,64},{48,80},{64,96},{80,112},{... | collective-permute-start | bytes 786440 | tf_op jit(solution)/shard_map/ppermute | solution.py:33
  152.5 0.0 collective-permute-done.6
  152.6 0.9 fusion.5
  153.4 6.0 %collective-permute-start.9 = (f32[4,128,128]{2,1,0:T(8,128)}, f32[4,128,128]{2,1,0:T(8,128)}, u32[]{:S(2)}, u32[]{:S(2)}) collective-permute-start(f32[4,128,128]{2,1,0:T(8,128)} %fusion.5), channel_id=1, source_target_pairs={{0,256},{16,272},{32,288},{48,304},{64,320},{80,336},{96,352},{112... | collective-permute-start | bytes 786440 | tf_op jit(solution)/shard_map/ppermute | solution.py:280
  159.5 0.0 collective-permute-done.10.partner
  159.5 0.0 collective-permute-done.15.theirs_0.theirs_1
  159.5 3.0 %collective-permute-done.16.their = f32[960,128]{1,0:T(8,128)S(1)} collective-permute-done((f32[960,128]{1,0:T(8,128)S(1)}, f32[960,128]{1,0:T(8,128)S(1)}, u32[]{:S(2)}, u32[]{:S(2)}) %collective-permute-start.16) | collective-permute-done | bytes 491552 | tf_op jit(solution)/shard_map/ppermute | solution.py:240
  162.5 7.6 %column.1 = f32[8,128]{1,0:T(8,128)S(1)} custom-call(s32[6]{0:T(128)S(1)} %stack.110.place, bf16[4,2,2,4,128,128]{5,4,3,2,1,0:T(8,128)(2,1)S(1)} %pad_maximum_fusion.1.acts, bf16[2,2,2,4,128,128]{5,4,3,2,1,0:T(8,128)(2,1)S(1)} %collective-permute-done.10.partner, bf16[4,6,320,256]{3,2,1,0:T(8,128)(2,1)} %pad_maximum_fusion.mine_0.mine_1, ...), custom_call_target="tpu_custom_call" | custom-call | flops 2013265920 | bytes 12582912 | tf_op jit(solution)/shard_map/column/pallas_call | solution.py:283
  170.1 0.0 copy-done.2
  170.1 8.5 %all_to_all.15 = f32[16,8,128]{2,1,0:T(8,128)S(1)} all-to-all(f32[16,8,128]{2,1,0:T(8,128)S(1)} %broadcast_in_dim.9), channel_id=1, replica_groups=mesh['fsdp'=32,'seq'=16] {'seq'}, dimensions={0} | all-to-all | bytes 131072 | tf_op jit(solution)/shard_map/all_to_all | solution.py:312
  178.6 0.0 collective-permute-done.7
  178.6 0.0 collective-permute-done.9
  178.6 1.3 fusion.8
  180.0 25.3 %all_to_all.16 = f32[4,136,128]{2,1,0:T(8,128)S(1)} all-to-all(f32[4,136,128]{2,1,0:T(8,128)S(1)} %pad_maximum_fusion.4), channel_id=1, replica_groups={{0,64,128,192},{16,80,144,208},{32,96,160,224},{48,112,176,240},{256,32..., dimensions={0} | all-to-all | bytes 557056 | tf_op jit(solution)/shard_map/all_to_all | solution.py:312
  205.3 0.6 broadcast_in_dim.11
  205.9 9.7 %all-to-all-start.2 = ((f32[8,8,128]{2,1,0:T(8,128)}), f32[8,8,128]{2,1,0:T(8,128)S(1)}, u32[]{:S(2)}, u32[]{:S(2)}) async-start(f32[8,8,128]{2,1,0:T(8,128)} %broadcast_in_dim.11), calls=%async_computation.2 | async-start | bytes 65536 | tf_op jit(solution)/shard_map/all_to_all | solution.py:312
  215.6 0.6 slice.84
  216.3 7.6 %all-to-all-done.2 = f32[8,8,128]{2,1,0:T(8,128)S(1)} async-done(((f32[8,8,128]{2,1,0:T(8,128)}), f32[8,8,128]{2,1,0:T(8,128)S(1)}, u32[]{:S(2)}, u32[]{:S(2)}) %all-to-all-start.2) | async-done | bytes 32800 | tf_op jit(solution)/shard_map/all_to_all | solution.py:312
  223.9 0.7 copy.35
  (29 shorter events, 0.2 us)
Async XLA Ops:
  7.2 93.9 %all-gather.4.cloned.1.call-start = ((), (), s32[]{:S(2)}) async-start(), calls=%async_computation.3 | async-start | bytes 8355840 | tf_op jit(solution)/shard_map/all_gather | solution.py:198
  12.1 57.3 %collective-permute-start.11 = (bf16[6,320,256]{2,1,0:T(8,128)(2,1)S(1)}, bf16[6,320,256]{2,1,0:T(8,128)(2,1)S(1)}, u32[]{:S(2)}, u32[]{:S(2)}) collective-permute-start(bf16[6,320,256]{2,1,0:T(8,128)(2,1)S(1)} %constant_dynamic-update-slice_fusion), channel_id=1, source_target_pairs={{4,0},{5,1},{6,2},{7,3},{8,4},{9,5},{10,6},{11,7},{12,8},{13,9},{1... | collective-permute-start | bytes 2949128 | tf_op jit(solution)/shard_map/ppermute | solution.py:37
  14.8 54.6 %collective-permute-start.12 = (bf16[6,320,256]{2,1,0:T(8,128)(2,1)S(1)}, bf16[6,320,256]{2,1,0:T(8,128)(2,1)S(1)}, u32[]{:S(2)}, u32[]{:S(2)}) collective-permute-start(bf16[6,320,256]{2,1,0:T(8,128)(2,1)S(1)} %constant_dynamic-update-slice_fusion), channel_id=1, source_target_pairs={{12,0},{13,1},{14,2},{15,3},{0,4},{1,5},{2,6},{3,7},{4,8},{5,9},{6... | collective-permute-start | bytes 2949128 | tf_op jit(solution)/shard_map/ppermute | solution.py:37
  22.4 7.7 %collective-permute-start = (bf16[2,128,128]{2,1,0:T(8,128)(2,1)S(1)}, bf16[2,128,128]{2,1,0:T(8,128)(2,1)S(1)}, u32[]{:S(2)}, u32[]{:S(2)}) collective-permute-start(bf16[2,128,128]{2,1,0:T(8,128)(2,1)S(1)} %pad_maximum_fusion.6), channel_id=1, source_target_pairs={{0,256},{16,272},{32,288},{48,304},{64,320},{80,336},{96,352},{112... | collective-permute-start | bytes 196616 | tf_op jit(solution)/shard_map/ppermute | solution.py:197
  61.6 31.2 %copy-start.3 = (bf16[8,2,128,128]{3,2,1,0:T(8,128)(2,1)}, bf16[8,2,128,128]{3,2,1,0:T(8,128)(2,1)S(1)}, u32[]{:S(2)}) copy-start(bf16[8,2,128,128]{3,2,1,0:T(8,128)(2,1)S(1)} %all-gather) | copy-start | bytes 1572868
  61.6 15.0 %collective-permute-start.2 = (bf16[4,2,128,128]{3,2,1,0:T(8,128)(2,1)S(1)}, bf16[4,2,128,128]{3,2,1,0:T(8,128)(2,1)S(1)}, u32[]{:S(2)}, u32[]{:S(2)}) collective-permute-start(bf16[4,2,128,128]{3,2,1,0:T(8,128)(2,1)S(1)} %get-tuple-element.36), channel_id=1, source_target_pairs={{32,0},{48,16},{64,32},{80,48},{96,64},{112,80},{128,96},{144,112}... | collective-permute-start | bytes 786440 | tf_op jit(solution)/shard_map/ppermute | solution.py:33
  63.5 24.8 %collective-permute-start.1 = (bf16[4,2,2,128,128]{4,3,2,1,0:T(8,128)(2,1)S(1)}, bf16[4,2,2,128,128]{4,3,2,1,0:T(8,128)(2,1)S(1)}, u32[]{:S(2)}, u32[]{:S(2)}) collective-permute-start(bf16[4,2,2,128,128]{4,3,2,1,0:T(8,128)(2,1)S(1)} %bitcast.59), channel_id=1, source_target_pairs={{16,0},{32,16},{48,32},{64,48},{80,64},{96,80},{112,96},{128,112},... | collective-permute-start | bytes 1572872 | tf_op jit(solution)/shard_map/ppermute | solution.py:33
  65.7 22.7 %collective-permute-start.4 = (bf16[4,2,2,128,128]{4,3,2,1,0:T(8,128)(2,1)S(1)}, bf16[4,2,2,128,128]{4,3,2,1,0:T(8,128)(2,1)S(1)}, u32[]{:S(2)}, u32[]{:S(2)}) collective-permute-start(bf16[4,2,2,128,128]{4,3,2,1,0:T(8,128)(2,1)S(1)} %bitcast.60), channel_id=1, source_target_pairs={{240,0},{0,16},{16,32},{32,48},{48,64},{64,80},{80,96},{96,112},{1... | collective-permute-start | bytes 1572872 | tf_op jit(solution)/shard_map/ppermute | solution.py:33
  69.5 18.9 %collective-permute-start.13 = (bf16[3,320,256]{2,1,0:T(8,128)(2,1)S(1)}, bf16[3,320,256]{2,1,0:T(8,128)(2,1)S(1)}, u32[]{:S(2)}, u32[]{:S(2)}) collective-permute-start(bf16[3,320,256]{2,1,0:T(8,128)(2,1)S(1)} %slice.48), channel_id=1, source_target_pairs={{4,0},{5,1},{6,2},{7,3},{8,4},{9,5},{10,6},{11,7},{12,8},{13,9},{1... | collective-permute-start | bytes 1474568 | tf_op jit(solution)/shard_map/ppermute | solution.py:37
  71.7 16.7 %collective-permute-start.14 = (bf16[3,320,256]{2,1,0:T(8,128)(2,1)S(1)}, bf16[3,320,256]{2,1,0:T(8,128)(2,1)S(1)}, u32[]{:S(2)}, u32[]{:S(2)}) collective-permute-start(bf16[3,320,256]{2,1,0:T(8,128)(2,1)S(1)} %slice.49), channel_id=1, source_target_pairs={{12,0},{13,1},{14,2},{15,3},{0,4},{1,5},{2,6},{3,7},{4,8},{5,9},{6... | collective-permute-start | bytes 1474568 | tf_op jit(solution)/shard_map/ppermute | solution.py:37
  76.6 11.8 %collective-permute-start.3 = (bf16[4,2,128,128]{3,2,1,0:T(8,128)(2,1)S(1)}, bf16[4,2,128,128]{3,2,1,0:T(8,128)(2,1)S(1)}, u32[]{:S(2)}, u32[]{:S(2)}) collective-permute-start(bf16[4,2,128,128]{3,2,1,0:T(8,128)(2,1)S(1)} %get-tuple-element.37), channel_id=1, source_target_pairs={{224,0},{240,16},{0,32},{16,48},{32,64},{48,80},{64,96},{80,112},{... | collective-permute-start | bytes 786440 | tf_op jit(solution)/shard_map/ppermute | solution.py:33
  88.4 4.4 %copy-start.6 = (bf16[4,2,128,128]{3,2,1,0:T(8,128)(2,1)}, bf16[4,2,128,128]{3,2,1,0:T(8,128)(2,1)S(1)}, u32[]{:S(2)}) copy-start(bf16[4,2,128,128]{3,2,1,0:T(8,128)(2,1)S(1)} %collective-permute-done.3) | copy-start | bytes 786436
  88.4 11.1 %copy-start.4 = (bf16[4,2,2,128,128]{4,3,2,1,0:T(8,128)(2,1)}, bf16[4,2,2,128,128]{4,3,2,1,0:T(8,128)(2,1)S(1)}, u32[]{:S(2)}) copy-start(bf16[4,2,2,128,128]{4,3,2,1,0:T(8,128)(2,1)S(1)} %collective-permute-done.1) | copy-start | bytes 1572868
  88.4 11.1 %copy-start.5 = (bf16[4,2,2,128,128]{4,3,2,1,0:T(8,128)(2,1)}, bf16[4,2,2,128,128]{4,3,2,1,0:T(8,128)(2,1)S(1)}, u32[]{:S(2)}) copy-start(bf16[4,2,2,128,128]{4,3,2,1,0:T(8,128)(2,1)S(1)} %collective-permute-done.4) | copy-start | bytes 1572868
  88.5 4.3 %copy-start.9 = (s32[128]{0:T(128)S(1)}, s32[128]{0:T(128)}, u32[]{:S(2)}) copy-start(s32[128]{0:T(128)} %param.11) | copy-start | bytes 1540
  90.7 68.8 %collective-permute-start.15 = (bf16[4,6,320,256]{3,2,1,0:T(8,128)(2,1)}, bf16[4,6,320,256]{3,2,1,0:T(8,128)(2,1)}, u32[]{:S(2)}, u32[]{:S(2)}) collective-permute-start(bf16[4,6,320,256]{3,2,1,0:T(8,128)(2,1)} %pad_maximum_fusion.mine_0.mine_1), channel_id=1, source_target_pairs={{0,1},{1,0},{2,3},{3,2},{4,5},{5,4},{6,7},{7,6},{8,9},{9,8},{10,11... | collective-permute-start | bytes 11796488 | tf_op jit(solution)/shard_map/ppermute | solution.py:272
  93.9 65.6 %collective-permute-start.10 = (bf16[2,2,2,4,128,128]{5,4,3,2,1,0:T(8,128)(2,1)}, bf16[2,2,2,4,128,128]{5,4,3,2,1,0:T(8,128)(2,1)S(1)}, u32[]{:S(2)}, u32[]{:S(2)}) collective-permute-start(bf16[2,2,2,4,128,128]{5,4,3,2,1,0:T(8,128)(2,1)} %fusion.3), channel_id=1, source_target_pairs={{0,2},{1,3},{2,0},{3,1},{4,6},{5,7},{6,4},{7,5},{8,10},{9,11},{10,... | collective-permute-start | bytes 3145736 | tf_op jit(solution)/shard_map/ppermute | solution.py:215
  101.1 3.2 %copy-start = (bf16[48,320,256]{2,1,0:T(8,128)(2,1)S(1)}, bf16[48,320,256]{2,1,0:T(8,128)(2,1)}, u32[]{:S(2)}) copy-start(bf16[48,320,256]{2,1,0:T(8,128)(2,1)} %all-gather.4.cloned.1.call-done) | copy-start | bytes 23592964
  104.3 6.2 %copy-start.1 = (bf16[48,320,256]{2,1,0:T(8,128)(2,1)S(1)}, bf16[48,320,256]{2,1,0:T(8,128)(2,1)}, u32[]{:S(2)}) copy-start(bf16[48,320,256]{2,1,0:T(8,128)(2,1)} %all-gather.4.cloned.1.call-done) | copy-start | bytes 23592964
  113.7 56.4 %copy-start.2 = (f32[2,4,128,128]{3,2,1,0:T(8,128)}, f32[2,4,128,128]{3,2,1,0:T(8,128)S(1)}, u32[]{:S(2)}) copy-start(f32[2,4,128,128]{3,2,1,0:T(8,128)S(1)} %get-tuple-element.23) | copy-start | bytes 1572868
  113.7 35.2 %collective-permute-start.5 = (f32[2,4,128,128]{3,2,1,0:T(8,128)S(1)}, f32[2,4,128,128]{3,2,1,0:T(8,128)S(1)}, u32[]{:S(2)}, u32[]{:S(2)}) collective-permute-start(f32[2,4,128,128]{3,2,1,0:T(8,128)S(1)} %get-tuple-element.24), channel_id=1, source_target_pairs={{240,0},{0,16},{16,32},{32,48},{48,64},{64,80},{80,96},{96,112},{1... | collective-permute-start | bytes 1572872 | tf_op jit(solution)/shard_map/ppermute | solution.py:33
  117.2 35.3 %collective-permute-start.6 = (f32[2,4,128,128]{3,2,1,0:T(8,128)S(1)}, f32[2,4,128,128]{3,2,1,0:T(8,128)S(1)}, u32[]{:S(2)}, u32[]{:S(2)}) collective-permute-start(f32[2,4,128,128]{3,2,1,0:T(8,128)S(1)} %get-tuple-element.25), channel_id=1, source_target_pairs={{16,0},{32,16},{48,32},{64,48},{80,64},{96,80},{112,96},{128,112},... | collective-permute-start | bytes 1572872 | tf_op jit(solution)/shard_map/ppermute | solution.py:33
  123.7 22.8 %collective-permute-start.8 = (f32[4,128,128]{2,1,0:T(8,128)S(1)}, f32[4,128,128]{2,1,0:T(8,128)S(1)}, u32[]{:S(2)}, u32[]{:S(2)}) collective-permute-start(f32[4,128,128]{2,1,0:T(8,128)S(1)} %get-tuple-element.27), channel_id=1, source_target_pairs={{32,0},{48,16},{64,32},{80,48},{96,64},{112,80},{128,96},{144,112}... | collective-permute-start | bytes 786440 | tf_op jit(solution)/shard_map/ppermute | solution.py:33
  146.5 16.0 %collective-permute-start.16 = (f32[960,128]{1,0:T(8,128)S(1)}, f32[960,128]{1,0:T(8,128)S(1)}, u32[]{:S(2)}, u32[]{:S(2)}) collective-permute-start(f32[960,128]{1,0:T(8,128)S(1)} %get-tuple-element.33.own), channel_id=1, source_target_pairs={{0,2},{1,3},{2,0},{3,1},{4,6},{5,7},{6,4},{7,5},{8,10},{9,11},{10,... | collective-permute-start | bytes 1474568 | tf_op jit(solution)/shard_map/ppermute | solution.py:240
  148.9 10.5 %copy-start.7 = (f32[2,4,128,128]{3,2,1,0:T(8,128)}, f32[2,4,128,128]{3,2,1,0:T(8,128)S(1)}, u32[]{:S(2)}) copy-start(f32[2,4,128,128]{3,2,1,0:T(8,128)S(1)} %collective-permute-done.5) | copy-start | bytes 1572868
  149.0 29.7 %collective-permute-start.7 = (f32[4,128,128]{2,1,0:T(8,128)S(1)}, f32[4,128,128]{2,1,0:T(8,128)}, u32[]{:S(2)}, u32[]{:S(2)}) collective-permute-start(f32[4,128,128]{2,1,0:T(8,128)S(1)} %get-tuple-element.26), channel_id=1, source_target_pairs={{224,0},{240,16},{0,32},{16,48},{32,64},{48,80},{64,96},{80,112},{... | collective-permute-start | bytes 786440 | tf_op jit(solution)/shard_map/ppermute | solution.py:33
  152.6 6.9 %copy-start.8 = (f32[2,4,128,128]{3,2,1,0:T(8,128)}, f32[2,4,128,128]{3,2,1,0:T(8,128)S(1)}, u32[]{:S(2)}) copy-start(f32[2,4,128,128]{3,2,1,0:T(8,128)S(1)} %collective-permute-done.6) | copy-start | bytes 1572868
  153.4 25.2 %collective-permute-start.9 = (f32[4,128,128]{2,1,0:T(8,128)}, f32[4,128,128]{2,1,0:T(8,128)}, u32[]{:S(2)}, u32[]{:S(2)}) collective-permute-start(f32[4,128,128]{2,1,0:T(8,128)} %fusion.5), channel_id=1, source_target_pairs={{0,256},{16,272},{32,288},{48,304},{64,320},{80,336},{96,352},{112... | collective-permute-start | bytes 786440 | tf_op jit(solution)/shard_map/ppermute | solution.py:280
  205.9 17.9 %all-to-all-start.2 = ((f32[8,8,128]{2,1,0:T(8,128)}), f32[8,8,128]{2,1,0:T(8,128)S(1)}, u32[]{:S(2)}, u32[]{:S(2)}) async-start(f32[8,8,128]{2,1,0:T(8,128)} %broadcast_in_dim.11), calls=%async_computation.2 | async-start | bytes 65536 | tf_op jit(solution)/shard_map/all_to_all | solution.py:312
Sparse Core Ops, SparseCore 0:
  10.1 71.3 all-gather.3

commit v9 on v8

--- a/solution.py
+++ b/solution.py
@@ -214,6 +214,13 @@
     )
     partner = lax.ppermute(partner, "seq", [(i, i ^ 2) for i in range(16)])
 
+    half_plus, half_minus, *_ = lax.optimization_barrier(
+        (half_plus, half_minus, plus, minus, two_x, two_g)
+    )
+    t_two = jnp.concatenate([half_plus, half_minus], axis=0)
+    mine = jnp.stack([stack_t, t_plus, t_two, t_minus])
+    theirs = lax.ppermute(mine, "seq", [(i, i ^ 1) for i in range(16)])
+
     hidden, factors = pl.pallas_call(
         primal_kernel,
         out_shape=(
@@ -237,6 +244,7 @@
         ),
         name="primal",
     )(place, acts, full_w, loss_mask.astype(F32)[None])
+    hidden, factors, theirs = lax.optimization_barrier((hidden, factors, theirs))
     their = lax.ppermute(factors, "seq", [(i, i ^ 2) for i in range(16)])
 
     by_x_hi = pl.BlockSpec((1, 4, 128, 128), lambda s, p: (s, 0, 0, 0))
@@ -264,22 +272,12 @@
         name="block_sums",
     )(place, hidden, full_w)
 
-    half_plus, half_minus, *_ = lax.optimization_barrier(
-        (half_plus, half_minus, plus, minus, two_x, two_g)
-    )
-    t_two = jnp.concatenate([half_plus, half_minus], axis=0)
-    mine = jnp.stack([stack_t, t_plus, t_two, t_minus])
-    theirs = lax.ppermute(mine, "seq", [(i, i ^ 1) for i in range(16)])
-
     up = z_shift(up, -1)
     down = z_shift(down, 1)
     two_up = z_shift(two_up, -2)
     two_down = z_shift(two_down, 2)
     away = kept[1] + up[1] + down[1] + two_down
-    partner, _ = lax.optimization_barrier((partner, away))
-    away = lax.ppermute(away, "fsdp", [(i, (i + 16) % 32) for i in range(32)])
-    partial = kept[0] + up[0] + down[0] + two_up + away
-
+    partner, _ = lax.optimization_barrier((partner, kept))
     terms = pl.pallas_call(
         column_kernel,
         out_shape=jax.ShapeDtypeStruct((8, 128), F32),
@@ -312,6 +310,9 @@
         return jnp.sum(lax.all_to_all(copies, axis, 0, 0, axis_index_groups=groups), axis=0)
 
     terms = sum_over(jnp.broadcast_to(terms[None], (16, 8, 128)), "seq", None)
+    away, terms = lax.optimization_barrier((away, terms))
+    away = lax.ppermute(away, "fsdp", [(i, (i + 16) % 32) for i in range(32)])
+    partial = kept[0] + up[0] + down[0] + two_up + away
     copies = jnp.broadcast_to(terms[None], (4, 8, 128))
     both = sum_over(jnp.concatenate([partial, copies], axis=1), "fsdp", Z_FAR)
     block_out = both[:128].astype(BF16)

time: 233 us -> 222 us (0.953)
  waiting for transfers between devices: 41.2 us -> 30.6 us
  blocking collectives: 65.3 us -> 62.3 us
    ppermute x8, waiting for transfers between devices: 25.4 us -> 7.69 us  [z_shift(): return lax.ppermute(array, 'fsdp', perm)]
    ppermute x1, waiting for transfers between devices: 0.01 us -> 7.07 us  [shards(): away = lax.ppermute(away, 'fsdp', [(i, (i + 16) % 32) for i in range(32)])]
    all_to_all x1 -> x2, starting transfers between devices: 9.69 us -> 15 us  [sum_over(): lax.all_to_all(copies, axis, 0, 0, axis_index_groups=groups)]
    ppermute x1, waiting for transfers between devices: 3.05 us -> 0.01 us  [shards(): their = lax.ppermute(factors, 'seq', [(i, i ^ 2) for i in range(16)])]
    all_to_all x2 -> x1, blocking collectives: 33.8 us -> 31.2 us  [sum_over(): lax.all_to_all(copies, axis, 0, 0, axis_index_groups=groups)]
    all_to_all x1 -> x2, waiting for transfers between devices: 7.61 us -> 10.1 us  [sum_over(): lax.all_to_all(copies, axis, 0, 0, axis_index_groups=groups)]
    unnamed x23 -> x21, local copies, waits for them, and re-layouts: 5.91 us -> 5.9 us
  transfers between devices with their start and end apart: 19 -> 20, of which waited for: 5 -> 6; matrix products, arithmetic and copies ran while one was open for 4% -> 5% of each run, Pallas kernels for 7% -> 8%
where the time goes in v9:
time: 222 us; the launch traced here: 220 us
  starting transfers between devices  76.3 us (34%)
  blocking collectives  62.3 us (28%)
  waiting for transfers between devices  30.6 us (14%)
  Pallas kernels  17.7 us (8%)
  between operations  14.5 us (7%)
  other arithmetic  10.2 us (5%)
  local copies, waits for them, and re-layouts  8.95 us (4%)
    all_to_all x1, blocking collectives, sum_over(): lax.all_to_all(copies, axis, 0, 0, axis_index_groups=groups)  31.2 us
    all_gather x1, blocking collectives, shards(): lax.all_gather(jnp.stack([both, other]), 'fsdp', axis=0, axis_index_group...  31.1 us
    ppermute x8, starting transfers between devices, z_shift(): return lax.ppermute(array, 'fsdp', perm)  30.4 us
    ppermute x4, starting transfers between devices, y_shift(): lax.ppermute(array, 'seq', [((i + 4 * step) % 16, i) for i in range(16)])  15.3 us
    all_to_all x2, starting transfers between devices, sum_over(): lax.all_to_all(copies, axis, 0, 0, axis_index_groups=groups)  15 us
    all_to_all x2, waiting for transfers between devices, sum_over(): lax.all_to_all(copies, axis, 0, 0, axis_index_groups=groups)  10.1 us
    ppermute x8, waiting for transfers between devices, z_shift(): return lax.ppermute(array, 'fsdp', perm)  7.69 us
    pallas_call x1, Pallas kernels, shards(): pl.pallas_call(column_kernel, out_shape=jax.ShapeDtypeStruct((8, 128), F3...  7.57 us
  transfers between devices with their start and end apart: 20, of which 6 were waited for; matrix products, arithmetic and copies ran while one was open for 5% of the time, Pallas kernels for 8%

profile of v9, /device:TPU:24, one launch (start us, length us, event | category | flops | bytes accessed | tf_op | source)
XLA Modules:
  0.0 220.5 jit_solution(4618687670258774189)
XLA Ops:
  7.2 0.0 all-gather.4.cloned.1.call-start
  7.2 1.9 pad_maximum_fusion.3
  9.1 0.0 all-gather.4.cloned.1.call-update
  9.1 1.0 constant_dynamic-update-slice_fusion.2
  10.1 1.0 constant_dynamic-update-slice_fusion.1
  11.1 1.0 constant_dynamic-update-slice_fusion
  12.1 7.5 %collective-permute-start.6 = (bf16[6,320,256]{2,1,0:T(8,128)(2,1)S(1)}, bf16[6,320,256]{2,1,0:T(8,128)(2,1)S(1)}, u32[]{:S(2)}, u32[]{:S(2)}) collective-permute-start(bf16[6,320,256]{2,1,0:T(8,128)(2,1)S(1)} %constant_dynamic-update-slice_fusion), channel_id=1, source_target_pairs={{12,0},{13,1},{14,2},{15,3},{0,4},{1,5},{2,6},{3,7},{4,8},{5,9},{6... | collective-permute-start | bytes 2949128 | tf_op jit(solution)/shard_map/ppermute | solution.py:37
  19.7 1.9 collective-permute-start.5
  21.6 0.8 pad_maximum_fusion.6
  22.4 1.9 collective-permute-start
  24.3 5.7 %collective-permute-done = bf16[2,128,128]{2,1,0:T(8,128)(2,1)S(1)} collective-permute-done((bf16[2,128,128]{2,1,0:T(8,128)(2,1)S(1)}, bf16[2,128,128]{2,1,0:T(8,128)(2,1)S(1)}, u32[]{:S(2)}, u32[]{:S(2)}) %collective-permute-start) | collective-permute-done | bytes 65568 | tf_op jit(solution)/shard_map/ppermute | solution.py:197
  30.0 31.1 %all-gather = bf16[8,2,128,128]{3,2,1,0:T(8,128)(2,1)S(1)} all-gather(bf16[2,2,128,128]{3,2,1,0:T(8,128)(2,1)S(1)} %pad_maximum_fusion.5), channel_id=2, replica_groups={{0,64,128,192},{16,80,144,208},{32,96,160,224},{48,112,176,240},{256,32..., dimensions={0}, use_global_device_ids=true | all-gather | bytes 655360 | tf_op jit(solution)/shard_map/all_gather | solution.py:202
  61.2 1.9 collective-permute-start.2
  63.1 2.8 %collective-permute-start.4 = (bf16[4,2,2,128,128]{4,3,2,1,0:T(8,128)(2,1)S(1)}, bf16[4,2,2,128,128]{4,3,2,1,0:T(8,128)(2,1)S(1)}, u32[]{:S(2)}, u32[]{:S(2)}) collective-permute-start(bf16[4,2,2,128,128]{4,3,2,1,0:T(8,128)(2,1)S(1)} %bitcast.59), channel_id=1, source_target_pairs={{240,0},{0,16},{16,32},{32,48},{48,64},{64,80},{80,96},{96,112},{1... | collective-permute-start | bytes 1572872 | tf_op jit(solution)/shard_map/ppermute | solution.py:33
  65.9 4.3 %collective-permute-start.1 = (bf16[4,2,2,128,128]{4,3,2,1,0:T(8,128)(2,1)S(1)}, bf16[4,2,2,128,128]{4,3,2,1,0:T(8,128)(2,1)S(1)}, u32[]{:S(2)}, u32[]{:S(2)}) collective-permute-start(bf16[4,2,2,128,128]{4,3,2,1,0:T(8,128)(2,1)S(1)} %bitcast.60), channel_id=1, source_target_pairs={{16,0},{32,16},{48,32},{64,48},{80,64},{96,80},{112,96},{128,112},... | collective-permute-start | bytes 1572872 | tf_op jit(solution)/shard_map/ppermute | solution.py:33
  70.2 0.0 collective-permute-done.6
  70.2 0.0 collective-permute-done.5
  70.3 1.9 collective-permute-start.8
  72.2 3.9 %collective-permute-start.7 = (bf16[3,320,256]{2,1,0:T(8,128)(2,1)S(1)}, bf16[3,320,256]{2,1,0:T(8,128)(2,1)S(1)}, u32[]{:S(2)}, u32[]{:S(2)}) collective-permute-start(bf16[3,320,256]{2,1,0:T(8,128)(2,1)S(1)} %slice.42), channel_id=1, source_target_pairs={{4,0},{5,1},{6,2},{7,3},{8,4},{9,5},{10,6},{11,7},{12,8},{13,9},{1... | collective-permute-start | bytes 1474568 | tf_op jit(solution)/shard_map/ppermute | solution.py:37
  76.1 0.0 collective-permute-done.2
  76.1 3.6 %collective-permute-start.3 = (bf16[4,2,128,128]{3,2,1,0:T(8,128)(2,1)S(1)}, bf16[4,2,128,128]{3,2,1,0:T(8,128)(2,1)S(1)}, u32[]{:S(2)}, u32[]{:S(2)}) collective-permute-start(bf16[4,2,128,128]{3,2,1,0:T(8,128)(2,1)S(1)} %get-tuple-element.47), channel_id=1, source_target_pairs={{224,0},{240,16},{0,32},{16,48},{32,64},{48,80},{64,96},{80,112},{... | collective-permute-start | bytes 786440 | tf_op jit(solution)/shard_map/ppermute | solution.py:33
  79.8 7.2 %collective-permute-done.3 = bf16[4,2,128,128]{3,2,1,0:T(8,128)(2,1)S(1)} collective-permute-done((bf16[4,2,128,128]{3,2,1,0:T(8,128)(2,1)S(1)}, bf16[4,2,128,128]{3,2,1,0:T(8,128)(2,1)S(1)}, u32[]{:S(2)}, u32[]{:S(2)}) %collective-permute-start.3) | collective-permute-done | bytes 262176 | tf_op jit(solution)/shard_map/ppermute | solution.py:33
  87.0 0.0 collective-permute-done.4
  87.0 0.0 collective-permute-done.1
  87.0 0.0 collective-permute-done.8
  87.0 0.0 collective-permute-done.7
  87.0 0.1 maximum_bitcast_fusion
  87.1 0.0 copy-start.8
  87.1 2.2 pad_maximum_fusion.mine_0.mine_1
  89.3 1.9 collective-permute-start.9
  91.3 1.1 fusion.3
  92.4 5.2 %collective-permute-start.14 = (bf16[2,2,2,4,128,128]{5,4,3,2,1,0:T(8,128)(2,1)}, bf16[2,2,2,4,128,128]{5,4,3,2,1,0:T(8,128)(2,1)S(1)}, u32[]{:S(2)}, u32[]{:S(2)}) collective-permute-start(bf16[2,2,2,4,128,128]{5,4,3,2,1,0:T(8,128)(2,1)} %fusion.3), channel_id=1, source_target_pairs={{0,2},{1,3},{2,0},{3,1},{4,6},{5,7},{6,4},{7,5},{8,10},{9,11},{10,... | collective-permute-start | bytes 3145736 | tf_op jit(solution)/shard_map/ppermute | solution.py:215
  97.7 0.1 stack.110.place
  97.8 1.6 pad_maximum_fusion.1.acts
  99.4 0.0 all-gather.4.cloned.1.call-done
  99.4 3.2 %copy-done = bf16[48,320,256]{2,1,0:T(8,128)(2,1)S(1)} copy-done((bf16[48,320,256]{2,1,0:T(8,128)(2,1)S(1)}, bf16[48,320,256]{2,1,0:T(8,128)(2,1)}, u32[]{:S(2)}) %copy-start) | copy-done | bytes 7864344
  102.7 6.2 %primal.1 = (bf16[128,320]{1,0:T(8,128)(2,1)S(1)}, f32[960,128]{1,0:T(8,128)S(1)}) custom-call(s32[6]{0:T(128)S(1)} %stack.110.place, bf16[4,2,2,4,128,128]{5,4,3,2,1,0:T(8,128)(2,1)S(1)} %pad_maximum_fusion.1.acts, bf16[2,4,2,3,320,256]{5,4,3,2,1,0:T(8,128)(2,1)S(1)} %bitcast.56, f32[1,128]{1,0:T(1,128)S(1)} %convert_bitcast_fusion.mask), custom_call_target="tpu_custom_call" | custom-call | flops 1006632960 | bytes 10485760 | tf_op jit(solution)/shard_map/primal/pallas_call | solution.py:224
  108.8 0.0 collective-permute-done.9.theirs_0.theirs_1
  108.9 1.9 collective-permute-start.15
  110.8 3.9 %block_sums.1 = (f32[2,4,128,128]{3,2,1,0:T(8,128)S(1)}, f32[2,4,128,128]{3,2,1,0:T(8,128)}, f32[2,4,128,128]{3,2,1,0:T(8,128)}, f32[4,128,128]{2,1,0:T(8,128)S(1)}, f32[4,128,128]{2,1,0:T(8,128)}) custom-call(s32[6]{0:T(128)S(1)} %stack.110.place, bf16[128,320]{1,0:T(8,128)(2,1)S(1)} %get-tuple-element.33.hidden, bf16[2,4,2,3,320,256]{5,4,3,2,1,0:T(8,128)(2,1)S(1)} %bitcast.57), custom_call_target="tpu_custom_call" | custom-call | flops 335544320 | bytes 5242880 | tf_op jit(solution)/shard_map/block_sums/pallas_call | solution.py:253
  114.7 3.6 %collective-permute-start.10 = (f32[2,4,128,128]{3,2,1,0:T(8,128)}, f32[2,4,128,128]{3,2,1,0:T(8,128)}, u32[]{:S(2)}, u32[]{:S(2)}) collective-permute-start(f32[2,4,128,128]{3,2,1,0:T(8,128)} %get-tuple-element.35), channel_id=1, source_target_pairs={{240,0},{0,16},{16,32},{32,48},{48,64},{64,80},{80,96},{96,112},{1... | collective-permute-start | bytes 1572872 | tf_op jit(solution)/shard_map/ppermute | solution.py:33
  118.3 7.5 %collective-permute-start.11 = (f32[2,4,128,128]{3,2,1,0:T(8,128)}, f32[2,4,128,128]{3,2,1,0:T(8,128)}, u32[]{:S(2)}, u32[]{:S(2)}) collective-permute-start(f32[2,4,128,128]{3,2,1,0:T(8,128)} %get-tuple-element.36), channel_id=1, source_target_pairs={{16,0},{32,16},{48,32},{64,48},{80,64},{96,80},{112,96},{128,112},... | collective-permute-start | bytes 1572872 | tf_op jit(solution)/shard_map/ppermute | solution.py:33
  125.8 4.4 %collective-permute-start.13 = (f32[4,128,128]{2,1,0:T(8,128)}, f32[4,128,128]{2,1,0:T(8,128)}, u32[]{:S(2)}, u32[]{:S(2)}) collective-permute-start(f32[4,128,128]{2,1,0:T(8,128)} %get-tuple-element.38), channel_id=1, source_target_pairs={{32,0},{48,16},{64,32},{80,48},{96,64},{112,80},{128,96},{144,112}... | collective-permute-start | bytes 786440 | tf_op jit(solution)/shard_map/ppermute | solution.py:33
  130.2 0.0 collective-permute-done.14.partner
  130.2 2.4 %collective-permute-start.12 = (f32[4,128,128]{2,1,0:T(8,128)S(1)}, f32[4,128,128]{2,1,0:T(8,128)}, u32[]{:S(2)}, u32[]{:S(2)}) collective-permute-start(f32[4,128,128]{2,1,0:T(8,128)S(1)} %get-tuple-element.37), channel_id=1, source_target_pairs={{224,0},{240,16},{0,32},{16,48},{32,64},{48,80},{64,96},{80,112},{... | collective-permute-start | bytes 786440 | tf_op jit(solution)/shard_map/ppermute | solution.py:33
  132.6 0.0 collective-permute-done.15.their
  132.6 7.6 %column.1 = f32[8,128]{1,0:T(8,128)S(1)} custom-call(s32[6]{0:T(128)S(1)} %stack.110.place, bf16[4,2,2,4,128,128]{5,4,3,2,1,0:T(8,128)(2,1)S(1)} %pad_maximum_fusion.1.acts, bf16[2,2,2,4,128,128]{5,4,3,2,1,0:T(8,128)(2,1)S(1)} %collective-permute-done.14.partner, bf16[4,6,320,256]{3,2,1,0:T(8,128)(2,1)} %pad_maximum_fusion.mine_0.mine_1, ...), custom_call_target="tpu_custom_call" | custom-call | flops 2013265920 | bytes 12582912 | tf_op jit(solution)/shard_map/column/pallas_call | solution.py:281
  140.1 0.6 broadcast_in_dim.9
  140.8 7.4 %all-to-all-start = ((f32[16,8,128]{2,1,0:T(8,128)}), f32[16,8,128]{2,1,0:T(8,128)S(1)}, u32[]{:S(2)}, u32[]{:S(2)}) async-start(f32[16,8,128]{2,1,0:T(8,128)} %broadcast_in_dim.9), calls=%async_computation | async-start | bytes 131072 | tf_op jit(solution)/shard_map/all_to_all | solution.py:310
  148.2 0.5 collective-permute-done.13
  148.6 0.0 collective-permute-done.10
  148.6 0.0 collective-permute-done.11
  148.6 1.2 fusion.5
  149.9 2.4 %all-to-all-done = f32[16,8,128]{2,1,0:T(8,128)S(1)} async-done(((f32[16,8,128]{2,1,0:T(8,128)}), f32[16,8,128]{2,1,0:T(8,128)S(1)}, u32[]{:S(2)}, u32[]{:S(2)}) %all-to-all-start) | async-done | bytes 65568 | tf_op jit(solution)/shard_map/all_to_all | solution.py:310
  152.3 4.6 %collective-permute-start.16 = (f32[4,128,128]{2,1,0:T(8,128)S(1)}, f32[4,128,128]{2,1,0:T(8,128)S(1)}, u32[]{:S(2)}, u32[]{:S(2)}) collective-permute-start(f32[4,128,128]{2,1,0:T(8,128)S(1)} %fusion.5), channel_id=1, source_target_pairs={{0,256},{16,272},{32,288},{48,304},{64,320},{80,336},{96,352},{112... | collective-permute-start | bytes 786440 | tf_op jit(solution)/shard_map/ppermute | solution.py:314
  157.0 0.0 collective-permute-done.12
  157.0 7.1 %collective-permute-done.16 = f32[4,128,128]{2,1,0:T(8,128)S(1)} collective-permute-done((f32[4,128,128]{2,1,0:T(8,128)S(1)}, f32[4,128,128]{2,1,0:T(8,128)S(1)}, u32[]{:S(2)}, u32[]{:S(2)}) %collective-permute-start.16) | collective-permute-done | bytes 262176 | tf_op jit(solution)/shard_map/ppermute | solution.py:314
  164.0 1.3 fusion.8
  165.3 31.2 %all_to_all.15 = f32[4,136,128]{2,1,0:T(8,128)S(1)} all-to-all(f32[4,136,128]{2,1,0:T(8,128)S(1)} %pad_maximum_fusion.4), channel_id=1, replica_groups={{0,64,128,192},{16,80,144,208},{32,96,160,224},{48,112,176,240},{256,32..., dimensions={0} | all-to-all | bytes 557056 | tf_op jit(solution)/shard_map/all_to_all | solution.py:310
  196.6 0.6 broadcast_in_dim.11
  197.2 7.6 %all-to-all-start.2 = ((f32[8,8,128]{2,1,0:T(8,128)}), f32[8,8,128]{2,1,0:T(8,128)S(1)}, u32[]{:S(2)}, u32[]{:S(2)}) async-start(f32[8,8,128]{2,1,0:T(8,128)} %broadcast_in_dim.11), calls=%async_computation.2 | async-start | bytes 65536 | tf_op jit(solution)/shard_map/all_to_all | solution.py:310
  204.7 0.6 slice.84
  205.4 7.6 %all-to-all-done.2 = f32[8,8,128]{2,1,0:T(8,128)S(1)} async-done(((f32[8,8,128]{2,1,0:T(8,128)}), f32[8,8,128]{2,1,0:T(8,128)S(1)}, u32[]{:S(2)}, u32[]{:S(2)}) %all-to-all-start.2) | async-done | bytes 32800 | tf_op jit(solution)/shard_map/all_to_all | solution.py:310
  213.0 0.7 copy.35
  (28 shorter events, 0.2 us)
Async XLA Ops:
  7.2 92.3 %all-gather.4.cloned.1.call-start = ((), (), s32[]{:S(2)}) async-start(), calls=%async_computation.3 | async-start | bytes 8355840 | tf_op jit(solution)/shard_map/all_gather | solution.py:198
  12.1 58.0 %collective-permute-start.6 = (bf16[6,320,256]{2,1,0:T(8,128)(2,1)S(1)}, bf16[6,320,256]{2,1,0:T(8,128)(2,1)S(1)}, u32[]{:S(2)}, u32[]{:S(2)}) collective-permute-start(bf16[6,320,256]{2,1,0:T(8,128)(2,1)S(1)} %constant_dynamic-update-slice_fusion), channel_id=1, source_target_pairs={{12,0},{13,1},{14,2},{15,3},{0,4},{1,5},{2,6},{3,7},{4,8},{5,9},{6... | collective-permute-start | bytes 2949128 | tf_op jit(solution)/shard_map/ppermute | solution.py:37
  19.7 50.5 %collective-permute-start.5 = (bf16[6,320,256]{2,1,0:T(8,128)(2,1)S(1)}, bf16[6,320,256]{2,1,0:T(8,128)(2,1)S(1)}, u32[]{:S(2)}, u32[]{:S(2)}) collective-permute-start(bf16[6,320,256]{2,1,0:T(8,128)(2,1)S(1)} %constant_dynamic-update-slice_fusion), channel_id=1, source_target_pairs={{4,0},{5,1},{6,2},{7,3},{8,4},{9,5},{10,6},{11,7},{12,8},{13,9},{1... | collective-permute-start | bytes 2949128 | tf_op jit(solution)/shard_map/ppermute | solution.py:37
  22.4 7.7 %collective-permute-start = (bf16[2,128,128]{2,1,0:T(8,128)(2,1)S(1)}, bf16[2,128,128]{2,1,0:T(8,128)(2,1)S(1)}, u32[]{:S(2)}, u32[]{:S(2)}) collective-permute-start(bf16[2,128,128]{2,1,0:T(8,128)(2,1)S(1)} %pad_maximum_fusion.6), channel_id=1, source_target_pairs={{0,256},{16,272},{32,288},{48,304},{64,320},{80,336},{96,352},{112... | collective-permute-start | bytes 196616 | tf_op jit(solution)/shard_map/ppermute | solution.py:197
  61.1 30.2 %copy-start.3 = (bf16[8,2,128,128]{3,2,1,0:T(8,128)(2,1)}, bf16[8,2,128,128]{3,2,1,0:T(8,128)(2,1)S(1)}, u32[]{:S(2)}) copy-start(bf16[8,2,128,128]{3,2,1,0:T(8,128)(2,1)S(1)} %all-gather) | copy-start | bytes 1572868
  61.2 15.0 %collective-permute-start.2 = (bf16[4,2,128,128]{3,2,1,0:T(8,128)(2,1)S(1)}, bf16[4,2,128,128]{3,2,1,0:T(8,128)(2,1)S(1)}, u32[]{:S(2)}, u32[]{:S(2)}) collective-permute-start(bf16[4,2,128,128]{3,2,1,0:T(8,128)(2,1)S(1)} %get-tuple-element.46), channel_id=1, source_target_pairs={{32,0},{48,16},{64,32},{80,48},{96,64},{112,80},{128,96},{144,112}... | collective-permute-start | bytes 786440 | tf_op jit(solution)/shard_map/ppermute | solution.py:33
  63.1 23.9 %collective-permute-start.4 = (bf16[4,2,2,128,128]{4,3,2,1,0:T(8,128)(2,1)S(1)}, bf16[4,2,2,128,128]{4,3,2,1,0:T(8,128)(2,1)S(1)}, u32[]{:S(2)}, u32[]{:S(2)}) collective-permute-start(bf16[4,2,2,128,128]{4,3,2,1,0:T(8,128)(2,1)S(1)} %bitcast.59), channel_id=1, source_target_pairs={{240,0},{0,16},{16,32},{32,48},{48,64},{64,80},{80,96},{96,112},{1... | collective-permute-start | bytes 1572872 | tf_op jit(solution)/shard_map/ppermute | solution.py:33
  65.9 21.1 %collective-permute-start.1 = (bf16[4,2,2,128,128]{4,3,2,1,0:T(8,128)(2,1)S(1)}, bf16[4,2,2,128,128]{4,3,2,1,0:T(8,128)(2,1)S(1)}, u32[]{:S(2)}, u32[]{:S(2)}) collective-permute-start(bf16[4,2,2,128,128]{4,3,2,1,0:T(8,128)(2,1)S(1)} %bitcast.60), channel_id=1, source_target_pairs={{16,0},{32,16},{48,32},{64,48},{80,64},{96,80},{112,96},{128,112},... | collective-permute-start | bytes 1572872 | tf_op jit(solution)/shard_map/ppermute | solution.py:33
  70.3 16.7 %collective-permute-start.8 = (bf16[3,320,256]{2,1,0:T(8,128)(2,1)S(1)}, bf16[3,320,256]{2,1,0:T(8,128)(2,1)S(1)}, u32[]{:S(2)}, u32[]{:S(2)}) collective-permute-start(bf16[3,320,256]{2,1,0:T(8,128)(2,1)S(1)} %slice.43), channel_id=1, source_target_pairs={{12,0},{13,1},{14,2},{15,3},{0,4},{1,5},{2,6},{3,7},{4,8},{5,9},{6... | collective-permute-start | bytes 1474568 | tf_op jit(solution)/shard_map/ppermute | solution.py:37
  72.2 14.8 %collective-permute-start.7 = (bf16[3,320,256]{2,1,0:T(8,128)(2,1)S(1)}, bf16[3,320,256]{2,1,0:T(8,128)(2,1)S(1)}, u32[]{:S(2)}, u32[]{:S(2)}) collective-permute-start(bf16[3,320,256]{2,1,0:T(8,128)(2,1)S(1)} %slice.42), channel_id=1, source_target_pairs={{4,0},{5,1},{6,2},{7,3},{8,4},{9,5},{10,6},{11,7},{12,8},{13,9},{1... | collective-permute-start | bytes 1474568 | tf_op jit(solution)/shard_map/ppermute | solution.py:37
  76.1 15.2 %copy-start.6 = (bf16[4,2,128,128]{3,2,1,0:T(8,128)(2,1)}, bf16[4,2,128,128]{3,2,1,0:T(8,128)(2,1)S(1)}, u32[]{:S(2)}) copy-start(bf16[4,2,128,128]{3,2,1,0:T(8,128)(2,1)S(1)} %collective-permute-done.2) | copy-start | bytes 786436
  76.1 10.8 %collective-permute-start.3 = (bf16[4,2,128,128]{3,2,1,0:T(8,128)(2,1)S(1)}, bf16[4,2,128,128]{3,2,1,0:T(8,128)(2,1)S(1)}, u32[]{:S(2)}, u32[]{:S(2)}) collective-permute-start(bf16[4,2,128,128]{3,2,1,0:T(8,128)(2,1)S(1)} %get-tuple-element.47), channel_id=1, source_target_pairs={{224,0},{240,16},{0,32},{16,48},{32,64},{48,80},{64,96},{80,112},{... | collective-permute-start | bytes 786440 | tf_op jit(solution)/shard_map/ppermute | solution.py:33
  87.0 4.3 %copy-start.7 = (bf16[4,2,128,128]{3,2,1,0:T(8,128)(2,1)}, bf16[4,2,128,128]{3,2,1,0:T(8,128)(2,1)S(1)}, u32[]{:S(2)}) copy-start(bf16[4,2,128,128]{3,2,1,0:T(8,128)(2,1)S(1)} %collective-permute-done.3) | copy-start | bytes 786436
  87.0 4.3 %copy-start.4 = (bf16[4,2,2,128,128]{4,3,2,1,0:T(8,128)(2,1)}, bf16[4,2,2,128,128]{4,3,2,1,0:T(8,128)(2,1)S(1)}, u32[]{:S(2)}) copy-start(bf16[4,2,2,128,128]{4,3,2,1,0:T(8,128)(2,1)S(1)} %collective-permute-done.4) | copy-start | bytes 1572868
  87.0 4.3 %copy-start.5 = (bf16[4,2,2,128,128]{4,3,2,1,0:T(8,128)(2,1)}, bf16[4,2,2,128,128]{4,3,2,1,0:T(8,128)(2,1)S(1)}, u32[]{:S(2)}) copy-start(bf16[4,2,2,128,128]{4,3,2,1,0:T(8,128)(2,1)S(1)} %collective-permute-done.1) | copy-start | bytes 1572868
  87.1 10.6 %copy-start.8 = (s32[128]{0:T(128)S(1)}, s32[128]{0:T(128)}, u32[]{:S(2)}) copy-start(s32[128]{0:T(128)} %param.11) | copy-start | bytes 1540
  89.3 19.5 %collective-permute-start.9 = (bf16[4,6,320,256]{3,2,1,0:T(8,128)(2,1)}, bf16[4,6,320,256]{3,2,1,0:T(8,128)(2,1)}, u32[]{:S(2)}, u32[]{:S(2)}) collective-permute-start(bf16[4,6,320,256]{3,2,1,0:T(8,128)(2,1)} %pad_maximum_fusion.mine_0.mine_1), channel_id=1, source_target_pairs={{0,1},{1,0},{2,3},{3,2},{4,5},{5,4},{6,7},{7,6},{8,9},{9,8},{10,11... | collective-permute-start | bytes 11796488 | tf_op jit(solution)/shard_map/ppermute | solution.py:222
  92.4 37.8 %collective-permute-start.14 = (bf16[2,2,2,4,128,128]{5,4,3,2,1,0:T(8,128)(2,1)}, bf16[2,2,2,4,128,128]{5,4,3,2,1,0:T(8,128)(2,1)S(1)}, u32[]{:S(2)}, u32[]{:S(2)}) collective-permute-start(bf16[2,2,2,4,128,128]{5,4,3,2,1,0:T(8,128)(2,1)} %fusion.3), channel_id=1, source_target_pairs={{0,2},{1,3},{2,0},{3,1},{4,6},{5,7},{6,4},{7,5},{8,10},{9,11},{10,... | collective-permute-start | bytes 3145736 | tf_op jit(solution)/shard_map/ppermute | solution.py:215
  99.4 3.2 %copy-start = (bf16[48,320,256]{2,1,0:T(8,128)(2,1)S(1)}, bf16[48,320,256]{2,1,0:T(8,128)(2,1)}, u32[]{:S(2)}) copy-start(bf16[48,320,256]{2,1,0:T(8,128)(2,1)} %all-gather.4.cloned.1.call-done) | copy-start | bytes 23592964
  102.7 8.1 %copy-start.1 = (bf16[48,320,256]{2,1,0:T(8,128)(2,1)S(1)}, bf16[48,320,256]{2,1,0:T(8,128)(2,1)}, u32[]{:S(2)}) copy-start(bf16[48,320,256]{2,1,0:T(8,128)(2,1)} %all-gather.4.cloned.1.call-done) | copy-start | bytes 23592964
  108.9 23.7 %collective-permute-start.15 = (f32[960,128]{1,0:T(8,128)S(1)}, f32[960,128]{1,0:T(8,128)S(1)}, u32[]{:S(2)}, u32[]{:S(2)}) collective-permute-start(f32[960,128]{1,0:T(8,128)S(1)} %get-tuple-element.41.own), channel_id=1, source_target_pairs={{0,2},{1,3},{2,0},{3,1},{4,6},{5,7},{6,4},{7,5},{8,10},{9,11},{10,... | collective-permute-start | bytes 1474568 | tf_op jit(solution)/shard_map/ppermute | solution.py:248
  114.7 25.4 %copy-start.2 = (f32[2,4,128,128]{3,2,1,0:T(8,128)}, f32[2,4,128,128]{3,2,1,0:T(8,128)S(1)}, u32[]{:S(2)}) copy-start(f32[2,4,128,128]{3,2,1,0:T(8,128)S(1)} %get-tuple-element.34) | copy-start | bytes 1572868
  114.7 33.9 %collective-permute-start.10 = (f32[2,4,128,128]{3,2,1,0:T(8,128)}, f32[2,4,128,128]{3,2,1,0:T(8,128)}, u32[]{:S(2)}, u32[]{:S(2)}) collective-permute-start(f32[2,4,128,128]{3,2,1,0:T(8,128)} %get-tuple-element.35), channel_id=1, source_target_pairs={{240,0},{0,16},{16,32},{32,48},{48,64},{64,80},{80,96},{96,112},{1... | collective-permute-start | bytes 1572872 | tf_op jit(solution)/shard_map/ppermute | solution.py:33
  118.3 30.3 %collective-permute-start.11 = (f32[2,4,128,128]{3,2,1,0:T(8,128)}, f32[2,4,128,128]{3,2,1,0:T(8,128)}, u32[]{:S(2)}, u32[]{:S(2)}) collective-permute-start(f32[2,4,128,128]{3,2,1,0:T(8,128)} %get-tuple-element.36), channel_id=1, source_target_pairs={{16,0},{32,16},{48,32},{64,48},{80,64},{96,80},{112,96},{128,112},... | collective-permute-start | bytes 1572872 | tf_op jit(solution)/shard_map/ppermute | solution.py:33
  125.8 22.8 %collective-permute-start.13 = (f32[4,128,128]{2,1,0:T(8,128)}, f32[4,128,128]{2,1,0:T(8,128)}, u32[]{:S(2)}, u32[]{:S(2)}) collective-permute-start(f32[4,128,128]{2,1,0:T(8,128)} %get-tuple-element.38), channel_id=1, source_target_pairs={{32,0},{48,16},{64,32},{80,48},{96,64},{112,80},{128,96},{144,112}... | collective-permute-start | bytes 786440 | tf_op jit(solution)/shard_map/ppermute | solution.py:33
  130.2 26.8 %collective-permute-start.12 = (f32[4,128,128]{2,1,0:T(8,128)S(1)}, f32[4,128,128]{2,1,0:T(8,128)}, u32[]{:S(2)}, u32[]{:S(2)}) collective-permute-start(f32[4,128,128]{2,1,0:T(8,128)S(1)} %get-tuple-element.37), channel_id=1, source_target_pairs={{224,0},{240,16},{0,32},{16,48},{32,64},{48,80},{64,96},{80,112},{... | collective-permute-start | bytes 786440 | tf_op jit(solution)/shard_map/ppermute | solution.py:33
  140.8 11.5 %all-to-all-start = ((f32[16,8,128]{2,1,0:T(8,128)}), f32[16,8,128]{2,1,0:T(8,128)S(1)}, u32[]{:S(2)}, u32[]{:S(2)}) async-start(f32[16,8,128]{2,1,0:T(8,128)} %broadcast_in_dim.9), calls=%async_computation | async-start | bytes 131072 | tf_op jit(solution)/shard_map/all_to_all | solution.py:310
  152.3 11.7 %collective-permute-start.16 = (f32[4,128,128]{2,1,0:T(8,128)S(1)}, f32[4,128,128]{2,1,0:T(8,128)S(1)}, u32[]{:S(2)}, u32[]{:S(2)}) collective-permute-start(f32[4,128,128]{2,1,0:T(8,128)S(1)} %fusion.5), channel_id=1, source_target_pairs={{0,256},{16,272},{32,288},{48,304},{64,320},{80,336},{96,352},{112... | collective-permute-start | bytes 786440 | tf_op jit(solution)/shard_map/ppermute | solution.py:314
  197.2 15.8 %all-to-all-start.2 = ((f32[8,8,128]{2,1,0:T(8,128)}), f32[8,8,128]{2,1,0:T(8,128)S(1)}, u32[]{:S(2)}, u32[]{:S(2)}) async-start(f32[8,8,128]{2,1,0:T(8,128)} %broadcast_in_dim.11), calls=%async_computation.2 | async-start | bytes 65536 | tf_op jit(solution)/shard_map/all_to_all | solution.py:310
Sparse Core Ops, SparseCore 0:
  10.1 71.4 all-gather.3

commit v10 on v9

--- a/solution.py
+++ b/solution.py
@@ -14,7 +14,7 @@
 NT = (((1,), (1,)), ((), ()))
 
 Z_FAR = [[h * 16 + q * 4 + r for q in range(4)] for h in range(2) for r in range(4)]
-X_AND_NEAR = [[h * 16 + q * 4 + r for h in range(2) for r in range(4)] for q in range(4)]
+Z_NEAR = [[h * 16 + q * 4 + r for r in range(4)] for h in range(2) for q in range(4)]
 
 
 def gelu_value_slope(value):
@@ -310,13 +310,15 @@
         return jnp.sum(lax.all_to_all(copies, axis, 0, 0, axis_index_groups=groups), axis=0)
 
     terms = sum_over(jnp.broadcast_to(terms[None], (16, 8, 128)), "seq", None)
-    away, terms = lax.optimization_barrier((away, terms))
+    away, terms, two_up = lax.optimization_barrier((away, terms, two_up))
+    away = jnp.concatenate([away.reshape(512, 128), terms], axis=0)
     away = lax.ppermute(away, "fsdp", [(i, (i + 16) % 32) for i in range(32)])
-    partial = kept[0] + up[0] + down[0] + two_up + away
+    partial = kept[0] + up[0] + down[0] + two_up + away[:512].reshape(4, 128, 128)
+    terms = terms + away[512:]
     copies = jnp.broadcast_to(terms[None], (4, 8, 128))
     both = sum_over(jnp.concatenate([partial, copies], axis=1), "fsdp", Z_FAR)
     block_out = both[:128].astype(BF16)
-    terms = sum_over(jnp.broadcast_to(both[None, 128:], (8, 8, 128)), "fsdp", X_AND_NEAR)
+    terms = sum_over(jnp.broadcast_to(both[None, 128:], (4, 8, 128)), "fsdp", Z_NEAR)
     return (block_out, terms[:EXAMPLES, :2])
 
 

time: 222 us -> 218 us (0.982)
  waiting for transfers between devices: 30.6 us -> 28.1 us
  starting transfers between devices: 76.3 us -> 74 us
    all_to_all x2, waiting for transfers between devices: 10.1 us -> 7.43 us  [sum_over(): lax.all_to_all(copies, axis, 0, 0, axis_index_groups=groups)]
    all_to_all x2, starting transfers between devices: 15 us -> 12.7 us  [sum_over(): lax.all_to_all(copies, axis, 0, 0, axis_index_groups=groups)]
where the time goes in v10:
time: 218 us; the launch traced here: 216 us
  starting transfers between devices  74 us (34%)
  blocking collectives  62.3 us (29%)
  waiting for transfers between devices  28.1 us (13%)
  Pallas kernels  17.7 us (8%)
  between operations  14.5 us (7%)
  other arithmetic  10.3 us (5%)
  local copies, waits for them, and re-layouts  8.97 us (4%)
    all_to_all x1, blocking collectives, sum_over(): lax.all_to_all(copies, axis, 0, 0, axis_index_groups=groups)  31.2 us
    all_gather x1, blocking collectives, shards(): lax.all_gather(jnp.stack([both, other]), 'fsdp', axis=0, axis_index_group...  31.1 us
    ppermute x8, starting transfers between devices, z_shift(): return lax.ppermute(array, 'fsdp', perm)  30.4 us
    ppermute x4, starting transfers between devices, y_shift(): lax.ppermute(array, 'seq', [((i + 4 * step) % 16, i) for i in range(16)])  15.3 us
    all_to_all x2, starting transfers between devices, sum_over(): lax.all_to_all(copies, axis, 0, 0, axis_index_groups=groups)  12.7 us
    ppermute x8, waiting for transfers between devices, z_shift(): return lax.ppermute(array, 'fsdp', perm)  7.69 us
    pallas_call x1, Pallas kernels, shards(): pl.pallas_call(column_kernel, out_shape=jax.ShapeDtypeStruct((8, 128), F3...  7.57 us
    all_to_all x2, waiting for transfers between devices, sum_over(): lax.all_to_all(copies, axis, 0, 0, axis_index_groups=groups)  7.43 us
  transfers between devices with their start and end apart: 20, of which 6 were waited for; matrix products, arithmetic and copies ran while one was open for 5% of the time, Pallas kernels for 8%

profile of v10, /device:TPU:24, one launch (start us, length us, event | category | flops | bytes accessed | tf_op | source)
XLA Modules:
  0.0 215.8 jit_solution(12359337389330912115)
XLA Ops:
  7.2 0.0 all-gather.4.cloned.1.call-start
  7.2 1.9 pad_maximum_fusion.3
  9.1 0.0 all-gather.4.cloned.1.call-update
  9.1 1.0 constant_dynamic-update-slice_fusion.2
  10.1 1.0 constant_dynamic-update-slice_fusion.1
  11.1 1.0 constant_dynamic-update-slice_fusion
  12.1 7.5 %collective-permute-start.6 = (bf16[6,320,256]{2,1,0:T(8,128)(2,1)S(1)}, bf16[6,320,256]{2,1,0:T(8,128)(2,1)S(1)}, u32[]{:S(2)}, u32[]{:S(2)}) collective-permute-start(bf16[6,320,256]{2,1,0:T(8,128)(2,1)S(1)} %constant_dynamic-update-slice_fusion), channel_id=1, source_target_pairs={{12,0},{13,1},{14,2},{15,3},{0,4},{1,5},{2,6},{3,7},{4,8},{5,9},{6... | collective-permute-start | bytes 2949128 | tf_op jit(solution)/shard_map/ppermute | solution.py:37
  19.7 1.9 collective-permute-start.5
  21.6 0.8 pad_maximum_fusion.7
  22.4 1.9 collective-permute-start
  24.3 5.7 %collective-permute-done = bf16[2,128,128]{2,1,0:T(8,128)(2,1)S(1)} collective-permute-done((bf16[2,128,128]{2,1,0:T(8,128)(2,1)S(1)}, bf16[2,128,128]{2,1,0:T(8,128)(2,1)S(1)}, u32[]{:S(2)}, u32[]{:S(2)}) %collective-permute-start) | collective-permute-done | bytes 65568 | tf_op jit(solution)/shard_map/ppermute | solution.py:197
  30.0 31.1 %all-gather = bf16[8,2,128,128]{3,2,1,0:T(8,128)(2,1)S(1)} all-gather(bf16[2,2,128,128]{3,2,1,0:T(8,128)(2,1)S(1)} %pad_maximum_fusion.6), channel_id=2, replica_groups={{0,64,128,192},{16,80,144,208},{32,96,160,224},{48,112,176,240},{256,32..., dimensions={0}, use_global_device_ids=true | all-gather | bytes 655360 | tf_op jit(solution)/shard_map/all_gather | solution.py:202
  61.2 1.9 collective-permute-start.2
  63.1 2.8 %collective-permute-start.4 = (bf16[4,2,2,128,128]{4,3,2,1,0:T(8,128)(2,1)S(1)}, bf16[4,2,2,128,128]{4,3,2,1,0:T(8,128)(2,1)S(1)}, u32[]{:S(2)}, u32[]{:S(2)}) collective-permute-start(bf16[4,2,2,128,128]{4,3,2,1,0:T(8,128)(2,1)S(1)} %bitcast.61), channel_id=1, source_target_pairs={{240,0},{0,16},{16,32},{32,48},{48,64},{64,80},{80,96},{96,112},{1... | collective-permute-start | bytes 1572872 | tf_op jit(solution)/shard_map/ppermute | solution.py:33
  65.9 4.3 %collective-permute-start.1 = (bf16[4,2,2,128,128]{4,3,2,1,0:T(8,128)(2,1)S(1)}, bf16[4,2,2,128,128]{4,3,2,1,0:T(8,128)(2,1)S(1)}, u32[]{:S(2)}, u32[]{:S(2)}) collective-permute-start(bf16[4,2,2,128,128]{4,3,2,1,0:T(8,128)(2,1)S(1)} %bitcast.62), channel_id=1, source_target_pairs={{16,0},{32,16},{48,32},{64,48},{80,64},{96,80},{112,96},{128,112},... | collective-permute-start | bytes 1572872 | tf_op jit(solution)/shard_map/ppermute | solution.py:33
  70.2 0.0 collective-permute-done.6
  70.2 0.0 collective-permute-done.5
  70.3 1.9 collective-permute-start.8
  72.2 3.9 %collective-permute-start.7 = (bf16[3,320,256]{2,1,0:T(8,128)(2,1)S(1)}, bf16[3,320,256]{2,1,0:T(8,128)(2,1)S(1)}, u32[]{:S(2)}, u32[]{:S(2)}) collective-permute-start(bf16[3,320,256]{2,1,0:T(8,128)(2,1)S(1)} %slice.48), channel_id=1, source_target_pairs={{4,0},{5,1},{6,2},{7,3},{8,4},{9,5},{10,6},{11,7},{12,8},{13,9},{1... | collective-permute-start | bytes 1474568 | tf_op jit(solution)/shard_map/ppermute | solution.py:37
  76.1 0.0 collective-permute-done.2
  76.1 3.6 %collective-permute-start.3 = (bf16[4,2,128,128]{3,2,1,0:T(8,128)(2,1)S(1)}, bf16[4,2,128,128]{3,2,1,0:T(8,128)(2,1)S(1)}, u32[]{:S(2)}, u32[]{:S(2)}) collective-permute-start(bf16[4,2,128,128]{3,2,1,0:T(8,128)(2,1)S(1)} %get-tuple-element.49), channel_id=1, source_target_pairs={{224,0},{240,16},{0,32},{16,48},{32,64},{48,80},{64,96},{80,112},{... | collective-permute-start | bytes 786440 | tf_op jit(solution)/shard_map/ppermute | solution.py:33
  79.8 7.2 %collective-permute-done.3 = bf16[4,2,128,128]{3,2,1,0:T(8,128)(2,1)S(1)} collective-permute-done((bf16[4,2,128,128]{3,2,1,0:T(8,128)(2,1)S(1)}, bf16[4,2,128,128]{3,2,1,0:T(8,128)(2,1)S(1)}, u32[]{:S(2)}, u32[]{:S(2)}) %collective-permute-start.3) | collective-permute-done | bytes 262176 | tf_op jit(solution)/shard_map/ppermute | solution.py:33
  87.0 0.0 collective-permute-done.4
  87.0 0.0 collective-permute-done.1
  87.0 0.0 collective-permute-done.8
  87.0 0.0 collective-permute-done.7
  87.0 0.1 maximum_bitcast_fusion
  87.1 0.0 copy-start.8
  87.1 2.2 %pad_maximum_fusion.mine_0.mine_1 = bf16[4,6,320,256]{3,2,1,0:T(8,128)(2,1)} fusion(bf16[1,6,320,256]{3,2,1,0:T(8,128)(2,1)S(1)} %bitcast.65, bf16[1,6,320,256]{3,2,1,0:T(8,128)(2,1)S(1)} %maximum_bitcast_fusion, bf16[1,6,320,256]{3,2,1,0:T(8,128)(2,1)S(1)} %bitcast.66, bf16[1,6,320,256]{3,2,1,0:T(8,128)(2,1)S(1)} %bitcast.71), kind=kLoop, calls=%fused_computation | loop fusion | flops 5898240 | bytes 7864320 | tf_op jit(solution)/shard_map/stack | solution.py:221
  89.3 1.9 collective-permute-start.9
  91.3 1.1 fusion.3
  92.4 5.2 %collective-permute-start.13 = (bf16[2,2,2,4,128,128]{5,4,3,2,1,0:T(8,128)(2,1)}, bf16[2,2,2,4,128,128]{5,4,3,2,1,0:T(8,128)(2,1)S(1)}, u32[]{:S(2)}, u32[]{:S(2)}) collective-permute-start(bf16[2,2,2,4,128,128]{5,4,3,2,1,0:T(8,128)(2,1)} %fusion.3), channel_id=1, source_target_pairs={{0,2},{1,3},{2,0},{3,1},{4,6},{5,7},{6,4},{7,5},{8,10},{9,11},{10,... | collective-permute-start | bytes 3145736 | tf_op jit(solution)/shard_map/ppermute | solution.py:215
  97.7 0.1 stack.110.place
  97.8 1.6 pad_maximum_fusion.1.acts
  99.4 0.0 all-gather.4.cloned.1.call-done
  99.4 3.2 %copy-done = bf16[48,320,256]{2,1,0:T(8,128)(2,1)S(1)} copy-done((bf16[48,320,256]{2,1,0:T(8,128)(2,1)S(1)}, bf16[48,320,256]{2,1,0:T(8,128)(2,1)}, u32[]{:S(2)}) %copy-start) | copy-done | bytes 7864344
  102.7 6.2 %primal.1 = (bf16[128,320]{1,0:T(8,128)(2,1)S(1)}, f32[960,128]{1,0:T(8,128)S(1)}) custom-call(s32[6]{0:T(128)S(1)} %stack.110.place, bf16[4,2,2,4,128,128]{5,4,3,2,1,0:T(8,128)(2,1)S(1)} %pad_maximum_fusion.1.acts, bf16[2,4,2,3,320,256]{5,4,3,2,1,0:T(8,128)(2,1)S(1)} %bitcast.58, f32[1,128]{1,0:T(1,128)S(1)} %convert_bitcast_fusion.mask), custom_call_target="tpu_custom_call" | custom-call | flops 1006632960 | bytes 10485760 | tf_op jit(solution)/shard_map/primal/pallas_call | solution.py:224
  108.8 0.0 collective-permute-done.9.theirs_0.theirs_1
  108.9 1.9 collective-permute-start.14
  110.8 3.9 %block_sums.1 = (f32[2,4,128,128]{3,2,1,0:T(8,128)S(1)}, f32[2,4,128,128]{3,2,1,0:T(8,128)}, f32[2,4,128,128]{3,2,1,0:T(8,128)}, f32[4,128,128]{2,1,0:T(8,128)S(1)}, f32[4,128,128]{2,1,0:T(8,128)}) custom-call(s32[6]{0:T(128)S(1)} %stack.110.place, bf16[128,320]{1,0:T(8,128)(2,1)S(1)} %get-tuple-element.34.hidden, bf16[2,4,2,3,320,256]{5,4,3,2,1,0:T(8,128)(2,1)S(1)} %bitcast.59), custom_call_target="tpu_custom_call" | custom-call | flops 335544320 | bytes 5242880 | tf_op jit(solution)/shard_map/block_sums/pallas_call | solution.py:253
  114.7 3.6 %collective-permute-start.10 = (f32[2,4,128,128]{3,2,1,0:T(8,128)}, f32[2,4,128,128]{3,2,1,0:T(8,128)}, u32[]{:S(2)}, u32[]{:S(2)}) collective-permute-start(f32[2,4,128,128]{3,2,1,0:T(8,128)} %get-tuple-element.36), channel_id=1, source_target_pairs={{240,0},{0,16},{16,32},{32,48},{48,64},{64,80},{80,96},{96,112},{1... | collective-permute-start | bytes 1572872 | tf_op jit(solution)/shard_map/ppermute | solution.py:33
  118.3 7.5 %collective-permute-start.11 = (f32[2,4,128,128]{3,2,1,0:T(8,128)}, f32[2,4,128,128]{3,2,1,0:T(8,128)}, u32[]{:S(2)}, u32[]{:S(2)}) collective-permute-start(f32[2,4,128,128]{3,2,1,0:T(8,128)} %get-tuple-element.37), channel_id=1, source_target_pairs={{16,0},{32,16},{48,32},{64,48},{80,64},{96,80},{112,96},{128,112},... | collective-permute-start | bytes 1572872 | tf_op jit(solution)/shard_map/ppermute | solution.py:33
  125.8 4.4 %collective-permute-start.12 = (f32[4,128,128]{2,1,0:T(8,128)}, f32[4,128,128]{2,1,0:T(8,128)}, u32[]{:S(2)}, u32[]{:S(2)}) collective-permute-start(f32[4,128,128]{2,1,0:T(8,128)} %get-tuple-element.38), channel_id=1, source_target_pairs={{32,0},{48,16},{64,32},{80,48},{96,64},{112,80},{128,96},{144,112}... | collective-permute-start | bytes 786440 | tf_op jit(solution)/shard_map/ppermute | solution.py:33
  130.2 0.0 collective-permute-done.13.partner
  130.2 2.4 %collective-permute-start.15 = (f32[4,128,128]{2,1,0:T(8,128)S(1)}, f32[4,128,128]{2,1,0:T(8,128)}, u32[]{:S(2)}, u32[]{:S(2)}) collective-permute-start(f32[4,128,128]{2,1,0:T(8,128)S(1)} %get-tuple-element.42), channel_id=1, source_target_pairs={{224,0},{240,16},{0,32},{16,48},{32,64},{48,80},{64,96},{80,112},{... | collective-permute-start | bytes 786440 | tf_op jit(solution)/shard_map/ppermute | solution.py:33
  132.6 0.0 collective-permute-done.14.their
  132.6 7.6 %column.1 = f32[8,128]{1,0:T(8,128)S(1)} custom-call(s32[6]{0:T(128)S(1)} %stack.110.place, bf16[4,2,2,4,128,128]{5,4,3,2,1,0:T(8,128)(2,1)S(1)} %pad_maximum_fusion.1.acts, bf16[2,2,2,4,128,128]{5,4,3,2,1,0:T(8,128)(2,1)S(1)} %collective-permute-done.13.partner, bf16[4,6,320,256]{3,2,1,0:T(8,128)(2,1)} %pad_maximum_fusion.mine_0.mine_1, ...), custom_call_target="tpu_custom_call" | custom-call | flops 2013265920 | bytes 12582912 | tf_op jit(solution)/shard_map/column/pallas_call | solution.py:281
  140.1 0.6 broadcast_in_dim.9
  140.8 7.4 %all-to-all-start = ((f32[16,8,128]{2,1,0:T(8,128)}), f32[16,8,128]{2,1,0:T(8,128)S(1)}, u32[]{:S(2)}, u32[]{:S(2)}) async-start(f32[16,8,128]{2,1,0:T(8,128)} %broadcast_in_dim.9), calls=%async_computation | async-start | bytes 131072 | tf_op jit(solution)/shard_map/all_to_all | solution.py:310
  148.2 0.5 collective-permute-done.12
  148.6 0.0 collective-permute-done.10
  148.6 0.0 collective-permute-done.11
  148.6 1.2 fusion.5
  149.9 2.4 %all-to-all-done = f32[16,8,128]{2,1,0:T(8,128)S(1)} async-done(((f32[16,8,128]{2,1,0:T(8,128)}), f32[16,8,128]{2,1,0:T(8,128)S(1)}, u32[]{:S(2)}, u32[]{:S(2)}) %all-to-all-start) | async-done | bytes 65568 | tf_op jit(solution)/shard_map/all_to_all | solution.py:310
  152.3 0.0 collective-permute-done.15
  152.4 4.6 %collective-permute-start.16 = (f32[520,128]{1,0:T(8,128)S(1)}, f32[520,128]{1,0:T(8,128)S(1)}, u32[]{:S(2)}, u32[]{:S(2)}) collective-permute-start(f32[520,128]{1,0:T(8,128)S(1)} %pad_maximum_fusion.5), channel_id=1, source_target_pairs={{0,256},{16,272},{32,288},{48,304},{64,320},{80,336},{96,352},{112... | collective-permute-start | bytes 798728 | tf_op jit(solution)/shard_map/ppermute | solution.py:315
  157.0 7.2 %collective-permute-done.16 = f32[520,128]{1,0:T(8,128)S(1)} collective-permute-done((f32[520,128]{1,0:T(8,128)S(1)}, f32[520,128]{1,0:T(8,128)S(1)}, u32[]{:S(2)}, u32[]{:S(2)}) %collective-permute-start.16) | collective-permute-done | bytes 266272 | tf_op jit(solution)/shard_map/ppermute | solution.py:315
  164.2 1.3 fusion.8
  165.5 31.2 %all_to_all.15 = f32[4,136,128]{2,1,0:T(8,128)S(1)} all-to-all(f32[4,136,128]{2,1,0:T(8,128)S(1)} %pad_maximum_fusion.4), channel_id=1, replica_groups={{0,64,128,192},{16,80,144,208},{32,96,160,224},{48,112,176,240},{256,32..., dimensions={0} | all-to-all | bytes 557056 | tf_op jit(solution)/shard_map/all_to_all | solution.py:310
  196.7 0.6 broadcast_in_dim.11
  197.3 5.3 %all-to-all-start.2 = ((f32[4,8,128]{2,1,0:T(8,128)}), f32[4,8,128]{2,1,0:T(8,128)S(1)}, u32[]{:S(2)}, u32[]{:S(2)}) async-start(f32[4,8,128]{2,1,0:T(8,128)} %broadcast_in_dim.11), calls=%async_computation.2 | async-start | bytes 32768 | tf_op jit(solution)/shard_map/all_to_all | solution.py:310
  202.7 0.6 slice.95
  203.3 5.0 %all-to-all-done.2 = f32[4,8,128]{2,1,0:T(8,128)S(1)} async-done(((f32[4,8,128]{2,1,0:T(8,128)}), f32[4,8,128]{2,1,0:T(8,128)S(1)}, u32[]{:S(2)}, u32[]{:S(2)}) %all-to-all-start.2) | async-done | bytes 16416 | tf_op jit(solution)/shard_map/all_to_all | solution.py:310
  208.3 0.7 copy.35
  (31 shorter events, 0.3 us)
Async XLA Ops:
  7.2 92.3 %all-gather.4.cloned.1.call-start = ((), (), s32[]{:S(2)}) async-start(), calls=%async_computation.3 | async-start | bytes 8355840 | tf_op jit(solution)/shard_map/all_gather | solution.py:198
  12.1 58.0 %collective-permute-start.6 = (bf16[6,320,256]{2,1,0:T(8,128)(2,1)S(1)}, bf16[6,320,256]{2,1,0:T(8,128)(2,1)S(1)}, u32[]{:S(2)}, u32[]{:S(2)}) collective-permute-start(bf16[6,320,256]{2,1,0:T(8,128)(2,1)S(1)} %constant_dynamic-update-slice_fusion), channel_id=1, source_target_pairs={{12,0},{13,1},{14,2},{15,3},{0,4},{1,5},{2,6},{3,7},{4,8},{5,9},{6... | collective-permute-start | bytes 2949128 | tf_op jit(solution)/shard_map/ppermute | solution.py:37
  19.7 50.5 %collective-permute-start.5 = (bf16[6,320,256]{2,1,0:T(8,128)(2,1)S(1)}, bf16[6,320,256]{2,1,0:T(8,128)(2,1)S(1)}, u32[]{:S(2)}, u32[]{:S(2)}) collective-permute-start(bf16[6,320,256]{2,1,0:T(8,128)(2,1)S(1)} %constant_dynamic-update-slice_fusion), channel_id=1, source_target_pairs={{4,0},{5,1},{6,2},{7,3},{8,4},{9,5},{10,6},{11,7},{12,8},{13,9},{1... | collective-permute-start | bytes 2949128 | tf_op jit(solution)/shard_map/ppermute | solution.py:37
  22.4 7.7 %collective-permute-start = (bf16[2,128,128]{2,1,0:T(8,128)(2,1)S(1)}, bf16[2,128,128]{2,1,0:T(8,128)(2,1)S(1)}, u32[]{:S(2)}, u32[]{:S(2)}) collective-permute-start(bf16[2,128,128]{2,1,0:T(8,128)(2,1)S(1)} %pad_maximum_fusion.7), channel_id=1, source_target_pairs={{0,256},{16,272},{32,288},{48,304},{64,320},{80,336},{96,352},{112... | collective-permute-start | bytes 196616 | tf_op jit(solution)/shard_map/ppermute | solution.py:197
  61.1 30.2 %copy-start.3 = (bf16[8,2,128,128]{3,2,1,0:T(8,128)(2,1)}, bf16[8,2,128,128]{3,2,1,0:T(8,128)(2,1)S(1)}, u32[]{:S(2)}) copy-start(bf16[8,2,128,128]{3,2,1,0:T(8,128)(2,1)S(1)} %all-gather) | copy-start | bytes 1572868
  61.2 15.0 %collective-permute-start.2 = (bf16[4,2,128,128]{3,2,1,0:T(8,128)(2,1)S(1)}, bf16[4,2,128,128]{3,2,1,0:T(8,128)(2,1)S(1)}, u32[]{:S(2)}, u32[]{:S(2)}) collective-permute-start(bf16[4,2,128,128]{3,2,1,0:T(8,128)(2,1)S(1)} %get-tuple-element.48), channel_id=1, source_target_pairs={{32,0},{48,16},{64,32},{80,48},{96,64},{112,80},{128,96},{144,112}... | collective-permute-start | bytes 786440 | tf_op jit(solution)/shard_map/ppermute | solution.py:33
  63.1 23.9 %collective-permute-start.4 = (bf16[4,2,2,128,128]{4,3,2,1,0:T(8,128)(2,1)S(1)}, bf16[4,2,2,128,128]{4,3,2,1,0:T(8,128)(2,1)S(1)}, u32[]{:S(2)}, u32[]{:S(2)}) collective-permute-start(bf16[4,2,2,128,128]{4,3,2,1,0:T(8,128)(2,1)S(1)} %bitcast.61), channel_id=1, source_target_pairs={{240,0},{0,16},{16,32},{32,48},{48,64},{64,80},{80,96},{96,112},{1... | collective-permute-start | bytes 1572872 | tf_op jit(solution)/shard_map/ppermute | solution.py:33
  65.9 21.1 %collective-permute-start.1 = (bf16[4,2,2,128,128]{4,3,2,1,0:T(8,128)(2,1)S(1)}, bf16[4,2,2,128,128]{4,3,2,1,0:T(8,128)(2,1)S(1)}, u32[]{:S(2)}, u32[]{:S(2)}) collective-permute-start(bf16[4,2,2,128,128]{4,3,2,1,0:T(8,128)(2,1)S(1)} %bitcast.62), channel_id=1, source_target_pairs={{16,0},{32,16},{48,32},{64,48},{80,64},{96,80},{112,96},{128,112},... | collective-permute-start | bytes 1572872 | tf_op jit(solution)/shard_map/ppermute | solution.py:33
  70.3 16.7 %collective-permute-start.8 = (bf16[3,320,256]{2,1,0:T(8,128)(2,1)S(1)}, bf16[3,320,256]{2,1,0:T(8,128)(2,1)S(1)}, u32[]{:S(2)}, u32[]{:S(2)}) collective-permute-start(bf16[3,320,256]{2,1,0:T(8,128)(2,1)S(1)} %slice.49), channel_id=1, source_target_pairs={{12,0},{13,1},{14,2},{15,3},{0,4},{1,5},{2,6},{3,7},{4,8},{5,9},{6... | collective-permute-start | bytes 1474568 | tf_op jit(solution)/shard_map/ppermute | solution.py:37
  72.2 14.8 %collective-permute-start.7 = (bf16[3,320,256]{2,1,0:T(8,128)(2,1)S(1)}, bf16[3,320,256]{2,1,0:T(8,128)(2,1)S(1)}, u32[]{:S(2)}, u32[]{:S(2)}) collective-permute-start(bf16[3,320,256]{2,1,0:T(8,128)(2,1)S(1)} %slice.48), channel_id=1, source_target_pairs={{4,0},{5,1},{6,2},{7,3},{8,4},{9,5},{10,6},{11,7},{12,8},{13,9},{1... | collective-permute-start | bytes 1474568 | tf_op jit(solution)/shard_map/ppermute | solution.py:37
  76.1 15.2 %copy-start.6 = (bf16[4,2,128,128]{3,2,1,0:T(8,128)(2,1)}, bf16[4,2,128,128]{3,2,1,0:T(8,128)(2,1)S(1)}, u32[]{:S(2)}) copy-start(bf16[4,2,128,128]{3,2,1,0:T(8,128)(2,1)S(1)} %collective-permute-done.2) | copy-start | bytes 786436
  76.1 10.8 %collective-permute-start.3 = (bf16[4,2,128,128]{3,2,1,0:T(8,128)(2,1)S(1)}, bf16[4,2,128,128]{3,2,1,0:T(8,128)(2,1)S(1)}, u32[]{:S(2)}, u32[]{:S(2)}) collective-permute-start(bf16[4,2,128,128]{3,2,1,0:T(8,128)(2,1)S(1)} %get-tuple-element.49), channel_id=1, source_target_pairs={{224,0},{240,16},{0,32},{16,48},{32,64},{48,80},{64,96},{80,112},{... | collective-permute-start | bytes 786440 | tf_op jit(solution)/shard_map/ppermute | solution.py:33
  87.0 4.3 %copy-start.7 = (bf16[4,2,128,128]{3,2,1,0:T(8,128)(2,1)}, bf16[4,2,128,128]{3,2,1,0:T(8,128)(2,1)S(1)}, u32[]{:S(2)}) copy-start(bf16[4,2,128,128]{3,2,1,0:T(8,128)(2,1)S(1)} %collective-permute-done.3) | copy-start | bytes 786436
  87.0 4.3 %copy-start.4 = (bf16[4,2,2,128,128]{4,3,2,1,0:T(8,128)(2,1)}, bf16[4,2,2,128,128]{4,3,2,1,0:T(8,128)(2,1)S(1)}, u32[]{:S(2)}) copy-start(bf16[4,2,2,128,128]{4,3,2,1,0:T(8,128)(2,1)S(1)} %collective-permute-done.4) | copy-start | bytes 1572868
  87.0 4.3 %copy-start.5 = (bf16[4,2,2,128,128]{4,3,2,1,0:T(8,128)(2,1)}, bf16[4,2,2,128,128]{4,3,2,1,0:T(8,128)(2,1)S(1)}, u32[]{:S(2)}) copy-start(bf16[4,2,2,128,128]{4,3,2,1,0:T(8,128)(2,1)S(1)} %collective-permute-done.1) | copy-start | bytes 1572868
  87.1 10.6 %copy-start.8 = (s32[128]{0:T(128)S(1)}, s32[128]{0:T(128)}, u32[]{:S(2)}) copy-start(s32[128]{0:T(128)} %param.11) | copy-start | bytes 1540
  89.3 19.5 %collective-permute-start.9 = (bf16[4,6,320,256]{3,2,1,0:T(8,128)(2,1)}, bf16[4,6,320,256]{3,2,1,0:T(8,128)(2,1)}, u32[]{:S(2)}, u32[]{:S(2)}) collective-permute-start(bf16[4,6,320,256]{3,2,1,0:T(8,128)(2,1)} %pad_maximum_fusion.mine_0.mine_1), channel_id=1, source_target_pairs={{0,1},{1,0},{2,3},{3,2},{4,5},{5,4},{6,7},{7,6},{8,9},{9,8},{10,11... | collective-permute-start | bytes 11796488 | tf_op jit(solution)/shard_map/ppermute | solution.py:222
  92.4 37.8 %collective-permute-start.13 = (bf16[2,2,2,4,128,128]{5,4,3,2,1,0:T(8,128)(2,1)}, bf16[2,2,2,4,128,128]{5,4,3,2,1,0:T(8,128)(2,1)S(1)}, u32[]{:S(2)}, u32[]{:S(2)}) collective-permute-start(bf16[2,2,2,4,128,128]{5,4,3,2,1,0:T(8,128)(2,1)} %fusion.3), channel_id=1, source_target_pairs={{0,2},{1,3},{2,0},{3,1},{4,6},{5,7},{6,4},{7,5},{8,10},{9,11},{10,... | collective-permute-start | bytes 3145736 | tf_op jit(solution)/shard_map/ppermute | solution.py:215
  99.4 3.2 %copy-start = (bf16[48,320,256]{2,1,0:T(8,128)(2,1)S(1)}, bf16[48,320,256]{2,1,0:T(8,128)(2,1)}, u32[]{:S(2)}) copy-start(bf16[48,320,256]{2,1,0:T(8,128)(2,1)} %all-gather.4.cloned.1.call-done) | copy-start | bytes 23592964
  102.7 8.1 %copy-start.1 = (bf16[48,320,256]{2,1,0:T(8,128)(2,1)S(1)}, bf16[48,320,256]{2,1,0:T(8,128)(2,1)}, u32[]{:S(2)}) copy-start(bf16[48,320,256]{2,1,0:T(8,128)(2,1)} %all-gather.4.cloned.1.call-done) | copy-start | bytes 23592964
  108.9 23.7 %collective-permute-start.14 = (f32[960,128]{1,0:T(8,128)S(1)}, f32[960,128]{1,0:T(8,128)S(1)}, u32[]{:S(2)}, u32[]{:S(2)}) collective-permute-start(f32[960,128]{1,0:T(8,128)S(1)} %get-tuple-element.41.own), channel_id=1, source_target_pairs={{0,2},{1,3},{2,0},{3,1},{4,6},{5,7},{6,4},{7,5},{8,10},{9,11},{10,... | collective-permute-start | bytes 1474568 | tf_op jit(solution)/shard_map/ppermute | solution.py:248
  114.7 25.4 %copy-start.2 = (f32[2,4,128,128]{3,2,1,0:T(8,128)}, f32[2,4,128,128]{3,2,1,0:T(8,128)S(1)}, u32[]{:S(2)}) copy-start(f32[2,4,128,128]{3,2,1,0:T(8,128)S(1)} %get-tuple-element.35) | copy-start | bytes 1572868
  114.7 33.9 %collective-permute-start.10 = (f32[2,4,128,128]{3,2,1,0:T(8,128)}, f32[2,4,128,128]{3,2,1,0:T(8,128)}, u32[]{:S(2)}, u32[]{:S(2)}) collective-permute-start(f32[2,4,128,128]{3,2,1,0:T(8,128)} %get-tuple-element.36), channel_id=1, source_target_pairs={{240,0},{0,16},{16,32},{32,48},{48,64},{64,80},{80,96},{96,112},{1... | collective-permute-start | bytes 1572872 | tf_op jit(solution)/shard_map/ppermute | solution.py:33
  118.3 30.3 %collective-permute-start.11 = (f32[2,4,128,128]{3,2,1,0:T(8,128)}, f32[2,4,128,128]{3,2,1,0:T(8,128)}, u32[]{:S(2)}, u32[]{:S(2)}) collective-permute-start(f32[2,4,128,128]{3,2,1,0:T(8,128)} %get-tuple-element.37), channel_id=1, source_target_pairs={{16,0},{32,16},{48,32},{64,48},{80,64},{96,80},{112,96},{128,112},... | collective-permute-start | bytes 1572872 | tf_op jit(solution)/shard_map/ppermute | solution.py:33
  125.8 22.8 %collective-permute-start.12 = (f32[4,128,128]{2,1,0:T(8,128)}, f32[4,128,128]{2,1,0:T(8,128)}, u32[]{:S(2)}, u32[]{:S(2)}) collective-permute-start(f32[4,128,128]{2,1,0:T(8,128)} %get-tuple-element.38), channel_id=1, source_target_pairs={{32,0},{48,16},{64,32},{80,48},{96,64},{112,80},{128,96},{144,112}... | collective-permute-start | bytes 786440 | tf_op jit(solution)/shard_map/ppermute | solution.py:33
  130.2 22.1 %collective-permute-start.15 = (f32[4,128,128]{2,1,0:T(8,128)S(1)}, f32[4,128,128]{2,1,0:T(8,128)}, u32[]{:S(2)}, u32[]{:S(2)}) collective-permute-start(f32[4,128,128]{2,1,0:T(8,128)S(1)} %get-tuple-element.42), channel_id=1, source_target_pairs={{224,0},{240,16},{0,32},{16,48},{32,64},{48,80},{64,96},{80,112},{... | collective-permute-start | bytes 786440 | tf_op jit(solution)/shard_map/ppermute | solution.py:33
  140.8 11.5 %all-to-all-start = ((f32[16,8,128]{2,1,0:T(8,128)}), f32[16,8,128]{2,1,0:T(8,128)S(1)}, u32[]{:S(2)}, u32[]{:S(2)}) async-start(f32[16,8,128]{2,1,0:T(8,128)} %broadcast_in_dim.9), calls=%async_computation | async-start | bytes 131072 | tf_op jit(solution)/shard_map/all_to_all | solution.py:310
  152.4 11.8 %collective-permute-start.16 = (f32[520,128]{1,0:T(8,128)S(1)}, f32[520,128]{1,0:T(8,128)S(1)}, u32[]{:S(2)}, u32[]{:S(2)}) collective-permute-start(f32[520,128]{1,0:T(8,128)S(1)} %pad_maximum_fusion.5), channel_id=1, source_target_pairs={{0,256},{16,272},{32,288},{48,304},{64,320},{80,336},{96,352},{112... | collective-permute-start | bytes 798728 | tf_op jit(solution)/shard_map/ppermute | solution.py:315
  197.3 10.9 %all-to-all-start.2 = ((f32[4,8,128]{2,1,0:T(8,128)}), f32[4,8,128]{2,1,0:T(8,128)S(1)}, u32[]{:S(2)}, u32[]{:S(2)}) async-start(f32[4,8,128]{2,1,0:T(8,128)} %broadcast_in_dim.11), calls=%async_computation.2 | async-start | bytes 32768 | tf_op jit(solution)/shard_map/all_to_all | solution.py:310
Sparse Core Ops, SparseCore 0:
  10.1 71.4 all-gather.3

commit v11 on v10

--- a/solution.py
+++ b/solution.py
@@ -215,7 +215,7 @@
     partner = lax.ppermute(partner, "seq", [(i, i ^ 2) for i in range(16)])
 
     half_plus, half_minus, *_ = lax.optimization_barrier(
-        (half_plus, half_minus, plus, minus, two_x, two_g)
+        (half_plus, half_minus, plus, minus, two_x, two_g, full_w)
     )
     t_two = jnp.concatenate([half_plus, half_minus], axis=0)
     mine = jnp.stack([stack_t, t_plus, t_two, t_minus])
@@ -315,10 +315,17 @@
     away = lax.ppermute(away, "fsdp", [(i, (i + 16) % 32) for i in range(32)])
     partial = kept[0] + up[0] + down[0] + two_up + away[:512].reshape(4, 128, 128)
     terms = terms + away[512:]
-    copies = jnp.broadcast_to(terms[None], (4, 8, 128))
-    both = sum_over(jnp.concatenate([partial, copies], axis=1), "fsdp", Z_FAR)
-    block_out = both[:128].astype(BF16)
-    terms = sum_over(jnp.broadcast_to(both[None, 128:], (4, 8, 128)), "fsdp", Z_NEAR)
+    for distance in (8, 4):
+        side = fsdp % 16 // distance % 2
+        count = distance // 4
+        halves = partial.reshape(2, count * 128, 128)
+        send = lax.dynamic_index_in_dim(halves, 1 - side, 0, False)
+        swap = [(i, i ^ distance) for i in range(32)]
+        got = lax.ppermute(jnp.concatenate([send, terms], axis=0), "fsdp", swap)
+        partial = lax.dynamic_index_in_dim(halves, side, 0, False) + got[: count * 128]
+        terms = terms + got[count * 128 :]
+    block_out = partial.astype(BF16)
+    terms = sum_over(jnp.broadcast_to(terms[None], (4, 8, 128)), "fsdp", Z_NEAR)
     return (block_out, terms[:EXAMPLES, :2])
 
 

time: 218 us -> 225 us (1.032)
  blocking collectives: 62.3 us -> 31.1 us
  starting transfers between devices: 74 us -> 97.1 us
  waiting for transfers between devices: 28.1 us -> 36.1 us
  local copies, waits for them, and re-layouts: 8.97 us -> 13.1 us
  other arithmetic: 10.3 us -> 13.5 us
    all_to_all x1 -> x0, blocking collectives: 31.2 us -> none  [sum_over(): lax.all_to_all(copies, axis, 0, 0, axis_index_groups=groups)]
    ppermute x0 -> x2, starting transfers between devices: none -> 18.9 us  [shards(): got = lax.ppermute(jnp.concatenate([send, terms], axis=0), 'fsdp', swap)]
    ppermute x0 -> x2, waiting for transfers between devices: none -> 7.94 us  [shards(): got = lax.ppermute(jnp.concatenate([send, terms], axis=0), 'fsdp', swap)]
    unnamed x21 -> x17, local copies, waits for them, and re-layouts: 5.9 us -> 10.6 us
    all_to_all x2, starting transfers between devices: 12.7 us -> 16.7 us  [sum_over(): lax.all_to_all(copies, axis, 0, 0, axis_index_groups=groups)]
  transfers between devices with their start and end apart: 20 -> 22, of which waited for: 6 -> 7; matrix products, arithmetic and copies ran while one was open for 5% -> 4% of each run, Pallas kernels for 8% -> 8%
where the time goes in v11:
time: 225 us; the launch traced here: 222 us
  starting transfers between devices  97.1 us (43%)
  waiting for transfers between devices  36.1 us (16%)
  blocking collectives  31.1 us (14%)
  Pallas kernels  16.9 us (8%)
  between operations  14.7 us (7%)
  other arithmetic  13.5 us (6%)
  local copies, waits for them, and re-layouts  13.1 us (6%)
    all_gather x1, blocking collectives, shards(): lax.all_gather(jnp.stack([both, other]), 'fsdp', axis=0, axis_index_group...  31.1 us
    ppermute x8, starting transfers between devices, z_shift(): return lax.ppermute(array, 'fsdp', perm)  30.7 us
    ppermute x2, starting transfers between devices, shards(): got = lax.ppermute(jnp.concatenate([send, terms], axis=0), 'fsdp', swap)  18.9 us
    all_to_all x2, starting transfers between devices, sum_over(): lax.all_to_all(copies, axis, 0, 0, axis_index_groups=groups)  16.7 us
    ppermute x4, starting transfers between devices, y_shift(): lax.ppermute(array, 'seq', [((i + 4 * step) % 16, i) for i in range(16)])  15.3 us
    unnamed x17, local copies, waits for them, and re-layouts  10.6 us
    all_to_all x2, waiting for transfers between devices, sum_over(): lax.all_to_all(copies, axis, 0, 0, axis_index_groups=groups)  8 us
    ppermute x2, waiting for transfers between devices, shards(): got = lax.ppermute(jnp.concatenate([send, terms], axis=0), 'fsdp', swap)  7.94 us
  transfers between devices with their start and end apart: 22, of which 7 were waited for; matrix products, arithmetic and copies ran while one was open for 4% of the time, Pallas kernels for 8%

profile of v11, /device:TPU:24, one launch (start us, length us, event | category | flops | bytes accessed | tf_op | source)
XLA Modules:
  0.0 222.4 jit_solution(211451817519075188)
XLA Ops:
  7.2 0.0 all-gather.4.cloned.1.call-start
  7.2 2.0 pad_maximum_fusion.3
  9.2 0.0 all-gather.4.cloned.1.call-update
  9.2 1.0 constant_dynamic-update-slice_fusion.2
  10.2 1.0 constant_dynamic-update-slice_fusion.1
  11.2 1.0 constant_dynamic-update-slice_fusion
  12.2 7.5 %collective-permute-start.6 = (bf16[6,320,256]{2,1,0:T(8,128)(2,1)S(1)}, bf16[6,320,256]{2,1,0:T(8,128)(2,1)S(1)}, u32[]{:S(2)}, u32[]{:S(2)}) collective-permute-start(bf16[6,320,256]{2,1,0:T(8,128)(2,1)S(1)} %constant_dynamic-update-slice_fusion), channel_id=1, source_target_pairs={{12,0},{13,1},{14,2},{15,3},{0,4},{1,5},{2,6},{3,7},{4,8},{5,9},{6... | collective-permute-start | bytes 2949128 | tf_op jit(solution)/shard_map/ppermute | solution.py:37
  19.7 1.9 collective-permute-start.5
  21.7 0.8 pad_maximum_fusion.8
  22.5 1.9 collective-permute-start
  24.4 5.7 %collective-permute-done = bf16[2,128,128]{2,1,0:T(8,128)(2,1)S(1)} collective-permute-done((bf16[2,128,128]{2,1,0:T(8,128)(2,1)S(1)}, bf16[2,128,128]{2,1,0:T(8,128)(2,1)S(1)}, u32[]{:S(2)}, u32[]{:S(2)}) %collective-permute-start) | collective-permute-done | bytes 65568 | tf_op jit(solution)/shard_map/ppermute | solution.py:197
  30.1 31.1 %all-gather = bf16[8,2,128,128]{3,2,1,0:T(8,128)(2,1)S(1)} all-gather(bf16[2,2,128,128]{3,2,1,0:T(8,128)(2,1)S(1)} %pad_maximum_fusion.6), channel_id=2, replica_groups={{0,64,128,192},{16,80,144,208},{32,96,160,224},{48,112,176,240},{256,32..., dimensions={0}, use_global_device_ids=true | all-gather | bytes 655360 | tf_op jit(solution)/shard_map/all_gather | solution.py:202
  61.3 1.9 collective-permute-start.2
  63.2 2.8 %collective-permute-start.4 = (bf16[4,2,2,128,128]{4,3,2,1,0:T(8,128)(2,1)S(1)}, bf16[4,2,2,128,128]{4,3,2,1,0:T(8,128)(2,1)S(1)}, u32[]{:S(2)}, u32[]{:S(2)}) collective-permute-start(bf16[4,2,2,128,128]{4,3,2,1,0:T(8,128)(2,1)S(1)} %bitcast.71), channel_id=1, source_target_pairs={{240,0},{0,16},{16,32},{32,48},{48,64},{64,80},{80,96},{96,112},{1... | collective-permute-start | bytes 1572872 | tf_op jit(solution)/shard_map/ppermute | solution.py:33
  66.0 4.3 %collective-permute-start.1 = (bf16[4,2,2,128,128]{4,3,2,1,0:T(8,128)(2,1)S(1)}, bf16[4,2,2,128,128]{4,3,2,1,0:T(8,128)(2,1)S(1)}, u32[]{:S(2)}, u32[]{:S(2)}) collective-permute-start(bf16[4,2,2,128,128]{4,3,2,1,0:T(8,128)(2,1)S(1)} %bitcast.72), channel_id=1, source_target_pairs={{16,0},{32,16},{48,32},{64,48},{80,64},{96,80},{112,96},{128,112},... | collective-permute-start | bytes 1572872 | tf_op jit(solution)/shard_map/ppermute | solution.py:33
  70.3 0.0 collective-permute-done.6
  70.3 0.0 collective-permute-done.5
  70.4 1.9 collective-permute-start.8
  72.3 3.9 %collective-permute-start.7 = (bf16[3,320,256]{2,1,0:T(8,128)(2,1)S(1)}, bf16[3,320,256]{2,1,0:T(8,128)(2,1)}, u32[]{:S(2)}, u32[]{:S(2)}) collective-permute-start(bf16[3,320,256]{2,1,0:T(8,128)(2,1)S(1)} %slice.53), channel_id=1, source_target_pairs={{4,0},{5,1},{6,2},{7,3},{8,4},{9,5},{10,6},{11,7},{12,8},{13,9},{1... | collective-permute-start | bytes 1474568 | tf_op jit(solution)/shard_map/ppermute | solution.py:37
  76.2 0.0 collective-permute-done.2
  76.2 3.6 %collective-permute-start.3 = (bf16[4,2,128,128]{3,2,1,0:T(8,128)(2,1)S(1)}, bf16[4,2,128,128]{3,2,1,0:T(8,128)(2,1)S(1)}, u32[]{:S(2)}, u32[]{:S(2)}) collective-permute-start(bf16[4,2,128,128]{3,2,1,0:T(8,128)(2,1)S(1)} %get-tuple-element.49), channel_id=1, source_target_pairs={{224,0},{240,16},{0,32},{16,48},{32,64},{48,80},{64,96},{80,112},{... | collective-permute-start | bytes 786440 | tf_op jit(solution)/shard_map/ppermute | solution.py:33
  79.9 7.0 %collective-permute-done.3 = bf16[4,2,128,128]{3,2,1,0:T(8,128)(2,1)S(1)} collective-permute-done((bf16[4,2,128,128]{3,2,1,0:T(8,128)(2,1)S(1)}, bf16[4,2,128,128]{3,2,1,0:T(8,128)(2,1)S(1)}, u32[]{:S(2)}, u32[]{:S(2)}) %collective-permute-start.3) | collective-permute-done | bytes 262176 | tf_op jit(solution)/shard_map/ppermute | solution.py:33
  86.9 0.0 collective-permute-done.4
  86.9 0.0 collective-permute-done.1
  86.9 0.0 collective-permute-done.8
  86.9 0.7 copy-done.4
  87.6 0.8 copy-done.5
  88.4 1.3 maximum_bitcast_fusion
  89.7 0.0 copy-start.6
  89.7 3.2 %pad_maximum_fusion.mine_0.mine_1 = bf16[4,6,320,256]{3,2,1,0:T(8,128)(2,1)} fusion(bf16[1,6,320,256]{3,2,1,0:T(8,128)(2,1)S(1)} %bitcast.75, bf16[1,6,320,256]{3,2,1,0:T(8,128)(2,1)S(1)} %maximum_bitcast_fusion, bf16[1,6,320,256]{3,2,1,0:T(8,128)(2,1)S(1)} %bitcast.76, bf16[1,6,320,256]{3,2,1,0:T(8,128)(2,1)} %bitcast.81), kind=kLoop, calls=%fused_computation | loop fusion | flops 5898240 | bytes 7864320 | tf_op jit(solution)/shard_map/stack | solution.py:221
  92.9 1.9 collective-permute-start.9
  94.8 2.1 fusion.3
  96.9 5.4 %collective-permute-start.13 = (bf16[2,2,2,4,128,128]{5,4,3,2,1,0:T(8,128)(2,1)}, bf16[2,2,2,4,128,128]{5,4,3,2,1,0:T(8,128)(2,1)S(1)}, u32[]{:S(2)}, u32[]{:S(2)}) collective-permute-start(bf16[2,2,2,4,128,128]{5,4,3,2,1,0:T(8,128)(2,1)} %fusion.3), channel_id=1, source_target_pairs={{0,2},{1,3},{2,0},{3,1},{4,6},{5,7},{6,4},{7,5},{8,10},{9,11},{10,... | collective-permute-start | bytes 3145736 | tf_op jit(solution)/shard_map/ppermute | solution.py:215
  102.4 0.1 stack.110.place
  102.5 1.2 pad_maximum_fusion.1.acts
  103.7 3.2 %copy-done = bf16[48,320,256]{2,1,0:T(8,128)(2,1)S(1)} copy-done((bf16[48,320,256]{2,1,0:T(8,128)(2,1)S(1)}, bf16[48,320,256]{2,1,0:T(8,128)(2,1)}, u32[]{:S(2)}) %copy-start) | copy-done | bytes 7864344
  106.9 6.2 %primal.1 = (bf16[128,320]{1,0:T(8,128)(2,1)S(1)}, f32[960,128]{1,0:T(8,128)S(1)}) custom-call(s32[6]{0:T(128)S(1)} %stack.110.place, bf16[4,2,2,4,128,128]{5,4,3,2,1,0:T(8,128)(2,1)S(1)} %pad_maximum_fusion.1.acts, bf16[2,4,2,3,320,256]{5,4,3,2,1,0:T(8,128)(2,1)S(1)} %bitcast.68, f32[1,128]{1,0:T(1,128)S(1)} %convert_bitcast_fusion.mask), custom_call_target="tpu_custom_call" | custom-call | flops 1006632960 | bytes 10485760 | tf_op jit(solution)/shard_map/primal/pallas_call | solution.py:224
  113.1 1.9 collective-permute-start.14
  115.0 3.2 %copy-done.1 = bf16[48,320,256]{2,1,0:T(8,128)(2,1)S(1)} copy-done((bf16[48,320,256]{2,1,0:T(8,128)(2,1)S(1)}, bf16[48,320,256]{2,1,0:T(8,128)(2,1)}, u32[]{:S(2)}) %copy-start.1) | copy-done | bytes 7864344
  118.2 3.2 %block_sums.1 = (f32[2,4,128,128]{3,2,1,0:T(8,128)S(1)}, f32[2,4,128,128]{3,2,1,0:T(8,128)S(1)}, f32[2,4,128,128]{3,2,1,0:T(8,128)S(1)}, f32[4,128,128]{2,1,0:T(8,128)S(1)}, f32[4,128,128]{2,1,0:T(8,128)S(1)}) custom-call(s32[6]{0:T(128)S(1)} %stack.110.place, bf16[128,320]{1,0:T(8,128)(2,1)S(1)} %get-tuple-element.34.hidden, ...), custom_call_target="tpu_custom_call" | custom-call | flops 335544320 | bytes 5242880 | tf_op jit(solution)/shard_map/block_sums/pallas_call | solution.py:253
  121.4 3.5 %collective-permute-start.10 = (f32[2,4,128,128]{3,2,1,0:T(8,128)S(1)}, f32[2,4,128,128]{3,2,1,0:T(8,128)}, u32[]{:S(2)}, u32[]{:S(2)}) collective-permute-start(f32[2,4,128,128]{3,2,1,0:T(8,128)S(1)} %get-tuple-element.36), channel_id=1, source_target_pairs={{240,0},{0,16},{16,32},{32,48},{48,64},{64,80},{80,96},{96,112},{1... | collective-permute-start | bytes 1572872 | tf_op jit(solution)/shard_map/ppermute | solution.py:33
  124.9 7.9 %collective-permute-start.11 = (f32[2,4,128,128]{3,2,1,0:T(8,128)S(1)}, f32[2,4,128,128]{3,2,1,0:T(8,128)}, u32[]{:S(2)}, u32[]{:S(2)}) collective-permute-start(f32[2,4,128,128]{3,2,1,0:T(8,128)S(1)} %get-tuple-element.37), channel_id=1, source_target_pairs={{16,0},{32,16},{48,32},{64,48},{80,64},{96,80},{112,96},{128,112},... | collective-permute-start | bytes 1572872 | tf_op jit(solution)/shard_map/ppermute | solution.py:33
  132.8 4.3 %collective-permute-start.12 = (f32[4,128,128]{2,1,0:T(8,128)S(1)}, f32[4,128,128]{2,1,0:T(8,128)S(1)}, u32[]{:S(2)}, u32[]{:S(2)}) collective-permute-start(f32[4,128,128]{2,1,0:T(8,128)S(1)} %get-tuple-element.38), channel_id=1, source_target_pairs={{32,0},{48,16},{64,32},{80,48},{96,64},{112,80},{128,96},{144,112}... | collective-permute-start | bytes 786440 | tf_op jit(solution)/shard_map/ppermute | solution.py:33
  137.1 2.5 %collective-permute-start.15 = (f32[4,128,128]{2,1,0:T(8,128)S(1)}, f32[4,128,128]{2,1,0:T(8,128)}, u32[]{:S(2)}, u32[]{:S(2)}) collective-permute-start(f32[4,128,128]{2,1,0:T(8,128)S(1)} %get-tuple-element.42), channel_id=1, source_target_pairs={{224,0},{240,16},{0,32},{16,48},{32,64},{48,80},{64,96},{80,112},{... | collective-permute-start | bytes 786440 | tf_op jit(solution)/shard_map/ppermute | solution.py:33
  139.6 0.0 collective-permute-done.14.their
  139.6 7.6 %column.1 = f32[8,128]{1,0:T(8,128)S(1)} custom-call(s32[6]{0:T(128)S(1)} %stack.110.place, bf16[4,2,2,4,128,128]{5,4,3,2,1,0:T(8,128)(2,1)S(1)} %pad_maximum_fusion.1.acts, bf16[2,2,2,4,128,128]{5,4,3,2,1,0:T(8,128)(2,1)S(1)} %collective-permute-done.13.partner, bf16[4,6,320,256]{3,2,1,0:T(8,128)(2,1)} %pad_maximum_fusion.mine_0.mine_1, ...), custom_call_target="tpu_custom_call" | custom-call | flops 2013265920 | bytes 12582912 | tf_op jit(solution)/shard_map/column/pallas_call | solution.py:281
  147.2 0.6 broadcast_in_dim.7
  147.8 7.4 %all-to-all-start = ((f32[16,8,128]{2,1,0:T(8,128)}), f32[16,8,128]{2,1,0:T(8,128)S(1)}, u32[]{:S(2)}, u32[]{:S(2)}) async-start(f32[16,8,128]{2,1,0:T(8,128)} %broadcast_in_dim.7), calls=%async_computation | async-start | bytes 131072 | tf_op jit(solution)/shard_map/all_to_all | solution.py:310
  155.2 0.0 collective-permute-done.12
  155.2 0.0 collective-permute-done.11
  155.2 1.1 fusion.5
  156.3 3.0 %all-to-all-done = f32[16,8,128]{2,1,0:T(8,128)S(1)} async-done(((f32[16,8,128]{2,1,0:T(8,128)}), f32[16,8,128]{2,1,0:T(8,128)S(1)}, u32[]{:S(2)}, u32[]{:S(2)}) %all-to-all-start) | async-done | bytes 65568 | tf_op jit(solution)/shard_map/all_to_all | solution.py:310
  159.4 4.4 %collective-permute-start.16 = (f32[520,128]{1,0:T(8,128)S(1)}, f32[520,128]{1,0:T(8,128)S(1)}, u32[]{:S(2)}, u32[]{:S(2)}) collective-permute-start(f32[520,128]{1,0:T(8,128)S(1)} %pad_maximum_fusion.4), channel_id=1, source_target_pairs={{0,256},{16,272},{32,288},{48,304},{64,320},{80,336},{96,352},{112... | collective-permute-start | bytes 798728 | tf_op jit(solution)/shard_map/ppermute | solution.py:315
  163.8 7.3 %collective-permute-done.16 = f32[520,128]{1,0:T(8,128)S(1)} collective-permute-done((f32[520,128]{1,0:T(8,128)S(1)}, f32[520,128]{1,0:T(8,128)S(1)}, u32[]{:S(2)}, u32[]{:S(2)}) %collective-permute-start.16) | collective-permute-done | bytes 266272 | tf_op jit(solution)/shard_map/ppermute | solution.py:315
  171.2 1.2 fusion.8
  172.4 10.0 %collective-permute-start.17 = (f32[264,128]{1,0:T(8,128)S(1)}, f32[264,128]{1,0:T(8,128)S(1)}, u32[]{:S(2)}, u32[]{:S(2)}) collective-permute-start(f32[264,128]{1,0:T(8,128)S(1)} %pad_maximum_fusion.5), channel_id=1, source_target_pairs={{0,128},{16,144},{32,160},{48,176},{64,192},{80,208},{96,224},{112... | collective-permute-start | bytes 405512 | tf_op jit(solution)/shard_map/ppermute | solution.py:324
  182.5 5.7 %collective-permute-done.17 = f32[264,128]{1,0:T(8,128)S(1)} collective-permute-done((f32[264,128]{1,0:T(8,128)S(1)}, f32[264,128]{1,0:T(8,128)S(1)}, u32[]{:S(2)}, u32[]{:S(2)}) %collective-permute-start.17) | collective-permute-done | bytes 135200 | tf_op jit(solution)/shard_map/ppermute | solution.py:324
  188.2 8.9 %collective-permute-start.18 = (f32[136,128]{1,0:T(8,128)S(1)}, f32[136,128]{1,0:T(8,128)S(1)}, u32[]{:S(2)}, u32[]{:S(2)}) collective-permute-start(f32[136,128]{1,0:T(8,128)S(1)} %pad_maximum_fusion.7), channel_id=1, source_target_pairs={{0,64},{16,80},{32,96},{48,112},{64,0},{80,16},{96,32},{112,48},{1... | collective-permute-start | bytes 208904 | tf_op jit(solution)/shard_map/ppermute | solution.py:324
  197.2 2.3 %collective-permute-done.18 = f32[136,128]{1,0:T(8,128)S(1)} collective-permute-done((f32[136,128]{1,0:T(8,128)S(1)}, f32[136,128]{1,0:T(8,128)S(1)}, u32[]{:S(2)}, u32[]{:S(2)}) %collective-permute-start.18) | collective-permute-done | bytes 69664 | tf_op jit(solution)/shard_map/ppermute | solution.py:324
  199.4 0.6 broadcast_in_dim.8
  200.0 9.3 %all-to-all-start.1 = ((f32[4,8,128]{2,1,0:T(8,128)}), f32[4,8,128]{2,1,0:T(8,128)S(1)}, u32[]{:S(2)}, u32[]{:S(2)}) async-start(f32[4,8,128]{2,1,0:T(8,128)} %broadcast_in_dim.8), calls=%async_computation.1 | async-start | bytes 32768 | tf_op jit(solution)/shard_map/all_to_all | solution.py:310
  209.3 0.6 fusion.9
  209.9 5.0 %all-to-all-done.1 = f32[4,8,128]{2,1,0:T(8,128)S(1)} async-done(((f32[4,8,128]{2,1,0:T(8,128)}), f32[4,8,128]{2,1,0:T(8,128)S(1)}, u32[]{:S(2)}, u32[]{:S(2)}) %all-to-all-start.1) | async-done | bytes 16416 | tf_op jit(solution)/shard_map/all_to_all | solution.py:310
  215.0 0.7 copy.35
  (33 shorter events, 0.3 us)
Async XLA Ops:
  7.2 81.2 %all-gather.4.cloned.1.call-start = ((), (), s32[]{:S(2)}) async-start(), calls=%async_computation.2 | async-start | bytes 8355840 | tf_op jit(solution)/shard_map/all_gather | solution.py:198
  12.2 74.7 %copy-start.2 = (bf16[6,320,256]{2,1,0:T(8,128)(2,1)}, bf16[6,320,256]{2,1,0:T(8,128)(2,1)S(1)}, u32[]{:S(2)}) copy-start(bf16[6,320,256]{2,1,0:T(8,128)(2,1)S(1)} %constant_dynamic-update-slice_fusion) | copy-start | bytes 2949124
  12.2 58.0 %collective-permute-start.6 = (bf16[6,320,256]{2,1,0:T(8,128)(2,1)S(1)}, bf16[6,320,256]{2,1,0:T(8,128)(2,1)S(1)}, u32[]{:S(2)}, u32[]{:S(2)}) collective-permute-start(bf16[6,320,256]{2,1,0:T(8,128)(2,1)S(1)} %constant_dynamic-update-slice_fusion), channel_id=1, source_target_pairs={{12,0},{13,1},{14,2},{15,3},{0,4},{1,5},{2,6},{3,7},{4,8},{5,9},{6... | collective-permute-start | bytes 2949128 | tf_op jit(solution)/shard_map/ppermute | solution.py:37
  19.7 50.5 %collective-permute-start.5 = (bf16[6,320,256]{2,1,0:T(8,128)(2,1)S(1)}, bf16[6,320,256]{2,1,0:T(8,128)(2,1)S(1)}, u32[]{:S(2)}, u32[]{:S(2)}) collective-permute-start(bf16[6,320,256]{2,1,0:T(8,128)(2,1)S(1)} %constant_dynamic-update-slice_fusion), channel_id=1, source_target_pairs={{4,0},{5,1},{6,2},{7,3},{8,4},{9,5},{10,6},{11,7},{12,8},{13,9},{1... | collective-permute-start | bytes 2949128 | tf_op jit(solution)/shard_map/ppermute | solution.py:37
  22.5 7.7 %collective-permute-start = (bf16[2,128,128]{2,1,0:T(8,128)(2,1)S(1)}, bf16[2,128,128]{2,1,0:T(8,128)(2,1)S(1)}, u32[]{:S(2)}, u32[]{:S(2)}) collective-permute-start(bf16[2,128,128]{2,1,0:T(8,128)(2,1)S(1)} %pad_maximum_fusion.8), channel_id=1, source_target_pairs={{0,256},{16,272},{32,288},{48,304},{64,320},{80,336},{96,352},{112... | collective-permute-start | bytes 196616 | tf_op jit(solution)/shard_map/ppermute | solution.py:197
  61.3 15.0 %collective-permute-start.2 = (bf16[4,2,128,128]{3,2,1,0:T(8,128)(2,1)S(1)}, bf16[4,2,128,128]{3,2,1,0:T(8,128)(2,1)S(1)}, u32[]{:S(2)}, u32[]{:S(2)}) collective-permute-start(bf16[4,2,128,128]{3,2,1,0:T(8,128)(2,1)S(1)} %get-tuple-element.48), channel_id=1, source_target_pairs={{32,0},{48,16},{64,32},{80,48},{96,64},{112,80},{128,96},{144,112}... | collective-permute-start | bytes 786440 | tf_op jit(solution)/shard_map/ppermute | solution.py:33
  63.2 23.7 %collective-permute-start.4 = (bf16[4,2,2,128,128]{4,3,2,1,0:T(8,128)(2,1)S(1)}, bf16[4,2,2,128,128]{4,3,2,1,0:T(8,128)(2,1)S(1)}, u32[]{:S(2)}, u32[]{:S(2)}) collective-permute-start(bf16[4,2,2,128,128]{4,3,2,1,0:T(8,128)(2,1)S(1)} %bitcast.71), channel_id=1, source_target_pairs={{240,0},{0,16},{16,32},{32,48},{48,64},{64,80},{80,96},{96,112},{1... | collective-permute-start | bytes 1572872 | tf_op jit(solution)/shard_map/ppermute | solution.py:33
  66.0 20.9 %collective-permute-start.1 = (bf16[4,2,2,128,128]{4,3,2,1,0:T(8,128)(2,1)S(1)}, bf16[4,2,2,128,128]{4,3,2,1,0:T(8,128)(2,1)S(1)}, u32[]{:S(2)}, u32[]{:S(2)}) collective-permute-start(bf16[4,2,2,128,128]{4,3,2,1,0:T(8,128)(2,1)S(1)} %bitcast.72), channel_id=1, source_target_pairs={{16,0},{32,16},{48,32},{64,48},{80,64},{96,80},{112,96},{128,112},... | collective-permute-start | bytes 1572872 | tf_op jit(solution)/shard_map/ppermute | solution.py:33
  70.4 16.6 %collective-permute-start.8 = (bf16[3,320,256]{2,1,0:T(8,128)(2,1)S(1)}, bf16[3,320,256]{2,1,0:T(8,128)(2,1)S(1)}, u32[]{:S(2)}, u32[]{:S(2)}) collective-permute-start(bf16[3,320,256]{2,1,0:T(8,128)(2,1)S(1)} %slice.54), channel_id=1, source_target_pairs={{12,0},{13,1},{14,2},{15,3},{0,4},{1,5},{2,6},{3,7},{4,8},{5,9},{6... | collective-permute-start | bytes 1474568 | tf_op jit(solution)/shard_map/ppermute | solution.py:37
  72.3 16.1 %collective-permute-start.7 = (bf16[3,320,256]{2,1,0:T(8,128)(2,1)S(1)}, bf16[3,320,256]{2,1,0:T(8,128)(2,1)}, u32[]{:S(2)}, u32[]{:S(2)}) collective-permute-start(bf16[3,320,256]{2,1,0:T(8,128)(2,1)S(1)} %slice.53), channel_id=1, source_target_pairs={{4,0},{5,1},{6,2},{7,3},{8,4},{9,5},{10,6},{11,7},{12,8},{13,9},{1... | collective-permute-start | bytes 1474568 | tf_op jit(solution)/shard_map/ppermute | solution.py:37
  76.2 10.7 %copy-start.3 = (bf16[4,2,128,128]{3,2,1,0:T(8,128)(2,1)}, bf16[4,2,128,128]{3,2,1,0:T(8,128)(2,1)S(1)}, u32[]{:S(2)}) copy-start(bf16[4,2,128,128]{3,2,1,0:T(8,128)(2,1)S(1)} %collective-permute-done.2) | copy-start | bytes 786436
  76.2 10.7 %collective-permute-start.3 = (bf16[4,2,128,128]{3,2,1,0:T(8,128)(2,1)S(1)}, bf16[4,2,128,128]{3,2,1,0:T(8,128)(2,1)S(1)}, u32[]{:S(2)}, u32[]{:S(2)}) collective-permute-start(bf16[4,2,128,128]{3,2,1,0:T(8,128)(2,1)S(1)} %get-tuple-element.49), channel_id=1, source_target_pairs={{224,0},{240,16},{0,32},{16,48},{32,64},{48,80},{64,96},{80,112},{... | collective-permute-start | bytes 786440 | tf_op jit(solution)/shard_map/ppermute | solution.py:33
  86.9 0.7 copy-start.4
  87.6 0.8 copy-start.5
  89.7 12.8 %copy-start.6 = (s32[128]{0:T(128)S(1)}, s32[128]{0:T(128)}, u32[]{:S(2)}) copy-start(s32[128]{0:T(128)} %param.11) | copy-start | bytes 1540
  92.9 20.2 %collective-permute-start.9 = (bf16[4,6,320,256]{3,2,1,0:T(8,128)(2,1)}, bf16[4,6,320,256]{3,2,1,0:T(8,128)(2,1)}, u32[]{:S(2)}, u32[]{:S(2)}) collective-permute-start(bf16[4,6,320,256]{3,2,1,0:T(8,128)(2,1)} %pad_maximum_fusion.mine_0.mine_1), channel_id=1, source_target_pairs={{0,1},{1,0},{2,3},{3,2},{4,5},{5,4},{6,7},{7,6},{8,9},{9,8},{10,11... | collective-permute-start | bytes 11796488 | tf_op jit(solution)/shard_map/ppermute | solution.py:222
  96.9 40.2 %collective-permute-start.13 = (bf16[2,2,2,4,128,128]{5,4,3,2,1,0:T(8,128)(2,1)}, bf16[2,2,2,4,128,128]{5,4,3,2,1,0:T(8,128)(2,1)S(1)}, u32[]{:S(2)}, u32[]{:S(2)}) collective-permute-start(bf16[2,2,2,4,128,128]{5,4,3,2,1,0:T(8,128)(2,1)} %fusion.3), channel_id=1, source_target_pairs={{0,2},{1,3},{2,0},{3,1},{4,6},{5,7},{6,4},{7,5},{8,10},{9,11},{10,... | collective-permute-start | bytes 3145736 | tf_op jit(solution)/shard_map/ppermute | solution.py:215
  103.6 3.2 %copy-start = (bf16[48,320,256]{2,1,0:T(8,128)(2,1)S(1)}, bf16[48,320,256]{2,1,0:T(8,128)(2,1)}, u32[]{:S(2)}) copy-start(bf16[48,320,256]{2,1,0:T(8,128)(2,1)} %all-gather.4.cloned.1.call-done) | copy-start | bytes 23592964
  113.1 26.5 %collective-permute-start.14 = (f32[960,128]{1,0:T(8,128)S(1)}, f32[960,128]{1,0:T(8,128)S(1)}, u32[]{:S(2)}, u32[]{:S(2)}) collective-permute-start(f32[960,128]{1,0:T(8,128)S(1)} %get-tuple-element.41.own), channel_id=1, source_target_pairs={{0,2},{1,3},{2,0},{3,1},{4,6},{5,7},{6,4},{7,5},{8,10},{9,11},{10,... | collective-permute-start | bytes 1474568 | tf_op jit(solution)/shard_map/ppermute | solution.py:248
  115.0 3.2 %copy-start.1 = (bf16[48,320,256]{2,1,0:T(8,128)(2,1)S(1)}, bf16[48,320,256]{2,1,0:T(8,128)(2,1)}, u32[]{:S(2)}) copy-start(bf16[48,320,256]{2,1,0:T(8,128)(2,1)} %all-gather.4.cloned.1.call-done) | copy-start | bytes 23592964
  121.4 33.8 %collective-permute-start.10 = (f32[2,4,128,128]{3,2,1,0:T(8,128)S(1)}, f32[2,4,128,128]{3,2,1,0:T(8,128)}, u32[]{:S(2)}, u32[]{:S(2)}) collective-permute-start(f32[2,4,128,128]{3,2,1,0:T(8,128)S(1)} %get-tuple-element.36), channel_id=1, source_target_pairs={{240,0},{0,16},{16,32},{32,48},{48,64},{64,80},{80,96},{96,112},{1... | collective-permute-start | bytes 1572872 | tf_op jit(solution)/shard_map/ppermute | solution.py:33
  124.9 30.3 %collective-permute-start.11 = (f32[2,4,128,128]{3,2,1,0:T(8,128)S(1)}, f32[2,4,128,128]{3,2,1,0:T(8,128)}, u32[]{:S(2)}, u32[]{:S(2)}) collective-permute-start(f32[2,4,128,128]{3,2,1,0:T(8,128)S(1)} %get-tuple-element.37), channel_id=1, source_target_pairs={{16,0},{32,16},{48,32},{64,48},{80,64},{96,80},{112,96},{128,112},... | collective-permute-start | bytes 1572872 | tf_op jit(solution)/shard_map/ppermute | solution.py:33
  132.8 22.4 %collective-permute-start.12 = (f32[4,128,128]{2,1,0:T(8,128)S(1)}, f32[4,128,128]{2,1,0:T(8,128)S(1)}, u32[]{:S(2)}, u32[]{:S(2)}) collective-permute-start(f32[4,128,128]{2,1,0:T(8,128)S(1)} %get-tuple-element.38), channel_id=1, source_target_pairs={{32,0},{48,16},{64,32},{80,48},{96,64},{112,80},{128,96},{144,112}... | collective-permute-start | bytes 786440 | tf_op jit(solution)/shard_map/ppermute | solution.py:33
  137.1 22.2 %collective-permute-start.15 = (f32[4,128,128]{2,1,0:T(8,128)S(1)}, f32[4,128,128]{2,1,0:T(8,128)}, u32[]{:S(2)}, u32[]{:S(2)}) collective-permute-start(f32[4,128,128]{2,1,0:T(8,128)S(1)} %get-tuple-element.42), channel_id=1, source_target_pairs={{224,0},{240,16},{0,32},{16,48},{32,64},{48,80},{64,96},{80,112},{... | collective-permute-start | bytes 786440 | tf_op jit(solution)/shard_map/ppermute | solution.py:33
  147.8 11.5 %all-to-all-start = ((f32[16,8,128]{2,1,0:T(8,128)}), f32[16,8,128]{2,1,0:T(8,128)S(1)}, u32[]{:S(2)}, u32[]{:S(2)}) async-start(f32[16,8,128]{2,1,0:T(8,128)} %broadcast_in_dim.7), calls=%async_computation | async-start | bytes 131072 | tf_op jit(solution)/shard_map/all_to_all | solution.py:310
  159.4 11.8 %collective-permute-start.16 = (f32[520,128]{1,0:T(8,128)S(1)}, f32[520,128]{1,0:T(8,128)S(1)}, u32[]{:S(2)}, u32[]{:S(2)}) collective-permute-start(f32[520,128]{1,0:T(8,128)S(1)} %pad_maximum_fusion.4), channel_id=1, source_target_pairs={{0,256},{16,272},{32,288},{48,304},{64,320},{80,336},{96,352},{112... | collective-permute-start | bytes 798728 | tf_op jit(solution)/shard_map/ppermute | solution.py:315
  172.4 15.7 %collective-permute-start.17 = (f32[264,128]{1,0:T(8,128)S(1)}, f32[264,128]{1,0:T(8,128)S(1)}, u32[]{:S(2)}, u32[]{:S(2)}) collective-permute-start(f32[264,128]{1,0:T(8,128)S(1)} %pad_maximum_fusion.5), channel_id=1, source_target_pairs={{0,128},{16,144},{32,160},{48,176},{64,192},{80,208},{96,224},{112... | collective-permute-start | bytes 405512 | tf_op jit(solution)/shard_map/ppermute | solution.py:324
  188.2 11.2 %collective-permute-start.18 = (f32[136,128]{1,0:T(8,128)S(1)}, f32[136,128]{1,0:T(8,128)S(1)}, u32[]{:S(2)}, u32[]{:S(2)}) collective-permute-start(f32[136,128]{1,0:T(8,128)S(1)} %pad_maximum_fusion.7), channel_id=1, source_target_pairs={{0,64},{16,80},{32,96},{48,112},{64,0},{80,16},{96,32},{112,48},{1... | collective-permute-start | bytes 208904 | tf_op jit(solution)/shard_map/ppermute | solution.py:324
  200.0 14.9 %all-to-all-start.1 = ((f32[4,8,128]{2,1,0:T(8,128)}), f32[4,8,128]{2,1,0:T(8,128)S(1)}, u32[]{:S(2)}, u32[]{:S(2)}) async-start(f32[4,8,128]{2,1,0:T(8,128)} %broadcast_in_dim.8), calls=%async_computation.1 | async-start | bytes 32768 | tf_op jit(solution)/shard_map/all_to_all | solution.py:310
Sparse Core Ops, SparseCore 0:
  10.1 71.4 all-gather.3

commit v12 on v11

--- a/solution.py
+++ b/solution.py
@@ -215,7 +215,7 @@
     partner = lax.ppermute(partner, "seq", [(i, i ^ 2) for i in range(16)])
 
     half_plus, half_minus, *_ = lax.optimization_barrier(
-        (half_plus, half_minus, plus, minus, two_x, two_g, full_w)
+        (half_plus, half_minus, plus, minus, two_x, two_g)
     )
     t_two = jnp.concatenate([half_plus, half_minus], axis=0)
     mine = jnp.stack([stack_t, t_plus, t_two, t_minus])

time: 225 us -> 220 us (0.978)
  local copies, waits for them, and re-layouts: 13.1 us -> 8.37 us
  starting transfers between devices: 97.1 us -> 101 us
  waiting for transfers between devices: 36.1 us -> 33.5 us
  other arithmetic: 13.5 us -> 10.9 us
    ppermute x2, starting transfers between devices: 18.9 us -> 25.2 us  [shards(): got = lax.ppermute(jnp.concatenate([send, terms], axis=0), 'fsdp', swap)]
    unnamed x17 -> x21, local copies, waits for them, and re-layouts: 10.6 us -> 5.9 us
    ppermute x2, waiting for transfers between devices: 7.94 us -> 5.53 us  [shards(): got = lax.ppermute(jnp.concatenate([send, terms], axis=0), 'fsdp', swap)]
  transfers between devices with their start and end apart: 22 -> 22, of which waited for: 7 -> 8; matrix products, arithmetic and copies ran while one was open for 4% -> 5% of each run, Pallas kernels for 8% -> 8%
where the time goes in v12:
time: 220 us; the launch traced here: 218 us
  starting transfers between devices  101 us (46%)
  waiting for transfers between devices  33.5 us (15%)
  blocking collectives  31.1 us (14%)
  Pallas kernels  17.7 us (8%)
  between operations  14.7 us (7%)
  other arithmetic  10.9 us (5%)
  local copies, waits for them, and re-layouts  8.37 us (4%)
    all_gather x1, blocking collectives, shards(): lax.all_gather(jnp.stack([both, other]), 'fsdp', axis=0, axis_index_group...  31.1 us
    ppermute x8, starting transfers between devices, z_shift(): return lax.ppermute(array, 'fsdp', perm)  30.4 us
    ppermute x2, starting transfers between devices, shards(): got = lax.ppermute(jnp.concatenate([send, terms], axis=0), 'fsdp', swap)  25.2 us
    ppermute x4, starting transfers between devices, y_shift(): lax.ppermute(array, 'seq', [((i + 4 * step) % 16, i) for i in range(16)])  15.3 us
    all_to_all x2, starting transfers between devices, sum_over(): lax.all_to_all(copies, axis, 0, 0, axis_index_groups=groups)  14.8 us
    ppermute x8, waiting for transfers between devices, z_shift(): return lax.ppermute(array, 'fsdp', perm)  7.69 us
    pallas_call x1, Pallas kernels, shards(): pl.pallas_call(column_kernel, out_shape=jax.ShapeDtypeStruct((8, 128), F3...  7.57 us
    all_to_all x2, waiting for transfers between devices, sum_over(): lax.all_to_all(copies, axis, 0, 0, axis_index_groups=groups)  7.42 us
  transfers between devices with their start and end apart: 22, of which 8 were waited for; matrix products, arithmetic and copies ran while one was open for 5% of the time, Pallas kernels for 8%

profile of v12, /device:TPU:24, one launch (start us, length us, event | category | flops | bytes accessed | tf_op | source)
XLA Modules:
  0.0 217.6 jit_solution(11980051480965859484)
XLA Ops:
  7.2 0.0 all-gather.4.cloned.1.call-start
  7.2 1.9 pad_maximum_fusion.3
  9.1 0.0 all-gather.4.cloned.1.call-update
  9.1 1.0 constant_dynamic-update-slice_fusion.2
  10.1 1.0 constant_dynamic-update-slice_fusion.1
  11.1 1.0 constant_dynamic-update-slice_fusion
  12.1 7.5 %collective-permute-start.6 = (bf16[6,320,256]{2,1,0:T(8,128)(2,1)S(1)}, bf16[6,320,256]{2,1,0:T(8,128)(2,1)S(1)}, u32[]{:S(2)}, u32[]{:S(2)}) collective-permute-start(bf16[6,320,256]{2,1,0:T(8,128)(2,1)S(1)} %constant_dynamic-update-slice_fusion), channel_id=1, source_target_pairs={{12,0},{13,1},{14,2},{15,3},{0,4},{1,5},{2,6},{3,7},{4,8},{5,9},{6... | collective-permute-start | bytes 2949128 | tf_op jit(solution)/shard_map/ppermute | solution.py:37
  19.7 1.9 collective-permute-start.5
  21.6 0.8 pad_maximum_fusion.8
  22.4 1.9 collective-permute-start
  24.3 5.7 %collective-permute-done = bf16[2,128,128]{2,1,0:T(8,128)(2,1)S(1)} collective-permute-done((bf16[2,128,128]{2,1,0:T(8,128)(2,1)S(1)}, bf16[2,128,128]{2,1,0:T(8,128)(2,1)S(1)}, u32[]{:S(2)}, u32[]{:S(2)}) %collective-permute-start) | collective-permute-done | bytes 65568 | tf_op jit(solution)/shard_map/ppermute | solution.py:197
  30.0 31.1 %all-gather = bf16[8,2,128,128]{3,2,1,0:T(8,128)(2,1)S(1)} all-gather(bf16[2,2,128,128]{3,2,1,0:T(8,128)(2,1)S(1)} %pad_maximum_fusion.6), channel_id=2, replica_groups={{0,64,128,192},{16,80,144,208},{32,96,160,224},{48,112,176,240},{256,32..., dimensions={0}, use_global_device_ids=true | all-gather | bytes 655360 | tf_op jit(solution)/shard_map/all_gather | solution.py:202
  61.2 1.9 collective-permute-start.2
  63.1 2.8 %collective-permute-start.4 = (bf16[4,2,2,128,128]{4,3,2,1,0:T(8,128)(2,1)S(1)}, bf16[4,2,2,128,128]{4,3,2,1,0:T(8,128)(2,1)S(1)}, u32[]{:S(2)}, u32[]{:S(2)}) collective-permute-start(bf16[4,2,2,128,128]{4,3,2,1,0:T(8,128)(2,1)S(1)} %bitcast.71), channel_id=1, source_target_pairs={{240,0},{0,16},{16,32},{32,48},{48,64},{64,80},{80,96},{96,112},{1... | collective-permute-start | bytes 1572872 | tf_op jit(solution)/shard_map/ppermute | solution.py:33
  65.9 4.3 %collective-permute-start.1 = (bf16[4,2,2,128,128]{4,3,2,1,0:T(8,128)(2,1)S(1)}, bf16[4,2,2,128,128]{4,3,2,1,0:T(8,128)(2,1)S(1)}, u32[]{:S(2)}, u32[]{:S(2)}) collective-permute-start(bf16[4,2,2,128,128]{4,3,2,1,0:T(8,128)(2,1)S(1)} %bitcast.72), channel_id=1, source_target_pairs={{16,0},{32,16},{48,32},{64,48},{80,64},{96,80},{112,96},{128,112},... | collective-permute-start | bytes 1572872 | tf_op jit(solution)/shard_map/ppermute | solution.py:33
  70.2 0.0 collective-permute-done.6
  70.2 0.0 collective-permute-done.5
  70.3 1.9 collective-permute-start.8
  72.2 3.9 %collective-permute-start.7 = (bf16[3,320,256]{2,1,0:T(8,128)(2,1)S(1)}, bf16[3,320,256]{2,1,0:T(8,128)(2,1)S(1)}, u32[]{:S(2)}, u32[]{:S(2)}) collective-permute-start(bf16[3,320,256]{2,1,0:T(8,128)(2,1)S(1)} %slice.53), channel_id=1, source_target_pairs={{4,0},{5,1},{6,2},{7,3},{8,4},{9,5},{10,6},{11,7},{12,8},{13,9},{1... | collective-permute-start | bytes 1474568 | tf_op jit(solution)/shard_map/ppermute | solution.py:37
  76.1 0.0 collective-permute-done.2
  76.1 3.6 %collective-permute-start.3 = (bf16[4,2,128,128]{3,2,1,0:T(8,128)(2,1)S(1)}, bf16[4,2,128,128]{3,2,1,0:T(8,128)(2,1)S(1)}, u32[]{:S(2)}, u32[]{:S(2)}) collective-permute-start(bf16[4,2,128,128]{3,2,1,0:T(8,128)(2,1)S(1)} %get-tuple-element.49), channel_id=1, source_target_pairs={{224,0},{240,16},{0,32},{16,48},{32,64},{48,80},{64,96},{80,112},{... | collective-permute-start | bytes 786440 | tf_op jit(solution)/shard_map/ppermute | solution.py:33
  79.8 7.2 %collective-permute-done.3 = bf16[4,2,128,128]{3,2,1,0:T(8,128)(2,1)S(1)} collective-permute-done((bf16[4,2,128,128]{3,2,1,0:T(8,128)(2,1)S(1)}, bf16[4,2,128,128]{3,2,1,0:T(8,128)(2,1)S(1)}, u32[]{:S(2)}, u32[]{:S(2)}) %collective-permute-start.3) | collective-permute-done | bytes 262176 | tf_op jit(solution)/shard_map/ppermute | solution.py:33
  87.0 0.0 collective-permute-done.4
  87.0 0.0 collective-permute-done.1
  87.0 0.0 collective-permute-done.7
  87.0 0.1 maximum_bitcast_fusion
  87.1 0.0 copy-start.8
  87.1 2.2 %pad_maximum_fusion.mine_0.mine_1 = bf16[4,6,320,256]{3,2,1,0:T(8,128)(2,1)} fusion(bf16[1,6,320,256]{3,2,1,0:T(8,128)(2,1)S(1)} %bitcast.75, bf16[1,6,320,256]{3,2,1,0:T(8,128)(2,1)S(1)} %maximum_bitcast_fusion, bf16[1,6,320,256]{3,2,1,0:T(8,128)(2,1)S(1)} %bitcast.76, bf16[1,6,320,256]{3,2,1,0:T(8,128)(2,1)S(1)} %bitcast.81), kind=kLoop, calls=%fused_computation | loop fusion | flops 5898240 | bytes 7864320 | tf_op jit(solution)/shard_map/stack | solution.py:221
  89.3 1.9 collective-permute-start.9
  91.3 1.1 fusion.3
  92.4 5.2 %collective-permute-start.13 = (bf16[2,2,2,4,128,128]{5,4,3,2,1,0:T(8,128)(2,1)}, bf16[2,2,2,4,128,128]{5,4,3,2,1,0:T(8,128)(2,1)S(1)}, u32[]{:S(2)}, u32[]{:S(2)}) collective-permute-start(bf16[2,2,2,4,128,128]{5,4,3,2,1,0:T(8,128)(2,1)} %fusion.3), channel_id=1, source_target_pairs={{0,2},{1,3},{2,0},{3,1},{4,6},{5,7},{6,4},{7,5},{8,10},{9,11},{10,... | collective-permute-start | bytes 3145736 | tf_op jit(solution)/shard_map/ppermute | solution.py:215
  97.7 0.1 stack.110.place
  97.8 1.6 pad_maximum_fusion.1.acts
  99.4 0.0 all-gather.4.cloned.1.call-done
  99.4 3.2 %copy-done = bf16[48,320,256]{2,1,0:T(8,128)(2,1)S(1)} copy-done((bf16[48,320,256]{2,1,0:T(8,128)(2,1)S(1)}, bf16[48,320,256]{2,1,0:T(8,128)(2,1)}, u32[]{:S(2)}) %copy-start) | copy-done | bytes 7864344
  102.7 6.2 %primal.1 = (bf16[128,320]{1,0:T(8,128)(2,1)S(1)}, f32[960,128]{1,0:T(8,128)S(1)}) custom-call(s32[6]{0:T(128)S(1)} %stack.110.place, bf16[4,2,2,4,128,128]{5,4,3,2,1,0:T(8,128)(2,1)S(1)} %pad_maximum_fusion.1.acts, bf16[2,4,2,3,320,256]{5,4,3,2,1,0:T(8,128)(2,1)S(1)} %bitcast.68, f32[1,128]{1,0:T(1,128)S(1)} %convert_bitcast_fusion.mask), custom_call_target="tpu_custom_call" | custom-call | flops 1006632960 | bytes 10485760 | tf_op jit(solution)/shard_map/primal/pallas_call | solution.py:224
  108.9 0.0 collective-permute-done.9.theirs_0.theirs_1
  108.9 1.9 collective-permute-start.14
  110.8 3.9 %block_sums.1 = (f32[2,4,128,128]{3,2,1,0:T(8,128)S(1)}, f32[2,4,128,128]{3,2,1,0:T(8,128)}, f32[2,4,128,128]{3,2,1,0:T(8,128)}, f32[4,128,128]{2,1,0:T(8,128)S(1)}, f32[4,128,128]{2,1,0:T(8,128)}) custom-call(s32[6]{0:T(128)S(1)} %stack.110.place, bf16[128,320]{1,0:T(8,128)(2,1)S(1)} %get-tuple-element.34.hidden, bf16[2,4,2,3,320,256]{5,4,3,2,1,0:T(8,128)(2,1)S(1)} %bitcast.69), custom_call_target="tpu_custom_call" | custom-call | flops 335544320 | bytes 5242880 | tf_op jit(solution)/shard_map/block_sums/pallas_call | solution.py:253
  114.7 3.7 %collective-permute-start.10 = (f32[2,4,128,128]{3,2,1,0:T(8,128)}, f32[2,4,128,128]{3,2,1,0:T(8,128)}, u32[]{:S(2)}, u32[]{:S(2)}) collective-permute-start(f32[2,4,128,128]{3,2,1,0:T(8,128)} %get-tuple-element.36), channel_id=1, source_target_pairs={{240,0},{0,16},{16,32},{32,48},{48,64},{64,80},{80,96},{96,112},{1... | collective-permute-start | bytes 1572872 | tf_op jit(solution)/shard_map/ppermute | solution.py:33
  118.4 7.4 %collective-permute-start.11 = (f32[2,4,128,128]{3,2,1,0:T(8,128)}, f32[2,4,128,128]{3,2,1,0:T(8,128)}, u32[]{:S(2)}, u32[]{:S(2)}) collective-permute-start(f32[2,4,128,128]{3,2,1,0:T(8,128)} %get-tuple-element.37), channel_id=1, source_target_pairs={{16,0},{32,16},{48,32},{64,48},{80,64},{96,80},{112,96},{128,112},... | collective-permute-start | bytes 1572872 | tf_op jit(solution)/shard_map/ppermute | solution.py:33
  125.8 4.4 %collective-permute-start.12 = (f32[4,128,128]{2,1,0:T(8,128)}, f32[4,128,128]{2,1,0:T(8,128)}, u32[]{:S(2)}, u32[]{:S(2)}) collective-permute-start(f32[4,128,128]{2,1,0:T(8,128)} %get-tuple-element.38), channel_id=1, source_target_pairs={{32,0},{48,16},{64,32},{80,48},{96,64},{112,80},{128,96},{144,112}... | collective-permute-start | bytes 786440 | tf_op jit(solution)/shard_map/ppermute | solution.py:33
  130.2 0.0 collective-permute-done.13.partner
  130.2 2.4 %collective-permute-start.15 = (f32[4,128,128]{2,1,0:T(8,128)S(1)}, f32[4,128,128]{2,1,0:T(8,128)}, u32[]{:S(2)}, u32[]{:S(2)}) collective-permute-start(f32[4,128,128]{2,1,0:T(8,128)S(1)} %get-tuple-element.42), channel_id=1, source_target_pairs={{224,0},{240,16},{0,32},{16,48},{32,64},{48,80},{64,96},{80,112},{... | collective-permute-start | bytes 786440 | tf_op jit(solution)/shard_map/ppermute | solution.py:33
  132.6 7.6 %column.1 = f32[8,128]{1,0:T(8,128)S(1)} custom-call(s32[6]{0:T(128)S(1)} %stack.110.place, bf16[4,2,2,4,128,128]{5,4,3,2,1,0:T(8,128)(2,1)S(1)} %pad_maximum_fusion.1.acts, bf16[2,2,2,4,128,128]{5,4,3,2,1,0:T(8,128)(2,1)S(1)} %collective-permute-done.13.partner, bf16[4,6,320,256]{3,2,1,0:T(8,128)(2,1)} %pad_maximum_fusion.mine_0.mine_1, ...), custom_call_target="tpu_custom_call" | custom-call | flops 2013265920 | bytes 12582912 | tf_op jit(solution)/shard_map/column/pallas_call | solution.py:281
  140.2 0.6 broadcast_in_dim.7
  140.8 7.4 %all-to-all-start = ((f32[16,8,128]{2,1,0:T(8,128)}), f32[16,8,128]{2,1,0:T(8,128)S(1)}, u32[]{:S(2)}, u32[]{:S(2)}) async-start(f32[16,8,128]{2,1,0:T(8,128)} %broadcast_in_dim.7), calls=%async_computation | async-start | bytes 131072 | tf_op jit(solution)/shard_map/all_to_all | solution.py:310
  148.2 0.5 collective-permute-done.12
  148.6 0.0 collective-permute-done.10
  148.6 0.0 collective-permute-done.11
  148.6 1.2 fusion.5
  149.9 2.4 %all-to-all-done = f32[16,8,128]{2,1,0:T(8,128)S(1)} async-done(((f32[16,8,128]{2,1,0:T(8,128)}), f32[16,8,128]{2,1,0:T(8,128)S(1)}, u32[]{:S(2)}, u32[]{:S(2)}) %all-to-all-start) | async-done | bytes 65568 | tf_op jit(solution)/shard_map/all_to_all | solution.py:310
  152.4 4.6 %collective-permute-start.16 = (f32[520,128]{1,0:T(8,128)S(1)}, f32[520,128]{1,0:T(8,128)S(1)}, u32[]{:S(2)}, u32[]{:S(2)}) collective-permute-start(f32[520,128]{1,0:T(8,128)S(1)} %pad_maximum_fusion.4), channel_id=1, source_target_pairs={{0,256},{16,272},{32,288},{48,304},{64,320},{80,336},{96,352},{112... | collective-permute-start | bytes 798728 | tf_op jit(solution)/shard_map/ppermute | solution.py:315
  157.1 7.1 %collective-permute-done.16 = f32[520,128]{1,0:T(8,128)S(1)} collective-permute-done((f32[520,128]{1,0:T(8,128)S(1)}, f32[520,128]{1,0:T(8,128)S(1)}, u32[]{:S(2)}, u32[]{:S(2)}) %collective-permute-start.16) | collective-permute-done | bytes 266272 | tf_op jit(solution)/shard_map/ppermute | solution.py:315
  164.2 1.3 fusion.8
  165.5 12.8 %collective-permute-start.17 = (f32[264,128]{1,0:T(8,128)S(1)}, f32[264,128]{1,0:T(8,128)S(1)}, u32[]{:S(2)}, u32[]{:S(2)}) collective-permute-start(f32[264,128]{1,0:T(8,128)S(1)} %pad_maximum_fusion.5), channel_id=1, source_target_pairs={{0,128},{16,144},{32,160},{48,176},{64,192},{80,208},{96,224},{112... | collective-permute-start | bytes 405512 | tf_op jit(solution)/shard_map/ppermute | solution.py:324
  178.4 3.3 %collective-permute-done.17 = f32[264,128]{1,0:T(8,128)S(1)} collective-permute-done((f32[264,128]{1,0:T(8,128)S(1)}, f32[264,128]{1,0:T(8,128)S(1)}, u32[]{:S(2)}, u32[]{:S(2)}) %collective-permute-start.17) | collective-permute-done | bytes 135200 | tf_op jit(solution)/shard_map/ppermute | solution.py:324
  181.7 12.5 %collective-permute-start.18 = (f32[136,128]{1,0:T(8,128)S(1)}, f32[136,128]{1,0:T(8,128)S(1)}, u32[]{:S(2)}, u32[]{:S(2)}) collective-permute-start(f32[136,128]{1,0:T(8,128)S(1)} %pad_maximum_fusion.7), channel_id=1, source_target_pairs={{0,64},{16,80},{32,96},{48,112},{64,0},{80,16},{96,32},{112,48},{1... | collective-permute-start | bytes 208904 | tf_op jit(solution)/shard_map/ppermute | solution.py:324
  194.2 2.3 %collective-permute-done.18 = f32[136,128]{1,0:T(8,128)S(1)} collective-permute-done((f32[136,128]{1,0:T(8,128)S(1)}, f32[136,128]{1,0:T(8,128)S(1)}, u32[]{:S(2)}, u32[]{:S(2)}) %collective-permute-start.18) | collective-permute-done | bytes 69664 | tf_op jit(solution)/shard_map/ppermute | solution.py:324
  196.4 0.6 broadcast_in_dim.8
  197.1 7.4 %all-to-all-start.1 = ((f32[4,8,128]{2,1,0:T(8,128)}), f32[4,8,128]{2,1,0:T(8,128)S(1)}, u32[]{:S(2)}, u32[]{:S(2)}) async-start(f32[4,8,128]{2,1,0:T(8,128)} %broadcast_in_dim.8), calls=%async_computation.1 | async-start | bytes 32768 | tf_op jit(solution)/shard_map/all_to_all | solution.py:310
  204.5 0.6 fusion.9
  205.1 5.0 %all-to-all-done.1 = f32[4,8,128]{2,1,0:T(8,128)S(1)} async-done(((f32[4,8,128]{2,1,0:T(8,128)}), f32[4,8,128]{2,1,0:T(8,128)S(1)}, u32[]{:S(2)}, u32[]{:S(2)}) %all-to-all-start.1) | async-done | bytes 16416 | tf_op jit(solution)/shard_map/all_to_all | solution.py:310
  210.1 0.7 copy.35
  (37 shorter events, 0.3 us)
Async XLA Ops:
  7.2 92.3 %all-gather.4.cloned.1.call-start = ((), (), s32[]{:S(2)}) async-start(), calls=%async_computation.2 | async-start | bytes 8355840 | tf_op jit(solution)/shard_map/all_gather | solution.py:198
  12.1 58.0 %collective-permute-start.6 = (bf16[6,320,256]{2,1,0:T(8,128)(2,1)S(1)}, bf16[6,320,256]{2,1,0:T(8,128)(2,1)S(1)}, u32[]{:S(2)}, u32[]{:S(2)}) collective-permute-start(bf16[6,320,256]{2,1,0:T(8,128)(2,1)S(1)} %constant_dynamic-update-slice_fusion), channel_id=1, source_target_pairs={{12,0},{13,1},{14,2},{15,3},{0,4},{1,5},{2,6},{3,7},{4,8},{5,9},{6... | collective-permute-start | bytes 2949128 | tf_op jit(solution)/shard_map/ppermute | solution.py:37
  19.7 50.5 %collective-permute-start.5 = (bf16[6,320,256]{2,1,0:T(8,128)(2,1)S(1)}, bf16[6,320,256]{2,1,0:T(8,128)(2,1)S(1)}, u32[]{:S(2)}, u32[]{:S(2)}) collective-permute-start(bf16[6,320,256]{2,1,0:T(8,128)(2,1)S(1)} %constant_dynamic-update-slice_fusion), channel_id=1, source_target_pairs={{4,0},{5,1},{6,2},{7,3},{8,4},{9,5},{10,6},{11,7},{12,8},{13,9},{1... | collective-permute-start | bytes 2949128 | tf_op jit(solution)/shard_map/ppermute | solution.py:37
  22.4 7.7 %collective-permute-start = (bf16[2,128,128]{2,1,0:T(8,128)(2,1)S(1)}, bf16[2,128,128]{2,1,0:T(8,128)(2,1)S(1)}, u32[]{:S(2)}, u32[]{:S(2)}) collective-permute-start(bf16[2,128,128]{2,1,0:T(8,128)(2,1)S(1)} %pad_maximum_fusion.8), channel_id=1, source_target_pairs={{0,256},{16,272},{32,288},{48,304},{64,320},{80,336},{96,352},{112... | collective-permute-start | bytes 196616 | tf_op jit(solution)/shard_map/ppermute | solution.py:197
  61.1 30.2 %copy-start.3 = (bf16[8,2,128,128]{3,2,1,0:T(8,128)(2,1)}, bf16[8,2,128,128]{3,2,1,0:T(8,128)(2,1)S(1)}, u32[]{:S(2)}) copy-start(bf16[8,2,128,128]{3,2,1,0:T(8,128)(2,1)S(1)} %all-gather) | copy-start | bytes 1572868
  61.2 15.0 %collective-permute-start.2 = (bf16[4,2,128,128]{3,2,1,0:T(8,128)(2,1)S(1)}, bf16[4,2,128,128]{3,2,1,0:T(8,128)(2,1)S(1)}, u32[]{:S(2)}, u32[]{:S(2)}) collective-permute-start(bf16[4,2,128,128]{3,2,1,0:T(8,128)(2,1)S(1)} %get-tuple-element.48), channel_id=1, source_target_pairs={{32,0},{48,16},{64,32},{80,48},{96,64},{112,80},{128,96},{144,112}... | collective-permute-start | bytes 786440 | tf_op jit(solution)/shard_map/ppermute | solution.py:33
  63.1 23.9 %collective-permute-start.4 = (bf16[4,2,2,128,128]{4,3,2,1,0:T(8,128)(2,1)S(1)}, bf16[4,2,2,128,128]{4,3,2,1,0:T(8,128)(2,1)S(1)}, u32[]{:S(2)}, u32[]{:S(2)}) collective-permute-start(bf16[4,2,2,128,128]{4,3,2,1,0:T(8,128)(2,1)S(1)} %bitcast.71), channel_id=1, source_target_pairs={{240,0},{0,16},{16,32},{32,48},{48,64},{64,80},{80,96},{96,112},{1... | collective-permute-start | bytes 1572872 | tf_op jit(solution)/shard_map/ppermute | solution.py:33
  65.9 21.1 %collective-permute-start.1 = (bf16[4,2,2,128,128]{4,3,2,1,0:T(8,128)(2,1)S(1)}, bf16[4,2,2,128,128]{4,3,2,1,0:T(8,128)(2,1)S(1)}, u32[]{:S(2)}, u32[]{:S(2)}) collective-permute-start(bf16[4,2,2,128,128]{4,3,2,1,0:T(8,128)(2,1)S(1)} %bitcast.72), channel_id=1, source_target_pairs={{16,0},{32,16},{48,32},{64,48},{80,64},{96,80},{112,96},{128,112},... | collective-permute-start | bytes 1572872 | tf_op jit(solution)/shard_map/ppermute | solution.py:33
  70.3 16.7 %collective-permute-start.8 = (bf16[3,320,256]{2,1,0:T(8,128)(2,1)S(1)}, bf16[3,320,256]{2,1,0:T(8,128)(2,1)S(1)}, u32[]{:S(2)}, u32[]{:S(2)}) collective-permute-start(bf16[3,320,256]{2,1,0:T(8,128)(2,1)S(1)} %slice.54), channel_id=1, source_target_pairs={{12,0},{13,1},{14,2},{15,3},{0,4},{1,5},{2,6},{3,7},{4,8},{5,9},{6... | collective-permute-start | bytes 1474568 | tf_op jit(solution)/shard_map/ppermute | solution.py:37
  72.2 14.8 %collective-permute-start.7 = (bf16[3,320,256]{2,1,0:T(8,128)(2,1)S(1)}, bf16[3,320,256]{2,1,0:T(8,128)(2,1)S(1)}, u32[]{:S(2)}, u32[]{:S(2)}) collective-permute-start(bf16[3,320,256]{2,1,0:T(8,128)(2,1)S(1)} %slice.53), channel_id=1, source_target_pairs={{4,0},{5,1},{6,2},{7,3},{8,4},{9,5},{10,6},{11,7},{12,8},{13,9},{1... | collective-permute-start | bytes 1474568 | tf_op jit(solution)/shard_map/ppermute | solution.py:37
  76.1 15.2 %copy-start.6 = (bf16[4,2,128,128]{3,2,1,0:T(8,128)(2,1)}, bf16[4,2,128,128]{3,2,1,0:T(8,128)(2,1)S(1)}, u32[]{:S(2)}) copy-start(bf16[4,2,128,128]{3,2,1,0:T(8,128)(2,1)S(1)} %collective-permute-done.2) | copy-start | bytes 786436
  76.1 10.8 %collective-permute-start.3 = (bf16[4,2,128,128]{3,2,1,0:T(8,128)(2,1)S(1)}, bf16[4,2,128,128]{3,2,1,0:T(8,128)(2,1)S(1)}, u32[]{:S(2)}, u32[]{:S(2)}) collective-permute-start(bf16[4,2,128,128]{3,2,1,0:T(8,128)(2,1)S(1)} %get-tuple-element.49), channel_id=1, source_target_pairs={{224,0},{240,16},{0,32},{16,48},{32,64},{48,80},{64,96},{80,112},{... | collective-permute-start | bytes 786440 | tf_op jit(solution)/shard_map/ppermute | solution.py:33
  87.0 4.3 %copy-start.7 = (bf16[4,2,128,128]{3,2,1,0:T(8,128)(2,1)}, bf16[4,2,128,128]{3,2,1,0:T(8,128)(2,1)S(1)}, u32[]{:S(2)}) copy-start(bf16[4,2,128,128]{3,2,1,0:T(8,128)(2,1)S(1)} %collective-permute-done.3) | copy-start | bytes 786436
  87.0 4.3 %copy-start.4 = (bf16[4,2,2,128,128]{4,3,2,1,0:T(8,128)(2,1)}, bf16[4,2,2,128,128]{4,3,2,1,0:T(8,128)(2,1)S(1)}, u32[]{:S(2)}) copy-start(bf16[4,2,2,128,128]{4,3,2,1,0:T(8,128)(2,1)S(1)} %collective-permute-done.4) | copy-start | bytes 1572868
  87.0 4.3 %copy-start.5 = (bf16[4,2,2,128,128]{4,3,2,1,0:T(8,128)(2,1)}, bf16[4,2,2,128,128]{4,3,2,1,0:T(8,128)(2,1)S(1)}, u32[]{:S(2)}) copy-start(bf16[4,2,2,128,128]{4,3,2,1,0:T(8,128)(2,1)S(1)} %collective-permute-done.1) | copy-start | bytes 1572868
  87.1 10.6 %copy-start.8 = (s32[128]{0:T(128)S(1)}, s32[128]{0:T(128)}, u32[]{:S(2)}) copy-start(s32[128]{0:T(128)} %param.11) | copy-start | bytes 1540
  89.3 19.5 %collective-permute-start.9 = (bf16[4,6,320,256]{3,2,1,0:T(8,128)(2,1)}, bf16[4,6,320,256]{3,2,1,0:T(8,128)(2,1)}, u32[]{:S(2)}, u32[]{:S(2)}) collective-permute-start(bf16[4,6,320,256]{3,2,1,0:T(8,128)(2,1)} %pad_maximum_fusion.mine_0.mine_1), channel_id=1, source_target_pairs={{0,1},{1,0},{2,3},{3,2},{4,5},{5,4},{6,7},{7,6},{8,9},{9,8},{10,11... | collective-permute-start | bytes 11796488 | tf_op jit(solution)/shard_map/ppermute | solution.py:222
  92.4 37.8 %collective-permute-start.13 = (bf16[2,2,2,4,128,128]{5,4,3,2,1,0:T(8,128)(2,1)}, bf16[2,2,2,4,128,128]{5,4,3,2,1,0:T(8,128)(2,1)S(1)}, u32[]{:S(2)}, u32[]{:S(2)}) collective-permute-start(bf16[2,2,2,4,128,128]{5,4,3,2,1,0:T(8,128)(2,1)} %fusion.3), channel_id=1, source_target_pairs={{0,2},{1,3},{2,0},{3,1},{4,6},{5,7},{6,4},{7,5},{8,10},{9,11},{10,... | collective-permute-start | bytes 3145736 | tf_op jit(solution)/shard_map/ppermute | solution.py:215
  99.4 3.2 %copy-start = (bf16[48,320,256]{2,1,0:T(8,128)(2,1)S(1)}, bf16[48,320,256]{2,1,0:T(8,128)(2,1)}, u32[]{:S(2)}) copy-start(bf16[48,320,256]{2,1,0:T(8,128)(2,1)} %all-gather.4.cloned.1.call-done) | copy-start | bytes 23592964
  102.7 8.1 %copy-start.1 = (bf16[48,320,256]{2,1,0:T(8,128)(2,1)S(1)}, bf16[48,320,256]{2,1,0:T(8,128)(2,1)}, u32[]{:S(2)}) copy-start(bf16[48,320,256]{2,1,0:T(8,128)(2,1)} %all-gather.4.cloned.1.call-done) | copy-start | bytes 23592964
  108.9 23.7 %collective-permute-start.14 = (f32[960,128]{1,0:T(8,128)S(1)}, f32[960,128]{1,0:T(8,128)S(1)}, u32[]{:S(2)}, u32[]{:S(2)}) collective-permute-start(f32[960,128]{1,0:T(8,128)S(1)} %get-tuple-element.41.own), channel_id=1, source_target_pairs={{0,2},{1,3},{2,0},{3,1},{4,6},{5,7},{6,4},{7,5},{8,10},{9,11},{10,... | collective-permute-start | bytes 1474568 | tf_op jit(solution)/shard_map/ppermute | solution.py:248
  114.7 25.4 %copy-start.2 = (f32[2,4,128,128]{3,2,1,0:T(8,128)}, f32[2,4,128,128]{3,2,1,0:T(8,128)S(1)}, u32[]{:S(2)}) copy-start(f32[2,4,128,128]{3,2,1,0:T(8,128)S(1)} %get-tuple-element.35) | copy-start | bytes 1572868
  114.7 33.9 %collective-permute-start.10 = (f32[2,4,128,128]{3,2,1,0:T(8,128)}, f32[2,4,128,128]{3,2,1,0:T(8,128)}, u32[]{:S(2)}, u32[]{:S(2)}) collective-permute-start(f32[2,4,128,128]{3,2,1,0:T(8,128)} %get-tuple-element.36), channel_id=1, source_target_pairs={{240,0},{0,16},{16,32},{32,48},{48,64},{64,80},{80,96},{96,112},{1... | collective-permute-start | bytes 1572872 | tf_op jit(solution)/shard_map/ppermute | solution.py:33
  118.4 30.3 %collective-permute-start.11 = (f32[2,4,128,128]{3,2,1,0:T(8,128)}, f32[2,4,128,128]{3,2,1,0:T(8,128)}, u32[]{:S(2)}, u32[]{:S(2)}) collective-permute-start(f32[2,4,128,128]{3,2,1,0:T(8,128)} %get-tuple-element.37), channel_id=1, source_target_pairs={{16,0},{32,16},{48,32},{64,48},{80,64},{96,80},{112,96},{128,112},... | collective-permute-start | bytes 1572872 | tf_op jit(solution)/shard_map/ppermute | solution.py:33
  125.8 22.8 %collective-permute-start.12 = (f32[4,128,128]{2,1,0:T(8,128)}, f32[4,128,128]{2,1,0:T(8,128)}, u32[]{:S(2)}, u32[]{:S(2)}) collective-permute-start(f32[4,128,128]{2,1,0:T(8,128)} %get-tuple-element.38), channel_id=1, source_target_pairs={{32,0},{48,16},{64,32},{80,48},{96,64},{112,80},{128,96},{144,112}... | collective-permute-start | bytes 786440 | tf_op jit(solution)/shard_map/ppermute | solution.py:33
  130.2 22.1 %collective-permute-start.15 = (f32[4,128,128]{2,1,0:T(8,128)S(1)}, f32[4,128,128]{2,1,0:T(8,128)}, u32[]{:S(2)}, u32[]{:S(2)}) collective-permute-start(f32[4,128,128]{2,1,0:T(8,128)S(1)} %get-tuple-element.42), channel_id=1, source_target_pairs={{224,0},{240,16},{0,32},{16,48},{32,64},{48,80},{64,96},{80,112},{... | collective-permute-start | bytes 786440 | tf_op jit(solution)/shard_map/ppermute | solution.py:33
  140.8 11.5 %all-to-all-start = ((f32[16,8,128]{2,1,0:T(8,128)}), f32[16,8,128]{2,1,0:T(8,128)S(1)}, u32[]{:S(2)}, u32[]{:S(2)}) async-start(f32[16,8,128]{2,1,0:T(8,128)} %broadcast_in_dim.7), calls=%async_computation | async-start | bytes 131072 | tf_op jit(solution)/shard_map/all_to_all | solution.py:310
  152.4 11.8 %collective-permute-start.16 = (f32[520,128]{1,0:T(8,128)S(1)}, f32[520,128]{1,0:T(8,128)S(1)}, u32[]{:S(2)}, u32[]{:S(2)}) collective-permute-start(f32[520,128]{1,0:T(8,128)S(1)} %pad_maximum_fusion.4), channel_id=1, source_target_pairs={{0,256},{16,272},{32,288},{48,304},{64,320},{80,336},{96,352},{112... | collective-permute-start | bytes 798728 | tf_op jit(solution)/shard_map/ppermute | solution.py:315
  165.5 16.1 %collective-permute-start.17 = (f32[264,128]{1,0:T(8,128)S(1)}, f32[264,128]{1,0:T(8,128)S(1)}, u32[]{:S(2)}, u32[]{:S(2)}) collective-permute-start(f32[264,128]{1,0:T(8,128)S(1)} %pad_maximum_fusion.5), channel_id=1, source_target_pairs={{0,128},{16,144},{32,160},{48,176},{64,192},{80,208},{96,224},{112... | collective-permute-start | bytes 405512 | tf_op jit(solution)/shard_map/ppermute | solution.py:324
  181.7 14.7 %collective-permute-start.18 = (f32[136,128]{1,0:T(8,128)S(1)}, f32[136,128]{1,0:T(8,128)S(1)}, u32[]{:S(2)}, u32[]{:S(2)}) collective-permute-start(f32[136,128]{1,0:T(8,128)S(1)} %pad_maximum_fusion.7), channel_id=1, source_target_pairs={{0,64},{16,80},{32,96},{48,112},{64,0},{80,16},{96,32},{112,48},{1... | collective-permute-start | bytes 208904 | tf_op jit(solution)/shard_map/ppermute | solution.py:324
  197.1 13.0 %all-to-all-start.1 = ((f32[4,8,128]{2,1,0:T(8,128)}), f32[4,8,128]{2,1,0:T(8,128)S(1)}, u32[]{:S(2)}, u32[]{:S(2)}) async-start(f32[4,8,128]{2,1,0:T(8,128)} %broadcast_in_dim.8), calls=%async_computation.1 | async-start | bytes 32768 | tf_op jit(solution)/shard_map/all_to_all | solution.py:310
Sparse Core Ops, SparseCore 0:
  10.1 71.4 all-gather.3
